TPU v7x, 32 devices: a whole 2x2x4 slice. The times are simulated.
32 devices in a mesh: seq: 2 (over y), seg: 16 (over z, x, core).
Axes of the slice: x: 2, y: 2, z: 4, core: 2. Of those that a mesh axis runs over, the one named last changes fastest.
Arguments:
- tokens: bfloat16 [32, 512, 512], P('seg', 'seq'), may hold values from -6 to 6
- memory: bfloat16 [32, 64, 512], P('seg', 'seq'), may hold values from -6 to 6
- lengths: int32 [32, 8], P('seg'), may hold values from 1 to 384, 512 in all within a row
- attn_gain: float32 [512], replicated, may hold values from 0.25 to 1.75
- query_weight: bfloat16 [512, 512], replicated, may hold values from -0.25 to 0.25
- pair_weight: bfloat16 [512, 1024], replicated, may hold values from -0.25 to 0.25
- out_weight: bfloat16 [512, 512], replicated, may hold values from -0.75 to 0.75
- ffn_gain: float32 [512], replicated, may hold values from 0.25 to 1.75
- ffn_in: bfloat16 [512, 2048], replicated, may hold values from -0.25 to 0.25
- ffn_out: bfloat16 [2048, 512], replicated, may hold values from -0.125 to 0.125
- write_query: bfloat16 [512, 512], replicated, may hold values from -0.25 to 0.25
- write_pair: bfloat16 [512, 1024], replicated, may hold values from -0.25 to 0.25
- write_out: bfloat16 [512, 512], replicated, may hold values from -1 to 1
- write_gate: bfloat16 [512, 512], replicated, may hold values from -0.25 to 0.25
- write_gain: float32 [512], replicated, may hold values from 0.25 to 1.75
- out_cotangent: bfloat16 [32, 512, 512], P('seg', 'seq'), may hold values from -6 to 6
- memory_cotangent: bfloat16 [32, 64, 512], P('seg', 'seq'), may hold values from -6 to 6
Outputs:
- out: bfloat16 [32, 512, 512], P('seg', 'seq')
- new_memory: bfloat16 [32, 64, 512], P('seg', 'seq')
- grad_tokens: float32 [32, 512, 512], P('seg', 'seq')
- grad_memory: float32 [32, 64, 512], P('seg', 'seq')
- grad_attn_gain: float32 [512], P('seg')
- grad_query_weight: float32 [512, 512], P('seg')
- grad_pair_weight: float32 [512, 1024], P('seg')
- grad_out_weight: float32 [512, 512], P('seg')
- grad_ffn_gain: float32 [512], P('seg')
- grad_ffn_in: float32 [512, 2048], P('seg')
- grad_ffn_out: float32 [2048, 512], P('seg')
- grad_write_query: float32 [512, 512], P('seg')
- grad_write_pair: float32 [512, 1024], P('seg')
- grad_write_out: float32 [512, 512], P('seg')
- grad_write_gate: float32 [512, 512], P('seg')
- grad_write_gain: float32 [512], P('seg')
Inputs may be any that keep to these rules, and one draw needn't show every extreme that they name: Each segment's 8 lengths sum to 512, and its longest document has exactly 384 tokens.
All inputs are finite; a program needn't handle non-finite values.
Results may differ from a plain program's by a relative error of at most 0.03.
Values may be sent and summed in bfloat16 or wider, within the bound.
No kernel may reach another device: no remote copies, remote signals or barrier semaphores. Data moves between devices by JAX's collectives and lax.ppermute only.
A program may use at most 128 MiB of HBM per device.

v0:
```python
import jax
import jax.numpy as jnp
from jax import lax
from jax.sharding import PartitionSpec as P

H = 8


EPSILON = 1e-05
MASKED_SCORE = -1e30


def passed_along(x, axis, by):
    peers = lax.axis_size(axis)
    pairs = [(i, i + by) for i in range(peers) if 0 <= i + by < peers]
    return lax.ppermute(x, axis, pairs)


def combined_all(value, axis, join):
    pieces = jax.tree.map(lambda part: lax.all_gather(part, axis), value)
    head = jax.tree.map(lambda part: part[0], pieces)
    tail = jax.tree.map(lambda part: part[1:], pieces)
    running, _ = lax.scan(lambda running, slab: (join(running, slab), None), head, tail)
    return running


def norm_rows(values, scales):
    average = jnp.mean(values, -1, keepdims=True)
    centred = values - average
    spread = jnp.mean(centred * centred, -1, keepdims=True)
    return centred * lax.rsqrt(spread + EPSILON) * scales


def product(left, weight):
    return jnp.einsum("sad,de->sae", left, weight, preferred_element_type=jnp.float32)


def back_product(grad, weight):
    return jnp.einsum("sae,de->sad", grad, weight, preferred_element_type=jnp.float32)


def weight_term(left, grad):
    return jnp.einsum("sad,sae->de", left, grad, preferred_element_type=jnp.float32)


def divide_into_heads(values, head_count):
    return values.reshape(values.shape[:-1] + (head_count, values.shape[-1] // head_count))


def merge_heads(values):
    return values.reshape(values.shape[:-2] + (values.shape[-2] * values.shape[-1],))


def doc_index(positions, bounds):
    return jnp.sum((positions[:, :, None] >= bounds[:, None, :]).astype(jnp.int32), -1)


def combine_totals(left_pair, right_pair):
    top_value = jnp.maximum(left_pair[0], right_pair[0])
    total = left_pair[1] * jnp.exp(left_pair[0] - top_value) + right_pair[1] * jnp.exp(
        right_pair[0] - top_value
    )
    return (top_value, total)


def shards(
    tokens,
    memory,
    lengths,
    attn_gain,
    query_weight,
    pair_weight,
    out_weight,
    ffn_gain,
    ffn_in,
    ffn_out,
    write_query,
    write_pair,
    write_out,
    write_gate,
    write_gain,
    out_cotangent,
    memory_cotangent,
):
    seg_count, row_count, hidden_width = tokens.shape
    half_slots = memory.shape[1]
    head_count = H
    score_scale = (hidden_width // head_count) ** (-0.5)
    seq_rank = lax.axis_index("seq")
    tok_float = tokens.astype(jnp.float32)
    mem_own = memory.astype(jnp.float32)
    mem_all = lax.all_gather(memory, "seq", axis=1, tiled=True)
    memory_entries = mem_all.shape[1]
    bounds = jnp.cumsum(lengths, axis=1)
    local_idx = jnp.arange(row_count, dtype=jnp.int32)
    local_pos = jnp.broadcast_to(seq_rank * row_count + local_idx, (seg_count, row_count))
    earlier_pos = local_pos - row_count
    local_doc = doc_index(local_pos, bounds)
    earlier_doc = doc_index(earlier_pos, bounds)
    causal = (local_idx[None, :] <= local_idx[:, None])[None]
    same_local = (local_doc[:, :, None] == local_doc[:, None, :]) & causal
    same_earlier = (local_doc[:, :, None] == earlier_doc[:, None, :]) & (earlier_pos >= 0)[
        :, None, :
    ]
    allowed = jnp.concatenate(
        [jnp.ones((seg_count, row_count, memory_entries), dtype=bool), same_earlier, same_local], 2
    )

    def attend_inputs():
        normed_x = norm_rows(tok_float, attn_gain).astype(jnp.bfloat16)
        normed_m = norm_rows(mem_all.astype(jnp.float32), attn_gain).astype(jnp.bfloat16)
        query = product(normed_x, query_weight).astype(jnp.bfloat16)
        pair_x = product(normed_x, pair_weight).astype(jnp.bfloat16)
        pair_m = product(normed_m, pair_weight).astype(jnp.bfloat16)
        pair_e = passed_along(pair_x, "seq", 1)
        pairs = jnp.concatenate([pair_m, pair_e, pair_x], 1)
        return (normed_x, normed_m, query, pairs)

    def scores_of(query, pairs):
        keys = divide_into_heads(pairs[..., :hidden_width], head_count)
        raw = (
            jnp.einsum(
                "srhd,skhd->shrk",
                divide_into_heads(query, head_count),
                keys,
                preferred_element_type=jnp.float32,
            )
            * score_scale
        )
        return jnp.where(allowed[:, None], raw, MASKED_SCORE)

    normed_x, normed_m, query, pairs = attend_inputs()
    masked = scores_of(query, pairs)
    top_score = jnp.max(masked, -1, keepdims=True)
    log_total = top_score + jnp.log(jnp.sum(jnp.exp(masked - top_score), -1, keepdims=True))
    probs = jnp.exp(masked - log_total).astype(jnp.bfloat16)
    mixed = jnp.einsum(
        "shrk,skhd->srhd",
        probs,
        divide_into_heads(pairs[..., hidden_width:], head_count),
        preferred_element_type=jnp.float32,
    )
    mixed = merge_heads(mixed).astype(jnp.bfloat16)
    resid = tok_float + product(mixed, out_weight)
    normed2 = norm_rows(resid, ffn_gain).astype(jnp.bfloat16)
    inner = product(normed2, ffn_in)
    act = jax.nn.gelu(inner).astype(jnp.bfloat16)
    out_low = (resid + product(act, ffn_out)).astype(jnp.bfloat16)
    writer_query_weight = product(normed_m, write_query).astype(jnp.bfloat16)
    writer_pair_weight = product(out_low, write_pair).astype(jnp.bfloat16)
    wkeys = divide_into_heads(writer_pair_weight[..., :hidden_width], head_count)
    wvalues = divide_into_heads(writer_pair_weight[..., hidden_width:], head_count)
    wraw = (
        jnp.einsum(
            "smhd,srhd->shmr",
            divide_into_heads(writer_query_weight, head_count),
            wkeys,
            preferred_element_type=jnp.float32,
        )
        * score_scale
    )
    wtop = jnp.max(wraw, -1)
    wtotal = jnp.sum(jnp.exp(wraw - wtop[..., None]), -1)
    glob_top, glob_total = combined_all((wtop, wtotal), "seq", combine_totals)
    wprob_f = jnp.exp(wraw - (glob_top + jnp.log(glob_total))[..., None])
    writer_probabilities = wprob_f.astype(jnp.bfloat16)
    wpart = merge_heads(
        jnp.einsum(
            "shmr,srhd->smhd", writer_probabilities, wvalues, preferred_element_type=jnp.float32
        )
    )
    writer_mixed_heads = lax.psum_scatter(
        wpart.astype(jnp.bfloat16), "seq", scatter_dimension=1, tiled=True
    )
    update = product(writer_mixed_heads, write_out)
    update_low = update.astype(jnp.bfloat16)
    gate = jax.nn.sigmoid(product(update_low, write_gate))
    blended = mem_own + gate * update
    new_memory = norm_rows(blended, write_gain).astype(jnp.bfloat16)
    _, pull_write = jax.vjp(norm_rows, blended, write_gain)
    d_blend, grad_write_gain = pull_write(memory_cotangent.astype(jnp.float32))
    d_gate_pre = (d_blend * update * gate * (1.0 - gate)).astype(jnp.bfloat16)
    grad_write_gate = weight_term(update_low, d_gate_pre)
    d_update = (d_blend * gate + back_product(d_gate_pre, write_gate)).astype(jnp.bfloat16)
    grad_write_out = weight_term(writer_mixed_heads, d_update)
    d_wmixed = back_product(d_update, write_out).astype(jnp.bfloat16)
    d_wmixed_all = divide_into_heads(
        lax.all_gather(d_wmixed, "seq", axis=1, tiled=True), head_count
    )
    d_wprob = jnp.einsum(
        "smhd,srhd->shmr", d_wmixed_all, wvalues, preferred_element_type=jnp.float32
    )
    wrow_part = jnp.sum(wprob_f * d_wprob, -1)
    wrow = lax.psum(wrow_part, "seq")
    d_wraw = (wprob_f * (d_wprob - wrow[..., None])).astype(jnp.bfloat16)
    d_wquery_part = (
        merge_heads(
            jnp.einsum("shmr,srhd->smhd", d_wraw, wkeys, preferred_element_type=jnp.float32)
        )
        * score_scale
    )
    d_wkey = (
        jnp.einsum(
            "shmr,smhd->srhd",
            d_wraw,
            divide_into_heads(writer_query_weight, head_count),
            preferred_element_type=jnp.float32,
        )
        * score_scale
    )
    d_wvalue = jnp.einsum(
        "shmr,smhd->srhd", writer_probabilities, d_wmixed_all, preferred_element_type=jnp.float32
    )
    d_wpair = jnp.concatenate([merge_heads(d_wkey), merge_heads(d_wvalue)], -1).astype(jnp.bfloat16)
    grad_write_pair = weight_term(out_low, d_wpair)
    d_out = out_cotangent.astype(jnp.float32) + back_product(d_wpair, write_pair)
    d_branch = d_out.astype(jnp.bfloat16)
    grad_ffn_out = weight_term(act, d_branch)
    d_act = lax.optimization_barrier(back_product(d_branch, ffn_out).astype(jnp.bfloat16)).astype(
        jnp.float32
    )
    _, pull_gelu = jax.vjp(jax.nn.gelu, inner)
    d_inner = pull_gelu(d_act)[0].astype(jnp.bfloat16)
    grad_ffn_in = weight_term(normed2, d_inner)
    _, pull_second = jax.vjp(norm_rows, resid, ffn_gain)
    d_resid_norm, grad_ffn_gain = pull_second(back_product(d_inner, ffn_in))
    d_resid = d_out + d_resid_norm
    d_attn = d_resid.astype(jnp.bfloat16)
    grad_out_weight = weight_term(mixed, d_attn)
    d_mixed = back_product(d_attn, out_weight).astype(jnp.bfloat16)
    normed_x2, normed_m2, query2, pairs2 = attend_inputs()
    masked2 = scores_of(query2, pairs2)
    probs_f = jnp.exp(masked2 - log_total)
    probs2 = probs_f.astype(jnp.bfloat16)
    keys2 = divide_into_heads(pairs2[..., :hidden_width], head_count)
    values2 = divide_into_heads(pairs2[..., hidden_width:], head_count)
    d_mixed_heads = divide_into_heads(d_mixed, head_count)
    d_prob = jnp.einsum(
        "srhd,skhd->shrk", d_mixed_heads, values2, preferred_element_type=jnp.float32
    )
    row_total = jnp.sum(probs_f * d_prob, -1, keepdims=True)
    d_raw = (probs_f * (d_prob - row_total)).astype(jnp.bfloat16)
    d_query = (
        merge_heads(jnp.einsum("shrk,skhd->srhd", d_raw, keys2, preferred_element_type=jnp.float32))
        * score_scale
    ).astype(jnp.bfloat16)
    d_key = (
        jnp.einsum(
            "shrk,srhd->skhd",
            d_raw,
            divide_into_heads(query2, head_count),
            preferred_element_type=jnp.float32,
        )
        * score_scale
    )
    d_value = jnp.einsum(
        "shrk,srhd->skhd", probs2, d_mixed_heads, preferred_element_type=jnp.float32
    )
    d_pairs = jnp.concatenate([merge_heads(d_key), merge_heads(d_value)], -1)
    d_pair_m_part = d_pairs[:, :memory_entries]
    d_pair_e = d_pairs[:, memory_entries : memory_entries + row_count]
    d_pair_x = d_pairs[:, memory_entries + row_count :]
    d_pair_x = (
        d_pair_x + passed_along(d_pair_e.astype(jnp.bfloat16), "seq", -1).astype(d_pair_e.dtype)
    ).astype(jnp.bfloat16)
    d_pair_m, d_wquery = (
        lax.psum_scatter(
            d_pair_m_part.astype(jnp.bfloat16), "seq", scatter_dimension=1, tiled=True
        ).astype(jnp.float32),
        lax.psum_scatter(
            d_wquery_part.astype(jnp.bfloat16), "seq", scatter_dimension=1, tiled=True
        ).astype(jnp.float32),
    )
    d_pair_m = d_pair_m.astype(jnp.bfloat16)
    d_wquery = d_wquery.astype(jnp.bfloat16)
    normed_m_own = lax.dynamic_slice_in_dim(normed_m2, seq_rank * half_slots, half_slots, 1)
    grad_query_weight = weight_term(normed_x2, d_query)
    grad_pair_weight = weight_term(normed_x2, d_pair_x) + weight_term(normed_m_own, d_pair_m)
    grad_write_query = weight_term(normed_m_own, d_wquery)
    d_normed_x = back_product(d_query, query_weight) + back_product(d_pair_x, pair_weight)
    d_normed_m = back_product(d_pair_m, pair_weight) + back_product(d_wquery, write_query)
    _, pull_tokens = jax.vjp(norm_rows, tok_float, attn_gain)
    d_tok_norm, gain_from_tokens = pull_tokens(d_normed_x)
    _, pull_memory = jax.vjp(norm_rows, mem_own, attn_gain)
    d_mem_norm, gain_from_memory = pull_memory(d_normed_m)
    grad_tokens = d_resid + d_tok_norm
    grad_memory = d_blend + d_mem_norm
    grad_attn_gain = gain_from_tokens + gain_from_memory
    terms = (
        grad_attn_gain,
        grad_query_weight,
        grad_pair_weight,
        grad_out_weight,
        grad_ffn_gain,
        grad_ffn_in,
        grad_ffn_out,
        grad_write_query,
        grad_write_pair,
        grad_write_out,
        grad_write_gate,
        grad_write_gain,
    )
    summed = lax.psum(
        (
            terms[0],
            terms[1],
            terms[2],
            terms[3],
            terms[4],
            terms[5],
            terms[6],
            terms[7],
            terms[8],
            terms[9],
            terms[10],
            terms[11],
        ),
        ("seq", "seg"),
    )
    seg_place = lax.axis_index("seg")
    seg_total = lax.axis_size("seg")
    shares = tuple(
        (
            lax.dynamic_slice_in_dim(
                member, seg_place * (member.shape[0] // seg_total), member.shape[0] // seg_total, 0
            )
            for member in summed
        )
    )
    return (
        out_low,
        new_memory,
        grad_tokens,
        grad_memory,
        shares[0],
        shares[1],
        shares[2],
        shares[3],
        shares[4],
        shares[5],
        shares[6],
        shares[7],
        shares[8],
        shares[9],
        shares[10],
        shares[11],
    )


def solution(mesh):
    in_specs = (
        P("seg", "seq", None),
        P("seg", "seq", None),
        P("seg", None),
        P(),
        P(),
        P(),
        P(),
        P(),
        P(),
        P(),
        P(),
        P(),
        P(),
        P(),
        P(),
        P("seg", "seq", None),
        P("seg", "seq", None),
    )
    out_specs = (
        P("seg", "seq", None),
        P("seg", "seq", None),
        P("seg", "seq", None),
        P("seg", "seq", None),
        P("seg"),
        P("seg", None),
        P("seg", None),
        P("seg", None),
        P("seg"),
        P("seg", None),
        P("seg", None),
        P("seg", None),
        P("seg", None),
        P("seg", None),
        P("seg", None),
        P("seg"),
    )
    return jax.shard_map(shards, mesh=mesh, in_specs=in_specs, out_specs=out_specs, check_vma=False)
```

profile of v0, /device:TPU:0, one launch (start us, length us, event | category | flops | bytes accessed | tf_op | source)
XLA Modules:
  0.0 563.8 jit_solution(6504653160239984064)
XLA Ops:
  10.0 3.1 convolution_convert_fusion.2
  13.2 5.8 %collective-permute-start = (bf16[2,256,1024]{2,1,0:T(8,128)(2,1)}, bf16[2,256,1024]{2,1,0:T(8,128)(2,1)}, u32[]{:S(2)}, u32[]{:S(2)}) collective-permute-start(bf16[2,256,1024]{2,1,0:T(8,128)(2,1)} %convolution_convert_fusion.2), channel_id=1, source_target_pairs={{0,16},{1,17},{2,18},{3,19},{4,20},{5,21},{6,22},{7,23},{8,24},{9,... | collective-permute-start | bytes 3145736 | tf_op jit(solution)/shard_map/ppermute | solution.py:16
  19.0 23.0 %all_gather.18 = bf16[2,64,512]{2,1,0:T(8,128)(2,1)S(1)} all-gather(bf16[2,32,512]{2,1,0:T(8,128)(2,1)S(1)} %copy-done.43), channel_id=1, replica_groups=mesh['seq'=2,'seg'=16] {'seq'}, dimensions={1}, use_global_device_ids=true | all-gather | bytes 196608 | tf_op jit(solution)/shard_map/all_gather | solution.py:92
  49.9 1.8 pad_maximum_fusion.1
  53.3 2.6 copy.111
  55.8 2.4 copy.113
  58.3 3.0 fusion
  61.3 1.9 exponential_reduce_fusion
  63.3 1.7 copy-done.2
  64.9 2.3 convolution_convert_fusion.6
  76.4 4.8 all-gather
  81.6 4.4 all-gather.1
  85.9 2.1 convolution_convert_fusion.8
  88.1 1.7 copy.118
  90.3 11.7 %reduce-scatter.4.cloned.1.call-done = bf16[2,32,512]{2,1,0:T(8,128)(2,1)} async-done(((bf16[2,64,512]{2,1,0:T(8,128)(2,1)}), bf16[2,32,512]{2,1,0:T(8,128)(2,1)}) %reduce-scatter.4.cloned.1.call-update) | async-done | bytes 65552 | tf_op jit(solution)/shard_map/reduce_scatter | solution.py:172
  103.3 2.0 fusion.116
  110.8 5.0 all_gather.23
  115.9 1.7 copy.144
  117.6 2.2 convolution_convert_fusion.4
  119.8 3.1 multiply_reduce_fusion.3
  122.8 2.1 copy.123
  124.9 5.7 %psum.91 = f32[2,8,64]{2,1,0:T(8,128)} all-reduce(f32[2,8,64]{2,1,0:T(8,128)} %get-tuple-element.81), channel_id=1, replica_groups=mesh['seq'=2,'seg'=16] {'seq'}, use_global_device_ids=true, to_apply=%region_19.20 | all-reduce | flops 1024 | bytes 8192 | tf_op jit(solution)/shard_map/psum | solution.py:194
  134.4 2.5 convolution_add_fusion.1
  136.9 3.3 convolution_convert_fusion
  140.2 3.0 fusion.5
  143.2 2.1 multiply_reduce_fusion.1
  149.7 7.8 %fusion.108 = f32[2,8,64,576]{3,2,1,0:T(8,128)} fusion(bf16[2,256,8,64]{1,3,2,0:T(8,128)(2,1)S(1)} %bitcast.174, f32[2,8,256,576]{2,3,1,0:T(8,128)} %copy-done.2, f32[2,8,256]{2,1,0:T(8,128)S(1)} %log_add_fusion, pred[2,256,576]{1,2,0:T(8,128)(4,1)S(1)} %pad_add_fusion), kind=kOutput, calls=%fused_computation.215 | convolution fusion | flops 311427072 | bytes 12632064 | tf_op jit(solution)/shard_map/shrk,srhd->skhd/dot_general | solution.py:256
  157.5 11.0 %multiply_reduce_fusion = (f32[2,8,256]{2,1,0:T(8,128)}, f32[2,8,256,576]{2,3,1,0:T(8,128)}) fusion(f32[2,8,256,576]{2,3,1,0:T(8,128)} %copy-done.2, f32[2,8,256]{2,1,0:T(8,128)S(1)} %log_add_fusion, pred[2,256,576]{1,2,0:T(8,128)(4,1)S(1)} %pad_add_fusion, bf16[2,256,8,64]{1,3,2,0:T(8,128)(2,1)} %bitcast.175, bf16[2,576,8,64]{1,3,2,0:T(8,128)(2,1)S(1)} %bitcast.161), kind=kOutput, calls=%fused_computation.1 | convolution fusion | flops 313782272 | bytes 20905984 | tf_op jit(solution)/shard_map/srhd,skhd->shrk/dot_general | solution.py:238
  169.5 11.3 %multiply_convert_fusion = bf16[2,8,256,576]{2,3,1,0:T(8,128)(2,1)} fusion(f32[2,8,256,576]{2,3,1,0:T(8,128)} %get-tuple-element.85, f32[2,8,256,576]{2,3,1,0:T(8,128)} %copy-done.2, f32[2,8,256]{2,1,0:T(8,128)} %get-tuple-element.84, f32[2,8,256]{2,1,0:T(8,128)S(1)} %log_add_fusion, pred[2,256,576]{1,2,0:T(8,128)(4,1)S(1)} %pad_add_fusion), kind=kLoop, calls=%fused_computation | loop fusion | flops 14155776 | bytes 23920640 | tf_op jit(solution)/shard_map/convert_element_type | solution.py:242
  180.8 5.5 convolution_multiply_fusion
  188.8 3.8 convolution_bitcast_fusion
  192.7 2.1 convolution_bitcast_fusion.2
  194.7 3.2 copy.127
  198.0 3.2 copy.126
  202.0 2.8 fusion.2
  207.3 1.7 convolution_bitcast_fusion.7
  214.0 5.0 convolution_bitcast_fusion.1
  219.0 2.2 convolution_bitcast_fusion.5
  221.1 9.6 %reduce-scatter.6.cloned.1.call-done = bf16[2,32,1024]{2,1,0:T(8,128)(2,1)} async-done(((bf16[2,64,1024]{2,1,0:T(8,128)(2,1)}), bf16[2,32,1024]{2,1,0:T(8,128)(2,1)}) %reduce-scatter.6.cloned.1.call-update) | async-done | bytes 131088 | tf_op jit(solution)/shard_map/reduce_scatter | solution.py:267
  232.1 2.8 collective-permute-done.1
  234.9 2.2 fusion.15
  237.1 2.2 bitcast_add_fusion
  243.9 2.1 fusion.45
  247.6 41.4 %all-reduce = (f32[512]{0:T(512)S(1)}, f32[512]{0:T(512)S(1)}, f32[512]{0:T(512)S(1)}) all-reduce(f32[512]{0:T(512)S(1)} %add.212, f32[512]{0:T(512)S(1)} %copy-done.77, f32[512]{0:T(512)S(1)} %copy-done.76), channel_id=1, replica_groups=mesh['seq'=2,'seg'=16] {'seq','seg'}, use_global_device_ids=true, to_apply=%region_33.34 | all-reduce | flops 1536 | bytes 12288 | tf_op jit(solution)/shard_map/psum | solution.py:303
  290.8 3.4 add_add_fusion.2
  294.2 249.0 %all-reduce.4.cloned.1.call-done = (f32[512,512]{1,0:T(8,128)}, f32[512,1024]{1,0:T(8,128)}, f32[512,512]{1,0:T(8,128)}, f32[512,2048]{1,0:T(8,128)}, f32[2048,5...) async-done(((f32[512,512]{1,0:T(8,128)}, f32[512,1024]{1,0:T(8,128)}, f32[512,512]{1,0:T(8,128)}, ...) | async-done | bytes 17825808 | tf_op jit(solution)/shard_map/psum | solution.py:303
  547.7 1.7 constant_dynamic-slice_fusion.5
  555.4 1.7 constant_dynamic-slice_fusion.4
  (264 shorter events, 68.0 us)
Async XLA Ops:
  7.2 61.0 %copy-start = (bf16[512,2048]{1,0:T(8,128)(2,1)S(1)}, bf16[512,2048]{1,0:T(8,128)(2,1)}, u32[]{:S(2)}) copy-start(bf16[512,2048]{1,0:T(8,128)(2,1)} %param.25) | copy-start | bytes 6291460
  7.2 35.3 %copy-start.6 = (bf16[2,256,512]{2,1,0:T(8,128)(2,1)S(1)}, bf16[2,256,512]{2,1,0:T(8,128)(2,1)}, u32[]{:S(2)}) copy-start(bf16[2,256,512]{2,1,0:T(8,128)(2,1)} %param.17) | copy-start | bytes 1572868
  7.2 35.1 %copy-start.55 = (f32[512]{0:T(512)S(1)}, f32[512]{0:T(512)}, u32[]{:S(2)}) copy-start(f32[512]{0:T(512)} %param.20) | copy-start | bytes 6148
  7.2 11.8 %copy-start.43 = (bf16[2,32,512]{2,1,0:T(8,128)(2,1)S(1)}, bf16[2,32,512]{2,1,0:T(8,128)(2,1)}, u32[]{:S(2)}) copy-start(bf16[2,32,512]{2,1,0:T(8,128)(2,1)} %param.18) | copy-start | bytes 196612
  7.2 35.3 %copy-start.50 = (bf16[512,512]{1,0:T(8,128)(2,1)S(1)}, bf16[512,512]{1,0:T(8,128)(2,1)}, u32[]{:S(2)}) copy-start(bf16[512,512]{1,0:T(8,128)(2,1)} %param.21) | copy-start | bytes 1572868
  7.2 94.8 %reduce-scatter.4.cloned.1.call-start = ((), (), s32[]{:S(2)}) async-start(), calls=%async_computation.3 | async-start | bytes 196608 | tf_op jit(solution)/shard_map/reduce_scatter | solution.py:172
  10.0 37.4 %copy-start.64 = (f32[2,256]{1,0:T(2,128)}, f32[2,256]{1,0:T(2,128)S(1)}, u32[]{:S(2)}) copy-start(f32[2,256]{1,0:T(2,128)S(1)} %fusion.44) | copy-start | bytes 6148
  10.0 37.4 %copy-start.60 = (f32[2,256]{1,0:T(2,128)}, f32[2,256]{1,0:T(2,128)S(1)}, u32[]{:S(2)}) copy-start(f32[2,256]{1,0:T(2,128)S(1)} %fusion.102) | copy-start | bytes 6148
  10.0 37.4 %copy-start.78 = (s32[2,8]{1,0:T(2,128)S(1)}, s32[2,8]{1,0:T(2,128)}, u32[]{:S(2)}) copy-start(s32[2,8]{1,0:T(2,128)} %param.19) | copy-start | bytes 196
  13.2 36.7 %collective-permute-start = (bf16[2,256,1024]{2,1,0:T(8,128)(2,1)}, bf16[2,256,1024]{2,1,0:T(8,128)(2,1)}, u32[]{:S(2)}, u32[]{:S(2)}) collective-permute-start(bf16[2,256,1024]{2,1,0:T(8,128)(2,1)} %convolution_convert_fusion.2), channel_id=1, source_target_pairs={{0,16},{1,17},{2,18},{3,19},{4,20},{5,21},{6,22},{7,23},{8,24},{9,... | collective-permute-start | bytes 3145736 | tf_op jit(solution)/shard_map/ppermute | solution.py:16
  42.5 5.5 copy-start.39
  45.1 13.2 %copy-start.25 = (bf16[2,256,512]{1,2,0:T(8,128)(2,1)}, bf16[2,256,512]{1,2,0:T(8,128)(2,1)S(1)}, u32[]{:S(2)}) copy-start(bf16[2,256,512]{1,2,0:T(8,128)(2,1)S(1)} %copy.112) | copy-start | bytes 1572868
  73.8 31.5 %copy-start.59 = (f32[512]{0:T(512)S(1)}, f32[512]{0:T(512)}, u32[]{:S(2)}) copy-start(f32[512]{0:T(512)} %param.31) | copy-start | bytes 6148
  89.8 129.2 %reduce-scatter.8.cloned.1.call-start = ((), (), s32[]{:S(2)}) async-start(), calls=%async_computation.5 | async-start | bytes 196608 | tf_op jit(solution)/shard_map/reduce_scatter | solution.py:270
  103.3 6.1 %copy-start.41 = (f32[2,32,512]{2,1,0:T(8,128)}, f32[2,32,512]{2,1,0:T(8,128)S(1)}, u32[]{:S(2)}) copy-start(f32[2,32,512]{2,1,0:T(8,128)S(1)} %fusion.57) | copy-start | bytes 393220
  105.3 5.5 copy-start.56
  105.3 5.5 copy-start.62
  134.4 5.8 %copy-start.10 = (f32[2,256,2048]{2,1,0:T(8,128)S(1)}, f32[2,256,2048]{2,1,0:T(8,128)}, u32[]{:S(2)}) copy-start(f32[2,256,2048]{2,1,0:T(8,128)} %copy-done.9) | copy-start | bytes 12582916
  136.9 9.0 %copy-start.27 = (f32[2,256,512]{2,1,0:T(8,128)}, f32[2,256,512]{2,1,0:T(8,128)S(1)}, u32[]{:S(2)}) copy-start(f32[2,256,512]{2,1,0:T(8,128)S(1)} %convolution_add_fusion.1) | copy-start | bytes 3145732
  145.8 11.7 %copy-start.16 = (f32[2,256,512]{2,1,0:T(8,128)}, f32[2,256,512]{2,1,0:T(8,128)S(1)}, u32[]{:S(2)}) copy-start(f32[2,256,512]{2,1,0:T(8,128)S(1)} %get-tuple-element.58) | copy-start | bytes 3145732
  145.9 11.7 %copy-start.68 = (f32[2,256]{1,0:T(2,128)}, f32[2,256]{1,0:T(2,128)S(1)}, u32[]{:S(2)}) copy-start(f32[2,256]{1,0:T(2,128)S(1)} %negate_multiply_fusion.1) | copy-start | bytes 6148
  149.7 7.8 %copy-start.19 = (bf16[2,576,512]{1,2,0:T(8,128)(2,1)S(1)}, bf16[2,576,512]{1,2,0:T(8,128)(2,1)}, u32[]{:S(2)}) copy-start(bf16[2,576,512]{1,2,0:T(8,128)(2,1)} %copy.111) | copy-start | bytes 3538948
  157.5 11.0 %copy-start.20 = (bf16[2,256,512]{1,2,0:T(8,128)(2,1)S(1)}, bf16[2,256,512]{1,2,0:T(8,128)(2,1)}, u32[]{:S(2)}) copy-start(bf16[2,256,512]{1,2,0:T(8,128)(2,1)} %copy.116) | copy-start | bytes 1572868
  157.5 11.0 %copy-start.22 = (bf16[2,8,64,256]{3,2,1,0:T(8,128)(2,1)S(1)}, bf16[2,8,64,256]{3,2,1,0:T(8,128)(2,1)}, u32[]{:S(2)}) copy-start(bf16[2,8,64,256]{3,2,1,0:T(8,128)(2,1)} %copy-done.21) | copy-start | bytes 1572868
  169.5 11.3 %copy-start.26 = (bf16[2,256,512]{1,2,0:T(8,128)(2,1)S(1)}, bf16[2,256,512]{1,2,0:T(8,128)(2,1)}, u32[]{:S(2)}) copy-start(bf16[2,256,512]{1,2,0:T(8,128)(2,1)} %copy-done.25) | copy-start | bytes 1572868
  180.8 5.5 copy-start.3
  180.8 5.5 copy-start.12
  188.8 18.4 %copy-start.33 = (bf16[2,8,64,256]{3,2,1,0:T(8,128)(2,1)}, bf16[2,8,64,256]{3,2,1,0:T(8,128)(2,1)S(1)}, u32[]{:S(2)}) copy-start(bf16[2,8,64,256]{3,2,1,0:T(8,128)(2,1)S(1)} %fusion.30) | copy-start | bytes 1572868
  194.7 6.4 %copy-start.45 = (bf16[2,8,64,64]{3,2,1,0:T(8,128)(2,1)S(1)}, bf16[2,8,64,64]{3,2,1,0:T(8,128)(2,1)}, u32[]{:S(2)}) copy-start(bf16[2,8,64,64]{3,2,1,0:T(8,128)(2,1)} %fusion.35) | copy-start | bytes 393220
  201.9 5.4 copy-start.7
  201.9 7.0 %copy-start.24 = (bf16[2,256,512]{2,1,0:T(8,128)(2,1)S(1)}, bf16[2,256,512]{2,1,0:T(8,128)(2,1)}, u32[]{:S(2)}) copy-start(bf16[2,256,512]{2,1,0:T(8,128)(2,1)} %copy-done.23) | copy-start | bytes 1572868
  202.0 28.8 %reduce-scatter.6.cloned.1.call-start = ((), (), s32[]{:S(2)}) async-start(), calls=%async_computation.4 | async-start | bytes 393216 | tf_op jit(solution)/shard_map/reduce_scatter | solution.py:267
  202.0 7.0 %copy-start.38 = (bf16[2,8,64,256]{3,2,1,0:T(8,128)(2,1)S(1)}, bf16[2,8,64,256]{3,2,1,0:T(8,128)(2,1)}, u32[]{:S(2)}) copy-start(bf16[2,8,64,256]{3,2,1,0:T(8,128)(2,1)} %copy-done.37) | copy-start | bytes 1572868
  204.8 6.4 %copy-start.36 = (f32[2,32,512]{2,1,0:T(8,128)S(1)}, f32[2,32,512]{2,1,0:T(8,128)}, u32[]{:S(2)}) copy-start(f32[2,32,512]{2,1,0:T(8,128)} %copy-done.35) | copy-start | bytes 393220
  204.8 6.4 %copy-start.42 = (f32[2,32,512]{2,1,0:T(8,128)S(1)}, f32[2,32,512]{2,1,0:T(8,128)}, u32[]{:S(2)}) copy-start(f32[2,32,512]{2,1,0:T(8,128)} %copy-done.41) | copy-start | bytes 393220
  204.9 6.4 %copy-start.44 = (bf16[2,32,512]{2,1,0:T(8,128)(2,1)S(1)}, bf16[2,32,512]{2,1,0:T(8,128)(2,1)}, u32[]{:S(2)}) copy-start(bf16[2,32,512]{2,1,0:T(8,128)(2,1)} %param.33) | copy-start | bytes 196612
  204.9 6.4 %copy-start.57 = (f32[2,32,512]{2,1,0:T(8,128)S(1)}, f32[2,32,512]{2,1,0:T(8,128)}, u32[]{:S(2)}) copy-start(f32[2,32,512]{2,1,0:T(8,128)} %copy-done.56) | copy-start | bytes 393220
  204.9 6.4 %copy-start.63 = (f32[2,32]{1,0:T(2,128)S(1)}, f32[2,32]{1,0:T(2,128)}, u32[]{:S(2)}) copy-start(f32[2,32]{1,0:T(2,128)} %copy-done.62) | copy-start | bytes 772
  204.9 6.4 %copy-start.71 = (f32[2,32]{1,0:T(2,128)S(1)}, f32[2,32]{1,0:T(2,128)}, u32[]{:S(2)}) copy-start(f32[2,32]{1,0:T(2,128)} %copy-done.70) | copy-start | bytes 772
  204.9 6.4 %copy-start.73 = (f32[2,32]{1,0:T(2,128)S(1)}, f32[2,32]{1,0:T(2,128)}, u32[]{:S(2)}) copy-start(f32[2,32]{1,0:T(2,128)} %copy-done.72) | copy-start | bytes 772
  204.9 6.4 %copy-start.75 = (f32[2,32]{1,0:T(2,128)S(1)}, f32[2,32]{1,0:T(2,128)}, u32[]{:S(2)}) copy-start(f32[2,32]{1,0:T(2,128)} %copy-done.74) | copy-start | bytes 772
  204.9 7.8 %copy-start.52 = (bf16[2,32,512]{2,1,0:T(8,128)(2,1)S(1)}, bf16[2,32,512]{2,1,0:T(8,128)(2,1)}, u32[]{:S(2)}) copy-start(bf16[2,32,512]{2,1,0:T(8,128)(2,1)} %copy-done.51) | copy-start | bytes 196612
  204.9 7.8 %copy-start.54 = (bf16[2,32,512]{2,1,0:T(8,128)(2,1)S(1)}, bf16[2,32,512]{2,1,0:T(8,128)(2,1)}, u32[]{:S(2)}) copy-start(bf16[2,32,512]{2,1,0:T(8,128)(2,1)} %reduce-scatter.4.cloned.1.call-done) | copy-start | bytes 196612
  206.0 29.0 %collective-permute-start.1 = (bf16[2,256,1024]{2,1,0:T(8,128)(2,1)}, bf16[2,256,1024]{2,1,0:T(8,128)(2,1)}, u32[]{:S(2)}, u32[]{:S(2)}) collective-permute-start(bf16[2,256,1024]{2,1,0:T(8,128)(2,1)} %slice.63), channel_id=1, source_target_pairs={{16,0},{17,1},{18,2},{19,3},{20,4},{21,5},{22,6},{23,7},{24,8},{25... | collective-permute-start | bytes 3145736 | tf_op jit(solution)/shard_map/ppermute | solution.py:16
  211.2 332.0 %all-reduce.4.cloned.1.call-start = ((), (), s32[]{:S(2)}) async-start(), calls=%async_computation.6 | async-start | bytes 35651584 | tf_op jit(solution)/shard_map/psum | solution.py:303
  212.7 6.3 %copy-start.40 = (bf16[2,64,512]{2,1,0:T(8,128)(2,1)S(1)}, bf16[2,64,512]{2,1,0:T(8,128)(2,1)}, u32[]{:S(2)}) copy-start(bf16[2,64,512]{2,1,0:T(8,128)(2,1)} %copy-done.39) | copy-start | bytes 393220
  242.5 48.3 %copy-start.69 = (f32[2,256]{1,0:T(2,128)S(1)}, f32[2,256]{1,0:T(2,128)}, u32[]{:S(2)}) copy-start(f32[2,256]{1,0:T(2,128)} %copy-done.68) | copy-start | bytes 6148
  246.1 311.0 %copy-start.1 = (bf16[512,2048]{1,0:T(8,128)(2,1)S(1)}, bf16[512,2048]{1,0:T(8,128)(2,1)}, u32[]{:S(2)}) copy-start(bf16[512,2048]{1,0:T(8,128)(2,1)} %param.25) | copy-start | bytes 6291460
  (42 other events, 115.1 us)
Sparse Core Ops, SparseCore 0:
  89.9 12.0 reduce-scatter.3
  202.0 11.2 reduce-scatter.7
  216.1 14.5 reduce-scatter.5
  239.6 303.6 all-reduce.3
where the time goes:
time: 569 us; the launch traced here: 564 us
  waiting for transfers between devices  273 us (48%)
  matrix products  95.4 us (17%)
  blocking collectives  84.3 us (15%)
  local copies, waits for them, and re-layouts  50.4 us (9%)
  other arithmetic  37.5 us (7%)
  between operations  15.1 us (3%)
  starting transfers between devices  7.69 us (1%)
    psum x1, waiting for transfers between devices, shards(): lax.psum((terms[0], terms[1], terms[2], terms[3], terms[4], terms[5], ter...  249 us
    psum x1, blocking collectives, shards(): lax.psum((terms[0], terms[1], terms[2], terms[3], terms[4], terms[5], ter...  41.4 us
    all_gather x1, blocking collectives, shards(): mem_all = lax.all_gather(memory, 'seq', axis=1, tiled=True)  23 us
    dot_general x10, matrix products, weight_term(): jnp.einsum('sad,sae->de', left, grad, preferred_element_type=jnp.float32)  22.4 us
    dot_general x10, matrix products, back_product(): jnp.einsum('sae,de->sad', grad, weight, preferred_element_type=jnp.float32)  16.3 us
    dynamic_slice x12, local copies, waits for them, and re-layouts, shards(): lax.dynamic_slice_in_dim(member, seg_place * (member.shape[0] // seg_tota...  15.6 us
    dot_general x10, matrix products, product(): jnp.einsum('sad,de->sae', left, weight, preferred_element_type=jnp.float32)  14.9 us
    reduce_scatter x1, waiting for transfers between devices, shards(): lax.psum_scatter(wpart.astype(jnp.bfloat16), 'seq', scatter_dimension=1,...  11.7 us
  transfers between devices with their start and end apart: 6, of which 4 were waited for; matrix products, arithmetic and copies ran while one was open for 7% of the time, Pallas kernels for 0%

commit v1 on v0

v1 whole, which is shorter than its diff:
```python
import functools

import jax
import jax.numpy as jnp
from jax import lax
from jax.experimental import pallas as pl
from jax.experimental.pallas import tpu as pltpu
from jax.sharding import PartitionSpec as P

H = 8
GROUPS = 16
EPSILON = 1e-05
MASKED = -1e30
F32 = jnp.float32
BF16 = jnp.bfloat16
VMEM_LIMIT = 56 * 1024 * 1024


def dot(a, b, ca=1, cb=0):
    return lax.dot_general(a, b, (((ca,), (cb,)), ((), ())), preferred_element_type=F32)


def norm_parts(v):
    centred = v - jnp.mean(v, -1, keepdims=True)
    r = lax.rsqrt(jnp.mean(centred * centred, -1, keepdims=True) + EPSILON)
    return centred * r, r


def norm_back(dy, xhat, r, gain):
    dx = dy * gain
    m1 = jnp.mean(dx, -1, keepdims=True)
    m2 = jnp.mean(dx * xhat, -1, keepdims=True)
    return r * (dx - m1 - xhat * m2), jnp.sum(dy * xhat, 0, keepdims=True)


def whole_rows(pair_ref, recv_ref, start, half, y, dst_ref):
    own = pl.multiple_of(y * half, half)
    other = pl.multiple_of((1 - y) * half, half)
    dst_ref[pl.ds(own, half), :] = pair_ref[y].astype(dst_ref.dtype)
    dst_ref[pl.ds(other, half), :] = recv_ref[start : start + half, :].astype(dst_ref.dtype)


def emit(grad, keep_ref, send_ref, offset, c):
    rows = grad.shape[0] // GROUPS
    g = grad.reshape(GROUPS // 2, 2, rows, grad.shape[1])
    zero, one = g[:, 0], g[:, 1]
    first = c == 0
    keep_ref[:, offset : offset + rows, :] = jnp.where(first, zero, one).astype(BF16)
    send_ref[:, offset : offset + rows, :] = jnp.where(first, one, zero).astype(BF16)


def lane_low(shape):
    return lax.broadcasted_iota(jnp.int32, shape, 1) < 64


def stacked_heads(block):
    low = lane_low(block.shape)
    zero = jnp.zeros_like(block)
    return jnp.concatenate([jnp.where(low, block, zero), jnp.where(low, zero, block)], 0)


def unstacked_heads(block):
    rows = block.shape[0] // 2
    top, bottom = block[:rows], block[rows:]
    return jnp.where(lane_low(top.shape), top, bottom)


def forward_kernel(
    place, lengths, tokens, memory, recv, attn_gain, query_weight, pair_weight, out_weight,
    ffn_gain, ffn_in, ffn_out, write_query,
    x_ref, mem_ref, nall_ref, qs_ref, kall_ref, vall_ref, p0, p1, p2, p3,
    mixed_ref, resid_ref, n2_ref, act_ref, dg_ref, out_ref, send_ref, wqs_ref,
):
    y = place[0]
    half, width = tokens.shape[1], tokens.shape[2]
    mhalf = memory.shape[1]
    slots = 2 * mhalf
    whole_rows(tokens, recv, 0, half, y, x_ref)
    whole_rows(memory, recv, half, mhalf, y, mem_ref)
    gain = attn_gain[...]
    xhat, _ = norm_parts(x_ref[...])
    nx = (xhat * gain).astype(BF16)
    mhat, _ = norm_parts(mem_ref[...])
    nm = (mhat * gain).astype(BF16)
    nall_ref[0:slots, :] = nm
    nall_ref[slots:128, :] = jnp.zeros((128 - slots, width), BF16)
    nall_ref[128:, :] = nx
    qs_ref[...] = (dot(nx, query_weight[...]) * 0.125).astype(BF16)
    nall = nall_ref[...]
    kall_ref[...] = dot(nall, pair_weight[:, :width]).astype(BF16)
    vall_ref[...] = dot(nall, pair_weight[:, width:]).astype(BF16)
    wqs_ref[...] = (dot(nm, write_query[...]) * 0.125).astype(BF16)
    bounds = []
    total = 0
    for k in range(lengths.shape[1]):
        total = total + lengths[y, k]
        bounds.append(total)
    rows = 2 * half
    pos_c = lax.broadcasted_iota(jnp.int32, (1, rows), 1)
    doc_c = sum([(pos_c >= b).astype(jnp.int32) for b in bounds])
    mem_bias = jnp.where(
        lax.broadcasted_iota(jnp.int32, (128, 128), 1) < slots, 0.0, MASKED
    ).astype(F32)
    for i, p_ref in enumerate((p0, p1, p2, p3)):
        w = 128 * (i + 2)
        cols = w - 128
        pos_r = lax.broadcasted_iota(jnp.int32, (128, 1), 0) + 128 * i
        doc_r = sum([(pos_r >= b).astype(jnp.int32) for b in bounds])
        ok = (doc_r == doc_c[:, :cols]) & (pos_c[:, :cols] <= pos_r)
        bias = jnp.concatenate([mem_bias, jnp.where(ok, 0.0, MASKED).astype(F32)], 1)
        for p in range(H // 2):
            lanes = slice(128 * p, 128 * p + 128)
            q01 = stacked_heads(qs_ref[128 * i : 128 * i + 128, lanes])
            s = dot(q01, kall_ref[0:w, lanes], 1, 1)
            s = (s.reshape(2, 128, w) + bias[None]).reshape(256, w)
            e = jnp.exp(s - jnp.max(s, -1, keepdims=True))
            pr = (e * (1.0 / jnp.sum(e, -1, keepdims=True))).astype(BF16)
            p_ref[p] = pr
            o = dot(pr, vall_ref[0:w, lanes])
            mixed_ref[128 * i : 128 * i + 128, lanes] = unstacked_heads(o).astype(BF16)
    resid = x_ref[...] + dot(mixed_ref[...], out_weight[...])
    resid_ref[...] = resid
    rhat, _ = norm_parts(resid)
    n2 = (rhat * ffn_gain[...]).astype(BF16)
    n2_ref[...] = n2
    ff = ffn_in.shape[1]
    k0 = 0.7978845608028654
    for j in range(ff // 512):
        cols = slice(512 * j, 512 * j + 512)
        v = dot(n2, ffn_in[:, cols])
        v2 = v * v
        t = jnp.tanh(k0 * (v + 0.044715 * (v2 * v)))
        h = 0.5 * (1.0 + t)
        act_ref[:, cols] = (v * h).astype(BF16)
        dg = h + (0.5 * v) * (1.0 - t * t) * (k0 + (3.0 * 0.044715 * k0) * v2)
        dg_ref[:, cols] = dg.astype(BF16)
    out = (resid_ref[...] + dot(act_ref[...], ffn_out[...])).astype(BF16)
    out_ref[...] = out
    send_ref[...] = out_ref[pl.ds(pl.multiple_of((1 - y) * half, half), half), :]


def head_mask(rows_per, width):
    shape = (H * rows_per, width)
    row_head = lax.broadcasted_iota(jnp.int32, shape, 0) // rows_per
    col_head = lax.broadcasted_iota(jnp.int32, shape, 1) // (width // H)
    return row_head == col_head


def block_diagonal(v, mask):
    return jnp.where(mask, jnp.concatenate([v] * H, 0), jnp.zeros((), v.dtype))


def diagonal_blocks(v, mask):
    rows = v.shape[0] // H
    v = jnp.where(mask, v, 0.0)
    return jnp.sum(v.reshape(H, rows, v.shape[1]), 0)


def write_kernel(
    place, out, wqs, mem, nall, memory_cotangent, recv, write_pair, write_out, write_gate,
    write_gain,
    keep_ref, send_ref, dwpair_ref, dwquery_ref, dblend_ref, newmem_ref, gain_ref, mc_ref,
):
    y, c = place[0], place[1]
    slots, width = wqs.shape
    mhalf = slots // 2
    whole_rows(memory_cotangent, recv, recv.shape[0] - mhalf, mhalf, y, mc_ref)
    o = out[...]
    wk = dot(o, write_pair[:, :width]).astype(BF16)
    wv = dot(o, write_pair[:, width:]).astype(BF16)
    mask = head_mask(slots, width)
    qbd = block_diagonal(wqs[...], mask)
    s = dot(qbd, wk, 1, 1)
    e = jnp.exp(s - jnp.max(s, -1, keepdims=True))
    pf = e * (1.0 / jnp.sum(e, -1, keepdims=True))
    pb = pf.astype(BF16)
    wmixed = diagonal_blocks(dot(pb, wv), mask).astype(BF16)
    update = dot(wmixed, write_out[...])
    update_low = update.astype(BF16)
    gate = jax.nn.sigmoid(dot(update_low, write_gate[...]))
    blended = mem[...] + gate * update
    bhat, br = norm_parts(blended)
    newmem_ref[...] = (bhat * write_gain[...]).astype(BF16)
    d_blend, d_gain = norm_back(mc_ref[...], bhat, br, write_gain[...])
    gain_ref[...] = d_gain
    dblend_ref[...] = d_blend
    d_gate_pre = (d_blend * update * gate * (1.0 - gate)).astype(BF16)
    d_update = (d_blend * gate + dot(d_gate_pre, write_gate[...], 1, 1)).astype(BF16)
    d_wmixed = dot(d_update, write_out[...], 1, 1).astype(BF16)
    emit(dot(update_low, d_gate_pre, 0, 0), keep_ref, send_ref, 128, c)
    emit(dot(wmixed, d_update, 0, 0), keep_ref, send_ref, 96, c)
    dbd = block_diagonal(d_wmixed, mask)
    dp = dot(dbd, wv, 1, 1)
    row = jnp.sum(pf * dp, -1, keepdims=True)
    ds = (pf * (dp - row)).astype(BF16)
    d_wquery = (diagonal_blocks(dot(ds, wk), mask) * 0.125).astype(BF16)
    dwquery_ref[...] = d_wquery
    dwk = dot(ds, qbd, 0, 0).astype(BF16)
    dwv = dot(pb, dbd, 0, 0).astype(BF16)
    dwpair_ref[:, :width] = dwk
    dwpair_ref[:, width:] = dwv
    emit(dot(nall[0:slots, :], d_wquery, 0, 0), keep_ref, send_ref, 0, c)
    emit(dot(o, dwk, 0, 0), keep_ref, send_ref, 32, c)
    emit(dot(o, dwv, 0, 0), keep_ref, send_ref, 64, c)


def ffn_back_kernel(
    place, dwpair, out_cotangent, recv, write_pair, act, dg, n2, resid, ffn_in, ffn_out, ffn_gain,
    keep_ref, send_ref, dresid_ref, gain_ref, dout_ref,
):
    y, c = place[0], place[1]
    half, width = out_cotangent.shape[1:]
    ff = ffn_in.shape[1]
    whole_rows(out_cotangent, recv, 0, half, y, dout_ref)
    d_out = dout_ref[...] + dot(dwpair[...], write_pair[...], 1, 1)
    dout_ref[...] = d_out
    d_branch = d_out.astype(BF16)
    rows = width // GROUPS
    deep = ff // GROUPS
    base = (ff // 512) * rows
    n2v = n2[...]
    total = None
    for j in range(ff // 512):
        cols = slice(512 * j, 512 * j + 512)
        d_act = dot(d_branch, ffn_out[cols, :], 1, 1).astype(BF16)
        d_inner = (d_act.astype(F32) * dg[:, cols].astype(F32)).astype(BF16)
        term = dot(d_inner, ffn_in[:, cols], 1, 1)
        total = term if total is None else total + term
        emit(dot(n2v, d_inner, 0, 0), keep_ref, send_ref, rows * j, c)
        grad = dot(act[:, cols], d_branch, 0, 0)
        g = grad.reshape(512 // (2 * deep), 2, deep, width)
        first = c == 0
        per = 512 // (2 * deep)
        keep_ref[per * j : per * (j + 1), base : base + deep, :] = jnp.where(
            first, g[:, 0], g[:, 1]
        ).astype(BF16)
        send_ref[per * j : per * (j + 1), base : base + deep, :] = jnp.where(
            first, g[:, 1], g[:, 0]
        ).astype(BF16)
    rhat, rr = norm_parts(resid[...])
    d_norm, d_gain = norm_back(total, rhat, rr, ffn_gain[...])
    gain_ref[...] = d_gain
    dresid_ref[...] = dout_ref[...] + d_norm


def attn_back_kernel(
    place, dresid, mixed, out_weight, qs, kall, vall, p0, p1, p2, p3, nall, x, mem, attn_gain,
    query_weight, pair_weight, write_query, dwquery, dblend, newmem, gain2, gain3,
    keep_ref, send_ref, own_tok_ref, own_mem_ref, own_new_ref, swap_ref,
    dk_ref, dv_ref, dm_ref, dq_ref, tok_ref, gmem_ref,
):
    y, c = place[0], place[1]
    width = dresid.shape[1]
    slots = mem.shape[0]
    half, mhalf = dresid.shape[0] // 2, slots // 2
    d_attn = dresid[...].astype(BF16)
    emit(dot(mixed[...], d_attn, 0, 0), keep_ref, send_ref, 96, c)
    dm_ref[...] = dot(d_attn, out_weight[...], 1, 1).astype(BF16)
    for p in range(H // 2):
        lanes = slice(128 * p, 128 * p + 128)
        for i, p_ref in reversed(list(enumerate((p0, p1, p2, p3)))):
            w = 128 * (i + 2)
            rows = slice(128 * i, 128 * i + 128)
            q01 = stacked_heads(qs[rows, lanes])
            dm01 = stacked_heads(dm_ref[rows, lanes])
            pb = p_ref[p]
            pf = pb.astype(F32)
            dp = dot(dm01, vall[0:w, lanes], 1, 1)
            t = pf * dp
            ds = (t - pf * jnp.sum(t, -1, keepdims=True)).astype(BF16)
            dq = unstacked_heads(dot(ds, kall[0:w, lanes])) * 0.125
            dq_ref[rows, lanes] = dq.astype(BF16)
            dk = dot(ds, q01, 0, 0)
            dv = dot(pb, dm01, 0, 0)
            if i == 3:
                dk_ref[0:w, lanes] = dk
                dv_ref[0:w, lanes] = dv
            else:
                dk_ref[0:w, lanes] += dk
                dv_ref[0:w, lanes] += dv
    dk = dk_ref[...].astype(BF16)
    dv = dv_ref[...].astype(BF16)
    dq = dq_ref[...]
    na = nall[...]
    emit(dot(na[128:], dq, 0, 0), keep_ref, send_ref, 0, c)
    emit(dot(na, dk, 0, 0), keep_ref, send_ref, 32, c)
    emit(dot(na, dv, 0, 0), keep_ref, send_ref, 64, c)
    d_all = dot(dk, pair_weight[:, :width], 1, 1) + dot(dv, pair_weight[:, width:], 1, 1)
    d_nx = d_all[128:] + dot(dq, query_weight[...], 1, 1)
    d_nm = d_all[:slots] + dot(dwquery[...], write_query[...], 1, 1)
    gain = attn_gain[...]
    xhat, xr = norm_parts(x[...])
    d_x, g_x = norm_back(d_nx, xhat, xr, gain)
    mhat, mr = norm_parts(mem[...])
    d_m, g_m = norm_back(d_nm, mhat, mr, gain)
    tok_ref[...] = dresid[...] + d_x
    gmem_ref[...] = dblend[...] + d_m
    own = pl.multiple_of(y * half, half)
    other = pl.multiple_of((1 - y) * half, half)
    mown = pl.multiple_of(y * mhalf, mhalf)
    mother = pl.multiple_of((1 - y) * mhalf, mhalf)
    own_tok_ref[...] = tok_ref[pl.ds(own, half), :]
    own_mem_ref[...] = gmem_ref[pl.ds(mown, mhalf), :]
    own_new_ref[...] = newmem[pl.ds(mown, mhalf), :]
    swap_ref[0:half, :] = tok_ref[pl.ds(other, half), :].astype(BF16)
    swap_ref[half : half + mhalf, :] = newmem[pl.ds(mother, mhalf), :]
    swap_ref[half + mhalf :, :] = gmem_ref[pl.ds(mother, mhalf), :].astype(BF16)
    gains = jnp.concatenate([g_x + g_m, gain2[...], gain3[...], jnp.zeros((29, width), F32)], 0)
    gains = jnp.broadcast_to(gains[None].astype(BF16), (GROUPS // 2, 32, width))
    keep_ref[:, 128:160, :] = gains
    send_ref[:, 128:160, :] = gains


def call(kernel, outs, scratch=(), smem=1, flops=0, nbytes=0):
    def run(*args):
        specs = [
            pl.BlockSpec(memory_space=pltpu.SMEM if i < smem else pltpu.VMEM)
            for i in range(len(args))
        ]
        return pl.pallas_call(
            kernel,
            out_shape=[jax.ShapeDtypeStruct(s, d) for s, d in outs],
            in_specs=specs,
            out_specs=[pl.BlockSpec(memory_space=pltpu.VMEM)] * len(outs),
            scratch_shapes=[pltpu.VMEM(s, d) for s, d in scratch],
            compiler_params=pltpu.CompilerParams(vmem_limit_bytes=VMEM_LIMIT),
            cost_estimate=pl.CostEstimate(flops=flops, bytes_accessed=nbytes, transcendentals=0),
        )(*args)

    return run


def other_of(axis, bit):
    size = lax.axis_size(axis)
    return [(i, i ^ bit) for i in range(size)]


def halves(total, axis, bit_value):
    size = total.shape[axis] // 2
    keep = lax.dynamic_slice_in_dim(total, bit_value * size, size, axis)
    send = lax.dynamic_slice_in_dim(total, (1 - bit_value) * size, size, axis)
    return keep, send


def added(keep, recv):
    return (keep.astype(F32) + recv.astype(F32)).astype(BF16)


def reduced_small(keep, send, rows_a):
    seg = lax.axis_index("seg")
    y = lax.axis_index("seq")
    x, z = (seg // 2) % 2, seg // 4
    total = added(keep, lax.ppermute(send, "seg", other_of("seg", 1)))
    r, w = total.shape[1:]
    a = total[:, :rows_a].reshape(4, 2, rows_a, w)
    b = total[:, rows_a:]
    take = lambda v, i, ax: lax.dynamic_index_in_dim(v, i, ax, keepdims=False)
    ra = lax.ppermute(take(a, 1 - x, 1), "seg", other_of("seg", 2))
    kb, sb = halves(b, 1, y)
    rb = lax.ppermute(sb, "seq", other_of("seq", 1))
    a = added(take(a, x, 1), ra)
    b = added(kb, rb).reshape(4, 2, (r - rows_a) // 2, w)
    ka, sa = halves(a, 1, y)
    ra = lax.ppermute(sa, "seq", other_of("seq", 1))
    rb = lax.ppermute(take(b, 1 - x, 1), "seg", other_of("seg", 2))
    t = jnp.concatenate([added(ka, ra), added(take(b, x, 1), rb)], 1)
    t = t.reshape(2, 2, r // 2, w)
    t = added(take(t, z % 2, 1), lax.ppermute(take(t, 1 - z % 2, 1), "seg", other_of("seg", 4)))
    t = added(take(t, z // 2, 0), lax.ppermute(take(t, 1 - z // 2, 0), "seg", other_of("seg", 8)))
    o = lax.ppermute(t, "seq", other_of("seq", 1))
    first = jnp.where(y == 0, t, o).astype(F32)
    second = jnp.where(y == 0, o, t).astype(F32)
    ha = rows_a // 2
    return jnp.concatenate([first[:ha], second[:ha], first[ha:], second[ha:]], 0)


def reduced_any(keep, send, pieces):
    groups = lax.axis_size("seg")
    c = lax.axis_index("seg") % 2
    first = jnp.where(c == 0, keep, send)
    second = jnp.where(c == 0, send, keep)
    total = jnp.stack([first, second], 1)
    total = total.reshape((GROUPS,) + keep.shape[1:])
    fine = groups // GROUPS
    parts = []
    at = 0
    for rows, shared in pieces:
        part = total[:, at : at + rows]
        if shared:
            part = jnp.broadcast_to(part[:, None], (GROUPS, fine) + part.shape[1:])
        else:
            part = part.reshape(GROUPS, fine, rows // fine, part.shape[2])
        parts.append(part.reshape(groups, -1, part.shape[-1]))
        at += rows
    total = jnp.concatenate(parts, 1)
    total = lax.psum_scatter(total.astype(F32), "seg", scatter_dimension=0, tiled=True)[0]
    return lax.psum(total, "seq")


def shards(
    tokens, memory, lengths, attn_gain, query_weight, pair_weight, out_weight, ffn_gain, ffn_in,
    ffn_out, write_query, write_pair, write_out, write_gate, write_gain, out_cotangent,
    memory_cotangent,
):
    half, width = tokens.shape[1:]
    mhalf = memory.shape[1]
    rows, slots, ff = 2 * half, 2 * mhalf, ffn_in.shape[1]
    padded = rows + 128
    groups = lax.axis_size("seg")
    y = lax.axis_index("seq")
    seg = lax.axis_index("seg")
    place = jnp.stack([y, seg % 2]).astype(jnp.int32)
    swap = other_of("seq", 1)
    pick = lambda v: lax.dynamic_index_in_dim(v, 1 - y, 0, keepdims=False)
    recv_a = lax.ppermute(jnp.concatenate([pick(tokens), pick(memory)], 0), "seq", swap)
    recv_b = lax.ppermute(
        jnp.concatenate([pick(out_cotangent), pick(memory_cotangent)], 0), "seq", swap
    )
    ag, fg, wg = attn_gain[None], ffn_gain[None], write_gain[None]
    big = ((rows, width), BF16)
    (
        x, mem, nall, qs, kall, vall, p0, p1, p2, p3, mixed, resid, n2, act, dg, out, out_send, wqs
    ) = call(
        forward_kernel,
        [
            ((rows, width), F32), ((slots, width), F32), ((padded, width), BF16), big,
            ((padded, width), BF16), ((padded, width), BF16),
            *[((H // 2, 256, 128 * (i + 2)), BF16) for i in range(4)],
            big, ((rows, width), F32), big, ((rows, ff), BF16), ((rows, ff), BF16), big,
            ((half, width), BF16), ((slots, width), BF16),
        ],
        smem=2, flops=2 * 3 * 10**9, nbytes=20 * 10**6,
    )(
        place, lengths, tokens, memory, recv_a, ag, query_weight, pair_weight, out_weight, fg,
        ffn_in, ffn_out, write_query,
    )
    out_recv = lax.ppermute(out_send, "seq", swap)
    keep1, send1, dwpair, dwquery, dblend, newmem, gain3 = call(
        write_kernel,
        [
            ((GROUPS // 2, 160, width), BF16), ((GROUPS // 2, 160, width), BF16),
            ((rows, 2 * width), BF16), ((slots, width), BF16), ((slots, width), F32),
            ((slots, width), BF16), ((1, width), F32),
        ],
        scratch=[((slots, width), F32)], flops=2 * 15 * 10**8, nbytes=10 * 10**6,
    )(
        place, out, wqs, mem, nall, memory_cotangent, recv_b, write_pair, write_out, write_gate, wg
    )
    keep2, send2, dresid, gain2 = call(
        ffn_back_kernel,
        [
            ((GROUPS // 2, 256, width), BF16), ((GROUPS // 2, 256, width), BF16),
            ((rows, width), F32), ((1, width), F32),
        ],
        scratch=[((rows, width), F32)], flops=2 * 25 * 10**8, nbytes=20 * 10**6,
    )(
        place, dwpair, out_cotangent, recv_b, write_pair, act, dg, n2, resid, ffn_in, ffn_out, fg
    )
    keep3, send3, own_tok, own_mem, own_new, swap_out = call(
        attn_back_kernel,
        [
            ((GROUPS // 2, 160, width), BF16), ((GROUPS // 2, 160, width), BF16),
            ((half, width), F32), ((mhalf, width), F32), ((mhalf, width), BF16),
            ((half + 2 * mhalf, width), BF16),
        ],
        scratch=[
            ((padded, width), F32), ((padded, width), F32), big, big, ((rows, width), F32),
            ((slots, width), F32),
        ],
        flops=2 * 3 * 10**9, nbytes=20 * 10**6,
    )(
        place, dresid, mixed, out_weight, qs, kall, vall, p0, p1, p2, p3, nall, x, mem, ag,
        query_weight, pair_weight, write_query, dwquery, dblend, newmem, gain2, gain3,
    )
    swapped = lax.ppermute(swap_out, "seq", swap)
    if groups == GROUPS:
        w1 = reduced_small(keep1, send1, 96)
        w2 = reduced_small(keep2, send2, 160)
        w3 = reduced_small(keep3, send3, 96)
    else:
        r = width // GROUPS
        w1 = reduced_any(keep1, send1, [(r, False)] * 5)
        w2 = reduced_any(keep2, send2, [(r, False)] * (ff // 512) + [(ff // GROUPS, False)])
        w3 = reduced_any(keep3, send3, [(r, False)] * 4 + [(32, True)])
    r = width // groups
    cut = lambda w, at, n: jnp.concatenate([w[(at + i) * r : (at + i + 1) * r] for i in range(n)], 1)
    gains = w3[4 * r :]
    gain_of = lambda i: lax.dynamic_slice_in_dim(gains[i], seg * r, r, 0)

    def both(own, recv):
        recv = recv.astype(own.dtype)
        return jnp.where(
            jnp.arange(2)[:, None, None] == y, own[None], recv[None]
        )

    own_out = lax.dynamic_slice_in_dim(out, y * half, half, 0)
    return (
        both(own_out, out_recv),
        both(own_new, swapped[half : half + mhalf]),
        both(own_tok, swapped[:half]),
        both(own_mem, swapped[half + mhalf :]),
        gain_of(0),
        w3[:r],
        cut(w3, 1, 2),
        w3[3 * r : 4 * r],
        gain_of(1),
        cut(w2, 0, ff // 512),
        w2[(ff // 512) * r :],
        w1[:r],
        cut(w1, 1, 2),
        w1[3 * r : 4 * r],
        w1[4 * r : 5 * r],
        gain_of(2),
    )


def solution(mesh):
    row = P("seg", "seq", None)
    grad = P("seg", None)
    in_specs = (row, row, P("seg", None)) + (P(),) * 12 + (row, row)
    out_specs = (row, row, row, row, P("seg"), grad, grad, grad, P("seg")) + (grad,) * 6 + (P("seg"),)
    return jax.shard_map(shards, mesh=mesh, in_specs=in_specs, out_specs=out_specs, check_vma=False)
```

time: 569 us -> 172 us (0.30)
  waiting for transfers between devices: 273 us -> 65.3 us
  matrix products: 95.4 us -> 0 us
  blocking collectives: 84.3 us -> 0 us
  Pallas kernels: 0 us -> 56.7 us
  local copies, waits for them, and re-layouts: 50.4 us -> 7.93 us
  other arithmetic: 37.5 us -> 9.82 us
  starting transfers between devices: 7.69 us -> 30.6 us
  between operations: 15.1 us -> 1.37 us
    psum x1 -> x0, waiting for transfers between devices: 249 us -> none  [shards(): lax.psum((terms[0], terms[1], terms[2], terms[3], terms[4], terms[5], ter...]
    dot_general x42 -> x0, matrix products: 95.4 us -> none  [the longest x10 22.4 us: weight_term(): jnp.einsum('sad,sae->de', left, grad, preferred_element_type=jnp.float32)]
    ppermute x2 -> x28, waiting for transfers between devices: 2.84 us -> 65.3 us  [the longest x3 12.1 us: reduced_small(): o = lax.ppermute(t, 'seq', other_of('seq', 1))]
    pallas_call x0 -> x4, Pallas kernels: none -> 56.7 us  [run(): pl.pallas_call(kernel, out_shape=[jax.ShapeDtypeStruct(s, d) for s, d in...]
    psum x2 -> x0, blocking collectives: 47.1 us -> none  [the longest x1 41.4 us: shards(): lax.psum((terms[0], terms[1], terms[2], terms[3], terms[4], terms[5], ter...]
    all_gather x4 -> x0, blocking collectives: 37.2 us -> none  [the longest x1 23 us: shards(): mem_all = lax.all_gather(memory, 'seq', axis=1, tiled=True)]
    ppermute x2 -> x28, starting transfers between devices: 7.12 us -> 30.6 us  [the longest x3 6.98 us: reduced_small(): lax.ppermute(take(t, 1 - z // 2, 0), 'seg', other_of('seg', 8))]
    reduce_scatter x3 -> x0, waiting for transfers between devices: 21.4 us -> none  [the longest x1 11.7 us: shards(): lax.psum_scatter(wpart.astype(jnp.bfloat16), 'seq', scatter_dimension=1,...]
  transfers between devices with their start and end apart: 6 -> 28, of which waited for: 4 -> 16; matrix products, arithmetic and copies ran while one was open for 7% -> 7% of each run, Pallas kernels for 0% -> 28%
where the time goes in v1:
time: 172 us
  waiting for transfers between devices  65.3 us (38%)
  Pallas kernels  56.7 us (33%)
  starting transfers between devices  30.6 us (18%)
  other arithmetic  9.82 us (6%)
  local copies, waits for them, and re-layouts  7.93 us (5%)
    pallas_call x4, Pallas kernels, run(): pl.pallas_call(kernel, out_shape=[jax.ShapeDtypeStruct(s, d) for s, d in...  56.7 us
    ppermute x3, waiting for transfers between devices, reduced_small(): o = lax.ppermute(t, 'seq', other_of('seq', 1))  12.1 us
    ppermute x1, waiting for transfers between devices, shards(): swapped = lax.ppermute(swap_out, 'seq', swap)  9.27 us
    ppermute x3, waiting for transfers between devices, reduced_small(): ra = lax.ppermute(take(a, 1 - x, 1), 'seg', other_of('seg', 2))  8.04 us
    ppermute x3, waiting for transfers between devices, reduced_small(): lax.ppermute(take(t, 1 - z % 2, 1), 'seg', other_of('seg', 4))  7.89 us
    ppermute x3, starting transfers between devices, reduced_small(): lax.ppermute(take(t, 1 - z // 2, 0), 'seg', other_of('seg', 8))  6.98 us
    ppermute x1, waiting for transfers between devices, shards(): lax.ppermute(jnp.concatenate([pick(tokens), pick(memory)], 0), 'seq', swap)  6.96 us
    ppermute x3, waiting for transfers between devices, reduced_small(): rb = lax.ppermute(sb, 'seq', other_of('seq', 1))  6.94 us
  transfers between devices with their start and end apart: 28, of which 16 were waited for; matrix products, arithmetic and copies ran while one was open for 7% of the time, Pallas kernels for 28%

profile of v1, /device:TPU:0, one launch (start us, length us, event | category | flops | bytes accessed | tf_op | source)
XLA Modules:
  0.0 171.6 jit_solution(10775234239556112440)
XLA Ops:
  0.7 1.0 dynamic-slice_bitcast_fusion.5
  1.7 0.8 dynamic-slice_bitcast_fusion.15
  2.5 3.0 %collective-permute-start = (bf16[288,512]{1,0:T(8,128)(2,1)S(1)}, bf16[288,512]{1,0:T(8,128)(2,1)S(1)}, u32[]{:S(2)}, u32[]{:S(2)}) collective-permute-start(bf16[288,512]{1,0:T(8,128)(2,1)S(1)} %pad_maximum_fusion.3), channel_id=1, source_target_pairs={{0,16},{16,0},{1,17},{17,1},{2,18},{18,2},{3,19},{19,3},{4,20},{20... | collective-permute-start | bytes 884744 | tf_op jit(solution)/shard_map/ppermute | solution.py:415
  6.4 7.0 %collective-permute-done.recv = bf16[288,512]{1,0:T(8,128)(2,1)S(1)} collective-permute-done((bf16[288,512]{1,0:T(8,128)(2,1)S(1)}, bf16[288,512]{1,0:T(8,128)(2,1)S(1)}, u32[]{:S(2)}, u32[]{:S(2)}) %collective-permute-start) | collective-permute-done | bytes 294944 | tf_op jit(solution)/shard_map/ppermute | solution.py:415
  13.4 0.7 copy-done.10
  14.1 17.9 %shard_map.288 = (f32[512,512]{1,0:T(8,128)}, f32[64,512]{1,0:T(8,128)}, bf16[640,512]{1,0:T(8,128)(2,1)}, bf16[512,512]{1,0:T(8,128)(2,1)}, bf16[640,512]{1,0:T...) custom-call(s32[2]{0:T(128)} %pad_add_fusion.place, ...), custom_call_target="tpu_custom_call" | custom-call | flops 6000000000 | bytes 20000000 | tf_op jit(solution)/shard_map/pallas_call | solution.py:320
  32.0 0.7 copy-done.9
  32.7 8.9 %shard_map.289 = (bf16[8,160,512]{2,1,0:T(8,128)(2,1)}, bf16[8,160,512]{2,1,0:T(8,128)(2,1)}, bf16[512,1024]{1,0:T(8,128)(2,1)}, bf16[64,512]{1,0:T(8,128)(2,1)}...) custom-call(s32[2]{0:T(128)} %pad_add_fusion.place, bf16[512,512]{1,0:T(8,128)(2,1)} %get-tuple-element.51.out, ...), custom_call_target="tpu_custom_call" | custom-call | flops 3000000000 | bytes 10000000 | tf_op jit(solution)/shard_map/pallas_call | solution.py:320
  41.7 12.6 %shard_map.290 = (bf16[8,256,512]{2,1,0:T(8,128)(2,1)}, bf16[8,256,512]{2,1,0:T(8,128)(2,1)}, f32[512,512]{1,0:T(8,128)}, f32[1,512]{1,0:T(1,128)}) custom-call(s32[2]{0:T(128)} %pad_add_fusion.place, bf16[512,1024]{1,0:T(8,128)(2,1)} %get-tuple-element.56.dwpair, bf16[2,256,512]{2,1,0:T(8,128)(2,1)} %out_cotangent.1, bf16[288,512]{1,0:T(8,128)(2,1)} %copy-done.9, ...), custom_call_target="tpu_custom_call" | custom-call | flops 5000000000 | bytes 20000000 | tf_op jit(solution)/shard_map/pallas_call | solution.py:320
  54.7 2.1 %collective-permute-start.1 = (bf16[256,512]{1,0:T(8,128)(2,1)S(1)}, bf16[256,512]{1,0:T(8,128)(2,1)S(1)}, u32[]{:S(2)}, u32[]{:S(2)}) collective-permute-start(bf16[256,512]{1,0:T(8,128)(2,1)S(1)} %copy-done.11), channel_id=1, source_target_pairs={{0,16},{16,0},{1,17},{17,1},{2,18},{18,2},{3,19},{19,3},{4,20},{20... | collective-permute-start | bytes 786440 | tf_op jit(solution)/shard_map/ppermute | solution.py:437
  56.8 17.3 %shard_map.291 = (bf16[8,160,512]{2,1,0:T(8,128)(2,1)}, bf16[8,160,512]{2,1,0:T(8,128)(2,1)}, f32[256,512]{1,0:T(8,128)}, f32[32,512]{1,0:T(8,128)}, bf16[32,512]{1,0:T(8,128)(2,1)}, /*index=5*/bf16[320,512]{1,0:T(8,128)(2,1)}) custom-call(s32[2]{0:T(128)} %pad_add_fusion.place, f32[512,512]{1,0:T(8,128)} %get-tuple-element.61.dresid, ...), custom_call_target="tpu_custom_call" | custom-call | flops 6000000000 | bytes 20000000 | tf_op jit(solution)/shard_map/pallas_call | solution.py:320
  74.3 0.9 broadcast_select_fusion.1
  75.3 9.3 %collective-permute-done.3 = bf16[320,512]{1,0:T(8,128)(2,1)S(1)} collective-permute-done((bf16[320,512]{1,0:T(8,128)(2,1)}, bf16[320,512]{1,0:T(8,128)(2,1)S(1)}, u32[]{:S(2)}, u32[]{:S(2)}) %collective-permute-start.3) | collective-permute-done | bytes 327712 | tf_op jit(solution)/shard_map/ppermute | solution.py:475
  84.5 0.7 broadcast_select_fusion.3
  85.3 0.7 broadcast_select_fusion.2
  86.1 1.2 broadcast_select_fusion
  88.5 0.8 copy-done.2
  89.9 1.6 collective-permute-start.21
  92.1 1.0 collective-permute-start.7
  93.1 4.3 %collective-permute-done.23 = bf16[8,32,512]{2,1,0:T(8,128)(2,1)S(1)} collective-permute-done((bf16[8,32,512]{2,1,0:T(8,128)(2,1)S(1)}, bf16[8,32,512]{2,1,0:T(8,128)(2,1)S(1)}, u32[]{:S(2)}, u32[]{:S(2)}) %collective-permute-start.23) | collective-permute-done | bytes 262176 | tf_op jit(solution)/shard_map/ppermute | solution.py:360
  97.5 1.6 collective-permute-start.24
  99.1 2.6 %collective-permute-done.7 = bf16[8,32,512]{2,1,0:T(8,128)(2,1)S(1)} collective-permute-done((bf16[8,32,512]{2,1,0:T(8,128)(2,1)S(1)}, bf16[8,32,512]{2,1,0:T(8,128)(2,1)S(1)}, u32[]{:S(2)}, u32[]{:S(2)}) %collective-permute-start.7) | collective-permute-done | bytes 262176 | tf_op jit(solution)/shard_map/ppermute | solution.py:360
  101.8 1.6 collective-permute-start.8
  104.1 6.3 %collective-permute-done.5 = bf16[4,96,512]{2,1,0:T(8,128)(2,1)S(1)} collective-permute-done((bf16[4,96,512]{2,1,0:T(8,128)(2,1)S(1)}, bf16[4,96,512]{2,1,0:T(8,128)(2,1)S(1)}, u32[]{:S(2)}, u32[]{:S(2)}) %collective-permute-start.5) | collective-permute-done | bytes 393248 | tf_op jit(solution)/shard_map/ppermute | solution.py:358
  110.5 1.0 collective-permute-start.6
  111.6 1.6 collective-permute-done.24
  113.2 1.4 collective-permute-done.8
  114.9 1.6 collective-permute-start.25
  116.6 1.4 collective-permute-start.9
  118.0 3.5 %collective-permute-done.25 = bf16[2,80,512]{2,1,0:T(8,128)(2,1)S(1)} collective-permute-done((bf16[2,80,512]{2,1,0:T(8,128)(2,1)S(1)}, bf16[2,80,512]{2,1,0:T(8,128)(2,1)S(1)}, u32[]{:S(2)}, u32[]{:S(2)}) %collective-permute-start.25) | collective-permute-done | bytes 163872 | tf_op jit(solution)/shard_map/ppermute | solution.py:368
  121.6 3.2 %collective-permute-start.26 = (bf16[80,512]{1,0:T(8,128)(2,1)S(1)}, bf16[80,512]{1,0:T(8,128)(2,1)S(1)}, u32[]{:S(2)}, u32[]{:S(2)}) collective-permute-start(bf16[80,512]{1,0:T(8,128)(2,1)S(1)} %dynamic-slice_bitcast_fusion.12), channel_id=1, source_target_pairs={{0,8},{1,9},{2,10},{3,11},{4,12},{5,13},{6,14},{7,15},{8,0},{9,1},... | collective-permute-start | bytes 245768 | tf_op jit(solution)/shard_map/ppermute | solution.py:369
  124.9 2.4 %collective-permute-start.10 = (bf16[80,512]{1,0:T(8,128)(2,1)S(1)}, bf16[80,512]{1,0:T(8,128)(2,1)S(1)}, u32[]{:S(2)}, u32[]{:S(2)}) collective-permute-start(bf16[80,512]{1,0:T(8,128)(2,1)S(1)} %dynamic-slice_bitcast_fusion.13), channel_id=1, source_target_pairs={{0,8},{1,9},{2,10},{3,11},{4,12},{5,13},{6,14},{7,15},{8,0},{9,1},... | collective-permute-start | bytes 245768 | tf_op jit(solution)/shard_map/ppermute | solution.py:369
  128.1 1.6 collective-permute-start.13
  129.7 0.7 collective-permute-start.15
  130.4 1.5 collective-permute-start.27
  131.9 0.7 collective-permute-start.11
  132.6 6.9 %collective-permute-done.27 = bf16[80,512]{1,0:T(8,128)(2,1)S(1)} collective-permute-done((bf16[80,512]{1,0:T(8,128)(2,1)S(1)}, bf16[80,512]{1,0:T(8,128)(2,1)S(1)}, u32[]{:S(2)}, u32[]{:S(2)}) %collective-permute-start.27) | collective-permute-done | bytes 81952 | tf_op jit(solution)/shard_map/ppermute | solution.py:370
  139.5 1.7 collective-permute-done.11
  141.5 1.7 %collective-permute-done.13 = bf16[4,160,512]{2,1,0:T(8,128)(2,1)S(1)} collective-permute-done((bf16[4,160,512]{2,1,0:T(8,128)(2,1)S(1)}, bf16[4,160,512]{2,1,0:T(8,128)(2,1)S(1)}, u32[]{:S(2)}, u32[]{:S(2)}) %collective-permute-start.13) | collective-permute-done | bytes 655392 | tf_op jit(solution)/shard_map/ppermute | solution.py:358
  144.2 2.9 %collective-permute-done.16 = bf16[4,48,512]{2,1,0:T(8,128)(2,1)S(1)} collective-permute-done((bf16[4,48,512]{2,1,0:T(8,128)(2,1)S(1)}, bf16[4,48,512]{2,1,0:T(8,128)(2,1)S(1)}, u32[]{:S(2)}, u32[]{:S(2)}) %collective-permute-start.16) | collective-permute-done | bytes 196640 | tf_op jit(solution)/shard_map/ppermute | solution.py:365
  147.2 3.4 %collective-permute-done.14 = bf16[4,80,512]{2,1,0:T(8,128)(2,1)S(1)} collective-permute-done((bf16[4,80,512]{2,1,0:T(8,128)(2,1)S(1)}, bf16[4,80,512]{2,1,0:T(8,128)(2,1)S(1)}, u32[]{:S(2)}, u32[]{:S(2)}) %collective-permute-start.14) | collective-permute-done | bytes 327712 | tf_op jit(solution)/shard_map/ppermute | solution.py:364
  150.8 1.7 collective-permute-start.17
  153.1 4.4 %collective-permute-done.17 = bf16[2,128,512]{2,1,0:T(8,128)(2,1)S(1)} collective-permute-done((bf16[2,128,512]{2,1,0:T(8,128)(2,1)S(1)}, bf16[2,128,512]{2,1,0:T(8,128)(2,1)S(1)}, u32[]{:S(2)}, u32[]{:S(2)}) %collective-permute-start.17) | collective-permute-done | bytes 262176 | tf_op jit(solution)/shard_map/ppermute | solution.py:368
  157.6 1.4 collective-permute-start.18
  160.3 4.6 %collective-permute-done.18 = bf16[128,512]{1,0:T(8,128)(2,1)S(1)} collective-permute-done((bf16[128,512]{1,0:T(8,128)(2,1)S(1)}, bf16[128,512]{1,0:T(8,128)(2,1)S(1)}, u32[]{:S(2)}, u32[]{:S(2)}) %collective-permute-start.18) | collective-permute-done | bytes 131104 | tf_op jit(solution)/shard_map/ppermute | solution.py:369
  166.5 3.6 %collective-permute-done.19 = bf16[128,512]{1,0:T(8,128)(2,1)S(1)} collective-permute-done((bf16[128,512]{1,0:T(8,128)(2,1)S(1)}, bf16[128,512]{1,0:T(8,128)(2,1)S(1)}, u32[]{:S(2)}, u32[]{:S(2)}) %collective-permute-start.19) | collective-permute-done | bytes 131104 | tf_op jit(solution)/shard_map/ppermute | solution.py:370
  170.2 0.7 pad_maximum_fusion.5
  170.9 0.7 fusion.8
  (122 shorter events, 11.4 us)
Async XLA Ops:
  0.6 4.9 %copy-start.4 = (bf16[2,256,512]{2,1,0:T(8,128)(2,1)S(1)}, bf16[2,256,512]{2,1,0:T(8,128)(2,1)}, u32[]{:S(2)}) copy-start(bf16[2,256,512]{2,1,0:T(8,128)(2,1)} %out_cotangent.1) | copy-start | bytes 1572868
  0.7 4.9 %copy-start.8 = (bf16[2,32,512]{2,1,0:T(8,128)(2,1)S(1)}, bf16[2,32,512]{2,1,0:T(8,128)(2,1)}, u32[]{:S(2)}) copy-start(bf16[2,32,512]{2,1,0:T(8,128)(2,1)} %memory_cotangent.1) | copy-start | bytes 196612
  2.5 10.9 %collective-permute-start = (bf16[288,512]{1,0:T(8,128)(2,1)S(1)}, bf16[288,512]{1,0:T(8,128)(2,1)S(1)}, u32[]{:S(2)}, u32[]{:S(2)}) collective-permute-start(bf16[288,512]{1,0:T(8,128)(2,1)S(1)} %pad_maximum_fusion.3), channel_id=1, source_target_pairs={{0,16},{16,0},{1,17},{17,1},{2,18},{18,2},{3,19},{19,3},{4,20},{20... | collective-permute-start | bytes 884744 | tf_op jit(solution)/shard_map/ppermute | solution.py:415
  5.6 26.4 %collective-permute-start.2 = (bf16[288,512]{1,0:T(8,128)(2,1)S(1)}, bf16[288,512]{1,0:T(8,128)(2,1)S(1)}, u32[]{:S(2)}, u32[]{:S(2)}) collective-permute-start(bf16[288,512]{1,0:T(8,128)(2,1)S(1)} %pad_maximum_fusion.4), channel_id=1, source_target_pairs={{0,16},{16,0},{1,17},{17,1},{2,18},{18,2},{3,19},{19,3},{4,20},{20... | collective-permute-start | bytes 884744 | tf_op jit(solution)/shard_map/ppermute | solution.py:416
  13.4 0.7 copy-start.10
  32.0 0.7 copy-start.9
  41.6 45.6 %collective-permute-start.20 = (bf16[8,160,512]{2,1,0:T(8,128)(2,1)}, bf16[8,160,512]{2,1,0:T(8,128)(2,1)S(1)}, u32[]{:S(2)}, u32[]{:S(2)}) collective-permute-start(bf16[8,160,512]{2,1,0:T(8,128)(2,1)} %get-tuple-element.85), channel_id=1, source_target_pairs={{0,1},{1,0},{2,3},{3,2},{4,5},{5,4},{6,7},{7,6},{8,9},{9,8},{10,11... | collective-permute-start | bytes 3932168 | tf_op jit(solution)/shard_map/ppermute | solution.py:353
  41.6 13.1 %copy-start.11 = (bf16[256,512]{1,0:T(8,128)(2,1)S(1)}, bf16[256,512]{1,0:T(8,128)(2,1)}, u32[]{:S(2)}) copy-start(bf16[256,512]{1,0:T(8,128)(2,1)} %get-tuple-element.52) | copy-start | bytes 786436
  54.2 73.0 %collective-permute-start.12 = (bf16[8,256,512]{2,1,0:T(8,128)(2,1)}, bf16[8,256,512]{2,1,0:T(8,128)(2,1)S(1)}, u32[]{:S(2)}, u32[]{:S(2)}) collective-permute-start(bf16[8,256,512]{2,1,0:T(8,128)(2,1)} %get-tuple-element.83), channel_id=1, source_target_pairs={{0,1},{1,0},{2,3},{3,2},{4,5},{5,4},{6,7},{7,6},{8,9},{9,8},{10,11... | collective-permute-start | bytes 6291464 | tf_op jit(solution)/shard_map/ppermute | solution.py:353
  54.7 19.6 %collective-permute-start.1 = (bf16[256,512]{1,0:T(8,128)(2,1)S(1)}, bf16[256,512]{1,0:T(8,128)(2,1)S(1)}, u32[]{:S(2)}, u32[]{:S(2)}) collective-permute-start(bf16[256,512]{1,0:T(8,128)(2,1)S(1)} %copy-done.11), channel_id=1, source_target_pairs={{0,16},{16,0},{1,17},{17,1},{2,18},{18,2},{3,19},{19,3},{4,20},{20... | collective-permute-start | bytes 786440 | tf_op jit(solution)/shard_map/ppermute | solution.py:437
  56.8 17.5 %copy-start.5 = (bf16[512,512]{1,0:T(8,128)(2,1)S(1)}, bf16[512,512]{1,0:T(8,128)(2,1)}, u32[]{:S(2)}) copy-start(bf16[512,512]{1,0:T(8,128)(2,1)} %get-tuple-element.51.out) | copy-start | bytes 1572868
  74.1 10.5 %copy-start.7 = (bf16[32,512]{1,0:T(8,128)(2,1)S(1)}, bf16[32,512]{1,0:T(8,128)(2,1)}, u32[]{:S(2)}) copy-start(bf16[32,512]{1,0:T(8,128)(2,1)} %get-tuple-element.76) | copy-start | bytes 98308
  74.1 11.2 %copy-start.6 = (f32[32,512]{1,0:T(8,128)S(1)}, f32[32,512]{1,0:T(8,128)}, u32[]{:S(2)}) copy-start(f32[32,512]{1,0:T(8,128)} %get-tuple-element.79) | copy-start | bytes 196612
  74.1 14.4 %collective-permute-start.4 = (bf16[8,160,512]{2,1,0:T(8,128)(2,1)}, bf16[8,160,512]{2,1,0:T(8,128)(2,1)S(1)}, u32[]{:S(2)}, u32[]{:S(2)}) collective-permute-start(bf16[8,160,512]{2,1,0:T(8,128)(2,1)} %get-tuple-element.81), channel_id=1, source_target_pairs={{0,1},{1,0},{2,3},{3,2},{4,5},{5,4},{6,7},{7,6},{8,9},{9,8},{10,11... | collective-permute-start | bytes 3932168 | tf_op jit(solution)/shard_map/ppermute | solution.py:353
  74.2 10.3 %collective-permute-start.3 = (bf16[320,512]{1,0:T(8,128)(2,1)}, bf16[320,512]{1,0:T(8,128)(2,1)S(1)}, u32[]{:S(2)}, u32[]{:S(2)}) collective-permute-start(bf16[320,512]{1,0:T(8,128)(2,1)} %get-tuple-element.77), channel_id=1, source_target_pairs={{0,16},{16,0},{1,17},{17,1},{2,18},{18,2},{3,19},{19,3},{4,20},{20... | collective-permute-start | bytes 983048 | tf_op jit(solution)/shard_map/ppermute | solution.py:475
  74.3 11.7 %copy-start.3 = (f32[256,512]{1,0:T(8,128)S(1)}, f32[256,512]{1,0:T(8,128)}, u32[]{:S(2)}) copy-start(f32[256,512]{1,0:T(8,128)} %get-tuple-element.78) | copy-start | bytes 1572868
  86.0 1.6 copy-start.1
  88.0 1.3 copy-start.2
  88.1 9.3 %collective-permute-start.23 = (bf16[8,32,512]{2,1,0:T(8,128)(2,1)S(1)}, bf16[8,32,512]{2,1,0:T(8,128)(2,1)S(1)}, u32[]{:S(2)}, u32[]{:S(2)}) collective-permute-start(bf16[8,32,512]{2,1,0:T(8,128)(2,1)S(1)} %constant_dynamic-slice_fusion.1), channel_id=1, source_target_pairs={{0,16},{16,0},{1,17},{17,1},{2,18},{18,2},{3,19},{19,3},{4,20},{20... | collective-permute-start | bytes 786440 | tf_op jit(solution)/shard_map/ppermute | solution.py:360
  89.9 13.5 %collective-permute-start.21 = (bf16[4,96,512]{2,1,0:T(8,128)(2,1)S(1)}, bf16[4,96,512]{2,1,0:T(8,128)(2,1)S(1)}, u32[]{:S(2)}, u32[]{:S(2)}) collective-permute-start(bf16[4,96,512]{2,1,0:T(8,128)(2,1)S(1)} %dynamic-slice_bitcast_fusion.1), channel_id=1, source_target_pairs={{0,2},{1,3},{2,0},{3,1},{4,6},{5,7},{6,4},{7,5},{8,10},{9,11},{10,... | collective-permute-start | bytes 1179656 | tf_op jit(solution)/shard_map/ppermute | solution.py:358
  91.5 18.9 %collective-permute-start.5 = (bf16[4,96,512]{2,1,0:T(8,128)(2,1)S(1)}, bf16[4,96,512]{2,1,0:T(8,128)(2,1)S(1)}, u32[]{:S(2)}, u32[]{:S(2)}) collective-permute-start(bf16[4,96,512]{2,1,0:T(8,128)(2,1)S(1)} %dynamic-slice_bitcast_fusion.2), channel_id=1, source_target_pairs={{0,2},{1,3},{2,0},{3,1},{4,6},{5,7},{6,4},{7,5},{8,10},{9,11},{10,... | collective-permute-start | bytes 1179656 | tf_op jit(solution)/shard_map/ppermute | solution.py:358
  92.1 9.6 %collective-permute-start.7 = (bf16[8,32,512]{2,1,0:T(8,128)(2,1)S(1)}, bf16[8,32,512]{2,1,0:T(8,128)(2,1)S(1)}, u32[]{:S(2)}, u32[]{:S(2)}) collective-permute-start(bf16[8,32,512]{2,1,0:T(8,128)(2,1)S(1)} %constant_dynamic-slice_fusion.7), channel_id=1, source_target_pairs={{0,16},{16,0},{1,17},{17,1},{2,18},{18,2},{3,19},{19,3},{4,20},{20... | collective-permute-start | bytes 786440 | tf_op jit(solution)/shard_map/ppermute | solution.py:360
  97.5 15.7 %collective-permute-start.24 = (bf16[4,32,512]{2,1,0:T(8,128)(2,1)S(1)}, bf16[4,32,512]{2,1,0:T(8,128)(2,1)S(1)}, u32[]{:S(2)}, u32[]{:S(2)}) collective-permute-start(bf16[4,32,512]{2,1,0:T(8,128)(2,1)S(1)} %dynamic-slice_bitcast_fusion.9), channel_id=1, source_target_pairs={{0,2},{1,3},{2,0},{3,1},{4,6},{5,7},{6,4},{7,5},{8,10},{9,11},{10,... | collective-permute-start | bytes 393224 | tf_op jit(solution)/shard_map/ppermute | solution.py:365
  101.8 12.9 %collective-permute-start.8 = (bf16[4,32,512]{2,1,0:T(8,128)(2,1)S(1)}, bf16[4,32,512]{2,1,0:T(8,128)(2,1)S(1)}, u32[]{:S(2)}, u32[]{:S(2)}) collective-permute-start(bf16[4,32,512]{2,1,0:T(8,128)(2,1)S(1)} %dynamic-slice_bitcast_fusion.11), channel_id=1, source_target_pairs={{0,2},{1,3},{2,0},{3,1},{4,6},{5,7},{6,4},{7,5},{8,10},{9,11},{10,... | collective-permute-start | bytes 393224 | tf_op jit(solution)/shard_map/ppermute | solution.py:365
  103.5 11.2 %collective-permute-start.22 = (bf16[4,48,512]{2,1,0:T(8,128)(2,1)S(1)}, bf16[4,48,512]{2,1,0:T(8,128)(2,1)S(1)}, u32[]{:S(2)}, u32[]{:S(2)}) collective-permute-start(bf16[4,48,512]{2,1,0:T(8,128)(2,1)S(1)} %constant_dynamic-slice_fusion.2), channel_id=1, source_target_pairs={{0,16},{16,0},{1,17},{17,1},{2,18},{18,2},{3,19},{19,3},{4,20},{20... | collective-permute-start | bytes 589832 | tf_op jit(solution)/shard_map/ppermute | solution.py:364
  110.5 6.0 %collective-permute-start.6 = (bf16[4,48,512]{2,1,0:T(8,128)(2,1)S(1)}, bf16[4,48,512]{2,1,0:T(8,128)(2,1)S(1)}, u32[]{:S(2)}, u32[]{:S(2)}) collective-permute-start(bf16[4,48,512]{2,1,0:T(8,128)(2,1)S(1)} %constant_dynamic-slice_fusion.8), channel_id=1, source_target_pairs={{0,16},{16,0},{1,17},{17,1},{2,18},{18,2},{3,19},{19,3},{4,20},{20... | collective-permute-start | bytes 589832 | tf_op jit(solution)/shard_map/ppermute | solution.py:364
  114.8 12.4 %copy-start = (bf16[8,256,512]{2,1,0:T(8,128)(2,1)S(1)}, bf16[8,256,512]{2,1,0:T(8,128)(2,1)}, u32[]{:S(2)}) copy-start(bf16[8,256,512]{2,1,0:T(8,128)(2,1)} %get-tuple-element.82) | copy-start | bytes 6291460
  114.9 6.7 %collective-permute-start.25 = (bf16[2,80,512]{2,1,0:T(8,128)(2,1)S(1)}, bf16[2,80,512]{2,1,0:T(8,128)(2,1)S(1)}, u32[]{:S(2)}, u32[]{:S(2)}) collective-permute-start(bf16[2,80,512]{2,1,0:T(8,128)(2,1)S(1)} %dynamic-slice_bitcast_fusion.7), channel_id=1, source_target_pairs={{0,4},{1,5},{2,6},{3,7},{4,0},{5,1},{6,2},{7,3},{8,12},{9,13},{10,... | collective-permute-start | bytes 491528 | tf_op jit(solution)/shard_map/ppermute | solution.py:368
  116.6 8.2 %collective-permute-start.9 = (bf16[2,80,512]{2,1,0:T(8,128)(2,1)S(1)}, bf16[2,80,512]{2,1,0:T(8,128)(2,1)S(1)}, u32[]{:S(2)}, u32[]{:S(2)}) collective-permute-start(bf16[2,80,512]{2,1,0:T(8,128)(2,1)S(1)} %dynamic-slice_bitcast_fusion.8), channel_id=1, source_target_pairs={{0,4},{1,5},{2,6},{3,7},{4,0},{5,1},{6,2},{7,3},{8,12},{9,13},{10,... | collective-permute-start | bytes 491528 | tf_op jit(solution)/shard_map/ppermute | solution.py:368
  121.6 8.8 %collective-permute-start.26 = (bf16[80,512]{1,0:T(8,128)(2,1)S(1)}, bf16[80,512]{1,0:T(8,128)(2,1)S(1)}, u32[]{:S(2)}, u32[]{:S(2)}) collective-permute-start(bf16[80,512]{1,0:T(8,128)(2,1)S(1)} %dynamic-slice_bitcast_fusion.12), channel_id=1, source_target_pairs={{0,8},{1,9},{2,10},{3,11},{4,12},{5,13},{6,14},{7,15},{8,0},{9,1},... | collective-permute-start | bytes 245768 | tf_op jit(solution)/shard_map/ppermute | solution.py:369
  124.9 7.0 %collective-permute-start.10 = (bf16[80,512]{1,0:T(8,128)(2,1)S(1)}, bf16[80,512]{1,0:T(8,128)(2,1)S(1)}, u32[]{:S(2)}, u32[]{:S(2)}) collective-permute-start(bf16[80,512]{1,0:T(8,128)(2,1)S(1)} %dynamic-slice_bitcast_fusion.13), channel_id=1, source_target_pairs={{0,8},{1,9},{2,10},{3,11},{4,12},{5,13},{6,14},{7,15},{8,0},{9,1},... | collective-permute-start | bytes 245768 | tf_op jit(solution)/shard_map/ppermute | solution.py:369
  128.1 15.1 %collective-permute-start.13 = (bf16[4,160,512]{2,1,0:T(8,128)(2,1)S(1)}, bf16[4,160,512]{2,1,0:T(8,128)(2,1)S(1)}, u32[]{:S(2)}, u32[]{:S(2)}) collective-permute-start(bf16[4,160,512]{2,1,0:T(8,128)(2,1)S(1)} %dynamic-slice_bitcast_fusion), channel_id=1, source_target_pairs={{0,2},{1,3},{2,0},{3,1},{4,6},{5,7},{6,4},{7,5},{8,10},{9,11},{10,... | collective-permute-start | bytes 1966088 | tf_op jit(solution)/shard_map/ppermute | solution.py:358
  129.7 11.6 %collective-permute-start.15 = (bf16[8,48,512]{2,1,0:T(8,128)(2,1)S(1)}, bf16[8,48,512]{2,1,0:T(8,128)(2,1)S(1)}, u32[]{:S(2)}, u32[]{:S(2)}) collective-permute-start(bf16[8,48,512]{2,1,0:T(8,128)(2,1)S(1)} %constant_dynamic-slice_fusion.3), channel_id=1, source_target_pairs={{0,16},{16,0},{1,17},{17,1},{2,18},{18,2},{3,19},{19,3},{4,20},{20... | collective-permute-start | bytes 1179656 | tf_op jit(solution)/shard_map/ppermute | solution.py:360
  130.4 9.0 %collective-permute-start.27 = (bf16[80,512]{1,0:T(8,128)(2,1)S(1)}, bf16[80,512]{1,0:T(8,128)(2,1)S(1)}, u32[]{:S(2)}, u32[]{:S(2)}) collective-permute-start(bf16[80,512]{1,0:T(8,128)(2,1)S(1)} %fusion.12), channel_id=1, source_target_pairs={{0,16},{16,0},{1,17},{17,1},{2,18},{18,2},{3,19},{19,3},{4,20},{20... | collective-permute-start | bytes 245768 | tf_op jit(solution)/shard_map/ppermute | solution.py:370
  131.9 9.3 %collective-permute-start.11 = (bf16[80,512]{1,0:T(8,128)(2,1)S(1)}, bf16[80,512]{1,0:T(8,128)(2,1)S(1)}, u32[]{:S(2)}, u32[]{:S(2)}) collective-permute-start(bf16[80,512]{1,0:T(8,128)(2,1)S(1)} %fusion.13), channel_id=1, source_target_pairs={{0,16},{16,0},{1,17},{17,1},{2,18},{18,2},{3,19},{19,3},{4,20},{20... | collective-permute-start | bytes 245768 | tf_op jit(solution)/shard_map/ppermute | solution.py:370
  141.4 5.7 %collective-permute-start.16 = (bf16[4,48,512]{2,1,0:T(8,128)(2,1)S(1)}, bf16[4,48,512]{2,1,0:T(8,128)(2,1)S(1)}, u32[]{:S(2)}, u32[]{:S(2)}) collective-permute-start(bf16[4,48,512]{2,1,0:T(8,128)(2,1)S(1)} %dynamic-slice_bitcast_fusion.6), channel_id=1, source_target_pairs={{0,2},{1,3},{2,0},{3,1},{4,6},{5,7},{6,4},{7,5},{8,10},{9,11},{10,... | collective-permute-start | bytes 589832 | tf_op jit(solution)/shard_map/ppermute | solution.py:365
  143.5 7.1 %collective-permute-start.14 = (bf16[4,80,512]{2,1,0:T(8,128)(2,1)S(1)}, bf16[4,80,512]{2,1,0:T(8,128)(2,1)S(1)}, u32[]{:S(2)}, u32[]{:S(2)}) collective-permute-start(bf16[4,80,512]{2,1,0:T(8,128)(2,1)S(1)} %constant_dynamic-slice_fusion.4), channel_id=1, source_target_pairs={{0,16},{16,0},{1,17},{17,1},{2,18},{18,2},{3,19},{19,3},{4,20},{20... | collective-permute-start | bytes 983048 | tf_op jit(solution)/shard_map/ppermute | solution.py:364
  150.8 6.7 %collective-permute-start.17 = (bf16[2,128,512]{2,1,0:T(8,128)(2,1)S(1)}, bf16[2,128,512]{2,1,0:T(8,128)(2,1)S(1)}, u32[]{:S(2)}, u32[]{:S(2)}) collective-permute-start(bf16[2,128,512]{2,1,0:T(8,128)(2,1)S(1)} %dynamic-slice_bitcast_fusion.3), channel_id=1, source_target_pairs={{0,4},{1,5},{2,6},{3,7},{4,0},{5,1},{6,2},{7,3},{8,12},{9,13},{10,... | collective-permute-start | bytes 786440 | tf_op jit(solution)/shard_map/ppermute | solution.py:368
  157.6 7.3 %collective-permute-start.18 = (bf16[128,512]{1,0:T(8,128)(2,1)S(1)}, bf16[128,512]{1,0:T(8,128)(2,1)S(1)}, u32[]{:S(2)}, u32[]{:S(2)}) collective-permute-start(bf16[128,512]{1,0:T(8,128)(2,1)S(1)} %dynamic-slice_bitcast_fusion.10), channel_id=1, source_target_pairs={{0,8},{1,9},{2,10},{3,11},{4,12},{5,13},{6,14},{7,15},{8,0},{9,1},... | collective-permute-start | bytes 393224 | tf_op jit(solution)/shard_map/ppermute | solution.py:369
  165.0 5.0 %collective-permute-start.19 = (bf16[128,512]{1,0:T(8,128)(2,1)S(1)}, bf16[128,512]{1,0:T(8,128)(2,1)S(1)}, u32[]{:S(2)}, u32[]{:S(2)}) collective-permute-start(bf16[128,512]{1,0:T(8,128)(2,1)S(1)} %fusion.10), channel_id=1, source_target_pairs={{0,16},{16,0},{1,17},{17,1},{2,18},{18,2},{3,19},{19,3},{4,20},{20... | collective-permute-start | bytes 393224 | tf_op jit(solution)/shard_map/ppermute | solution.py:370

commit v2 on v1

v2 whole, which is shorter than its diff:
```python
import jax
import jax.numpy as jnp
from jax import lax
from jax.experimental import pallas as pl
from jax.experimental.pallas import tpu as pltpu
from jax.sharding import PartitionSpec as P

H = 8
GROUPS = 16
EPSILON = 1e-05
MASKED = -1e30
F32 = jnp.float32
BF16 = jnp.bfloat16
VMEM_LIMIT = 56 * 1024 * 1024


def part(place, half, own):
    index = place[0] if own else 1 - place[0]
    return pl.ds(pl.multiple_of(index * half, half), half)


def call(body, ins, outs, scratch=(), flops=0, nbytes=0, limit=16, home=True):
    kinds = [kind for kind, _ in ins]
    arrays = [
        pltpu.with_memory_space_constraint(a, pltpu.VMEM) if kind == "v" else a for kind, a in ins
    ]
    spaces = {"s": pltpu.SMEM, "v": pltpu.VMEM, "d": pl.ANY}

    def kernel(*refs):
        given = [r for kind, r in zip(kinds, refs) if kind != "d"]
        body(*given, *refs[len(ins) :])

    shape = (lambda s, d: pltpu.VMEM(s, d)) if home else jax.ShapeDtypeStruct
    return pl.pallas_call(
        kernel,
        out_shape=[shape(s, d) for s, d in outs],
        in_specs=[pl.BlockSpec(memory_space=spaces[kind]) for kind in kinds],
        out_specs=[pl.BlockSpec(memory_space=pltpu.VMEM)] * len(outs),
        scratch_shapes=[pltpu.VMEM(s, d) for s, d in scratch],
        compiler_params=pltpu.CompilerParams(vmem_limit_bytes=limit * 1024 * 1024),
        cost_estimate=pl.CostEstimate(flops=flops, bytes_accessed=nbytes, transcendentals=0),
    )(*arrays)


def dot(a, b, ca=1, cb=0):
    return lax.dot_general(a, b, (((ca,), (cb,)), ((), ())), preferred_element_type=F32)


def norm_parts(v):
    centred = v - jnp.mean(v, -1, keepdims=True)
    r = lax.rsqrt(jnp.mean(centred * centred, -1, keepdims=True) + EPSILON)
    return centred * r, r


def norm_back(dy, xhat, r, gain):
    dx = dy * gain
    m1 = jnp.mean(dx, -1, keepdims=True)
    m2 = jnp.mean(dx * xhat, -1, keepdims=True)
    return r * (dx - m1 - xhat * m2), jnp.sum(dy * xhat, 0, keepdims=True)


def emit_rows(grad, rows, ks_ref, offset, c, first=0):
    pairs = grad.shape[0] // (2 * rows)
    g = grad.astype(BF16).reshape(pairs, 2, rows, grad.shape[1])
    where = (slice(first, first + pairs), slice(offset, offset + rows), slice(None))
    even, odd = g[:, 0], g[:, 1]
    send_ref, keep_ref = ks_ref
    keep_ref[where] = jnp.where(c == 0, even, odd)
    send_ref[where] = jnp.where(c == 0, odd, even)


def whole_rows(place, pair_ref, recv_ref, start, half):
    own, other = pair_ref[place[0]], recv_ref[start : start + half, :]
    first = place[0] == 0
    return jnp.concatenate([jnp.where(first, own, other), jnp.where(first, other, own)], 0)


def lane_low(shape):
    return lax.broadcasted_iota(jnp.int32, shape, 1) < 64


def stacked_heads(block):
    low = lane_low(block.shape)
    zero = jnp.zeros_like(block)
    return jnp.concatenate([jnp.where(low, block, zero), jnp.where(low, zero, block)], 0)


def unstacked_heads(block):
    rows = block.shape[0] // 2
    top, bottom = block[:rows], block[rows:]
    return jnp.where(lane_low(top.shape), top, bottom)


def head_mask(rows_per, width):
    shape = (H * rows_per, width)
    row_head = lax.broadcasted_iota(jnp.int32, shape, 0) // rows_per
    col_head = lax.broadcasted_iota(jnp.int32, shape, 1) // (width // H)
    return row_head == col_head


def block_diagonal(v, mask):
    return jnp.where(mask, jnp.concatenate([v] * H, 0), jnp.zeros((), v.dtype))


def diagonal_blocks(v, mask):
    rows = v.shape[0] // H
    v = jnp.where(mask, v, 0.0)
    return jnp.sum(v.reshape(H, rows, v.shape[1]), 0)


def forward_body(
    place, lengths, tokens, memory, recv, attn_gain, query_weight, pair_weight, write_query, out_weight,
    ffn_gain, ffn_in, ffn_out,
    x, mem, nall, qs, kall, vall, p0, p1, p2, p3, mixed, resid, n2, act, dg,
    out_send, out_own, out, wqs,
):
    y = place[0]
    width = pair_weight.shape[0]
    rows = x.shape[0]
    slots = mem.shape[0]
    half = rows // 2
    x[...] = whole_rows(place, tokens, recv, 0, half)
    mem[...] = whole_rows(place, memory, recv, half, slots // 2)
    gain = attn_gain[...]
    xhat, _ = norm_parts(x[...].astype(F32))
    nx = (xhat * gain).astype(BF16)
    mhat, _ = norm_parts(mem[...].astype(F32))
    nm = (mhat * gain).astype(BF16)
    nall[0:slots, :] = nm
    nall[slots:128, :] = jnp.zeros((128 - slots, width), BF16)
    nall[128:, :] = nx
    qs[...] = (dot(nx, query_weight[...]) * 0.125).astype(BF16)
    na = nall[...]
    kall[...] = dot(na, pair_weight[:, :width]).astype(BF16)
    vall[...] = dot(na, pair_weight[:, width:]).astype(BF16)
    wqs[...] = (dot(nm, write_query[...]) * 0.125).astype(BF16)
    bounds = []
    total = 0
    for k in range(lengths.shape[1]):
        total = total + lengths[y, k]
        bounds.append(total)
    pos_c = lax.broadcasted_iota(jnp.int32, (1, rows), 1)
    doc_c = sum([(pos_c >= b).astype(jnp.int32) for b in bounds])
    mem_bias = jnp.where(
        lax.broadcasted_iota(jnp.int32, (128, 128), 1) < slots, 0.0, MASKED
    ).astype(F32)
    for i, p_out in enumerate((p0, p1, p2, p3)):
        w = 128 * (i + 2)
        cols = w - 128
        pos_r = lax.broadcasted_iota(jnp.int32, (128, 1), 0) + 128 * i
        doc_r = sum([(pos_r >= b).astype(jnp.int32) for b in bounds])
        ok = (doc_r == doc_c[:, :cols]) & (pos_c[:, :cols] <= pos_r)
        bias = jnp.concatenate([mem_bias, jnp.where(ok, 0.0, MASKED).astype(F32)], 1)
        for p in range(H // 2):
            lanes = slice(128 * p, 128 * p + 128)
            q01 = stacked_heads(qs[128 * i : 128 * i + 128, lanes])
            s = dot(q01, kall[0:w, lanes], 1, 1)
            s = (s.reshape(2, 128, w) + bias[None]).reshape(256, w)
            e = jnp.exp(s - jnp.max(s, -1, keepdims=True))
            pr = (e * (1.0 / jnp.sum(e, -1, keepdims=True))).astype(BF16)
            p_out[p] = pr
            o = dot(pr, vall[0:w, lanes])
            mixed[128 * i : 128 * i + 128, lanes] = unstacked_heads(o).astype(BF16)
    r = x[...].astype(F32) + dot(mixed[...], out_weight[...])
    resid[...] = r
    rhat, _ = norm_parts(r)
    n2v = (rhat * ffn_gain[...]).astype(BF16)
    n2[...] = n2v
    ff = ffn_in.shape[1]
    k0 = 0.7978845608028654
    for j in range(ff // 512):
        cols = slice(512 * j, 512 * j + 512)
        v = dot(n2v, ffn_in[:, cols])
        v2 = v * v
        t = jnp.tanh(k0 * (v + 0.044715 * (v2 * v)))
        h = 0.5 * (1.0 + t)
        act[:, cols] = (v * h).astype(BF16)
        d = h + (0.5 * v) * (1.0 - t * t) * (k0 + (3.0 * 0.044715 * k0) * v2)
        dg[:, cols] = d.astype(BF16)
    out[...] = (resid[...] + dot(act[...], ffn_out[...])).astype(BF16)
    out_own[...] = out[part(place, half, True), :]
    out_send[...] = out[part(place, half, False), :]


def write_body(
    place, out, wqs, mem, memory_cotangent, recv, write_pair, write_out, write_gate, write_gain, nall,
    send, keep, dwpair, dwquery, dblend, own_new, newmem, gain_out,
):
    c, ks = place[1], (send, keep)
    slots, width = wqs.shape
    o = out[...]
    wk = dot(o, write_pair[:, :width]).astype(BF16)
    wv = dot(o, write_pair[:, width:]).astype(BF16)
    mask = head_mask(slots, width)
    qbd = block_diagonal(wqs[...], mask)
    s = dot(qbd, wk, 1, 1)
    e = jnp.exp(s - jnp.max(s, -1, keepdims=True))
    pf = e * (1.0 / jnp.sum(e, -1, keepdims=True))
    pb = pf.astype(BF16)
    wmixed = diagonal_blocks(dot(pb, wv), mask).astype(BF16)
    update = dot(wmixed, write_out[...])
    update_low = update.astype(BF16)
    gate = jax.nn.sigmoid(dot(update_low, write_gate[...]))
    blended = mem[...].astype(F32) + gate * update
    bhat, br = norm_parts(blended)
    gain = write_gain[...]
    newmem[...] = (bhat * gain).astype(BF16)
    mhalf = slots // 2
    own_new[...] = newmem[part(place, mhalf, True), :]
    mc = whole_rows(place, memory_cotangent, recv, recv.shape[0] - mhalf, mhalf).astype(F32)
    d_blend, d_gain = norm_back(mc, bhat, br, gain)
    gain_out[...] = d_gain
    dblend[...] = d_blend
    d_gate_pre = (d_blend * update * gate * (1.0 - gate)).astype(BF16)
    d_update = (d_blend * gate + dot(d_gate_pre, write_gate[...], 1, 1)).astype(BF16)
    d_wmixed = dot(d_update, write_out[...], 1, 1).astype(BF16)
    emit_rows(dot(update_low, d_gate_pre, 0, 0), 32, ks, 128, c)
    emit_rows(dot(wmixed, d_update, 0, 0), 32, ks, 96, c)
    dbd = block_diagonal(d_wmixed, mask)
    dp = dot(dbd, wv, 1, 1)
    row = jnp.sum(pf * dp, -1, keepdims=True)
    ds = (pf * (dp - row)).astype(BF16)
    d_wquery = (diagonal_blocks(dot(ds, wk), mask) * 0.125).astype(BF16)
    dwquery[...] = d_wquery
    dwk = dot(ds, qbd, 0, 0).astype(BF16)
    dwv = dot(pb, dbd, 0, 0).astype(BF16)
    dwpair[:, :width] = dwk
    dwpair[:, width:] = dwv
    emit_rows(dot(nall[0:slots, :], d_wquery, 0, 0), 32, ks, 0, c)
    emit_rows(dot(o, dwk, 0, 0), 32, ks, 32, c)
    emit_rows(dot(o, dwv, 0, 0), 32, ks, 64, c)


def ffn_back_body(
    place, dwpair, write_pair, out_cotangent, recv, ffn_out, dg, ffn_in, act, n2,
    send, keep, total_out, dout_out,
):
    c, ks = place[1], (send, keep)
    width, ff = ffn_in.shape
    rows, deep = width // GROUPS, ff // GROUPS
    cot = whole_rows(place, out_cotangent, recv, 0, out_cotangent.shape[1])
    d_out = cot.astype(F32) + dot(dwpair[...], write_pair[...], 1, 1)
    dout_out[...] = d_out
    d_branch = d_out.astype(BF16)
    total = None
    for j in range(ff // 512):
        cols = slice(512 * j, 512 * j + 512)
        d_act = dot(d_branch, ffn_out[cols, :], 1, 1).astype(BF16)
        d_inner = (d_act.astype(F32) * dg[:, cols].astype(F32)).astype(BF16)
        term = dot(d_inner, ffn_in[:, cols], 1, 1)
        total = term if total is None else total + term
        emit_rows(dot(n2[...], d_inner, 0, 0), rows, ks, rows * j, c)
        emit_rows(
            dot(act[:, cols], d_branch, 0, 0),
            deep, ks, rows * (ff // 512), c, 512 // (2 * deep) * j,
        )
    total_out[...] = total


def resid_back_body(
    place, total, dout, resid, ffn_gain, out_weight,
    dresid, dmixed, gain_out,
):
    rhat, rr = norm_parts(resid[...])
    d_norm, d_gain = norm_back(total[...], rhat, rr, ffn_gain[...])
    gain_out[...] = d_gain
    d = dout[...] + d_norm
    dresid[...] = d
    dmixed[...] = dot(d.astype(BF16), out_weight[...], 1, 1).astype(BF16)


def attn_back_body(
    place, qs, dm, vall, p3, kall, p2, p1, p0,
    dq_out, dk_out, dv_out, dk_ref, dv_ref,
):
    for p in range(H // 2):
        lanes = slice(128 * p, 128 * p + 128)
        for i, p_in in reversed(list(enumerate((p0, p1, p2, p3)))):
            w = 128 * (i + 2)
            rows = slice(128 * i, 128 * i + 128)
            q01 = stacked_heads(qs[rows, lanes])
            dm01 = stacked_heads(dm[rows, lanes])
            dp = dot(dm01, vall[0:w, lanes], 1, 1)
            pb = p_in[p]
            pf = pb.astype(F32)
            t = pf * dp
            ds = (t - pf * jnp.sum(t, -1, keepdims=True)).astype(BF16)
            dq = unstacked_heads(dot(ds, kall[0:w, lanes])) * 0.125
            dq_out[rows, lanes] = dq.astype(BF16)
            dk = dot(ds, q01, 0, 0)
            dv = dot(pb, dm01, 0, 0)
            if i == 3:
                dk_ref[0:w, lanes] = dk
                dv_ref[0:w, lanes] = dv
            else:
                dk_ref[0:w, lanes] += dk
                dv_ref[0:w, lanes] += dv
    dk_out[...] = dk_ref[...].astype(BF16)
    dv_out[...] = dv_ref[...].astype(BF16)


def input_back_body(
    place, nall, dq, dk, dv, pair_weight, query_weight, dwquery, write_query, x, mem, attn_gain,
    dresid, dblend, mixed, gain2, gain3, newmem,
    send, keep, own_tok, own_mem, swap, gtok, gmem,
):
    c, ks = place[1], (send, keep)
    rows, width = x.shape
    slots = mem.shape[0]
    half, mhalf = rows // 2, slots // 2
    na = nall[...]
    dqv = dq[...]
    emit_rows(dot(na[128:], dqv, 0, 0), 32, ks, 0, c)
    emit_rows(dot(na, dk[...], 0, 0), 32, ks, 32, c)
    emit_rows(dot(na, dv[...], 0, 0), 32, ks, 64, c)
    emit_rows(dot(mixed[...], dresid[...].astype(BF16), 0, 0), 32, ks, 96, c)
    d_all = dot(dk[...], pair_weight[:, :width], 1, 1)
    d_all = d_all + dot(dv[...], pair_weight[:, width:], 1, 1)
    d_nx = d_all[128:] + dot(dqv, query_weight[...], 1, 1)
    d_nm = d_all[:slots] + dot(dwquery[...], write_query[...], 1, 1)
    gain = attn_gain[...]
    xhat, xr = norm_parts(x[...].astype(F32))
    d_x, g_x = norm_back(d_nx, xhat, xr, gain)
    mhat, mr = norm_parts(mem[...].astype(F32))
    d_m, g_m = norm_back(d_nm, mhat, mr, gain)
    gains = jnp.concatenate(
        [g_x + g_m, gain2[...], gain3[...], jnp.zeros((29, width), F32)], 0
    ).astype(BF16)
    for one in ks:
        one[:, 128:160, :] = jnp.broadcast_to(gains, (GROUPS // 2, 32, width))
    gtok[...] = dresid[...] + d_x
    gmem[...] = dblend[...] + d_m
    own_tok[...] = gtok[part(place, half, True), :]
    own_mem[...] = gmem[part(place, mhalf, True), :]
    other = part(place, half, False)
    mother = part(place, mhalf, False)
    swap[0:half, :] = gtok[other, :].astype(BF16)
    swap[half : half + mhalf, :] = newmem[mother, :]
    swap[half + mhalf :, :] = gmem[mother, :].astype(BF16)


BIT = {"y": 0, "x": 2, "z": 3, "h": 4}


def other_of(axis, bit):
    return [(i, i ^ bit) for i in range(lax.axis_size(axis))]


def exchanged(send, label):
    if label == "y":
        return lax.ppermute(send, "seq", other_of("seq", 1))
    return lax.ppermute(send, "seg", other_of("seg", {"x": 2, "z": 4, "h": 8, "c": 1}[label]))


class Stream:
    def __init__(self, keep, recv, dims, start, rows):
        self.keep, self.recv, self.dims, self.start, self.rows = keep, recv, dims, start, rows


def stage(place, streams, labels, joined=False, deps=()):
    ins = [("s", place)]
    index = {}
    for s in streams:
        for arr in (s.keep, s.recv):
            if id(arr) not in index:
                index[id(arr)] = len(ins)
                ins.append(("v", arr))
    n_arrays = len(ins)
    ins += [("d", d) for d in deps]
    width = streams[0].keep.shape[-1]
    shapes, new_dims, new_rows = [], [], []
    for s, label in zip(streams, labels):
        rows = s.rows // 2 if label == "y" else s.rows
        dims = s.dims.replace(label, "")
        new_dims.append(dims)
        new_rows.append(rows)
        shapes.append((2,) * len(dims) + (rows, width))
    if joined:
        shapes = [(sum(new_rows), width)]
    outs = []
    for shape in shapes:
        outs += [(shape, BF16)] * 2

    def body(place, *refs):
        given, made = refs[: n_arrays - 1], refs[n_arrays - 1 :]

        def value(s, label, own, arr):
            bit = place[BIT[label]]
            bit = bit if own else 1 - bit
            where = []
            for d in s.dims:
                where.append(bit if d == label else slice(None))
            if label == "y":
                half = s.rows // 2
                where.append(pl.ds(pl.multiple_of(s.start + bit * half, 16), half))
            else:
                where.append(slice(s.start, s.start + s.rows))
            return given[index[id(arr)] - 1][tuple(where) + (slice(None),)].astype(F32)

        for own in (False, True):
            at = 0
            for k, (s, label) in enumerate(zip(streams, labels)):
                total = (value(s, label, own, s.keep) + value(s, label, own, s.recv)).astype(BF16)
                target = made[(0 if joined else 2 * k) + (0 if own else 1)]
                if joined:
                    target[at : at + new_rows[k], :] = total
                    at += new_rows[k]
                else:
                    target[...] = total

    results = call(body, ins, outs, flops=10**6, nbytes=10**6)
    if joined:
        return results[0], results[1]
    return [
        (results[2 * k], results[2 * k + 1], new_dims[k], new_rows[k]) for k in range(len(streams))
    ]


def added(place, keep, recv):
    def body(place, keep, recv, total):
        total[...] = (keep[...].astype(F32) + recv[...].astype(F32)).astype(BF16)

    (total,) = call(
        body,
        [("s", place), ("v", keep), ("v", recv)],
        [(keep.shape, BF16)],
        flops=10**6, nbytes=10**6,
    )
    return total


def reduced_any(keep, send, pieces):
    groups = lax.axis_size("seg")
    c = lax.axis_index("seg") % 2
    first = jnp.where(c == 0, keep, send)
    second = jnp.where(c == 0, send, keep)
    total = jnp.stack([first, second], 1)
    total = total.reshape((GROUPS,) + keep.shape[1:])
    fine = groups // GROUPS
    parts = []
    at = 0
    for rows, shared in pieces:
        piece = total[:, at : at + rows]
        if shared:
            piece = jnp.broadcast_to(piece[:, None], (GROUPS, fine) + piece.shape[1:])
        else:
            piece = piece.reshape(GROUPS, fine, rows // fine, piece.shape[2])
        parts.append(piece.reshape(groups, -1, piece.shape[-1]))
        at += rows
    total = jnp.concatenate(parts, 1)
    total = lax.psum_scatter(total.astype(F32), "seg", scatter_dimension=0, tiled=True)[0]
    return lax.psum(total, "seq")


def final_parts(place, one, two, ff):
    width = one[0].shape[-1]
    r = width // GROUPS
    n = ff // 512
    shapes = [
        (r, width), (r, 2 * width), (r, width), (r, ff), (ff // GROUPS, width),
        (r, width), (r, 2 * width), (r, width), (r, width), (8, width),
    ]

    def body(place, t1, o1, t2, o2, gq, gp, go, gfi, gfo, gwq, gwp, gwo, gwg, gains, full1, full2):
        y = place[0]
        for t, o, full, streams in ((t1, o1, full1, one[2]), (t2, o2, full2, two[2])):
            at = start = 0
            for rows in streams:
                half = rows // 2
                for ref, own in ((t, True), (o, False)):
                    index = y if own else 1 - y
                    full[pl.ds(pl.multiple_of(start + index * half, 16), half), :] = ref[
                        at : at + half, :
                    ].astype(F32)
                at += half
                start += rows
        gq[...] = full2[0:r, :]
        gp[:, :width] = full2[r : 2 * r, :]
        gp[:, width:] = full2[2 * r : 3 * r, :]
        go[...] = full2[3 * r : 4 * r, :]
        gains[...] = full2[4 * r : 4 * r + 8, :]
        gwq[...] = full1[0:r, :]
        gwp[:, :width] = full1[r : 2 * r, :]
        gwp[:, width:] = full1[2 * r : 3 * r, :]
        gwo[...] = full1[3 * r : 4 * r, :]
        gwg[...] = full1[4 * r : 5 * r, :]
        for j in range(n):
            gfi[:, 512 * j : 512 * j + 512] = full1[(5 + j) * r : (6 + j) * r, :]
        gfo[...] = full1[(5 + n) * r :, :]

    ins = [("s", place)] + [("v", a) for a in (one[0], one[1], two[0], two[1])]
    return call(
        body, ins, [(s, F32) for s in shapes],
        scratch=[((sum(one[2]), width), F32), ((sum(two[2]), width), F32)],
        flops=10**6, nbytes=10**6, home=False,
    )


def shards(
    tokens, memory, lengths, attn_gain, query_weight, pair_weight, out_weight, ffn_gain, ffn_in,
    ffn_out, write_query, write_pair, write_out, write_gate, write_gain, out_cotangent,
    memory_cotangent,
):
    half, width = tokens.shape[1:]
    mhalf = memory.shape[1]
    rows, slots, ff = 2 * half, 2 * mhalf, ffn_in.shape[1]
    padded = rows + 128
    groups = lax.axis_size("seg")
    y = lax.axis_index("seq")
    seg = lax.axis_index("seg")
    place = jnp.stack([y, seg % 2, (seg // 2) % 2, (seg // 4) % 2, (seg // 8) % 2])
    place = place.astype(jnp.int32)
    sc = ("s", place)
    pick = lambda v: lax.dynamic_index_in_dim(v, 1 - y, 0, keepdims=False)
    recv_a = exchanged(jnp.concatenate([pick(tokens), pick(memory)], 0), "y")
    recv_b = exchanged(jnp.concatenate([pick(out_cotangent), pick(memory_cotangent)], 0), "y")
    ag, fg, wg = attn_gain[None], ffn_gain[None], write_gain[None]
    v = lambda *arrs: [("v", a) for a in arrs]
    big = ((rows, width), BF16)
    wide = ((padded, width), BF16)
    deep = ((rows, ff), BF16)
    half_b = ((half, width), BF16)
    keep_send = lambda n: [((GROUPS // 2, n, width), BF16)] * 2
    small = ((slots, width), BF16)
    full_f = ((rows, width), F32)
    gain_row = ((1, width), F32)
    (
        x, mem, nall, qs, kall, vall, p0, p1, p2, p3, mixed, resid, n2, act, dg,
        out_send, out_own, out, wqs,
    ) = call(
        forward_body,
        [sc, ("s", lengths)] + v(tokens, memory, recv_a, ag, query_weight, pair_weight, write_query, out_weight, fg, ffn_in, ffn_out),
        [big, small, wide, big, wide, wide]
        + [((H // 2, 256, 128 * (i + 2)), BF16) for i in range(4)]
        + [big, full_f, big, deep, deep, half_b, half_b, big, small],
        flops=2 * 6 * 10**9, nbytes=20 * 10**6,
    )
    out_recv = exchanged(out_send, "y")
    send0, keep0, dwpair, dwquery, dblend, own_new, newmem, gain3 = call(
        write_body,
        [sc] + v(out, wqs, mem, memory_cotangent, recv_b, write_pair, write_out, write_gate, wg, nall),
        [
            *keep_send(160), ((rows, 2 * width), BF16), small,
            ((slots, width), F32), ((mhalf, width), BF16), small, gain_row,
        ],
        flops=2 * 3 * 10**9, nbytes=10 * 10**6,
    )
    small_mesh = groups == GROUPS
    send1, keep1, total, dout = call(
        ffn_back_body,
        [sc] + v(dwpair, write_pair, out_cotangent, recv_b, ffn_out, dg, ffn_in, act, n2),
        [*keep_send(256), full_f, full_f],
        flops=2 * 5 * 10**9, nbytes=20 * 10**6,
    )
    dresid, dmixed, gain2 = call(
        resid_back_body, [sc] + v(total, dout, resid, fg, out_weight), [full_f, big, gain_row],
        flops=2 * 10**9, nbytes=5 * 10**6,
    )
    deps1, deps2 = [], []
    if small_mesh:
        cube = lambda a: a.reshape((2, 2, 2) + a.shape[1:])
        recv0, recv1 = exchanged(send0, "c"), exchanged(send1, "c")
        k0, r0, k1, r1 = cube(keep0), cube(recv0), cube(keep1), cube(recv1)
        streams = [
            Stream(k0, r0, "hzx", 0, 160), Stream(k1, r1, "hzx", 0, 128),
            Stream(k1, r1, "hzx", 128, 128),
        ]
        orders = ("xyz", "yzx", "zxy")

        def moved(parts, step):
            return [
                Stream(keep, exchanged(send, orders[k][step]), dims, 0, r)
                for k, (keep, send, dims, r) in enumerate(parts)
            ]

        labels = lambda step: [o[step] for o in orders]
        parts = stage(place, streams, labels(0), deps=[dresid])
        deps1 = [("d", p[0]) for p in parts]
        streams = moved(parts, 0)
    dq, dk, dv = call(
        attn_back_body,
        [sc] + v(qs, dmixed, vall, p3, kall, p2, p1, p0) + deps1,
        [big, wide, wide],
        scratch=[((padded, width), F32)] * 2,
        flops=2 * 6 * 10**9, nbytes=20 * 10**6,
    )
    if small_mesh:
        parts = stage(place, streams, labels(1), deps=[dq])
        deps2 = [("d", p[0]) for p in parts]
        streams = moved(parts, 1)
    send2, keep2, own_tok, own_mem, swap = call(
        input_back_body,
        [sc]
        + v(
            nall, dq, dk, dv, pair_weight, query_weight, dwquery, write_query, x, mem, ag, dresid,
            dblend, mixed, gain2, gain3, newmem,
        )
        + deps2,
        [
            *keep_send(160), ((half, width), F32), ((mhalf, width), F32),
            ((half + 2 * mhalf, width), BF16),
        ],
        scratch=[((rows, width), F32), ((slots, width), F32)],
        flops=2 * 3 * 10**9, nbytes=20 * 10**6,
    )
    swapped = exchanged(swap, "y")
    r = width // groups
    if small_mesh:
        recv2 = exchanged(send2, "c")
        k2, r2 = cube(keep2), cube(recv2)
        keep, send = stage_three(place, streams, labels(2), swap)
        t1 = added(place, keep, exchanged(send, "h"))
        o1 = exchanged(t1, "y")
        late = [
            Stream(k2, r2, "hzx", 0, 64), Stream(k2, r2, "hzx", 64, 32),
            Stream(k2, r2, "hzx", 96, 64),
        ]
        late = moved(stage(place, late, labels(0)), 0)
        late = moved(stage(place, late, labels(1)), 1)
        late = moved(stage(place, late, labels(2)), 2)
        keep, send = stage(place, late, "hhh", joined=True)
        t2 = added(place, keep, exchanged(send, "h"))
        o2 = exchanged(t2, "y")
        gq, gp, go, gfi, gfo, gwq, gwp, gwo, gwg, gains = final_parts(
            place, (t1, o1, (160, 128, 128)), (t2, o2, (64, 32, 64)), ff
        )
    else:
        w = width // GROUPS
        w0 = reduced_any(keep0, send0, [(w, False)] * 5)
        w1 = reduced_any(keep1, send1, [(w, False)] * (ff // 512) + [(ff // GROUPS, False)])
        w2 = reduced_any(keep2, send2, [(w, False)] * 4 + [(32, True)])
        cut = lambda a, at, n: jnp.concatenate(
            [a[(at + i) * r : (at + i + 1) * r] for i in range(n)], 1
        )
        gq, gp, go, gains = cut(w2, 0, 1), cut(w2, 1, 2), cut(w2, 3, 1), w2[4 * r :]
        gfi, gfo = cut(w1, 0, ff // 512), w1[(ff // 512) * r :]
        gwq, gwp, gwo, gwg = cut(w0, 0, 1), cut(w0, 1, 2), cut(w0, 3, 1), cut(w0, 4, 1)
    gain_of = lambda i: lax.dynamic_slice_in_dim(gains[i], seg * r, r, 0)

    def both(own, recv):
        recv = recv.astype(own.dtype)
        return jnp.where(jnp.arange(2)[:, None, None] == y, own[None], recv[None])

    return (
        both(out_own, out_recv),
        both(own_new, swapped[half : half + mhalf]),
        both(own_tok, swapped[:half]),
        both(own_mem, swapped[half + mhalf :]),
        gain_of(0), gq, gp, go, gain_of(1), gfi, gfo, gwq, gwp, gwo, gwg, gain_of(2),
    )


def stage_three(place, streams, labels, dep):
    parts = stage(place, streams, labels, deps=[dep])
    moved = [
        Stream(keep, exchanged(send, label), dims, 0, r)
        for label, (keep, send, dims, r) in zip(labels, parts)
    ]
    return stage(place, moved, "hhh", joined=True)


def solution(mesh):
    row = P("seg", "seq", None)
    grad = P("seg", None)
    in_specs = (row, row, P("seg", None)) + (P(),) * 12 + (row, row)
    out_specs = (row, row, row, row, P("seg"), grad, grad, grad, P("seg")) + (grad,) * 6 + (P("seg"),)
    return jax.shard_map(shards, mesh=mesh, in_specs=in_specs, out_specs=out_specs, check_vma=False)
```

time: 172 us -> 145 us (0.84)
  waiting for transfers between devices: 65.3 us -> 40.9 us
  Pallas kernels: 56.7 us -> 50.2 us
  local copies, waits for them, and re-layouts: 7.93 us -> 12.5 us
  other arithmetic: 9.82 us -> 7.01 us
    ppermute x28 -> x29, waiting for transfers between devices: 65.3 us -> 40.9 us  [the longest x12 23.9 us: exchanged(): return lax.ppermute(send, 'seq', other_of('seq', 1))]
    pallas_call x4 -> x17, Pallas kernels: 56.7 us -> 50.2 us  [call(): pl.pallas_call(kernel, out_shape=[shape(s, d) for s, d in outs], in_specs...]
    unnamed x24 -> x70, local copies, waits for them, and re-layouts: 2.69 us -> 7.68 us
    concatenate x8 -> x1, other arithmetic: 2.88 us -> 0.02 us  [shards(): recv_a = exchanged(jnp.concatenate([pick(tokens), pick(memory)], 0), 'y')]
    convert_element_type x24 -> x0, other arithmetic: 2.76 us -> none  [the longest x21 2.66 us: added(): return (keep.astype(F32) + recv.astype(F32)).astype(BF16)]
    slice x19 -> x0, local copies, waits for them, and re-layouts: 1.79 us -> none  [the longest x2 0.69 us: reduced_small(): second[ha:]]
    squeeze x4, local copies, waits for them, and re-layouts: 1.82 us -> 3.6 us  [shards(): pick = lambda v: lax.dynamic_index_in_dim(v, 1 - y, 0, keepdims=False)]
    convert_element_type x2, other arithmetic: 0.06 us -> 1.78 us  [both(): recv = recv.astype(own.dtype)]
  transfers between devices with their start and end apart: 28 -> 29, of which waited for: 16 -> 15; matrix products, arithmetic and copies ran while one was open for 7% -> 6% of each run, Pallas kernels for 28% -> 21%
where the time goes in v2:
time: 145 us; the launch traced here: 144 us
  Pallas kernels  50.2 us (35%)
  waiting for transfers between devices  40.9 us (28%)
  starting transfers between devices  32.2 us (22%)
  local copies, waits for them, and re-layouts  12.5 us (9%)
  other arithmetic  7.01 us (5%)
    pallas_call x17, Pallas kernels, call(): pl.pallas_call(kernel, out_shape=[shape(s, d) for s, d in outs], in_specs...  50.2 us
    ppermute x12, waiting for transfers between devices, exchanged(): return lax.ppermute(send, 'seq', other_of('seq', 1))  23.9 us
    ppermute x17, starting transfers between devices, exchanged(): lax.ppermute(send, 'seg', other_of('seg', {'x': 2, 'z': 4, 'h': 8, 'c': 1...  19.4 us
    ppermute x17, waiting for transfers between devices, exchanged(): lax.ppermute(send, 'seg', other_of('seg', {'x': 2, 'z': 4, 'h': 8, 'c': 1...  16.9 us
    ppermute x12, starting transfers between devices, exchanged(): return lax.ppermute(send, 'seq', other_of('seq', 1))  12.8 us
    unnamed x70, local copies, waits for them, and re-layouts  7.68 us
    select_n x4, other arithmetic, both(): return jnp.where(jnp.arange(2)[:, None, None] == y, own[None], recv[None])  4.47 us
    squeeze x4, local copies, waits for them, and re-layouts, shards(): pick = lambda v: lax.dynamic_index_in_dim(v, 1 - y, 0, keepdims=False)  3.6 us
  transfers between devices with their start and end apart: 29, of which 15 were waited for; matrix products, arithmetic and copies ran while one was open for 6% of the time, Pallas kernels for 21%

profile of v2, /device:TPU:0, one launch (start us, length us, event | category | flops | bytes accessed | tf_op | source)
XLA Modules:
  0.0 144.0 jit_solution(14330112793723031143)
XLA Ops:
  0.7 0.9 dynamic-slice_bitcast_fusion.3
  1.6 1.0 dynamic-slice_bitcast_fusion.1
  2.6 3.0 %collective-permute-start = (bf16[288,512]{1,0:T(8,128)(2,1)S(1)}, bf16[288,512]{1,0:T(8,128)(2,1)S(1)}, u32[]{:S(2)}, u32[]{:S(2)}) collective-permute-start(bf16[288,512]{1,0:T(8,128)(2,1)S(1)} %pad_maximum_fusion), channel_id=1, source_target_pairs={{0,16},{16,0},{1,17},{17,1},{2,18},{18,2},{3,19},{19,3},{4,20},{20... | collective-permute-start | bytes 884744 | tf_op jit(solution)/shard_map/ppermute | solution.py:351
  6.4 1.0 dynamic-slice_bitcast_fusion
  8.2 5.3 %collective-permute-done.refs_4_ = bf16[288,512]{1,0:T(8,128)(2,1)S(1)} collective-permute-done((bf16[288,512]{1,0:T(8,128)(2,1)S(1)}, bf16[288,512]{1,0:T(8,128)(2,1)S(1)}, u32[]{:S(2)}, u32[]{:S(2)}) %collective-permute-start) | collective-permute-done | bytes 294944 | tf_op jit(solution)/shard_map/ppermute | solution.py:351
  14.3 1.6 %copy-done.14 = bf16[512,2048]{1,0:T(8,128)(2,1)S(1)} copy-done((bf16[512,2048]{1,0:T(8,128)(2,1)S(1)}, bf16[512,2048]{1,0:T(8,128)(2,1)}, u32[]{:S(2)}) %copy-start.14) | copy-done | bytes 2097176
  15.9 1.6 %copy-done.16 = bf16[2048,512]{1,0:T(8,128)(2,1)S(1)} copy-done((bf16[2048,512]{1,0:T(8,128)(2,1)S(1)}, bf16[2048,512]{1,0:T(8,128)(2,1)}, u32[]{:S(2)}) %copy-start.16) | copy-done | bytes 2097176
  17.4 1.0 copy-done.25
  18.5 1.0 copy-done.27
  19.5 1.0 copy-done.30
  20.5 13.8 %shard_map.288 = (bf16[512,512]{1,0:T(8,128)(2,1)S(1)}, bf16[64,512]{1,0:T(8,128)(2,1)S(1)}, bf16[640,512]{1,0:T(8,128)(2,1)S(1)}, bf16[512,512]{1,0:T(8,128)(2,...) custom-call(s32[5]{0:T(128)S(1)} %stack.23.refs_0_, ...), custom_call_target="tpu_custom_call" | custom-call | flops 12000000000 | bytes 20000000 | tf_op jit(solution)/shard_map/pallas_call | solution.py:34
  34.4 6.1 %shard_map.289 = (bf16[8,160,512]{2,1,0:T(8,128)(2,1)S(1)}, bf16[8,160,512]{2,1,0:T(8,128)(2,1)S(1)}, bf16[512,1024]{1,0:T(8,128)(2,1)S(1)}, bf16[64,512]{1,0:T(...) custom-call(s32[5]{0:T(128)S(1)} %stack.23.refs_0_, ...), custom_call_target="tpu_custom_call" | custom-call | flops 6000000000 | bytes 10000000 | tf_op jit(solution)/shard_map/pallas_call | solution.py:34
  41.1 6.2 %shard_map.290 = (bf16[8,256,512]{2,1,0:T(8,128)(2,1)S(1)}, bf16[8,256,512]{2,1,0:T(8,128)(2,1)S(1)}, f32[512,512]{1,0:T(8,128)S(1)}, f32[512,512]{1,0:T(8,128)S(1)}) custom-call(s32[5]{0:T(128)S(1)} %stack.23.refs_0_, bf16[512,1024]{1,0:T(8,128)(2,1)S(1)} %get-tuple-element.116.refs_1_, bf16[512,1024]{1,0:T(8,128)(2,1)S(1)} %copy-done.18, ...), custom_call_target="tpu_custom_call" | custom-call | flops 10000000000 | bytes 20000000 | tf_op jit(solution)/shard_map/pallas_call | solution.py:34
  47.9 1.6 %shard_map.291 = (f32[512,512]{1,0:T(8,128)S(1)}, bf16[512,512]{1,0:T(8,128)(2,1)S(1)}, f32[1,512]{1,0:T(1,128)S(1)}) custom-call(s32[5]{0:T(128)S(1)} %stack.23.refs_0_, f32[512,512]{1,0:T(8,128)S(1)} %get-tuple-element.120.refs_1_, f32[512,512]{1,0:T(8,128)S(1)} %get-tuple-element.121.refs_2_, f32[512,512]{1,0:T(8,128)S(1)} %get-tuple-element.122.refs_3_, ...), custom_call_target="tpu_custom_call" | custom-call | flops 2000000000 | bytes 5000000 | tf_op jit(solution)/shard_map/pallas_call | solution.py:34
  49.5 3.9 %collective-permute-done.3 = bf16[8,160,512]{2,1,0:T(8,128)(2,1)S(1)} collective-permute-done((bf16[8,160,512]{2,1,0:T(8,128)(2,1)S(1)}, bf16[8,160,512]{2,1,0:T(8,128)(2,1)S(1)}, u32[]{:S(2)}, u32[]{:S(2)}) %collective-permute-start.3) | collective-permute-done | bytes 1310752 | tf_op jit(solution)/shard_map/ppermute | solution.py:352
  53.4 1.3 shard_map.292
  54.7 2.1 %collective-permute-start.6 = (bf16[2,2,2,64,512]{4,3,2,1,0:T(8,128)(2,1)S(1)}, bf16[2,2,2,64,512]{4,3,2,1,0:T(8,128)(2,1)S(1)}, u32[]{:S(2)}, u32[]{:S(2)}) collective-permute-start(bf16[2,2,2,64,512]{4,3,2,1,0:T(8,128)(2,1)S(1)} %get-tuple-element.149), channel_id=1, source_target_pairs={{0,16},{16,0},{1,17},{17,1},{2,18},{18,2},{3,19},{19,3},{4,20},{20... | collective-permute-start | bytes 1572872 | tf_op jit(solution)/shard_map/ppermute | solution.py:351
  56.9 1.6 %collective-permute-start.7 = (bf16[2,2,128,512]{3,2,1,0:T(8,128)(2,1)S(1)}, bf16[2,2,128,512]{3,2,1,0:T(8,128)(2,1)S(1)}, u32[]{:S(2)}, u32[]{:S(2)}) collective-permute-start(bf16[2,2,128,512]{3,2,1,0:T(8,128)(2,1)S(1)} %get-tuple-element.150), channel_id=1, source_target_pairs={{0,4},{1,5},{2,6},{3,7},{4,0},{5,1},{6,2},{7,3},{8,12},{9,13},{10,... | collective-permute-start | bytes 1572872 | tf_op jit(solution)/shard_map/ppermute | solution.py:352
  58.4 1.5 %collective-permute-start.5 = (bf16[2,2,160,512]{3,2,1,0:T(8,128)(2,1)S(1)}, bf16[2,2,160,512]{3,2,1,0:T(8,128)(2,1)S(1)}, u32[]{:S(2)}, u32[]{:S(2)}) collective-permute-start(bf16[2,2,160,512]{3,2,1,0:T(8,128)(2,1)S(1)} %get-tuple-element.148), channel_id=1, source_target_pairs={{0,2},{1,3},{2,0},{3,1},{4,6},{5,7},{6,4},{7,5},{8,10},{9,11},{10,... | collective-permute-start | bytes 1966088 | tf_op jit(solution)/shard_map/ppermute | solution.py:352
  59.9 8.5 %shard_map.293 = (bf16[512,512]{1,0:T(8,128)(2,1)S(1)}, bf16[640,512]{1,0:T(8,128)(2,1)S(1)}, bf16[640,512]{1,0:T(8,128)(2,1)S(1)}) custom-call(s32[5]{0:T(128)S(1)} %stack.23.refs_0_, bf16[512,512]{1,0:T(8,128)(2,1)S(1)} %get-tuple-element.115.refs_1_, bf16[512,512]{1,0:T(8,128)(2,1)S(1)} %get-tuple-element.123.refs_2_, ...), custom_call_target="tpu_custom_call" | custom-call | flops 12000000000 | bytes 20000000 | tf_op jit(solution)/shard_map/pallas_call | solution.py:34
  69.1 1.5 %collective-permute-done.7.refs_6_ = bf16[2,2,128,512]{3,2,1,0:T(8,128)(2,1)S(1)} collective-permute-done((bf16[2,2,128,512]{3,2,1,0:T(8,128)(2,1)S(1)}, bf16[2,2,128,512]{3,2,1,0:T(8,128)(2,1)S(1)}, u32[]{:S(2)}, u32[]{:S(2)}) %collective-permute-start.7) | collective-permute-done | bytes 524320 | tf_op jit(solution)/shard_map/ppermute | solution.py:352
  70.5 4.1 %collective-permute-done.5.refs_2_ = bf16[2,2,160,512]{3,2,1,0:T(8,128)(2,1)S(1)} collective-permute-done((bf16[2,2,160,512]{3,2,1,0:T(8,128)(2,1)S(1)}, bf16[2,2,160,512]{3,2,1,0:T(8,128)(2,1)S(1)}, u32[]{:S(2)}, u32[]{:S(2)}) %collective-permute-start.5) | collective-permute-done | bytes 655392 | tf_op jit(solution)/shard_map/ppermute | solution.py:352
  74.7 1.7 %shard_map.294 = (bf16[2,2,80,512]{3,2,1,0:T(8,128)(2,1)S(1)}, bf16[2,2,80,512]{3,2,1,0:T(8,128)(2,1)}, bf16[2,2,64,512]{3,2,1,0:T(8,128)(2,1)S(1)}, bf16[2,2,64...) custom-call(s32[5]{0:T(128)S(1)} %stack.23.refs_0_, ...), custom_call_target="tpu_custom_call" | custom-call | flops 1000000 | bytes 1000000 | tf_op jit(solution)/shard_map/pallas_call | solution.py:34
  76.4 3.7 %shard_map.295 = (bf16[8,160,512]{2,1,0:T(8,128)(2,1)S(1)}, bf16[8,160,512]{2,1,0:T(8,128)(2,1)S(1)}, f32[256,512]{1,0:T(8,128)S(1)}, f32[32,512]{1,0:T(8,128)S(1)}, bf16[320,512]{1,0:T(8,128)(2,1)S(1)}) custom-call(s32[5]{0:T(128)S(1)} %stack.23.refs_0_, bf16[640,512]{1,0:T(8,128)(2,1)S(1)} %get-tuple-element.113.refs_10_.refs_1_, ...), custom_call_target="tpu_custom_call" | custom-call | flops 6000000000 | bytes 20000000 | tf_op jit(solution)/shard_map/pallas_call | solution.py:34
  81.0 1.6 %collective-permute-start.11 = (bf16[2,128,512]{2,1,0:T(8,128)(2,1)}, bf16[2,128,512]{2,1,0:T(8,128)(2,1)}, u32[]{:S(2)}, u32[]{:S(2)}) collective-permute-start(bf16[2,128,512]{2,1,0:T(8,128)(2,1)} %get-tuple-element.159), channel_id=1, source_target_pairs={{0,2},{1,3},{2,0},{3,1},{4,6},{5,7},{6,4},{7,5},{8,10},{9,11},{10,... | collective-permute-start | bytes 786440 | tf_op jit(solution)/shard_map/ppermute | solution.py:352
  82.6 1.5 %collective-permute-start.9 = (bf16[2,2,80,512]{3,2,1,0:T(8,128)(2,1)}, bf16[2,2,80,512]{3,2,1,0:T(8,128)(2,1)}, u32[]{:S(2)}, u32[]{:S(2)}) collective-permute-start(bf16[2,2,80,512]{3,2,1,0:T(8,128)(2,1)} %get-tuple-element.157), channel_id=1, source_target_pairs={{0,16},{16,0},{1,17},{17,1},{2,18},{18,2},{3,19},{19,3},{4,20},{20... | collective-permute-start | bytes 983048 | tf_op jit(solution)/shard_map/ppermute | solution.py:351
  85.6 4.1 %collective-permute-done.1 = bf16[256,512]{1,0:T(8,128)(2,1)} collective-permute-done((bf16[256,512]{1,0:T(8,128)(2,1)}, bf16[256,512]{1,0:T(8,128)(2,1)}, u32[]{:S(2)}, u32[]{:S(2)}) %collective-permute-start.1) | collective-permute-done | bytes 262176 | tf_op jit(solution)/shard_map/ppermute | solution.py:351
  89.6 1.5 %collective-permute-start.18 = (bf16[2,2,64,512]{3,2,1,0:T(8,128)(2,1)S(1)}, bf16[2,2,64,512]{3,2,1,0:T(8,128)(2,1)S(1)}, u32[]{:S(2)}, u32[]{:S(2)}) collective-permute-start(bf16[2,2,64,512]{3,2,1,0:T(8,128)(2,1)S(1)} %get-tuple-element.171), channel_id=1, source_target_pairs={{0,2},{1,3},{2,0},{3,1},{4,6},{5,7},{6,4},{7,5},{8,10},{9,11},{10,... | collective-permute-start | bytes 786440 | tf_op jit(solution)/shard_map/ppermute | solution.py:352
  91.6 1.9 %broadcast_select_fusion.1 = bf16[2,256,512]{2,1,0:T(8,128)(2,1)} fusion(pred[2]{0:T(512)(128)(4,1)S(1)} %iota_compare_fusion, bf16[256,512]{1,0:T(8,128)(2,1)} %collective-permute-done.1, bf16[256,512]{1,0:T(8,128)(2,1)S(1)} %copy-done.7), kind=kLoop, calls=%fused_computation.1 | loop fusion | flops 262144 | bytes 1048578 | tf_op jit(solution)/shard_map/jit(_where)/select_n | solution.py:642
  93.4 3.2 %collective-permute-done.9.refs_2_ = bf16[2,2,80,512]{3,2,1,0:T(8,128)(2,1)} collective-permute-done((bf16[2,2,80,512]{3,2,1,0:T(8,128)(2,1)}, bf16[2,2,80,512]{3,2,1,0:T(8,128)(2,1)}, u32[]{:S(2)}, u32[]{:S(2)}) %collective-permute-start.9) | collective-permute-done | bytes 327712 | tf_op jit(solution)/shard_map/ppermute | solution.py:351
  96.7 1.3 shard_map.296
  98.0 1.5 %collective-permute-start.13 = (bf16[2,64,512]{2,1,0:T(8,128)(2,1)S(1)}, bf16[2,64,512]{2,1,0:T(8,128)(2,1)S(1)}, u32[]{:S(2)}, u32[]{:S(2)}) collective-permute-start(bf16[2,64,512]{2,1,0:T(8,128)(2,1)S(1)} %get-tuple-element.163), channel_id=1, source_target_pairs={{0,2},{1,3},{2,0},{3,1},{4,6},{5,7},{6,4},{7,5},{8,10},{9,11},{10,... | collective-permute-start | bytes 393224 | tf_op jit(solution)/shard_map/ppermute | solution.py:352
  100.1 3.6 %collective-permute-done.8 = bf16[320,512]{1,0:T(8,128)(2,1)} collective-permute-done((bf16[320,512]{1,0:T(8,128)(2,1)S(1)}, bf16[320,512]{1,0:T(8,128)(2,1)}, u32[]{:S(2)}, u32[]{:S(2)}) %collective-permute-start.8) | collective-permute-done | bytes 327712 | tf_op jit(solution)/shard_map/ppermute | solution.py:351
  104.2 1.0 slice_convert_fusion
  105.2 3.5 %collective-permute-done.19.refs_4_ = bf16[2,2,2,16,512]{4,3,2,1,0:T(8,128)(2,1)S(1)} collective-permute-done((bf16[2,2,2,16,512]{4,3,2,1,0:T(8,128)(2,1)S(1)}, bf16[2,2,2,16,512]{4,3,2,1,0:T(8,128)(2,1)S(1)}, u32[]{:S(2)}, u32[]{:S(2)}) %collective-permute-start.19) | collective-permute-done | bytes 131104 | tf_op jit(solution)/shard_map/ppermute | solution.py:351
  110.3 1.6 %collective-permute-start.23 = (bf16[2,64,512]{2,1,0:T(8,128)(2,1)S(1)}, bf16[2,64,512]{2,1,0:T(8,128)(2,1)S(1)}, u32[]{:S(2)}, u32[]{:S(2)}) collective-permute-start(bf16[2,64,512]{2,1,0:T(8,128)(2,1)S(1)} %get-tuple-element.181), channel_id=1, source_target_pairs={{0,2},{1,3},{2,0},{3,1},{4,6},{5,7},{6,4},{7,5},{8,10},{9,11},{10,... | collective-permute-start | bytes 393224 | tf_op jit(solution)/shard_map/ppermute | solution.py:352
  111.9 1.2 broadcast_select_fusion
  113.8 0.9 collective-permute-start.12
  115.9 1.7 %collective-permute-start.25 = (bf16[2,16,512]{2,1,0:T(8,128)(2,1)S(1)}, bf16[2,16,512]{2,1,0:T(8,128)(2,1)S(1)}, u32[]{:S(2)}, u32[]{:S(2)}) collective-permute-start(bf16[2,16,512]{2,1,0:T(8,128)(2,1)S(1)} %get-tuple-element.185), channel_id=1, source_target_pairs={{0,2},{1,3},{2,0},{3,1},{4,6},{5,7},{6,4},{7,5},{8,10},{9,11},{10,... | collective-permute-start | bytes 98312 | tf_op jit(solution)/shard_map/ppermute | solution.py:352
  117.6 1.6 %collective-permute-start.24 = (bf16[2,32,512]{2,1,0:T(8,128)(2,1)S(1)}, bf16[2,32,512]{2,1,0:T(8,128)(2,1)S(1)}, u32[]{:S(2)}, u32[]{:S(2)}) collective-permute-start(bf16[2,32,512]{2,1,0:T(8,128)(2,1)S(1)} %get-tuple-element.183), channel_id=1, source_target_pairs={{0,4},{1,5},{2,6},{3,7},{4,0},{5,1},{6,2},{7,3},{8,12},{9,13},{10,... | collective-permute-start | bytes 196616 | tf_op jit(solution)/shard_map/ppermute | solution.py:352
  119.2 1.5 %collective-permute-start.26 = (bf16[2,32,512]{2,1,0:T(8,128)(2,1)S(1)}, bf16[2,32,512]{2,1,0:T(8,128)(2,1)S(1)}, u32[]{:S(2)}, u32[]{:S(2)}) collective-permute-start(bf16[2,32,512]{2,1,0:T(8,128)(2,1)S(1)} %get-tuple-element.187), channel_id=1, source_target_pairs={{0,16},{16,0},{1,17},{17,1},{2,18},{18,2},{3,19},{19,3},{4,20},{20... | collective-permute-start | bytes 196616 | tf_op jit(solution)/shard_map/ppermute | solution.py:351
  122.2 2.7 %collective-permute-start.15 = (bf16[208,512]{1,0:T(8,128)(2,1)S(1)}, bf16[208,512]{1,0:T(8,128)(2,1)S(1)}, u32[]{:S(2)}, u32[]{:S(2)}) collective-permute-start(bf16[208,512]{1,0:T(8,128)(2,1)S(1)} %get-tuple-element.167), channel_id=1, source_target_pairs={{0,8},{1,9},{2,10},{3,11},{4,12},{5,13},{6,14},{7,15},{8,0},{9,1},... | collective-permute-start | bytes 638984 | tf_op jit(solution)/shard_map/ppermute | solution.py:352
  125.4 1.3 collective-permute-start.27
  127.4 6.4 %collective-permute-done.15.refs_2_ = bf16[208,512]{1,0:T(8,128)(2,1)S(1)} collective-permute-done((bf16[208,512]{1,0:T(8,128)(2,1)S(1)}, bf16[208,512]{1,0:T(8,128)(2,1)S(1)}, u32[]{:S(2)}, u32[]{:S(2)}) %collective-permute-start.15) | collective-permute-done | bytes 213024 | tf_op jit(solution)/shard_map/ppermute | solution.py:352
  135.6 1.6 %collective-permute-start.28 = (bf16[80,512]{1,0:T(8,128)(2,1)S(1)}, bf16[80,512]{1,0:T(8,128)(2,1)S(1)}, u32[]{:S(2)}, u32[]{:S(2)}) collective-permute-start(bf16[80,512]{1,0:T(8,128)(2,1)S(1)} %shard_map.303.refs_3_), channel_id=1, source_target_pairs={{0,16},{16,0},{1,17},{17,1},{2,18},{18,2},{3,19},{19,3},{4,20},{20... | collective-permute-start | bytes 245768 | tf_op jit(solution)/shard_map/ppermute | solution.py:351
  137.9 2.5 %collective-permute-done.16.refs_2_ = bf16[208,512]{1,0:T(8,128)(2,1)S(1)} collective-permute-done((bf16[208,512]{1,0:T(8,128)(2,1)S(1)}, bf16[208,512]{1,0:T(8,128)(2,1)S(1)}, u32[]{:S(2)}, u32[]{:S(2)}) %collective-permute-start.16) | collective-permute-done | bytes 213024 | tf_op jit(solution)/shard_map/ppermute | solution.py:351
  140.4 0.9 collective-permute-done.28.refs_4_
  141.2 1.6 %shard_map.304 = (f32[32,512]{1,0:T(8,128)}, f32[32,1024]{1,0:T(8,128)}, f32[32,512]{1,0:T(8,128)}, f32[32,2048]{1,0:T(8,128)}, f32[128,512]{1,0:T(8,128)}, /*in...) custom-call(s32[5]{0:T(128)S(1)} %stack.23.refs_0_, ...), custom_call_target="tpu_custom_call" | custom-call | flops 1000000 | bytes 1000000 | tf_op jit(solution)/shard_map/pallas_call | solution.py:34
  (114 shorter events, 17.9 us)
Async XLA Ops:
  0.6 13.6 %copy-start.12 = (bf16[2,32,512]{2,1,0:T(8,128)(2,1)S(1)}, bf16[2,32,512]{2,1,0:T(8,128)(2,1)}, u32[]{:S(2)}) copy-start(bf16[2,32,512]{2,1,0:T(8,128)(2,1)} %refs_3_.2) | copy-start | bytes 196612
  0.7 13.6 %copy-start.8 = (bf16[2,256,512]{2,1,0:T(8,128)(2,1)S(1)}, bf16[2,256,512]{2,1,0:T(8,128)(2,1)}, u32[]{:S(2)}) copy-start(bf16[2,256,512]{2,1,0:T(8,128)(2,1)} %refs_2_.2) | copy-start | bytes 1572868
  0.7 13.6 %copy-start.23 = (bf16[512,512]{1,0:T(8,128)(2,1)S(1)}, bf16[512,512]{1,0:T(8,128)(2,1)}, u32[]{:S(2)}) copy-start(bf16[512,512]{1,0:T(8,128)(2,1)} %refs_5_.4) | copy-start | bytes 1572868
  0.7 13.5 %copy-start.19 = (bf16[512,1024]{1,0:T(8,128)(2,1)S(1)}, bf16[512,1024]{1,0:T(8,128)(2,1)}, u32[]{:S(2)}) copy-start(bf16[512,1024]{1,0:T(8,128)(2,1)} %refs_5_.5) | copy-start | bytes 3145732
  0.7 13.5 %copy-start.32 = (f32[512]{0:T(512)S(1)}, f32[512]{0:T(512)}, u32[]{:S(2)}) copy-start(f32[512]{0:T(512)} %param.24) | copy-start | bytes 6148
  0.7 13.5 %copy-start.33 = (f32[512]{0:T(512)S(1)}, f32[512]{0:T(512)}, u32[]{:S(2)}) copy-start(f32[512]{0:T(512)} %param.20) | copy-start | bytes 6148
  0.7 13.5 %copy-start.34 = (s32[2,8]{1,0:T(2,128)S(1)}, s32[2,8]{1,0:T(2,128)}, u32[]{:S(2)}) copy-start(s32[2,8]{1,0:T(2,128)} %refs_1_.1) | copy-start | bytes 196
  2.6 10.9 %collective-permute-start = (bf16[288,512]{1,0:T(8,128)(2,1)S(1)}, bf16[288,512]{1,0:T(8,128)(2,1)S(1)}, u32[]{:S(2)}, u32[]{:S(2)}) collective-permute-start(bf16[288,512]{1,0:T(8,128)(2,1)S(1)} %pad_maximum_fusion), channel_id=1, source_target_pairs={{0,16},{16,0},{1,17},{17,1},{2,18},{18,2},{3,19},{19,3},{4,20},{20... | collective-permute-start | bytes 884744 | tf_op jit(solution)/shard_map/ppermute | solution.py:351
  8.1 26.1 %collective-permute-start.2 = (bf16[288,512]{1,0:T(8,128)(2,1)}, bf16[288,512]{1,0:T(8,128)(2,1)}, u32[]{:S(2)}, u32[]{:S(2)}) collective-permute-start(bf16[288,512]{1,0:T(8,128)(2,1)} %pad_maximum_fusion.1), channel_id=1, source_target_pairs={{0,16},{16,0},{1,17},{17,1},{2,18},{18,2},{3,19},{19,3},{4,20},{20... | collective-permute-start | bytes 884744 | tf_op jit(solution)/shard_map/ppermute | solution.py:351
  20.5 13.8 %copy-start.13 = (bf16[2,32,512]{2,1,0:T(8,128)(2,1)S(1)}, bf16[2,32,512]{2,1,0:T(8,128)(2,1)}, u32[]{:S(2)}) copy-start(bf16[2,32,512]{2,1,0:T(8,128)(2,1)} %refs_4_.1) | copy-start | bytes 196612
  20.5 13.8 %copy-start.18 = (bf16[512,1024]{1,0:T(8,128)(2,1)S(1)}, bf16[512,1024]{1,0:T(8,128)(2,1)}, u32[]{:S(2)}) copy-start(bf16[512,1024]{1,0:T(8,128)(2,1)} %refs_2_.3) | copy-start | bytes 3145732
  20.5 13.8 %copy-start.21 = (bf16[512,512]{1,0:T(8,128)(2,1)S(1)}, bf16[512,512]{1,0:T(8,128)(2,1)}, u32[]{:S(2)}) copy-start(bf16[512,512]{1,0:T(8,128)(2,1)} %refs_7_.4) | copy-start | bytes 1572868
  20.5 13.8 %copy-start.22 = (bf16[512,512]{1,0:T(8,128)(2,1)S(1)}, bf16[512,512]{1,0:T(8,128)(2,1)}, u32[]{:S(2)}) copy-start(bf16[512,512]{1,0:T(8,128)(2,1)} %refs_8_.4) | copy-start | bytes 1572868
  20.5 13.8 %copy-start.31 = (f32[512]{0:T(512)S(1)}, f32[512]{0:T(512)}, u32[]{:S(2)}) copy-start(f32[512]{0:T(512)} %param.31) | copy-start | bytes 6148
  47.3 6.1 %collective-permute-start.4 = (bf16[8,256,512]{2,1,0:T(8,128)(2,1)S(1)}, bf16[8,256,512]{2,1,0:T(8,128)(2,1)S(1)}, u32[]{:S(2)}, u32[]{:S(2)}) collective-permute-start(bf16[8,256,512]{2,1,0:T(8,128)(2,1)S(1)} %get-tuple-element.133), channel_id=1, source_target_pairs={{0,1},{1,0},{2,3},{3,2},{4,5},{5,4},{6,7},{7,6},{8,9},{9,8},{10,11... | collective-permute-start | bytes 6291464 | tf_op jit(solution)/shard_map/ppermute | solution.py:352
  47.4 6.0 %collective-permute-start.3 = (bf16[8,160,512]{2,1,0:T(8,128)(2,1)S(1)}, bf16[8,160,512]{2,1,0:T(8,128)(2,1)S(1)}, u32[]{:S(2)}, u32[]{:S(2)}) collective-permute-start(bf16[8,160,512]{2,1,0:T(8,128)(2,1)S(1)} %get-tuple-element.131), channel_id=1, source_target_pairs={{0,1},{1,0},{2,3},{3,2},{4,5},{5,4},{6,7},{7,6},{8,9},{9,8},{10,11... | collective-permute-start | bytes 3932168 | tf_op jit(solution)/shard_map/ppermute | solution.py:352
  54.7 14.3 %collective-permute-start.6 = (bf16[2,2,2,64,512]{4,3,2,1,0:T(8,128)(2,1)S(1)}, bf16[2,2,2,64,512]{4,3,2,1,0:T(8,128)(2,1)S(1)}, u32[]{:S(2)}, u32[]{:S(2)}) collective-permute-start(bf16[2,2,2,64,512]{4,3,2,1,0:T(8,128)(2,1)S(1)} %get-tuple-element.149), channel_id=1, source_target_pairs={{0,16},{16,0},{1,17},{17,1},{2,18},{18,2},{3,19},{19,3},{4,20},{20... | collective-permute-start | bytes 1572872 | tf_op jit(solution)/shard_map/ppermute | solution.py:351
  56.9 13.7 %collective-permute-start.7 = (bf16[2,2,128,512]{3,2,1,0:T(8,128)(2,1)S(1)}, bf16[2,2,128,512]{3,2,1,0:T(8,128)(2,1)S(1)}, u32[]{:S(2)}, u32[]{:S(2)}) collective-permute-start(bf16[2,2,128,512]{3,2,1,0:T(8,128)(2,1)S(1)} %get-tuple-element.150), channel_id=1, source_target_pairs={{0,4},{1,5},{2,6},{3,7},{4,0},{5,1},{6,2},{7,3},{8,12},{9,13},{10,... | collective-permute-start | bytes 1572872 | tf_op jit(solution)/shard_map/ppermute | solution.py:352
  58.4 16.2 %collective-permute-start.5 = (bf16[2,2,160,512]{3,2,1,0:T(8,128)(2,1)S(1)}, bf16[2,2,160,512]{3,2,1,0:T(8,128)(2,1)S(1)}, u32[]{:S(2)}, u32[]{:S(2)}) collective-permute-start(bf16[2,2,160,512]{3,2,1,0:T(8,128)(2,1)S(1)} %get-tuple-element.148), channel_id=1, source_target_pairs={{0,2},{1,3},{2,0},{3,1},{4,6},{5,7},{6,4},{7,5},{8,10},{9,11},{10,... | collective-permute-start | bytes 1966088 | tf_op jit(solution)/shard_map/ppermute | solution.py:352
  68.4 7.9 %copy-start.20 = (bf16[512,1024]{1,0:T(8,128)(2,1)S(1)}, bf16[512,1024]{1,0:T(8,128)(2,1)}, u32[]{:S(2)}) copy-start(bf16[512,1024]{1,0:T(8,128)(2,1)} %refs_5_.5) | copy-start | bytes 3145732
  68.4 7.9 %copy-start.26 = (bf16[512,512]{1,0:T(8,128)(2,1)S(1)}, bf16[512,512]{1,0:T(8,128)(2,1)}, u32[]{:S(2)}) copy-start(bf16[512,512]{1,0:T(8,128)(2,1)} %refs_6_.5) | copy-start | bytes 1572868
  68.4 7.9 %copy-start.28 = (bf16[512,512]{1,0:T(8,128)(2,1)S(1)}, bf16[512,512]{1,0:T(8,128)(2,1)}, u32[]{:S(2)}) copy-start(bf16[512,512]{1,0:T(8,128)(2,1)} %refs_8_.5) | copy-start | bytes 1572868
  80.1 4.1 %collective-permute-start.17 = (bf16[8,160,512]{2,1,0:T(8,128)(2,1)S(1)}, bf16[8,160,512]{2,1,0:T(8,128)(2,1)S(1)}, u32[]{:S(2)}, u32[]{:S(2)}) collective-permute-start(bf16[8,160,512]{2,1,0:T(8,128)(2,1)S(1)} %get-tuple-element.169), channel_id=1, source_target_pairs={{0,1},{1,0},{2,3},{3,2},{4,5},{5,4},{6,7},{7,6},{8,9},{9,8},{10,11... | collective-permute-start | bytes 3932168 | tf_op jit(solution)/shard_map/ppermute | solution.py:352
  80.1 9.5 %collective-permute-start.1 = (bf16[256,512]{1,0:T(8,128)(2,1)}, bf16[256,512]{1,0:T(8,128)(2,1)}, u32[]{:S(2)}, u32[]{:S(2)}) collective-permute-start(bf16[256,512]{1,0:T(8,128)(2,1)} %get-tuple-element.109), channel_id=1, source_target_pairs={{0,16},{16,0},{1,17},{17,1},{2,18},{18,2},{3,19},{19,3},{4,20},{20... | collective-permute-start | bytes 786440 | tf_op jit(solution)/shard_map/ppermute | solution.py:351
  80.7 10.4 %collective-permute-start.10 = (bf16[2,2,64,512]{3,2,1,0:T(8,128)(2,1)}, bf16[2,2,64,512]{3,2,1,0:T(8,128)(2,1)}, u32[]{:S(2)}, u32[]{:S(2)}) collective-permute-start(bf16[2,2,64,512]{3,2,1,0:T(8,128)(2,1)} %get-tuple-element.158), channel_id=1, source_target_pairs={{0,4},{1,5},{2,6},{3,7},{4,0},{5,1},{6,2},{7,3},{8,12},{9,13},{10,... | collective-permute-start | bytes 786440 | tf_op jit(solution)/shard_map/ppermute | solution.py:352
  81.0 12.4 %collective-permute-start.11 = (bf16[2,128,512]{2,1,0:T(8,128)(2,1)}, bf16[2,128,512]{2,1,0:T(8,128)(2,1)}, u32[]{:S(2)}, u32[]{:S(2)}) collective-permute-start(bf16[2,128,512]{2,1,0:T(8,128)(2,1)} %get-tuple-element.159), channel_id=1, source_target_pairs={{0,2},{1,3},{2,0},{3,1},{4,6},{5,7},{6,4},{7,5},{8,10},{9,11},{10,... | collective-permute-start | bytes 786440 | tf_op jit(solution)/shard_map/ppermute | solution.py:352
  82.6 14.0 %collective-permute-start.9 = (bf16[2,2,80,512]{3,2,1,0:T(8,128)(2,1)}, bf16[2,2,80,512]{3,2,1,0:T(8,128)(2,1)}, u32[]{:S(2)}, u32[]{:S(2)}) collective-permute-start(bf16[2,2,80,512]{3,2,1,0:T(8,128)(2,1)} %get-tuple-element.157), channel_id=1, source_target_pairs={{0,16},{16,0},{1,17},{17,1},{2,18},{18,2},{3,19},{19,3},{4,20},{20... | collective-permute-start | bytes 983048 | tf_op jit(solution)/shard_map/ppermute | solution.py:351
  84.2 19.5 %collective-permute-start.8 = (bf16[320,512]{1,0:T(8,128)(2,1)S(1)}, bf16[320,512]{1,0:T(8,128)(2,1)}, u32[]{:S(2)}, u32[]{:S(2)}) collective-permute-start(bf16[320,512]{1,0:T(8,128)(2,1)S(1)} %get-tuple-element.154.refs_7_), channel_id=1, source_target_pairs={{0,16},{16,0},{1,17},{17,1},{2,18},{18,2},{3,19},{19,3},{4,20},{20... | collective-permute-start | bytes 983048 | tf_op jit(solution)/shard_map/ppermute | solution.py:351
  84.7 12.0 %copy-start.1 = (bf16[2,2,80,512]{3,2,1,0:T(8,128)(2,1)S(1)}, bf16[2,2,80,512]{3,2,1,0:T(8,128)(2,1)}, u32[]{:S(2)}) copy-start(bf16[2,2,80,512]{3,2,1,0:T(8,128)(2,1)} %copy-done) | copy-start | bytes 983044
  84.7 12.0 %copy-start.3 = (bf16[2,2,64,512]{3,2,1,0:T(8,128)(2,1)S(1)}, bf16[2,2,64,512]{3,2,1,0:T(8,128)(2,1)}, u32[]{:S(2)}) copy-start(bf16[2,2,64,512]{3,2,1,0:T(8,128)(2,1)} %copy-done.2) | copy-start | bytes 786436
  84.7 12.0 %copy-start.5 = (bf16[2,128,512]{2,1,0:T(8,128)(2,1)S(1)}, bf16[2,128,512]{2,1,0:T(8,128)(2,1)}, u32[]{:S(2)}) copy-start(bf16[2,128,512]{2,1,0:T(8,128)(2,1)} %copy-done.4) | copy-start | bytes 786436
  89.6 19.1 %collective-permute-start.18 = (bf16[2,2,64,512]{3,2,1,0:T(8,128)(2,1)S(1)}, bf16[2,2,64,512]{3,2,1,0:T(8,128)(2,1)S(1)}, u32[]{:S(2)}, u32[]{:S(2)}) collective-permute-start(bf16[2,2,64,512]{3,2,1,0:T(8,128)(2,1)S(1)} %get-tuple-element.171), channel_id=1, source_target_pairs={{0,2},{1,3},{2,0},{3,1},{4,6},{5,7},{6,4},{7,5},{8,10},{9,11},{10,... | collective-permute-start | bytes 786440 | tf_op jit(solution)/shard_map/ppermute | solution.py:352
  91.1 17.6 %collective-permute-start.20 = (bf16[2,2,64,512]{3,2,1,0:T(8,128)(2,1)S(1)}, bf16[2,2,64,512]{3,2,1,0:T(8,128)(2,1)S(1)}, u32[]{:S(2)}, u32[]{:S(2)}) collective-permute-start(bf16[2,2,64,512]{3,2,1,0:T(8,128)(2,1)S(1)} %get-tuple-element.175), channel_id=1, source_target_pairs={{0,4},{1,5},{2,6},{3,7},{4,0},{5,1},{6,2},{7,3},{8,12},{9,13},{10,... | collective-permute-start | bytes 786440 | tf_op jit(solution)/shard_map/ppermute | solution.py:352
  98.0 21.2 %collective-permute-start.13 = (bf16[2,64,512]{2,1,0:T(8,128)(2,1)S(1)}, bf16[2,64,512]{2,1,0:T(8,128)(2,1)S(1)}, u32[]{:S(2)}, u32[]{:S(2)}) collective-permute-start(bf16[2,64,512]{2,1,0:T(8,128)(2,1)S(1)} %get-tuple-element.163), channel_id=1, source_target_pairs={{0,2},{1,3},{2,0},{3,1},{4,6},{5,7},{6,4},{7,5},{8,10},{9,11},{10,... | collective-permute-start | bytes 393224 | tf_op jit(solution)/shard_map/ppermute | solution.py:352
  99.5 21.9 %collective-permute-start.14 = (bf16[2,64,512]{2,1,0:T(8,128)(2,1)S(1)}, bf16[2,64,512]{2,1,0:T(8,128)(2,1)S(1)}, u32[]{:S(2)}, u32[]{:S(2)}) collective-permute-start(bf16[2,64,512]{2,1,0:T(8,128)(2,1)S(1)} %get-tuple-element.165), channel_id=1, source_target_pairs={{0,16},{16,0},{1,17},{17,1},{2,18},{18,2},{3,19},{19,3},{4,20},{20... | collective-permute-start | bytes 393224 | tf_op jit(solution)/shard_map/ppermute | solution.py:351
  103.7 5.1 %collective-permute-start.19 = (bf16[2,2,2,16,512]{4,3,2,1,0:T(8,128)(2,1)S(1)}, bf16[2,2,2,16,512]{4,3,2,1,0:T(8,128)(2,1)S(1)}, u32[]{:S(2)}, u32[]{:S(2)}) collective-permute-start(bf16[2,2,2,16,512]{4,3,2,1,0:T(8,128)(2,1)S(1)} %get-tuple-element.173), channel_id=1, source_target_pairs={{0,16},{16,0},{1,17},{17,1},{2,18},{18,2},{3,19},{19,3},{4,20},{20... | collective-permute-start | bytes 393224 | tf_op jit(solution)/shard_map/ppermute | solution.py:351
  109.4 4.3 %collective-permute-start.22 = (bf16[2,2,16,512]{3,2,1,0:T(8,128)(2,1)S(1)}, bf16[2,2,16,512]{3,2,1,0:T(8,128)(2,1)S(1)}, u32[]{:S(2)}, u32[]{:S(2)}) collective-permute-start(bf16[2,2,16,512]{3,2,1,0:T(8,128)(2,1)S(1)} %get-tuple-element.179), channel_id=1, source_target_pairs={{0,4},{1,5},{2,6},{3,7},{4,0},{5,1},{6,2},{7,3},{8,12},{9,13},{10,... | collective-permute-start | bytes 196616 | tf_op jit(solution)/shard_map/ppermute | solution.py:352
  109.9 5.0 %collective-permute-start.21 = (bf16[2,2,32,512]{3,2,1,0:T(8,128)(2,1)S(1)}, bf16[2,2,32,512]{3,2,1,0:T(8,128)(2,1)S(1)}, u32[]{:S(2)}, u32[]{:S(2)}) collective-permute-start(bf16[2,2,32,512]{3,2,1,0:T(8,128)(2,1)S(1)} %get-tuple-element.177), channel_id=1, source_target_pairs={{0,16},{16,0},{1,17},{17,1},{2,18},{18,2},{3,19},{19,3},{4,20},{20... | collective-permute-start | bytes 393224 | tf_op jit(solution)/shard_map/ppermute | solution.py:351
  110.3 5.0 %collective-permute-start.23 = (bf16[2,64,512]{2,1,0:T(8,128)(2,1)S(1)}, bf16[2,64,512]{2,1,0:T(8,128)(2,1)S(1)}, u32[]{:S(2)}, u32[]{:S(2)}) collective-permute-start(bf16[2,64,512]{2,1,0:T(8,128)(2,1)S(1)} %get-tuple-element.181), channel_id=1, source_target_pairs={{0,2},{1,3},{2,0},{3,1},{4,6},{5,7},{6,4},{7,5},{8,10},{9,11},{10,... | collective-permute-start | bytes 393224 | tf_op jit(solution)/shard_map/ppermute | solution.py:352
  113.1 24.1 %copy-start.11 = (bf16[32,512]{1,0:T(8,128)(2,1)S(1)}, bf16[32,512]{1,0:T(8,128)(2,1)}, u32[]{:S(2)}) copy-start(bf16[32,512]{1,0:T(8,128)(2,1)} %copy-done.10) | copy-start | bytes 98308
  113.8 7.7 %collective-permute-start.12 = (bf16[2,80,512]{2,1,0:T(8,128)(2,1)S(1)}, bf16[2,80,512]{2,1,0:T(8,128)(2,1)S(1)}, u32[]{:S(2)}, u32[]{:S(2)}) collective-permute-start(bf16[2,80,512]{2,1,0:T(8,128)(2,1)S(1)} %get-tuple-element.161), channel_id=1, source_target_pairs={{0,4},{1,5},{2,6},{3,7},{4,0},{5,1},{6,2},{7,3},{8,12},{9,13},{10,... | collective-permute-start | bytes 491528 | tf_op jit(solution)/shard_map/ppermute | solution.py:352
  115.9 8.9 %collective-permute-start.25 = (bf16[2,16,512]{2,1,0:T(8,128)(2,1)S(1)}, bf16[2,16,512]{2,1,0:T(8,128)(2,1)S(1)}, u32[]{:S(2)}, u32[]{:S(2)}) collective-permute-start(bf16[2,16,512]{2,1,0:T(8,128)(2,1)S(1)} %get-tuple-element.185), channel_id=1, source_target_pairs={{0,2},{1,3},{2,0},{3,1},{4,6},{5,7},{6,4},{7,5},{8,10},{9,11},{10,... | collective-permute-start | bytes 98312 | tf_op jit(solution)/shard_map/ppermute | solution.py:352
  117.6 7.2 %collective-permute-start.24 = (bf16[2,32,512]{2,1,0:T(8,128)(2,1)S(1)}, bf16[2,32,512]{2,1,0:T(8,128)(2,1)S(1)}, u32[]{:S(2)}, u32[]{:S(2)}) collective-permute-start(bf16[2,32,512]{2,1,0:T(8,128)(2,1)S(1)} %get-tuple-element.183), channel_id=1, source_target_pairs={{0,4},{1,5},{2,6},{3,7},{4,0},{5,1},{6,2},{7,3},{8,12},{9,13},{10,... | collective-permute-start | bytes 196616 | tf_op jit(solution)/shard_map/ppermute | solution.py:352
  119.2 5.7 %collective-permute-start.26 = (bf16[2,32,512]{2,1,0:T(8,128)(2,1)S(1)}, bf16[2,32,512]{2,1,0:T(8,128)(2,1)S(1)}, u32[]{:S(2)}, u32[]{:S(2)}) collective-permute-start(bf16[2,32,512]{2,1,0:T(8,128)(2,1)S(1)} %get-tuple-element.187), channel_id=1, source_target_pairs={{0,16},{16,0},{1,17},{17,1},{2,18},{18,2},{3,19},{19,3},{4,20},{20... | collective-permute-start | bytes 196616 | tf_op jit(solution)/shard_map/ppermute | solution.py:351
  122.2 11.7 %collective-permute-start.15 = (bf16[208,512]{1,0:T(8,128)(2,1)S(1)}, bf16[208,512]{1,0:T(8,128)(2,1)S(1)}, u32[]{:S(2)}, u32[]{:S(2)}) collective-permute-start(bf16[208,512]{1,0:T(8,128)(2,1)S(1)} %get-tuple-element.167), channel_id=1, source_target_pairs={{0,8},{1,9},{2,10},{3,11},{4,12},{5,13},{6,14},{7,15},{8,0},{9,1},... | collective-permute-start | bytes 638984 | tf_op jit(solution)/shard_map/ppermute | solution.py:352
  125.4 9.6 %collective-permute-start.27 = (bf16[80,512]{1,0:T(8,128)(2,1)S(1)}, bf16[80,512]{1,0:T(8,128)(2,1)S(1)}, u32[]{:S(2)}, u32[]{:S(2)}) collective-permute-start(bf16[80,512]{1,0:T(8,128)(2,1)S(1)} %get-tuple-element.189), channel_id=1, source_target_pairs={{0,8},{1,9},{2,10},{3,11},{4,12},{5,13},{6,14},{7,15},{8,0},{9,1},... | collective-permute-start | bytes 245768 | tf_op jit(solution)/shard_map/ppermute | solution.py:352
  134.5 5.9 %collective-permute-start.16 = (bf16[208,512]{1,0:T(8,128)(2,1)S(1)}, bf16[208,512]{1,0:T(8,128)(2,1)S(1)}, u32[]{:S(2)}, u32[]{:S(2)}) collective-permute-start(bf16[208,512]{1,0:T(8,128)(2,1)S(1)} %shard_map.298.refs_1_), channel_id=1, source_target_pairs={{0,16},{16,0},{1,17},{17,1},{2,18},{18,2},{3,19},{19,3},{4,20},{20... | collective-permute-start | bytes 638984 | tf_op jit(solution)/shard_map/ppermute | solution.py:351
  135.6 5.6 %collective-permute-start.28 = (bf16[80,512]{1,0:T(8,128)(2,1)S(1)}, bf16[80,512]{1,0:T(8,128)(2,1)S(1)}, u32[]{:S(2)}, u32[]{:S(2)}) collective-permute-start(bf16[80,512]{1,0:T(8,128)(2,1)S(1)} %shard_map.303.refs_3_), channel_id=1, source_target_pairs={{0,16},{16,0},{1,17},{17,1},{2,18},{18,2},{3,19},{19,3},{4,20},{20... | collective-permute-start | bytes 245768 | tf_op jit(solution)/shard_map/ppermute | solution.py:351
  (16 other events, 58.8 us)

commit v3 on v2

--- a/solution.py
+++ b/solution.py
@@ -19,24 +19,54 @@
     return pl.ds(pl.multiple_of(index * half, half), half)
 
 
+class Fetched:
+    def __init__(self, source, ref, sem):
+        self.ref, self.copy, self.waited = ref, pltpu.make_async_copy(source, ref, sem), False
+
+    def __call__(self):
+        if not self.waited:
+            self.copy.wait()
+            self.waited = True
+        return self.ref
+
+
+def position():
+    seg = lax.axis_index("seg")
+    return [lax.axis_index("seq")] + [(seg >> k) & 1 for k in range(4)]
+
+
 def call(body, ins, outs, scratch=(), flops=0, nbytes=0, limit=16, home=True):
     kinds = [kind for kind, _ in ins]
     arrays = [
         pltpu.with_memory_space_constraint(a, pltpu.VMEM) if kind == "v" else a for kind, a in ins
     ]
-    spaces = {"s": pltpu.SMEM, "v": pltpu.VMEM, "d": pl.ANY}
+    spaces = {"s": pltpu.SMEM, "v": pltpu.VMEM, "d": pl.ANY, "h": pl.ANY}
+    fetched = [pltpu.VMEM(a.shape, a.dtype) for kind, a in ins if kind == "h"]
+    n_io = len(ins) + len(outs)
 
     def kernel(*refs):
-        given = [r for kind, r in zip(kinds, refs) if kind != "d"]
-        body(*given, *refs[len(ins) :])
+        given, at = [], 0
+        for kind, r in zip(kinds, refs):
+            if kind == "h":
+                r = Fetched(r, refs[n_io + at], refs[-1].at[at])
+                r.copy.start()
+                at += 1
+            if kind != "d":
+                given.append(r)
+        end = -1 if fetched else len(refs)
+        body(position(), *given, *refs[len(ins) : n_io], *refs[n_io + at : end])
+        for r in given:
+            if isinstance(r, Fetched):
+                r()
 
     shape = (lambda s, d: pltpu.VMEM(s, d)) if home else jax.ShapeDtypeStruct
+    sems = [pltpu.SemaphoreType.DMA((len(fetched),))] if fetched else []
     return pl.pallas_call(
         kernel,
         out_shape=[shape(s, d) for s, d in outs],
         in_specs=[pl.BlockSpec(memory_space=spaces[kind]) for kind in kinds],
         out_specs=[pl.BlockSpec(memory_space=pltpu.VMEM)] * len(outs),
-        scratch_shapes=[pltpu.VMEM(s, d) for s, d in scratch],
+        scratch_shapes=fetched + [pltpu.VMEM(s, d) for s, d in scratch] + sems,
         compiler_params=pltpu.CompilerParams(vmem_limit_bytes=limit * 1024 * 1024),
         cost_estimate=pl.CostEstimate(flops=flops, bytes_accessed=nbytes, transcendentals=0),
     )(*arrays)
@@ -232,41 +262,48 @@
 
 
 def ffn_back_body(
-    place, dwpair, write_pair, out_cotangent, recv, ffn_out, dg, ffn_in, act, n2,
-    send, keep, total_out, dout_out,
+    place, dwpair, write_pair, out_cotangent, recv, ffn_out, dg, act,
+    send, keep, dout_out, dinner,
 ):
     c, ks = place[1], (send, keep)
-    width, ff = ffn_in.shape
-    rows, deep = width // GROUPS, ff // GROUPS
+    ff, width = ffn_out.shape
+    deep = ff // GROUPS
     cot = whole_rows(place, out_cotangent, recv, 0, out_cotangent.shape[1])
     d_out = cot.astype(F32) + dot(dwpair[...], write_pair[...], 1, 1)
     dout_out[...] = d_out
     d_branch = d_out.astype(BF16)
-    total = None
     for j in range(ff // 512):
         cols = slice(512 * j, 512 * j + 512)
         d_act = dot(d_branch, ffn_out[cols, :], 1, 1).astype(BF16)
-        d_inner = (d_act.astype(F32) * dg[:, cols].astype(F32)).astype(BF16)
-        term = dot(d_inner, ffn_in[:, cols], 1, 1)
-        total = term if total is None else total + term
-        emit_rows(dot(n2[...], d_inner, 0, 0), rows, ks, rows * j, c)
+        dinner[:, cols] = (d_act.astype(F32) * dg[:, cols].astype(F32)).astype(BF16)
         emit_rows(
-            dot(act[:, cols], d_branch, 0, 0),
-            deep, ks, rows * (ff // 512), c, 512 // (2 * deep) * j,
+            dot(act[:, cols], d_branch, 0, 0), deep, ks, 0, c, 512 // (2 * deep) * j,
         )
-    total_out[...] = total
+
+
+def inner_back_body(
+    place, dinner, n2, ffn_in,
+    send, keep, total,
+):
+    rows = ffn_in.shape[0] // GROUPS
+    for j in range(ffn_in.shape[1] // 512):
+        cols = slice(512 * j, 512 * j + 512)
+        emit_rows(dot(n2[...], dinner[:, cols], 0, 0), rows, (send, keep), rows * j, place[1])
+    total[...] = dot(dinner[...], ffn_in[...], 1, 1)
 
 
 def resid_back_body(
-    place, total, dout, resid, ffn_gain, out_weight,
-    dresid, dmixed, gain_out,
+    place, total, dout, resid, ffn_gain, out_weight, mixed,
+    send, keep, dresid, dmixed, gain_out,
 ):
     rhat, rr = norm_parts(resid[...])
     d_norm, d_gain = norm_back(total[...], rhat, rr, ffn_gain[...])
     gain_out[...] = d_gain
     d = dout[...] + d_norm
     dresid[...] = d
-    dmixed[...] = dot(d.astype(BF16), out_weight[...], 1, 1).astype(BF16)
+    d_attn = d.astype(BF16)
+    emit_rows(dot(mixed[...], d_attn, 0, 0), 32, (send, keep), 0, place[1])
+    dmixed[...] = dot(d_attn, out_weight[...], 1, 1).astype(BF16)
 
 
 def attn_back_body(
@@ -301,7 +338,7 @@
 
 def input_back_body(
     place, nall, dq, dk, dv, pair_weight, query_weight, dwquery, write_query, x, mem, attn_gain,
-    dresid, dblend, mixed, gain2, gain3, newmem,
+    dresid, dblend, gain2, gain3, newmem,
     send, keep, own_tok, own_mem, swap, gtok, gmem,
 ):
     c, ks = place[1], (send, keep)
@@ -313,7 +350,6 @@
     emit_rows(dot(na[128:], dqv, 0, 0), 32, ks, 0, c)
     emit_rows(dot(na, dk[...], 0, 0), 32, ks, 32, c)
     emit_rows(dot(na, dv[...], 0, 0), 32, ks, 64, c)
-    emit_rows(dot(mixed[...], dresid[...].astype(BF16), 0, 0), 32, ks, 96, c)
     d_all = dot(dk[...], pair_weight[:, :width], 1, 1)
     d_all = d_all + dot(dv[...], pair_weight[:, width:], 1, 1)
     d_nx = d_all[128:] + dot(dqv, query_weight[...], 1, 1)
@@ -324,10 +360,10 @@
     mhat, mr = norm_parts(mem[...].astype(F32))
     d_m, g_m = norm_back(d_nm, mhat, mr, gain)
     gains = jnp.concatenate(
-        [g_x + g_m, gain2[...], gain3[...], jnp.zeros((29, width), F32)], 0
+        [g_x + g_m, gain2[...], gain3[...], jnp.zeros((13, width), F32)], 0
     ).astype(BF16)
     for one in ks:
-        one[:, 128:160, :] = jnp.broadcast_to(gains, (GROUPS // 2, 32, width))
+        one[:, 96:112, :] = jnp.broadcast_to(gains, (GROUPS // 2, 16, width))
     gtok[...] = dresid[...] + d_x
     gmem[...] = dblend[...] + d_m
     own_tok[...] = gtok[part(place, half, True), :]
@@ -357,8 +393,8 @@
         self.keep, self.recv, self.dims, self.start, self.rows = keep, recv, dims, start, rows
 
 
-def stage(place, streams, labels, joined=False, deps=()):
-    ins = [("s", place)]
+def stage(streams, labels, joined=False, deps=(), tail=False):
+    ins = []
     index = {}
     for s in streams:
         for arr in (s.keep, s.recv):
@@ -377,12 +413,14 @@
         shapes.append((2,) * len(dims) + (rows, width))
     if joined:
         shapes = [(sum(new_rows), width)]
+    if tail:
+        shapes = shapes[:-2] + [shapes[-2][:-2] + (new_rows[-2] + new_rows[-1], width)]
     outs = []
     for shape in shapes:
         outs += [(shape, BF16)] * 2
 
     def body(place, *refs):
-        given, made = refs[: n_arrays - 1], refs[n_arrays - 1 :]
+        given, made = refs[:n_arrays], refs[n_arrays:]
 
         def value(s, label, own, arr):
             bit = place[BIT[label]]
@@ -395,38 +433,116 @@
                 where.append(pl.ds(pl.multiple_of(s.start + bit * half, 16), half))
             else:
                 where.append(slice(s.start, s.start + s.rows))
-            return given[index[id(arr)] - 1][tuple(where) + (slice(None),)].astype(F32)
+            return given[index[id(arr)]][tuple(where) + (slice(None),)].astype(F32)
 
         for own in (False, True):
             at = 0
             for k, (s, label) in enumerate(zip(streams, labels)):
                 total = (value(s, label, own, s.keep) + value(s, label, own, s.recv)).astype(BF16)
-                target = made[(0 if joined else 2 * k) + (0 if own else 1)]
+                last = tail and k == len(streams) - 1
+                target = made[(0 if joined else 2 * (k - last)) + (0 if own else 1)]
                 if joined:
                     target[at : at + new_rows[k], :] = total
                     at += new_rows[k]
+                elif last:
+                    target[..., new_rows[k - 1] :, :] = total
+                elif tail and k == len(streams) - 2:
+                    target[..., : new_rows[k], :] = total
                 else:
                     target[...] = total
 
     results = call(body, ins, outs, flops=10**6, nbytes=10**6)
     if joined:
         return results[0], results[1]
+    if tail:
+        new_rows = new_rows[:-2] + [new_rows[-2] + new_rows[-1]]
     return [
-        (results[2 * k], results[2 * k + 1], new_dims[k], new_rows[k]) for k in range(len(streams))
+        (results[2 * k], results[2 * k + 1], new_dims[k], n) for k, n in enumerate(new_rows)
     ]
 
 
-def added(place, keep, recv):
+def added(keep, recv, deps=()):
     def body(place, keep, recv, total):
         total[...] = (keep[...].astype(F32) + recv[...].astype(F32)).astype(BF16)
 
     (total,) = call(
         body,
-        [("s", place), ("v", keep), ("v", recv)],
+        [("v", keep), ("v", recv)] + [("d", d) for d in deps],
         [(keep.shape, BF16)],
         flops=10**6, nbytes=10**6,
     )
     return total
+
+
+def in_hbm(a):
+    return pltpu.with_memory_space_constraint(a, pltpu.HBM)
+
+
+def packed(body_rows, extra_rows):
+    half, width = body_rows.shape[1:]
+    extra = extra_rows.shape[1]
+
+    def kernel(a, b, o, sem):
+        other = 1 - lax.axis_index("seq")
+        copies = [
+            pltpu.make_async_copy(a.at[other], o.at[0:half], sem.at[0]),
+            pltpu.make_async_copy(b.at[other], o.at[half:], sem.at[1]),
+        ]
+        for copy in copies:
+            copy.start()
+        for copy in copies:
+            copy.wait()
+
+    return pl.pallas_call(
+        kernel,
+        out_shape=pltpu.VMEM((half + extra, width), body_rows.dtype),
+        in_specs=[pl.BlockSpec(memory_space=pltpu.HBM)] * 2,
+        out_specs=pl.BlockSpec(memory_space=pltpu.VMEM),
+        scratch_shapes=[pltpu.SemaphoreType.DMA((2,))],
+        compiler_params=pltpu.CompilerParams(vmem_limit_bytes=4 * 1024 * 1024),
+    )(in_hbm(body_rows), in_hbm(extra_rows))
+
+
+def assembled(own, recv, dtypes, deps=()):
+    width = own[0].shape[1]
+
+    def body(place, *refs):
+        n = len(own)
+        start = 0
+        for mine, out in zip(refs[:n], refs[n + 1 :]):
+            rows = mine.shape[0]
+            out[place[0]] = mine[...].astype(out.dtype)
+            out[1 - place[0]] = refs[n][start : start + rows, :].astype(out.dtype)
+            start += rows
+
+    return call(
+        body,
+        [("v", a) for a in own] + [("v", recv)] + [("d", d) for d in deps],
+        [((2,) + a.shape, d) for a, d in zip(own, dtypes)],
+        flops=10**6, nbytes=10**6, home=False,
+    )
+
+
+def fetched_weights(weights):
+    def kernel(*refs):
+        n = len(weights)
+        copies = [
+            pltpu.make_async_copy(refs[k], refs[n + k], refs[-1].at[k]) for k in range(n)
+        ]
+        for copy in copies:
+            copy.start()
+        for copy in copies:
+            copy.wait()
+
+    return pl.pallas_call(
+        kernel,
+        out_shape=[pltpu.VMEM(a.shape, a.dtype) for a in weights],
+        in_specs=[pl.BlockSpec(memory_space=pltpu.HBM)] * len(weights),
+        out_specs=[pl.BlockSpec(memory_space=pltpu.VMEM)] * len(weights),
+        scratch_shapes=[pltpu.SemaphoreType.DMA((len(weights),))],
+        compiler_params=pltpu.CompilerParams(vmem_limit_bytes=4 * 1024 * 1024),
+        cost_estimate=pl.CostEstimate(flops=10**9, bytes_accessed=10**7, transcendentals=0),
+    )(*[in_hbm(a) for a in weights])
 
 
 def reduced_any(keep, send, pieces):
@@ -452,47 +568,49 @@
     return lax.psum(total, "seq")
 
 
-def final_parts(place, one, two, ff):
-    width = one[0].shape[-1]
+def final_parts(one, two, ff):
+    t1, o1, split = one
+    t2, o2 = two
+    width = t1.shape[-1]
     r = width // GROUPS
     n = ff // 512
     shapes = [
         (r, width), (r, 2 * width), (r, width), (r, ff), (ff // GROUPS, width),
-        (r, width), (r, 2 * width), (r, width), (r, width), (8, width),
+        (r, width), (r, 2 * width), (r, width), (r, width), (r,), (r,), (r,),
     ]
 
-    def body(place, t1, o1, t2, o2, gq, gp, go, gfi, gfo, gwq, gwp, gwo, gwg, gains, full1, full2):
+    def body(place, t1, o1, t2, o2, gq, gp, go, gfi, gfo, gwq, gwp, gwo, gwg, g0, g1, g2, full):
         y = place[0]
-        for t, o, full, streams in ((t1, o1, full1, one[2]), (t2, o2, full2, two[2])):
-            at = start = 0
-            for rows in streams:
-                half = rows // 2
-                for ref, own in ((t, True), (o, False)):
-                    index = y if own else 1 - y
-                    full[pl.ds(pl.multiple_of(start + index * half, 16), half), :] = ref[
-                        at : at + half, :
-                    ].astype(F32)
-                at += half
-                start += rows
-        gq[...] = full2[0:r, :]
-        gp[:, :width] = full2[r : 2 * r, :]
-        gp[:, width:] = full2[2 * r : 3 * r, :]
-        go[...] = full2[3 * r : 4 * r, :]
-        gains[...] = full2[4 * r : 4 * r + 8, :]
-        gwq[...] = full1[0:r, :]
-        gwp[:, :width] = full1[r : 2 * r, :]
-        gwp[:, width:] = full1[2 * r : 3 * r, :]
-        gwo[...] = full1[3 * r : 4 * r, :]
-        gwg[...] = full1[4 * r : 5 * r, :]
+        at = start = 0
+        for rows in split:
+            half = rows // 2
+            for ref, index in ((t1, y), (o1, 1 - y)):
+                full[pl.ds(pl.multiple_of(start + index * half, 16), half), :] = ref[
+                    at : at + half, :
+                ].astype(F32)
+            at += half
+            start += rows
+        total = (t2[...].astype(F32) + o2[...].astype(F32))
+        gq[...] = total[0:r, :]
+        gp[:, :width] = total[r : 2 * r, :]
+        gp[:, width:] = total[2 * r : 3 * r, :]
+        seg = lax.axis_index("seg")
+        gains = pltpu.roll(total[3 * r : 3 * r + 8, :], (width - seg * r) % width, 1)
+        for k, ref in enumerate((g0, g1, g2)):
+            ref[...] = gains[k, :r]
+        gwq[...] = full[0:r, :]
+        gwp[:, :width] = full[r : 2 * r, :]
+        gwp[:, width:] = full[2 * r : 3 * r, :]
+        gwo[...] = full[3 * r : 4 * r, :]
+        gwg[...] = full[4 * r : 5 * r, :]
         for j in range(n):
-            gfi[:, 512 * j : 512 * j + 512] = full1[(5 + j) * r : (6 + j) * r, :]
-        gfo[...] = full1[(5 + n) * r :, :]
-
-    ins = [("s", place)] + [("v", a) for a in (one[0], one[1], two[0], two[1])]
+            gfi[:, 512 * j : 512 * j + 512] = full[(5 + j) * r : (6 + j) * r, :]
+        gfo[...] = full[(5 + n) * r : (5 + n) * r + ff // GROUPS, :]
+        go[...] = full[(5 + n) * r + ff // GROUPS :, :]
+
     return call(
-        body, ins, [(s, F32) for s in shapes],
-        scratch=[((sum(one[2]), width), F32), ((sum(two[2]), width), F32)],
-        flops=10**6, nbytes=10**6, home=False,
+        body, [("v", a) for a in (t1, o1, t2, o2)], [(s, F32) for s in shapes],
+        scratch=[((sum(split), width), F32)], flops=10**6, nbytes=10**6, home=False,
     )
 
 
@@ -506,16 +624,21 @@
     rows, slots, ff = 2 * half, 2 * mhalf, ffn_in.shape[1]
     padded = rows + 128
     groups = lax.axis_size("seg")
-    y = lax.axis_index("seq")
-    seg = lax.axis_index("seg")
-    place = jnp.stack([y, seg % 2, (seg // 2) % 2, (seg // 4) % 2, (seg // 8) % 2])
-    place = place.astype(jnp.int32)
-    sc = ("s", place)
-    pick = lambda v: lax.dynamic_index_in_dim(v, 1 - y, 0, keepdims=False)
-    recv_a = exchanged(jnp.concatenate([pick(tokens), pick(memory)], 0), "y")
-    recv_b = exchanged(jnp.concatenate([pick(out_cotangent), pick(memory_cotangent)], 0), "y")
+    recv_a = exchanged(packed(tokens, memory), "y")
+    recv_b = exchanged(packed(out_cotangent, memory_cotangent), "y")
+    (
+        tokens, memory, out_cotangent, memory_cotangent, query_weight, pair_weight, out_weight,
+        ffn_in, ffn_out, write_query, write_pair, write_out, write_gate,
+    ) = fetched_weights(
+        (
+            tokens, memory, out_cotangent, memory_cotangent, query_weight, pair_weight, out_weight,
+            ffn_in, ffn_out, write_query, write_pair, write_out, write_gate,
+        )
+    )
     ag, fg, wg = attn_gain[None], ffn_gain[None], write_gain[None]
     v = lambda *arrs: [("v", a) for a in arrs]
+    h = lambda *arrs: [("h", a) for a in arrs]
+    deps = lambda *arrs: [("d", a) for a in arrs]
     big = ((rows, width), BF16)
     wide = ((padded, width), BF16)
     deep = ((rows, ff), BF16)
@@ -529,16 +652,17 @@
         out_send, out_own, out, wqs,
     ) = call(
         forward_body,
-        [sc, ("s", lengths)] + v(tokens, memory, recv_a, ag, query_weight, pair_weight, write_query, out_weight, fg, ffn_in, ffn_out),
+        [("s", lengths)] + v(tokens, memory, recv_a, ag, query_weight, pair_weight)
+        + v(write_query, out_weight, fg, ffn_in, ffn_out),
         [big, small, wide, big, wide, wide]
         + [((H // 2, 256, 128 * (i + 2)), BF16) for i in range(4)]
         + [big, full_f, big, deep, deep, half_b, half_b, big, small],
-        flops=2 * 6 * 10**9, nbytes=20 * 10**6,
+        flops=2 * 6 * 10**9, nbytes=20 * 10**6, limit=16,
     )
     out_recv = exchanged(out_send, "y")
     send0, keep0, dwpair, dwquery, dblend, own_new, newmem, gain3 = call(
         write_body,
-        [sc] + v(out, wqs, mem, memory_cotangent, recv_b, write_pair, write_out, write_gate, wg, nall),
+        v(out, wqs, mem, memory_cotangent, recv_b, write_pair, write_out, write_gate, wg, nall),
         [
             *keep_send(160), ((rows, 2 * width), BF16), small,
             ((slots, width), F32), ((mhalf, width), BF16), small, gain_row,
@@ -546,117 +670,128 @@
         flops=2 * 3 * 10**9, nbytes=10 * 10**6,
     )
     small_mesh = groups == GROUPS
-    send1, keep1, total, dout = call(
+    cube = lambda a: a.reshape((2, 2, 2) + a.shape[1:])
+    pair = lambda keep, send: (cube(keep), cube(exchanged(send, "c")))
+    deps0 = deps1 = []
+    send1, keep1, dout, dinner = call(
         ffn_back_body,
-        [sc] + v(dwpair, write_pair, out_cotangent, recv_b, ffn_out, dg, ffn_in, act, n2),
-        [*keep_send(256), full_f, full_f],
+        v(dwpair, write_pair, out_cotangent, recv_b, ffn_out, dg, act) + deps(out_recv),
+        [*keep_send(128), full_f, deep],
         flops=2 * 5 * 10**9, nbytes=20 * 10**6,
     )
-    dresid, dmixed, gain2 = call(
-        resid_back_body, [sc] + v(total, dout, resid, fg, out_weight), [full_f, big, gain_row],
-        flops=2 * 10**9, nbytes=5 * 10**6,
-    )
-    deps1, deps2 = [], []
     if small_mesh:
-        cube = lambda a: a.reshape((2, 2, 2) + a.shape[1:])
-        recv0, recv1 = exchanged(send0, "c"), exchanged(send1, "c")
-        k0, r0, k1, r1 = cube(keep0), cube(recv0), cube(keep1), cube(recv1)
+        send0, _ = lax.optimization_barrier((send0, out_recv))
+        k0, r0 = pair(keep0, send0)
+        deps0 = deps(r0)
+    send4, keep4, total = call(
+        inner_back_body, v(dinner, n2, ffn_in) + deps0, [*keep_send(128), full_f],
+        flops=10**9, nbytes=20 * 10**6,
+    )
+    if small_mesh:
+        k1, r1 = pair(keep1, send1)
+        deps0 = deps(r1)
+    send3, keep3, dresid, dmixed, gain2 = call(
+        resid_back_body, v(total, dout, resid, fg, out_weight, mixed) + deps0,
+        [*keep_send(32), full_f, big, gain_row],
+        flops=10**8, nbytes=10**6,
+    )
+    orders = ("xyz", "yzx", "zxy")
+    late_orders = ("xz", "zx")
+
+    def moved(parts, labels):
+        return [
+            Stream(keep, exchanged(send, label), dims, 0, r)
+            for label, (keep, send, dims, r) in zip(labels, parts)
+        ]
+
+    nth = lambda these, step: [o[step] for o in these]
+    if small_mesh:
+        k4, r4 = pair(keep4, send4)
+        k3, r3 = pair(keep3, send3)
         streams = [
-            Stream(k0, r0, "hzx", 0, 160), Stream(k1, r1, "hzx", 0, 128),
-            Stream(k1, r1, "hzx", 128, 128),
+            Stream(k0, r0, "hzx", 0, 160), Stream(k4, r4, "hzx", 0, 128),
+            Stream(k1, r1, "hzx", 0, 128), Stream(k3, r3, "hzx", 0, 32),
         ]
-        orders = ("xyz", "yzx", "zxy")
-
-        def moved(parts, step):
-            return [
-                Stream(keep, exchanged(send, orders[k][step]), dims, 0, r)
-                for k, (keep, send, dims, r) in enumerate(parts)
-            ]
-
-        labels = lambda step: [o[step] for o in orders]
-        parts = stage(place, streams, labels(0), deps=[dresid])
-        deps1 = [("d", p[0]) for p in parts]
-        streams = moved(parts, 0)
+        parts = stage_joined(streams, nth(orders, 0), [])
+        deps1 = deps(parts[0][0])
+        first = moved(parts, nth(orders, 0))
     dq, dk, dv = call(
         attn_back_body,
-        [sc] + v(qs, dmixed, vall, p3, kall, p2, p1, p0) + deps1,
+        v(qs, dmixed, vall, p3, kall, p2, p1, p0) + deps1,
         [big, wide, wide],
         scratch=[((padded, width), F32)] * 2,
         flops=2 * 6 * 10**9, nbytes=20 * 10**6,
     )
-    if small_mesh:
-        parts = stage(place, streams, labels(1), deps=[dq])
-        deps2 = [("d", p[0]) for p in parts]
-        streams = moved(parts, 1)
     send2, keep2, own_tok, own_mem, swap = call(
         input_back_body,
-        [sc]
-        + v(
+        v(
             nall, dq, dk, dv, pair_weight, query_weight, dwquery, write_query, x, mem, ag, dresid,
-            dblend, mixed, gain2, gain3, newmem,
-        )
-        + deps2,
+            dblend, gain2, gain3, newmem,
+        ),
         [
-            *keep_send(160), ((half, width), F32), ((mhalf, width), F32),
+            *keep_send(112), ((half, width), F32), ((mhalf, width), F32),
             ((half + 2 * mhalf, width), BF16),
         ],
         scratch=[((rows, width), F32), ((slots, width), F32)],
         flops=2 * 3 * 10**9, nbytes=20 * 10**6,
     )
-    swapped = exchanged(swap, "y")
     r = width // groups
+    (out_both,) = assembled([out_own], out_recv, [BF16])
     if small_mesh:
-        recv2 = exchanged(send2, "c")
-        k2, r2 = cube(keep2), cube(recv2)
-        keep, send = stage_three(place, streams, labels(2), swap)
-        t1 = added(place, keep, exchanged(send, "h"))
+        chain = [send2]
+
+        def each(streams, labels):
+            results = []
+            for stream, label in zip(streams, labels):
+                ((keep, send, dims, n),) = stage([stream], [label], deps=chain[-1:])
+                results.append((keep, send, dims, n))
+                chain.append(keep)
+            return moved(results, labels)
+
+        second = each(first, nth(orders, 1))
+        send2, swap, _ = lax.optimization_barrier((send2, swap, chain[-1]))
+        k2, r2 = pair(keep2, send2)
+        late = [Stream(k2, r2, "hzx", 0, 64), Stream(k2, r2, "hzx", 64, 48)]
+        late = each(late, nth(late_orders, 0))
+        third = each(second, nth(orders, 2))
+        late = late_second = each(late, nth(late_orders, 1))
+        late = [chain[-1:]]
+        keep, send = stage(third, "hhh", joined=True, deps=[late[0][0]])
+        recv = exchanged(send, "h")
+        late_keep, late_send = stage(late_second, "hh", joined=True, deps=[keep])
+        late_recv = exchanged(late_send, "h")
+        t1 = added(keep, recv, deps=[late_keep])
         o1 = exchanged(t1, "y")
-        late = [
-            Stream(k2, r2, "hzx", 0, 64), Stream(k2, r2, "hzx", 64, 32),
-            Stream(k2, r2, "hzx", 96, 64),
-        ]
-        late = moved(stage(place, late, labels(0)), 0)
-        late = moved(stage(place, late, labels(1)), 1)
-        late = moved(stage(place, late, labels(2)), 2)
-        keep, send = stage(place, late, "hhh", joined=True)
-        t2 = added(place, keep, exchanged(send, "h"))
+        t2 = added(late_keep, late_recv, deps=[t1])
         o2 = exchanged(t2, "y")
-        gq, gp, go, gfi, gfo, gwq, gwp, gwo, gwg, gains = final_parts(
-            place, (t1, o1, (160, 128, 128)), (t2, o2, (64, 32, 64)), ff
+        gq, gp, go, gfi, gfo, gwq, gwp, gwo, gwg, *gains = final_parts(
+            (t1, o1, (160, 128, 160)), (t2, o2), ff
         )
     else:
         w = width // GROUPS
         w0 = reduced_any(keep0, send0, [(w, False)] * 5)
-        w1 = reduced_any(keep1, send1, [(w, False)] * (ff // 512) + [(ff // GROUPS, False)])
-        w2 = reduced_any(keep2, send2, [(w, False)] * 4 + [(32, True)])
+        gfo = reduced_any(keep1, send1, [(ff // GROUPS, False)])
+        w1 = reduced_any(keep4, send4, [(w, False)] * (ff // 512))
+        w2 = reduced_any(keep2, send2, [(w, False)] * 3 + [(16, True)])
+        go = reduced_any(keep3, send3, [(w, False)])
         cut = lambda a, at, n: jnp.concatenate(
             [a[(at + i) * r : (at + i + 1) * r] for i in range(n)], 1
         )
-        gq, gp, go, gains = cut(w2, 0, 1), cut(w2, 1, 2), cut(w2, 3, 1), w2[4 * r :]
-        gfi, gfo = cut(w1, 0, ff // 512), w1[(ff // 512) * r :]
+        gq, gp = cut(w2, 0, 1), cut(w2, 1, 2)
+        gfi = cut(w1, 0, ff // 512)
         gwq, gwp, gwo, gwg = cut(w0, 0, 1), cut(w0, 1, 2), cut(w0, 3, 1), cut(w0, 4, 1)
-    gain_of = lambda i: lax.dynamic_slice_in_dim(gains[i], seg * r, r, 0)
-
-    def both(own, recv):
-        recv = recv.astype(own.dtype)
-        return jnp.where(jnp.arange(2)[:, None, None] == y, own[None], recv[None])
-
+        at = lax.axis_index("seg") * r
+        gains = [lax.dynamic_slice_in_dim(w2[3 * r + i], at, r, 0) for i in range(3)]
+    swapped = exchanged(swap, "y")
+    tok_both, new_both, mem_both = assembled([own_tok, own_new, own_mem], swapped, [F32, BF16, F32])
     return (
-        both(out_own, out_recv),
-        both(own_new, swapped[half : half + mhalf]),
-        both(own_tok, swapped[:half]),
-        both(own_mem, swapped[half + mhalf :]),
-        gain_of(0), gq, gp, go, gain_of(1), gfi, gfo, gwq, gwp, gwo, gwg, gain_of(2),
-    )
-
-
-def stage_three(place, streams, labels, dep):
-    parts = stage(place, streams, labels, deps=[dep])
-    moved = [
-        Stream(keep, exchanged(send, label), dims, 0, r)
-        for label, (keep, send, dims, r) in zip(labels, parts)
-    ]
-    return stage(place, moved, "hhh", joined=True)
+        out_both, new_both, tok_both, mem_both,
+        gains[0], gq, gp, go, gains[1], gfi, gfo, gwq, gwp, gwo, gwg, gains[2],
+    )
+
+
+def stage_joined(streams, labels, deps):
+    return stage(streams, list(labels) + [labels[-1]], tail=True, deps=deps)
 
 
 def solution(mesh):

time: 145 us -> 105 us (0.72)
  waiting for transfers between devices: 40.9 us -> 26.5 us
  local copies, waits for them, and re-layouts: 12.5 us -> 0.03 us
  other arithmetic: 7.01 us -> 0 us
  Pallas kernels: 50.2 us -> 46.7 us
  starting transfers between devices: 32.2 us -> 30.7 us
    ppermute x12 -> x9, waiting for transfers between devices: 23.9 us -> 10.6 us  [exchanged(): return lax.ppermute(send, 'seq', other_of('seq', 1))]
    pallas_call x17 -> x25, Pallas kernels: 50.2 us -> 40.8 us  [call(): pl.pallas_call(kernel, out_shape=[shape(s, d) for s, d in outs], in_specs...]
    unnamed x70 -> x8, local copies, waits for them, and re-layouts: 7.68 us -> 0.03 us
    pallas_call x0 -> x3, Pallas kernels: none -> 5.91 us  [the longest x1 3.97 us: fetched_weights(): pl.pallas_call(kernel, out_shape=[pltpu.VMEM(a.shape, a.dtype) for a in w...]
    select_n x4 -> x0, other arithmetic: 4.47 us -> none  [both(): return jnp.where(jnp.arange(2)[:, None, None] == y, own[None], recv[None])]
    squeeze x4 -> x0, local copies, waits for them, and re-layouts: 3.6 us -> none  [shards(): pick = lambda v: lax.dynamic_index_in_dim(v, 1 - y, 0, keepdims=False)]
    convert_element_type x2 -> x0, other arithmetic: 1.78 us -> none  [both(): recv = recv.astype(own.dtype)]
    ppermute x12 -> x9, starting transfers between devices: 12.8 us -> 12.3 us  [exchanged(): return lax.ppermute(send, 'seq', other_of('seq', 1))]
  transfers between devices with their start and end apart: 29 -> 26, of which waited for: 15 -> 14; matrix products, arithmetic and copies ran while one was open for 6% -> 0% of each run, Pallas kernels for 21% -> 42%
where the time goes in v3:
time: 105 us
  Pallas kernels  46.7 us (44%)
  starting transfers between devices  30.7 us (29%)
  waiting for transfers between devices  26.5 us (25%)
  between operations  1.05 us (1%)
    pallas_call x25, Pallas kernels, call(): pl.pallas_call(kernel, out_shape=[shape(s, d) for s, d in outs], in_specs...  40.8 us
    ppermute x17, starting transfers between devices, exchanged(): lax.ppermute(send, 'seg', other_of('seg', {'x': 2, 'z': 4, 'h': 8, 'c': 1...  18.5 us
    ppermute x17, waiting for transfers between devices, exchanged(): lax.ppermute(send, 'seg', other_of('seg', {'x': 2, 'z': 4, 'h': 8, 'c': 1...  15.9 us
    ppermute x9, starting transfers between devices, exchanged(): return lax.ppermute(send, 'seq', other_of('seq', 1))  12.3 us
    ppermute x9, waiting for transfers between devices, exchanged(): return lax.ppermute(send, 'seq', other_of('seq', 1))  10.6 us
    pallas_call x1, Pallas kernels, fetched_weights(): pl.pallas_call(kernel, out_shape=[pltpu.VMEM(a.shape, a.dtype) for a in w...  3.97 us
  transfers between devices with their start and end apart: 26, of which 14 were waited for; matrix products, arithmetic and copies ran while one was open for 0% of the time, Pallas kernels for 42%

profile of v3, /device:TPU:0, one launch (start us, length us, event | category | flops | bytes accessed | tf_op | source)
XLA Modules:
  0.0 105.1 jit_solution(13426102856355364486)
XLA Ops:
  0.6 1.0 shard_map.289
  1.6 3.0 %collective-permute-start = (bf16[288,512]{1,0:T(8,128)(2,1)S(1)}, bf16[288,512]{1,0:T(8,128)(2,1)S(1)}, u32[]{:S(2)}, u32[]{:S(2)}) collective-permute-start(bf16[288,512]{1,0:T(8,128)(2,1)S(1)} %shard_map.289), channel_id=1, source_target_pairs={{0,16},{16,0},{1,17},{17,1},{2,18},{18,2},{3,19},{19,3},{4,20},{20... | collective-permute-start | bytes 884744 | tf_op jit(solution)/shard_map/ppermute | solution.py:387
  4.7 1.0 shard_map.292
  5.8 4.0 %shard_map.288 = (bf16[2,256,512]{2,1,0:T(8,128)(2,1)S(1)}, bf16[2,32,512]{2,1,0:T(8,128)(2,1)S(1)}, bf16[2,256,512]{2,1,0:T(8,128)(2,1)S(1)}, bf16[2,32,512]{2,...) custom-call(bf16[2,256,512]{2,1,0:T(8,128)(2,1)} %a.2, ...), custom_call_target="tpu_custom_call" | custom-call | flops 1000000000 | bytes 10000000 | tf_op jit(solution)/shard_map/pallas_call | solution.py:537
  9.7 2.8 %collective-permute-done.refs_3_ = bf16[288,512]{1,0:T(8,128)(2,1)S(1)} collective-permute-done((bf16[288,512]{1,0:T(8,128)(2,1)S(1)}, bf16[288,512]{1,0:T(8,128)(2,1)S(1)}, u32[]{:S(2)}, u32[]{:S(2)}) %collective-permute-start) | collective-permute-done | bytes 294944 | tf_op jit(solution)/shard_map/ppermute | solution.py:387
  12.5 13.1 %shard_map.290 = (bf16[512,512]{1,0:T(8,128)(2,1)S(1)}, bf16[64,512]{1,0:T(8,128)(2,1)S(1)}, bf16[640,512]{1,0:T(8,128)(2,1)S(1)}, bf16[512,512]{1,0:T(8,128)(2,...) custom-call(s32[2,8]{1,0:T(2,128)S(1)} %copy-done.3, ...), custom_call_target="tpu_custom_call" | custom-call | flops 12000000000 | bytes 20000000 | tf_op jit(solution)/shard_map/pallas_call | solution.py:64
  25.6 2.1 %collective-permute-start.1 = (bf16[256,512]{1,0:T(8,128)(2,1)S(1)}, bf16[256,512]{1,0:T(8,128)(2,1)S(1)}, u32[]{:S(2)}, u32[]{:S(2)}) collective-permute-start(bf16[256,512]{1,0:T(8,128)(2,1)S(1)} %get-tuple-element.133), channel_id=1, source_target_pairs={{0,16},{16,0},{1,17},{17,1},{2,18},{18,2},{3,19},{19,3},{4,20},{20... | collective-permute-start | bytes 786440 | tf_op jit(solution)/shard_map/ppermute | solution.py:387
  27.7 5.0 %shard_map.293 = (bf16[8,160,512]{2,1,0:T(8,128)(2,1)S(1)}, bf16[8,160,512]{2,1,0:T(8,128)(2,1)S(1)}, bf16[512,1024]{1,0:T(8,128)(2,1)S(1)}, bf16[64,512]{1,0:T(...) custom-call(bf16[512,512]{1,0:T(8,128)(2,1)S(1)} %get-tuple-element., ...), custom_call_target="tpu_custom_call" | custom-call | flops 6000000000 | bytes 10000000 | tf_op jit(solution)/shard_map/pallas_call | solution.py:64
  32.8 3.0 %shard_map.294 = (bf16[8,128,512]{2,1,0:T(8,128)(2,1)S(1)}, bf16[8,128,512]{2,1,0:T(8,128)(2,1)S(1)}, f32[512,512]{1,0:T(8,128)S(1)}, bf16[512,2048]{1,0:T(8,128)(2,1)S(1)}) custom-call(bf16[512,1024]{1,0:T(8,128)(2,1)S(1)} %get-tuple-element.143.refs_0_, bf16[512,1024]{1,0:T(8,128)(2,1)S(1)} %get-tuple-element.140.refs_5_.refs_1_, ...), custom_call_target="tpu_custom_call" | custom-call | flops 10000000000 | bytes 20000000 | tf_op jit(solution)/shard_map/pallas_call | solution.py:64
  35.8 0.6 collective-permute-start.4
  36.3 2.4 %shard_map.295 = (bf16[8,128,512]{2,1,0:T(8,128)(2,1)S(1)}, bf16[8,128,512]{2,1,0:T(8,128)(2,1)S(1)}, f32[512,512]{1,0:T(8,128)S(1)}) custom-call(bf16[512,2048]{1,0:T(8,128)(2,1)S(1)} %get-tuple-element.147.refs_0_, bf16[512,512]{1,0:T(8,128)(2,1)S(1)} %get-tuple-element.148.refs_1_, bf16[512,2048]{1,0:T(8,128)(2,1)S(1)} %get-tuple-element.130.refs_10_.refs_2_, ...), custom_call_target="tpu_custom_call" | custom-call | flops 1000000000 | bytes 20000000 | tf_op jit(solution)/shard_map/pallas_call | solution.py:64
  38.9 1.5 %shard_map.296 = (bf16[8,32,512]{2,1,0:T(8,128)(2,1)S(1)}, bf16[8,32,512]{2,1,0:T(8,128)(2,1)S(1)}, f32[512,512]{1,0:T(8,128)S(1)}, bf16[512,512]{1,0:T(8,128)(2,1)S(1)}, f32[1,512]{1,0:T(1,128)S(1)}) custom-call(f32[512,512]{1,0:T(8,128)S(1)} %get-tuple-element.151.refs_0_, f32[512,512]{1,0:T(8,128)S(1)} %get-tuple-element.152.refs_1_, ...), custom_call_target="tpu_custom_call" | custom-call | flops 100000000 | bytes 1000000 | tf_op jit(solution)/shard_map/pallas_call | solution.py:64
  40.3 0.5 collective-permute-start.6
  40.9 1.2 %collective-permute-done.6 = bf16[8,32,512]{2,1,0:T(8,128)(2,1)S(1)} collective-permute-done((bf16[8,32,512]{2,1,0:T(8,128)(2,1)S(1)}, bf16[8,32,512]{2,1,0:T(8,128)(2,1)S(1)}, u32[]{:S(2)}, u32[]{:S(2)}) %collective-permute-start.6) | collective-permute-done | bytes 262176 | tf_op jit(solution)/shard_map/ppermute | solution.py:388
  42.0 0.8 shard_map.297
  42.9 1.6 %collective-permute-start.9 = (bf16[2,2,160,512]{3,2,1,0:T(8,128)(2,1)S(1)}, bf16[2,2,160,512]{3,2,1,0:T(8,128)(2,1)S(1)}, u32[]{:S(2)}, u32[]{:S(2)}) collective-permute-start(bf16[2,2,160,512]{3,2,1,0:T(8,128)(2,1)S(1)} %get-tuple-element.189), channel_id=1, source_target_pairs={{0,2},{1,3},{2,0},{3,1},{4,6},{5,7},{6,4},{7,5},{8,10},{9,11},{10,... | collective-permute-start | bytes 1966088 | tf_op jit(solution)/shard_map/ppermute | solution.py:388
  44.5 1.3 %collective-permute-start.8 = (bf16[2,2,2,64,512]{4,3,2,1,0:T(8,128)(2,1)S(1)}, bf16[2,2,2,64,512]{4,3,2,1,0:T(8,128)(2,1)S(1)}, u32[]{:S(2)}, u32[]{:S(2)}) collective-permute-start(bf16[2,2,2,64,512]{4,3,2,1,0:T(8,128)(2,1)S(1)} %get-tuple-element.188), channel_id=1, source_target_pairs={{0,16},{16,0},{1,17},{17,1},{2,18},{18,2},{3,19},{19,3},{4,20},{20... | collective-permute-start | bytes 1572872 | tf_op jit(solution)/shard_map/ppermute | solution.py:387
  45.8 1.6 %collective-permute-start.7 = (bf16[2,2,160,512]{3,2,1,0:T(8,128)(2,1)S(1)}, bf16[2,2,160,512]{3,2,1,0:T(8,128)(2,1)S(1)}, u32[]{:S(2)}, u32[]{:S(2)}) collective-permute-start(bf16[2,2,160,512]{3,2,1,0:T(8,128)(2,1)S(1)} %get-tuple-element.186), channel_id=1, source_target_pairs={{0,4},{1,5},{2,6},{3,7},{4,0},{5,1},{6,2},{7,3},{8,12},{9,13},{10,... | collective-permute-start | bytes 1966088 | tf_op jit(solution)/shard_map/ppermute | solution.py:388
  47.4 8.0 %shard_map.298 = (bf16[512,512]{1,0:T(8,128)(2,1)S(1)}, bf16[640,512]{1,0:T(8,128)(2,1)S(1)}, bf16[640,512]{1,0:T(8,128)(2,1)S(1)}) custom-call(bf16[512,512]{1,0:T(8,128)(2,1)S(1)} %get-tuple-element.135.refs_0_, bf16[512,512]{1,0:T(8,128)(2,1)S(1)} %get-tuple-element.156.refs_1_, bf16[640,512]{1,0:T(8,128)(2,1)S(1)} %get-tuple-element.157.refs_2_, ...), custom_call_target="tpu_custom_call" | custom-call | flops 12000000000 | bytes 20000000 | tf_op jit(solution)/shard_map/pallas_call | solution.py:64
  55.3 2.9 %shard_map.299 = (bf16[8,112,512]{2,1,0:T(8,128)(2,1)S(1)}, bf16[8,112,512]{2,1,0:T(8,128)(2,1)S(1)}, f32[256,512]{1,0:T(8,128)S(1)}, f32[32,512]{1,0:T(8,128)S(1)}, bf16[320,512]{1,0:T(8,128)(2,1)S(1)}) custom-call(bf16[640,512]{1,0:T(8,128)(2,1)S(1)} %get-tuple-element.134.refs_9_.refs_0_, bf16[512,512]{1,0:T(8,128)(2,1)S(1)} %get-tuple-element.170.refs_1_, ...), custom_call_target="tpu_custom_call" | custom-call | flops 6000000000 | bytes 20000000 | tf_op jit(solution)/shard_map/pallas_call | solution.py:64
  58.2 1.8 %collective-permute-done.9.refs_1_ = bf16[2,2,160,512]{3,2,1,0:T(8,128)(2,1)S(1)} collective-permute-done((bf16[2,2,160,512]{3,2,1,0:T(8,128)(2,1)S(1)}, bf16[2,2,160,512]{3,2,1,0:T(8,128)(2,1)S(1)}, u32[]{:S(2)}, u32[]{:S(2)}) %collective-permute-start.9) | collective-permute-done | bytes 655392 | tf_op jit(solution)/shard_map/ppermute | solution.py:388
  60.3 2.0 %collective-permute-done.7.refs_1_ = bf16[2,2,160,512]{3,2,1,0:T(8,128)(2,1)S(1)} collective-permute-done((bf16[2,2,160,512]{3,2,1,0:T(8,128)(2,1)S(1)}, bf16[2,2,160,512]{3,2,1,0:T(8,128)(2,1)S(1)}, u32[]{:S(2)}, u32[]{:S(2)}) %collective-permute-start.7) | collective-permute-done | bytes 655392 | tf_op jit(solution)/shard_map/ppermute | solution.py:388
  62.5 0.8 collective-permute-start.11
  63.2 0.5 collective-permute-start.16
  63.7 1.6 %collective-permute-start.14 = (bf16[2,2,64,512]{3,2,1,0:T(8,128)(2,1)S(1)}, bf16[2,2,64,512]{3,2,1,0:T(8,128)(2,1)S(1)}, u32[]{:S(2)}, u32[]{:S(2)}) collective-permute-start(bf16[2,2,64,512]{3,2,1,0:T(8,128)(2,1)S(1)} %get-tuple-element.204), channel_id=1, source_target_pairs={{0,4},{1,5},{2,6},{3,7},{4,0},{5,1},{6,2},{7,3},{8,12},{9,13},{10,... | collective-permute-start | bytes 786440 | tf_op jit(solution)/shard_map/ppermute | solution.py:388
  65.5 1.6 %collective-permute-start.19 = (bf16[2,2,64,512]{3,2,1,0:T(8,128)(2,1)S(1)}, bf16[2,2,64,512]{3,2,1,0:T(8,128)(2,1)S(1)}, u32[]{:S(2)}, u32[]{:S(2)}) collective-permute-start(bf16[2,2,64,512]{3,2,1,0:T(8,128)(2,1)S(1)} %get-tuple-element.211), channel_id=1, source_target_pairs={{0,2},{1,3},{2,0},{3,1},{4,6},{5,7},{6,4},{7,5},{8,10},{9,11},{10,... | collective-permute-start | bytes 786440 | tf_op jit(solution)/shard_map/ppermute | solution.py:388
  67.2 0.5 collective-permute-start.18
  67.7 4.9 %collective-permute-done.11.refs_1_ = bf16[2,2,80,512]{3,2,1,0:T(8,128)(2,1)S(1)} collective-permute-done((bf16[2,2,80,512]{3,2,1,0:T(8,128)(2,1)S(1)}, bf16[2,2,80,512]{3,2,1,0:T(8,128)(2,1)S(1)}, u32[]{:S(2)}, u32[]{:S(2)}) %collective-permute-start.11) | collective-permute-done | bytes 327712 | tf_op jit(solution)/shard_map/ppermute | solution.py:387
  73.0 0.8 collective-permute-done.16.refs_1_
  73.9 1.4 %collective-permute-start.17 = (bf16[2,80,512]{2,1,0:T(8,128)(2,1)S(1)}, bf16[2,80,512]{2,1,0:T(8,128)(2,1)S(1)}, u32[]{:S(2)}, u32[]{:S(2)}) collective-permute-start(bf16[2,80,512]{2,1,0:T(8,128)(2,1)S(1)} %get-tuple-element.209), channel_id=1, source_target_pairs={{0,16},{16,0},{1,17},{17,1},{2,18},{18,2},{3,19},{19,3},{4,20},{20... | collective-permute-start | bytes 491528 | tf_op jit(solution)/shard_map/ppermute | solution.py:387
  75.3 1.6 %collective-permute-start.13 = (bf16[2,80,512]{2,1,0:T(8,128)(2,1)S(1)}, bf16[2,80,512]{2,1,0:T(8,128)(2,1)S(1)}, u32[]{:S(2)}, u32[]{:S(2)}) collective-permute-start(bf16[2,80,512]{2,1,0:T(8,128)(2,1)S(1)} %get-tuple-element.203), channel_id=1, source_target_pairs={{0,4},{1,5},{2,6},{3,7},{4,0},{5,1},{6,2},{7,3},{8,12},{9,13},{10,... | collective-permute-start | bytes 491528 | tf_op jit(solution)/shard_map/ppermute | solution.py:388
  76.8 0.8 collective-permute-start.15
  77.6 1.8 %collective-permute-done.19.refs_1_ = bf16[2,2,64,512]{3,2,1,0:T(8,128)(2,1)S(1)} collective-permute-done((bf16[2,2,64,512]{3,2,1,0:T(8,128)(2,1)S(1)}, bf16[2,2,64,512]{3,2,1,0:T(8,128)(2,1)S(1)}, u32[]{:S(2)}, u32[]{:S(2)}) %collective-permute-start.19) | collective-permute-done | bytes 262176 | tf_op jit(solution)/shard_map/ppermute | solution.py:388
  79.5 2.2 %collective-permute-done.15.refs_3_ = bf16[2,64,512]{2,1,0:T(8,128)(2,1)S(1)} collective-permute-done((bf16[2,64,512]{2,1,0:T(8,128)(2,1)S(1)}, bf16[2,64,512]{2,1,0:T(8,128)(2,1)S(1)}, u32[]{:S(2)}, u32[]{:S(2)}) %collective-permute-start.15) | collective-permute-done | bytes 131104 | tf_op jit(solution)/shard_map/ppermute | solution.py:388
  81.9 2.7 %collective-permute-start.20 = (bf16[224,512]{1,0:T(8,128)(2,1)S(1)}, bf16[224,512]{1,0:T(8,128)(2,1)S(1)}, u32[]{:S(2)}, u32[]{:S(2)}) collective-permute-start(bf16[224,512]{1,0:T(8,128)(2,1)S(1)} %get-tuple-element.215), channel_id=1, source_target_pairs={{0,8},{1,9},{2,10},{3,11},{4,12},{5,13},{6,14},{7,15},{8,0},{9,1},... | collective-permute-start | bytes 688136 | tf_op jit(solution)/shard_map/ppermute | solution.py:388
  84.6 1.2 %collective-permute-start.21 = (bf16[2,64,512]{2,1,0:T(8,128)(2,1)S(1)}, bf16[2,64,512]{2,1,0:T(8,128)(2,1)S(1)}, u32[]{:S(2)}, u32[]{:S(2)}) collective-permute-start(bf16[2,64,512]{2,1,0:T(8,128)(2,1)S(1)} %get-tuple-element.216), channel_id=1, source_target_pairs={{0,4},{1,5},{2,6},{3,7},{4,0},{5,1},{6,2},{7,3},{8,12},{9,13},{10,... | collective-permute-start | bytes 393224 | tf_op jit(solution)/shard_map/ppermute | solution.py:388
  85.8 0.6 collective-permute-start.22
  86.3 1.3 %collective-permute-start.10 = (bf16[320,512]{1,0:T(8,128)(2,1)S(1)}, bf16[320,512]{1,0:T(8,128)(2,1)S(1)}, u32[]{:S(2)}, u32[]{:S(2)}) collective-permute-start(bf16[320,512]{1,0:T(8,128)(2,1)S(1)} %get-tuple-element.193), channel_id=1, source_target_pairs={{0,16},{16,0},{1,17},{17,1},{2,18},{18,2},{3,19},{19,3},{4,20},{20... | collective-permute-start | bytes 983048 | tf_op jit(solution)/shard_map/ppermute | solution.py:387
  87.7 2.7 %collective-permute-done.22.refs_3_ = bf16[2,48,512]{2,1,0:T(8,128)(2,1)S(1)} collective-permute-done((bf16[2,48,512]{2,1,0:T(8,128)(2,1)S(1)}, bf16[2,48,512]{2,1,0:T(8,128)(2,1)S(1)}, u32[]{:S(2)}, u32[]{:S(2)}) %collective-permute-start.22) | collective-permute-done | bytes 98336 | tf_op jit(solution)/shard_map/ppermute | solution.py:388
  90.8 3.1 %collective-permute-start.24 = (bf16[112,512]{1,0:T(8,128)(2,1)S(1)}, bf16[112,512]{1,0:T(8,128)(2,1)S(1)}, u32[]{:S(2)}, u32[]{:S(2)}) collective-permute-start(bf16[112,512]{1,0:T(8,128)(2,1)S(1)} %get-tuple-element.219), channel_id=1, source_target_pairs={{0,8},{1,9},{2,10},{3,11},{4,12},{5,13},{6,14},{7,15},{8,0},{9,1},... | collective-permute-start | bytes 344072 | tf_op jit(solution)/shard_map/ppermute | solution.py:388
  93.9 1.4 %collective-permute-done.20.refs_1_ = bf16[224,512]{1,0:T(8,128)(2,1)S(1)} collective-permute-done((bf16[224,512]{1,0:T(8,128)(2,1)S(1)}, bf16[224,512]{1,0:T(8,128)(2,1)S(1)}, u32[]{:S(2)}, u32[]{:S(2)}) %collective-permute-start.20) | collective-permute-done | bytes 229408 | tf_op jit(solution)/shard_map/ppermute | solution.py:388
  95.3 0.6 collective-permute-start.23
  95.9 1.4 %collective-permute-done.24.refs_1_ = bf16[112,512]{1,0:T(8,128)(2,1)S(1)} collective-permute-done((bf16[112,512]{1,0:T(8,128)(2,1)S(1)}, bf16[112,512]{1,0:T(8,128)(2,1)S(1)}, u32[]{:S(2)}, u32[]{:S(2)}) %collective-permute-start.24) | collective-permute-done | bytes 114720 | tf_op jit(solution)/shard_map/ppermute | solution.py:388
  97.4 1.6 %collective-permute-start.25 = (bf16[112,512]{1,0:T(8,128)(2,1)S(1)}, bf16[112,512]{1,0:T(8,128)(2,1)S(1)}, u32[]{:S(2)}, u32[]{:S(2)}) collective-permute-start(bf16[112,512]{1,0:T(8,128)(2,1)S(1)} %shard_map.314.refs_2_), channel_id=1, source_target_pairs={{0,16},{16,0},{1,17},{17,1},{2,18},{18,2},{3,19},{19,3},{4,20},{20... | collective-permute-start | bytes 344072 | tf_op jit(solution)/shard_map/ppermute | solution.py:387
  99.0 0.8 shard_map.291
  99.8 1.1 %shard_map.303 = (f32[2,256,512]{2,1,0:T(8,128)}, bf16[2,32,512]{2,1,0:T(8,128)(2,1)}, f32[2,32,512]{2,1,0:T(8,128)}) custom-call(f32[256,512]{1,0:T(8,128)S(1)} %get-tuple-element.180.refs_0_, bf16[32,512]{1,0:T(8,128)(2,1)S(1)} %get-tuple-element.181.refs_1_, f32[32,512]{1,0:T(8,128)S(1)} %get-tuple-element.182.refs_2_, ...), custom_call_target="tpu_custom_call" | custom-call | flops 1000000 | bytes 1000000 | tf_op jit(solution)/shard_map/pallas_call | solution.py:64
  100.9 2.9 %collective-permute-done.25.refs_3_ = bf16[112,512]{1,0:T(8,128)(2,1)S(1)} collective-permute-done((bf16[112,512]{1,0:T(8,128)(2,1)S(1)}, bf16[112,512]{1,0:T(8,128)(2,1)S(1)}, u32[]{:S(2)}, u32[]{:S(2)}) %collective-permute-start.25) | collective-permute-done | bytes 114720 | tf_op jit(solution)/shard_map/ppermute | solution.py:387
  103.9 1.0 shard_map.315
  (40 shorter events, 2.3 us)
Async XLA Ops:
  1.6 10.9 %collective-permute-start = (bf16[288,512]{1,0:T(8,128)(2,1)S(1)}, bf16[288,512]{1,0:T(8,128)(2,1)S(1)}, u32[]{:S(2)}, u32[]{:S(2)}) collective-permute-start(bf16[288,512]{1,0:T(8,128)(2,1)S(1)} %shard_map.289), channel_id=1, source_target_pairs={{0,16},{16,0},{1,17},{17,1},{2,18},{18,2},{3,19},{19,3},{4,20},{20... | collective-permute-start | bytes 884744 | tf_op jit(solution)/shard_map/ppermute | solution.py:387
  5.6 6.9 %copy-start = (f32[512]{0:T(512)S(1)}, f32[512]{0:T(512)}, u32[]{:S(2)}) copy-start(f32[512]{0:T(512)} %param.24) | copy-start | bytes 6148
  5.7 6.9 %copy-start.2 = (f32[512]{0:T(512)S(1)}, f32[512]{0:T(512)}, u32[]{:S(2)}) copy-start(f32[512]{0:T(512)} %param.20) | copy-start | bytes 6148
  5.7 6.8 %copy-start.3 = (s32[2,8]{1,0:T(2,128)S(1)}, s32[2,8]{1,0:T(2,128)}, u32[]{:S(2)}) copy-start(s32[2,8]{1,0:T(2,128)} %refs_0_.3) | copy-start | bytes 196
  5.7 22.0 %collective-permute-start.2 = (bf16[288,512]{1,0:T(8,128)(2,1)S(1)}, bf16[288,512]{1,0:T(8,128)(2,1)S(1)}, u32[]{:S(2)}, u32[]{:S(2)}) collective-permute-start(bf16[288,512]{1,0:T(8,128)(2,1)S(1)} %shard_map.292), channel_id=1, source_target_pairs={{0,16},{16,0},{1,17},{17,1},{2,18},{18,2},{3,19},{19,3},{4,20},{20... | collective-permute-start | bytes 884744 | tf_op jit(solution)/shard_map/ppermute | solution.py:387
  12.5 15.2 %copy-start.1 = (f32[512]{0:T(512)S(1)}, f32[512]{0:T(512)}, u32[]{:S(2)}) copy-start(f32[512]{0:T(512)} %param.31) | copy-start | bytes 6148
  25.6 7.1 %collective-permute-start.1 = (bf16[256,512]{1,0:T(8,128)(2,1)S(1)}, bf16[256,512]{1,0:T(8,128)(2,1)S(1)}, u32[]{:S(2)}, u32[]{:S(2)}) collective-permute-start(bf16[256,512]{1,0:T(8,128)(2,1)S(1)} %get-tuple-element.133), channel_id=1, source_target_pairs={{0,16},{16,0},{1,17},{17,1},{2,18},{18,2},{3,19},{19,3},{4,20},{20... | collective-permute-start | bytes 786440 | tf_op jit(solution)/shard_map/ppermute | solution.py:387
  32.7 3.7 %collective-permute-start.3 = (bf16[8,160,512]{2,1,0:T(8,128)(2,1)S(1)}, bf16[8,160,512]{2,1,0:T(8,128)(2,1)S(1)}, u32[]{:S(2)}, u32[]{:S(2)}) collective-permute-start(bf16[8,160,512]{2,1,0:T(8,128)(2,1)S(1)} %get-tuple-element.150), channel_id=1, source_target_pairs={{0,1},{1,0},{2,3},{3,2},{4,5},{5,4},{6,7},{7,6},{8,9},{9,8},{10,11... | collective-permute-start | bytes 3932168 | tf_op jit(solution)/shard_map/ppermute | solution.py:388
  35.8 3.1 %collective-permute-start.4 = (bf16[8,128,512]{2,1,0:T(8,128)(2,1)S(1)}, bf16[8,128,512]{2,1,0:T(8,128)(2,1)S(1)}, u32[]{:S(2)}, u32[]{:S(2)}) collective-permute-start(bf16[8,128,512]{2,1,0:T(8,128)(2,1)S(1)} %get-tuple-element.155), channel_id=1, source_target_pairs={{0,1},{1,0},{2,3},{3,2},{4,5},{5,4},{6,7},{7,6},{8,9},{9,8},{10,11... | collective-permute-start | bytes 3145736 | tf_op jit(solution)/shard_map/ppermute | solution.py:388
  38.8 3.3 %collective-permute-start.5 = (bf16[8,128,512]{2,1,0:T(8,128)(2,1)S(1)}, bf16[8,128,512]{2,1,0:T(8,128)(2,1)S(1)}, u32[]{:S(2)}, u32[]{:S(2)}) collective-permute-start(bf16[8,128,512]{2,1,0:T(8,128)(2,1)S(1)} %get-tuple-element.165), channel_id=1, source_target_pairs={{0,1},{1,0},{2,3},{3,2},{4,5},{5,4},{6,7},{7,6},{8,9},{9,8},{10,11... | collective-permute-start | bytes 3145736 | tf_op jit(solution)/shard_map/ppermute | solution.py:388
  40.3 1.7 %collective-permute-start.6 = (bf16[8,32,512]{2,1,0:T(8,128)(2,1)S(1)}, bf16[8,32,512]{2,1,0:T(8,128)(2,1)S(1)}, u32[]{:S(2)}, u32[]{:S(2)}) collective-permute-start(bf16[8,32,512]{2,1,0:T(8,128)(2,1)S(1)} %get-tuple-element.168), channel_id=1, source_target_pairs={{0,1},{1,0},{2,3},{3,2},{4,5},{5,4},{6,7},{7,6},{8,9},{9,8},{10,11... | collective-permute-start | bytes 786440 | tf_op jit(solution)/shard_map/ppermute | solution.py:388
  42.9 17.1 %collective-permute-start.9 = (bf16[2,2,160,512]{3,2,1,0:T(8,128)(2,1)S(1)}, bf16[2,2,160,512]{3,2,1,0:T(8,128)(2,1)S(1)}, u32[]{:S(2)}, u32[]{:S(2)}) collective-permute-start(bf16[2,2,160,512]{3,2,1,0:T(8,128)(2,1)S(1)} %get-tuple-element.189), channel_id=1, source_target_pairs={{0,2},{1,3},{2,0},{3,1},{4,6},{5,7},{6,4},{7,5},{8,10},{9,11},{10,... | collective-permute-start | bytes 1966088 | tf_op jit(solution)/shard_map/ppermute | solution.py:388
  44.5 15.6 %collective-permute-start.8 = (bf16[2,2,2,64,512]{4,3,2,1,0:T(8,128)(2,1)S(1)}, bf16[2,2,2,64,512]{4,3,2,1,0:T(8,128)(2,1)S(1)}, u32[]{:S(2)}, u32[]{:S(2)}) collective-permute-start(bf16[2,2,2,64,512]{4,3,2,1,0:T(8,128)(2,1)S(1)} %get-tuple-element.188), channel_id=1, source_target_pairs={{0,16},{16,0},{1,17},{17,1},{2,18},{18,2},{3,19},{19,3},{4,20},{20... | collective-permute-start | bytes 1572872 | tf_op jit(solution)/shard_map/ppermute | solution.py:387
  45.8 16.4 %collective-permute-start.7 = (bf16[2,2,160,512]{3,2,1,0:T(8,128)(2,1)S(1)}, bf16[2,2,160,512]{3,2,1,0:T(8,128)(2,1)S(1)}, u32[]{:S(2)}, u32[]{:S(2)}) collective-permute-start(bf16[2,2,160,512]{3,2,1,0:T(8,128)(2,1)S(1)} %get-tuple-element.186), channel_id=1, source_target_pairs={{0,4},{1,5},{2,6},{3,7},{4,0},{5,1},{6,2},{7,3},{8,12},{9,13},{10,... | collective-permute-start | bytes 1966088 | tf_op jit(solution)/shard_map/ppermute | solution.py:388
  62.4 2.9 %collective-permute-start.12 = (bf16[8,112,512]{2,1,0:T(8,128)(2,1)S(1)}, bf16[8,112,512]{2,1,0:T(8,128)(2,1)S(1)}, u32[]{:S(2)}, u32[]{:S(2)}) collective-permute-start(bf16[8,112,512]{2,1,0:T(8,128)(2,1)S(1)} %get-tuple-element.199.refs_2_), channel_id=1, source_target_pairs={{0,1},{1,0},{2,3},{3,2},{4,5},{5,4},{6,7},{7,6},{8,9},{9,8},{10,11... | collective-permute-start | bytes 2752520 | tf_op jit(solution)/shard_map/ppermute | solution.py:388
  62.5 10.1 %collective-permute-start.11 = (bf16[2,2,80,512]{3,2,1,0:T(8,128)(2,1)S(1)}, bf16[2,2,80,512]{3,2,1,0:T(8,128)(2,1)S(1)}, u32[]{:S(2)}, u32[]{:S(2)}) collective-permute-start(bf16[2,2,80,512]{3,2,1,0:T(8,128)(2,1)S(1)} %get-tuple-element.197), channel_id=1, source_target_pairs={{0,16},{16,0},{1,17},{17,1},{2,18},{18,2},{3,19},{19,3},{4,20},{20... | collective-permute-start | bytes 983048 | tf_op jit(solution)/shard_map/ppermute | solution.py:387
  63.2 10.6 %collective-permute-start.16 = (bf16[2,160,512]{2,1,0:T(8,128)(2,1)S(1)}, bf16[2,160,512]{2,1,0:T(8,128)(2,1)S(1)}, u32[]{:S(2)}, u32[]{:S(2)}) collective-permute-start(bf16[2,160,512]{2,1,0:T(8,128)(2,1)S(1)} %get-tuple-element.207), channel_id=1, source_target_pairs={{0,2},{1,3},{2,0},{3,1},{4,6},{5,7},{6,4},{7,5},{8,10},{9,11},{10,... | collective-permute-start | bytes 983048 | tf_op jit(solution)/shard_map/ppermute | solution.py:388
  63.7 9.2 %collective-permute-start.14 = (bf16[2,2,64,512]{3,2,1,0:T(8,128)(2,1)S(1)}, bf16[2,2,64,512]{3,2,1,0:T(8,128)(2,1)S(1)}, u32[]{:S(2)}, u32[]{:S(2)}) collective-permute-start(bf16[2,2,64,512]{3,2,1,0:T(8,128)(2,1)S(1)} %get-tuple-element.204), channel_id=1, source_target_pairs={{0,4},{1,5},{2,6},{3,7},{4,0},{5,1},{6,2},{7,3},{8,12},{9,13},{10,... | collective-permute-start | bytes 786440 | tf_op jit(solution)/shard_map/ppermute | solution.py:388
  65.5 13.9 %collective-permute-start.19 = (bf16[2,2,64,512]{3,2,1,0:T(8,128)(2,1)S(1)}, bf16[2,2,64,512]{3,2,1,0:T(8,128)(2,1)S(1)}, u32[]{:S(2)}, u32[]{:S(2)}) collective-permute-start(bf16[2,2,64,512]{3,2,1,0:T(8,128)(2,1)S(1)} %get-tuple-element.211), channel_id=1, source_target_pairs={{0,2},{1,3},{2,0},{3,1},{4,6},{5,7},{6,4},{7,5},{8,10},{9,11},{10,... | collective-permute-start | bytes 786440 | tf_op jit(solution)/shard_map/ppermute | solution.py:388
  67.2 12.3 %collective-permute-start.18 = (bf16[2,2,48,512]{3,2,1,0:T(8,128)(2,1)S(1)}, bf16[2,2,48,512]{3,2,1,0:T(8,128)(2,1)S(1)}, u32[]{:S(2)}, u32[]{:S(2)}) collective-permute-start(bf16[2,2,48,512]{3,2,1,0:T(8,128)(2,1)S(1)} %get-tuple-element.210), channel_id=1, source_target_pairs={{0,4},{1,5},{2,6},{3,7},{4,0},{5,1},{6,2},{7,3},{8,12},{9,13},{10,... | collective-permute-start | bytes 589832 | tf_op jit(solution)/shard_map/ppermute | solution.py:388
  73.9 7.9 %collective-permute-start.17 = (bf16[2,80,512]{2,1,0:T(8,128)(2,1)S(1)}, bf16[2,80,512]{2,1,0:T(8,128)(2,1)S(1)}, u32[]{:S(2)}, u32[]{:S(2)}) collective-permute-start(bf16[2,80,512]{2,1,0:T(8,128)(2,1)S(1)} %get-tuple-element.209), channel_id=1, source_target_pairs={{0,16},{16,0},{1,17},{17,1},{2,18},{18,2},{3,19},{19,3},{4,20},{20... | collective-permute-start | bytes 491528 | tf_op jit(solution)/shard_map/ppermute | solution.py:387
  75.3 6.5 %collective-permute-start.13 = (bf16[2,80,512]{2,1,0:T(8,128)(2,1)S(1)}, bf16[2,80,512]{2,1,0:T(8,128)(2,1)S(1)}, u32[]{:S(2)}, u32[]{:S(2)}) collective-permute-start(bf16[2,80,512]{2,1,0:T(8,128)(2,1)S(1)} %get-tuple-element.203), channel_id=1, source_target_pairs={{0,4},{1,5},{2,6},{3,7},{4,0},{5,1},{6,2},{7,3},{8,12},{9,13},{10,... | collective-permute-start | bytes 491528 | tf_op jit(solution)/shard_map/ppermute | solution.py:388
  76.8 5.0 %collective-permute-start.15 = (bf16[2,64,512]{2,1,0:T(8,128)(2,1)S(1)}, bf16[2,64,512]{2,1,0:T(8,128)(2,1)S(1)}, u32[]{:S(2)}, u32[]{:S(2)}) collective-permute-start(bf16[2,64,512]{2,1,0:T(8,128)(2,1)S(1)} %get-tuple-element.206), channel_id=1, source_target_pairs={{0,2},{1,3},{2,0},{3,1},{4,6},{5,7},{6,4},{7,5},{8,10},{9,11},{10,... | collective-permute-start | bytes 393224 | tf_op jit(solution)/shard_map/ppermute | solution.py:388
  81.9 13.4 %collective-permute-start.20 = (bf16[224,512]{1,0:T(8,128)(2,1)S(1)}, bf16[224,512]{1,0:T(8,128)(2,1)S(1)}, u32[]{:S(2)}, u32[]{:S(2)}) collective-permute-start(bf16[224,512]{1,0:T(8,128)(2,1)S(1)} %get-tuple-element.215), channel_id=1, source_target_pairs={{0,8},{1,9},{2,10},{3,11},{4,12},{5,13},{6,14},{7,15},{8,0},{9,1},... | collective-permute-start | bytes 688136 | tf_op jit(solution)/shard_map/ppermute | solution.py:388
  84.6 6.2 %collective-permute-start.21 = (bf16[2,64,512]{2,1,0:T(8,128)(2,1)S(1)}, bf16[2,64,512]{2,1,0:T(8,128)(2,1)S(1)}, u32[]{:S(2)}, u32[]{:S(2)}) collective-permute-start(bf16[2,64,512]{2,1,0:T(8,128)(2,1)S(1)} %get-tuple-element.216), channel_id=1, source_target_pairs={{0,4},{1,5},{2,6},{3,7},{4,0},{5,1},{6,2},{7,3},{8,12},{9,13},{10,... | collective-permute-start | bytes 393224 | tf_op jit(solution)/shard_map/ppermute | solution.py:388
  85.8 4.6 %collective-permute-start.22 = (bf16[2,48,512]{2,1,0:T(8,128)(2,1)S(1)}, bf16[2,48,512]{2,1,0:T(8,128)(2,1)S(1)}, u32[]{:S(2)}, u32[]{:S(2)}) collective-permute-start(bf16[2,48,512]{2,1,0:T(8,128)(2,1)S(1)} %get-tuple-element.217), channel_id=1, source_target_pairs={{0,2},{1,3},{2,0},{3,1},{4,6},{5,7},{6,4},{7,5},{8,10},{9,11},{10,... | collective-permute-start | bytes 294920 | tf_op jit(solution)/shard_map/ppermute | solution.py:388
  86.3 13.5 %collective-permute-start.10 = (bf16[320,512]{1,0:T(8,128)(2,1)S(1)}, bf16[320,512]{1,0:T(8,128)(2,1)S(1)}, u32[]{:S(2)}, u32[]{:S(2)}) collective-permute-start(bf16[320,512]{1,0:T(8,128)(2,1)S(1)} %get-tuple-element.193), channel_id=1, source_target_pairs={{0,16},{16,0},{1,17},{17,1},{2,18},{18,2},{3,19},{19,3},{4,20},{20... | collective-permute-start | bytes 983048 | tf_op jit(solution)/shard_map/ppermute | solution.py:387
  90.8 6.5 %collective-permute-start.24 = (bf16[112,512]{1,0:T(8,128)(2,1)S(1)}, bf16[112,512]{1,0:T(8,128)(2,1)S(1)}, u32[]{:S(2)}, u32[]{:S(2)}) collective-permute-start(bf16[112,512]{1,0:T(8,128)(2,1)S(1)} %get-tuple-element.219), channel_id=1, source_target_pairs={{0,8},{1,9},{2,10},{3,11},{4,12},{5,13},{6,14},{7,15},{8,0},{9,1},... | collective-permute-start | bytes 344072 | tf_op jit(solution)/shard_map/ppermute | solution.py:388
  95.3 8.5 %collective-permute-start.23 = (bf16[224,512]{1,0:T(8,128)(2,1)S(1)}, bf16[224,512]{1,0:T(8,128)(2,1)S(1)}, u32[]{:S(2)}, u32[]{:S(2)}) collective-permute-start(bf16[224,512]{1,0:T(8,128)(2,1)S(1)} %shard_map.313.refs_2_.refs_0_), channel_id=1, source_target_pairs={{0,16},{16,0},{1,17},{17,1},{2,18},{18,2},{3,19},{19,3},{4,20},{20... | collective-permute-start | bytes 688136 | tf_op jit(solution)/shard_map/ppermute | solution.py:387
  97.4 6.5 %collective-permute-start.25 = (bf16[112,512]{1,0:T(8,128)(2,1)S(1)}, bf16[112,512]{1,0:T(8,128)(2,1)S(1)}, u32[]{:S(2)}, u32[]{:S(2)}) collective-permute-start(bf16[112,512]{1,0:T(8,128)(2,1)S(1)} %shard_map.314.refs_2_), channel_id=1, source_target_pairs={{0,16},{16,0},{1,17},{17,1},{2,18},{18,2},{3,19},{19,3},{4,20},{20... | collective-permute-start | bytes 344072 | tf_op jit(solution)/shard_map/ppermute | solution.py:387

commit v4 on v3

--- a/solution.py
+++ b/solution.py
@@ -138,11 +138,21 @@
     return jnp.sum(v.reshape(H, rows, v.shape[1]), 0)
 
 
+def in_steps(items, stages):
+    held = {}
+    for step in range(len(items) + len(stages) - 1):
+        for k, stage_of in enumerate(stages):
+            n = step - k
+            if 0 <= n < len(items):
+                given = () if k == 0 else (held.pop((n, k - 1)),)
+                held[n, k] = stage_of(*items[n], *given)
+
+
 def forward_body(
     place, lengths, tokens, memory, recv, attn_gain, query_weight, pair_weight, write_query, out_weight,
     ffn_gain, ffn_in, ffn_out,
     x, mem, nall, qs, kall, vall, p0, p1, p2, p3, mixed, resid, n2, act, dg,
-    out_send, out_own, out, wqs,
+    out_send, out_own, out, wqs, kt, vt,
 ):
     y = place[0]
     width = pair_weight.shape[0]
@@ -169,45 +179,85 @@
     for k in range(lengths.shape[1]):
         total = total + lengths[y, k]
         bounds.append(total)
-    pos_c = lax.broadcasted_iota(jnp.int32, (1, rows), 1)
-    doc_c = sum([(pos_c >= b).astype(jnp.int32) for b in bounds])
+    pos_k = lax.broadcasted_iota(jnp.int32, (rows, 1), 0)
+    doc_k = sum([(pos_k >= b).astype(jnp.int32) for b in bounds])
     mem_bias = jnp.where(
-        lax.broadcasted_iota(jnp.int32, (128, 128), 1) < slots, 0.0, MASKED
+        lax.broadcasted_iota(jnp.int32, (128, 128), 0) < slots, 0.0, MASKED
     ).astype(F32)
-    for i, p_out in enumerate((p0, p1, p2, p3)):
-        w = 128 * (i + 2)
-        cols = w - 128
-        pos_r = lax.broadcasted_iota(jnp.int32, (128, 1), 0) + 128 * i
-        doc_r = sum([(pos_r >= b).astype(jnp.int32) for b in bounds])
-        ok = (doc_r == doc_c[:, :cols]) & (pos_c[:, :cols] <= pos_r)
-        bias = jnp.concatenate([mem_bias, jnp.where(ok, 0.0, MASKED).astype(F32)], 1)
-        for p in range(H // 2):
-            lanes = slice(128 * p, 128 * p + 128)
-            q01 = stacked_heads(qs[128 * i : 128 * i + 128, lanes])
-            s = dot(q01, kall[0:w, lanes], 1, 1)
-            s = (s.reshape(2, 128, w) + bias[None]).reshape(256, w)
-            e = jnp.exp(s - jnp.max(s, -1, keepdims=True))
-            pr = (e * (1.0 / jnp.sum(e, -1, keepdims=True))).astype(BF16)
-            p_out[p] = pr
-            o = dot(pr, vall[0:w, lanes])
-            mixed[128 * i : 128 * i + 128, lanes] = unstacked_heads(o).astype(BF16)
-    r = x[...].astype(F32) + dot(mixed[...], out_weight[...])
-    resid[...] = r
-    rhat, _ = norm_parts(r)
-    n2v = (rhat * ffn_gain[...]).astype(BF16)
-    n2[...] = n2v
+    kt[...] = kall[...].T
+    vt[...] = vall[...].T
+    biases = []
+    for i in range(4):
+        cols = 128 * (i + 1)
+        pos_q = lax.broadcasted_iota(jnp.int32, (1, 128), 1) + 128 * i
+        doc_q = sum([(pos_q >= b).astype(jnp.int32) for b in bounds])
+        ok = (doc_k[:cols] == doc_q) & (pos_k[:cols] <= pos_q)
+        bias = jnp.concatenate([mem_bias, jnp.where(ok, 0.0, MASKED).astype(F32)], 0)
+        biases.append(jnp.concatenate([bias, bias], 1))
+
+    def score(i, p):
+        w, lanes = 128 * (i + 2), slice(128 * p, 128 * p + 128)
+        q01 = stacked_heads(qs[128 * i : 128 * i + 128, lanes])
+        return dot(kall[0:w, lanes], q01, 1, 1)
+
+    def soften(i, p, s):
+        s = s + biases[i]
+        e = jnp.exp(s - jnp.max(s, 0, keepdims=True))
+        pr = (e * (1.0 / jnp.sum(e, 0, keepdims=True))).astype(BF16)
+        (p0, p1, p2, p3)[i][p] = pr
+        return pr
+
+    def mix(i, p, pr):
+        w, lanes = 128 * (i + 2), slice(128 * p, 128 * p + 128)
+        queries = slice(128 * i, 128 * i + 128)
+        o = dot(vt[lanes, 0:w], pr).astype(BF16)
+        mixed[128 * p : 128 * p + 64, queries] = o[:64, :128]
+        mixed[128 * p + 64 : 128 * p + 128, queries] = o[64:, 128:]
+
+    in_steps(
+        [(i, p) for i in range(4) for p in range(H // 2)], (score, soften, mix)
+    )
     ff = ffn_in.shape[1]
     k0 = 0.7978845608028654
-    for j in range(ff // 512):
-        cols = slice(512 * j, 512 * j + 512)
-        v = dot(n2v, ffn_in[:, cols])
+    step = 512
+    chunks = ff // step
+
+    def top(block):
+        at = slice(half * block, half * block + half)
+        r = x[at, :].astype(F32) + dot(mixed[:, at], out_weight[...], 0, 0)
+        resid[at, :] = r
+        rhat, _ = norm_parts(r)
+        n2[at, :] = (rhat * ffn_gain[...]).astype(BF16)
+
+    def inner(block, j):
+        if block == 0 and j == 1:
+            top(1)
+        return dot(n2[half * block : half * block + half, :], ffn_in[:, step * j : step * j + step])
+
+    def gelu(block, j, v):
+        at = (slice(half * block, half * block + half), slice(step * j, step * j + step))
         v2 = v * v
-        t = jnp.tanh(k0 * (v + 0.044715 * (v2 * v)))
-        h = 0.5 * (1.0 + t)
-        act[:, cols] = (v * h).astype(BF16)
-        d = h + (0.5 * v) * (1.0 - t * t) * (k0 + (3.0 * 0.044715 * k0) * v2)
-        dg[:, cols] = d.astype(BF16)
-    out[...] = (resid[...] + dot(act[...], ffn_out[...])).astype(BF16)
+        h = 0.5 * jnp.tanh(v * (k0 + (0.044715 * k0) * v2)) + 0.5
+        act[at] = (v * h).astype(BF16)
+        w = v * (2.0 * k0 + (6.0 * 0.044715 * k0) * v2)
+        dg[at] = (h + h * (1.0 - h) * w).astype(BF16)
+
+    def bottom(block):
+        at = slice(half * block, half * block + half)
+        out[at, :] = (resid[at, :] + dot(act[at, :], ffn_out[...])).astype(BF16)
+
+    top(0)
+    held = None
+    for n in range(2 * chunks + 1):
+        now = None
+        if n < 2 * chunks:
+            now = inner(n // chunks, n % chunks)
+        if held is not None:
+            gelu(*held)
+        if n == chunks + 1:
+            bottom(0)
+        held = (n // chunks, n % chunks, now)
+    bottom(1)
     out_own[...] = out[part(place, half, True), :]
     out_send[...] = out[part(place, half, False), :]
 
@@ -302,36 +352,48 @@
     d = dout[...] + d_norm
     dresid[...] = d
     d_attn = d.astype(BF16)
-    emit_rows(dot(mixed[...], d_attn, 0, 0), 32, (send, keep), 0, place[1])
+    emit_rows(dot(mixed[...], d_attn), 32, (send, keep), 0, place[1])
     dmixed[...] = dot(d_attn, out_weight[...], 1, 1).astype(BF16)
 
 
 def attn_back_body(
-    place, qs, dm, vall, p3, kall, p2, p1, p0,
-    dq_out, dk_out, dv_out, dk_ref, dv_ref,
+    place, qs, dm, vall, p3, kt, p2, p1, p0,
+    dq_out, dk_out, dv_out, dk_ref, dv_ref, dqt_ref,
 ):
-    for p in range(H // 2):
-        lanes = slice(128 * p, 128 * p + 128)
-        for i, p_in in reversed(list(enumerate((p0, p1, p2, p3)))):
-            w = 128 * (i + 2)
-            rows = slice(128 * i, 128 * i + 128)
-            q01 = stacked_heads(qs[rows, lanes])
-            dm01 = stacked_heads(dm[rows, lanes])
-            dp = dot(dm01, vall[0:w, lanes], 1, 1)
-            pb = p_in[p]
-            pf = pb.astype(F32)
-            t = pf * dp
-            ds = (t - pf * jnp.sum(t, -1, keepdims=True)).astype(BF16)
-            dq = unstacked_heads(dot(ds, kall[0:w, lanes])) * 0.125
-            dq_out[rows, lanes] = dq.astype(BF16)
-            dk = dot(ds, q01, 0, 0)
-            dv = dot(pb, dm01, 0, 0)
-            if i == 3:
-                dk_ref[0:w, lanes] = dk
-                dv_ref[0:w, lanes] = dv
-            else:
-                dk_ref[0:w, lanes] += dk
-                dv_ref[0:w, lanes] += dv
+    probs = (p0, p1, p2, p3)
+
+    def first(i, p):
+        w, lanes = 128 * (i + 2), slice(128 * p, 128 * p + 128)
+        dm01 = stacked_heads(dm[128 * i : 128 * i + 128, lanes])
+        dv = dot(probs[i][p], dm01)
+        if i == 3:
+            dv_ref[0:w, lanes] = dv
+        else:
+            dv_ref[0:w, lanes] += dv
+        return dot(vall[0:w, lanes], dm01, 1, 1)
+
+    def second(i, p, dp):
+        pf = probs[i][p].astype(F32)
+        t = pf * dp
+        return (t - pf * jnp.sum(t, 0, keepdims=True)).astype(BF16)
+
+    def third(i, p, ds):
+        w, lanes = 128 * (i + 2), slice(128 * p, 128 * p + 128)
+        rows = slice(128 * i, 128 * i + 128)
+        q01 = stacked_heads(qs[rows, lanes])
+        dqt = (dot(kt[lanes, 0:w], ds) * 0.125).astype(BF16)
+        dqt_ref[128 * p : 128 * p + 64, rows] = dqt[:64, :128]
+        dqt_ref[128 * p + 64 : 128 * p + 128, rows] = dqt[64:, 128:]
+        dk = dot(ds, q01)
+        if i == 3:
+            dk_ref[0:w, lanes] = dk
+        else:
+            dk_ref[0:w, lanes] += dk
+
+    in_steps(
+        [(i, p) for p in range(H // 2) for i in (3, 2, 1, 0)], (first, second, third)
+    )
+    dq_out[...] = dqt_ref[...].T
     dk_out[...] = dk_ref[...].astype(BF16)
     dv_out[...] = dv_ref[...].astype(BF16)
 
@@ -649,14 +711,15 @@
     gain_row = ((1, width), F32)
     (
         x, mem, nall, qs, kall, vall, p0, p1, p2, p3, mixed, resid, n2, act, dg,
-        out_send, out_own, out, wqs,
+        out_send, out_own, out, wqs, kt,
     ) = call(
         forward_body,
         [("s", lengths)] + v(tokens, memory, recv_a, ag, query_weight, pair_weight)
         + v(write_query, out_weight, fg, ffn_in, ffn_out),
         [big, small, wide, big, wide, wide]
-        + [((H // 2, 256, 128 * (i + 2)), BF16) for i in range(4)]
-        + [big, full_f, big, deep, deep, half_b, half_b, big, small],
+        + [((H // 2, 128 * (i + 2), 256), BF16) for i in range(4)]
+        + [big, full_f, big, deep, deep, half_b, half_b, big, small, ((width, padded), BF16)],
+        scratch=[((width, padded), BF16)],
         flops=2 * 6 * 10**9, nbytes=20 * 10**6, limit=16,
     )
     out_recv = exchanged(out_send, "y")
@@ -717,9 +780,9 @@
         first = moved(parts, nth(orders, 0))
     dq, dk, dv = call(
         attn_back_body,
-        v(qs, dmixed, vall, p3, kall, p2, p1, p0) + deps1,
+        v(qs, dmixed, vall, p3, kt, p2, p1, p0) + deps1,
         [big, wide, wide],
-        scratch=[((padded, width), F32)] * 2,
+        scratch=[((padded, width), F32)] * 2 + [big],
         flops=2 * 6 * 10**9, nbytes=20 * 10**6,
     )
     send2, keep2, own_tok, own_mem, swap = call(

time: 105 us -> 103 us (0.981)
  Pallas kernels: 46.7 us -> 41.2 us
  waiting for transfers between devices: 26.5 us -> 30 us
    pallas_call x25, Pallas kernels: 40.8 us -> 35.3 us  [call(): pl.pallas_call(kernel, out_shape=[shape(s, d) for s, d in outs], in_specs...]
    ppermute x17, waiting for transfers between devices: 15.9 us -> 19.4 us  [exchanged(): lax.ppermute(send, 'seg', other_of('seg', {'x': 2, 'z': 4, 'h': 8, 'c': 1...]
  transfers between devices with their start and end apart: 26 -> 26, of which waited for: 14 -> 14; matrix products, arithmetic and copies ran while one was open for 0% -> 0% of each run, Pallas kernels for 42% -> 37%
where the time goes in v4:
time: 103 us
  Pallas kernels  41.2 us (40%)
  starting transfers between devices  30.5 us (30%)
  waiting for transfers between devices  30 us (29%)
  between operations  1.05 us (1%)
    pallas_call x25, Pallas kernels, call(): pl.pallas_call(kernel, out_shape=[shape(s, d) for s, d in outs], in_specs...  35.3 us
    ppermute x17, waiting for transfers between devices, exchanged(): lax.ppermute(send, 'seg', other_of('seg', {'x': 2, 'z': 4, 'h': 8, 'c': 1...  19.4 us
    ppermute x17, starting transfers between devices, exchanged(): lax.ppermute(send, 'seg', other_of('seg', {'x': 2, 'z': 4, 'h': 8, 'c': 1...  18.5 us
    ppermute x9, starting transfers between devices, exchanged(): return lax.ppermute(send, 'seq', other_of('seq', 1))  12 us
    ppermute x9, waiting for transfers between devices, exchanged(): return lax.ppermute(send, 'seq', other_of('seq', 1))  10.7 us
    pallas_call x1, Pallas kernels, fetched_weights(): pl.pallas_call(kernel, out_shape=[pltpu.VMEM(a.shape, a.dtype) for a in w...  3.97 us
  transfers between devices with their start and end apart: 26, of which 14 were waited for; matrix products, arithmetic and copies ran while one was open for 0% of the time, Pallas kernels for 37%

profile of v4, /device:TPU:0, one launch (start us, length us, event | category | flops | bytes accessed | tf_op | source)
XLA Modules:
  0.0 102.8 jit_solution(2518414730011500530)
XLA Ops:
  0.6 1.0 shard_map.289
  1.6 3.0 %collective-permute-start = (bf16[288,512]{1,0:T(8,128)(2,1)S(1)}, bf16[288,512]{1,0:T(8,128)(2,1)S(1)}, u32[]{:S(2)}, u32[]{:S(2)}) collective-permute-start(bf16[288,512]{1,0:T(8,128)(2,1)S(1)} %shard_map.289), channel_id=1, source_target_pairs={{0,16},{16,0},{1,17},{17,1},{2,18},{18,2},{3,19},{19,3},{4,20},{20... | collective-permute-start | bytes 884744 | tf_op jit(solution)/shard_map/ppermute | solution.py:449
  4.7 1.0 shard_map.292
  5.8 4.0 %shard_map.288 = (bf16[2,256,512]{2,1,0:T(8,128)(2,1)S(1)}, bf16[2,32,512]{2,1,0:T(8,128)(2,1)S(1)}, bf16[2,256,512]{2,1,0:T(8,128)(2,1)S(1)}, bf16[2,32,512]{2,...) custom-call(bf16[2,256,512]{2,1,0:T(8,128)(2,1)} %a.2, ...), custom_call_target="tpu_custom_call" | custom-call | flops 1000000000 | bytes 10000000 | tf_op jit(solution)/shard_map/pallas_call | solution.py:599
  9.7 2.8 %collective-permute-done.refs_3_ = bf16[288,512]{1,0:T(8,128)(2,1)S(1)} collective-permute-done((bf16[288,512]{1,0:T(8,128)(2,1)S(1)}, bf16[288,512]{1,0:T(8,128)(2,1)S(1)}, u32[]{:S(2)}, u32[]{:S(2)}) %collective-permute-start) | collective-permute-done | bytes 294944 | tf_op jit(solution)/shard_map/ppermute | solution.py:449
  12.5 10.8 %shard_map.290 = (bf16[512,512]{1,0:T(8,128)(2,1)S(1)}, bf16[64,512]{1,0:T(8,128)(2,1)S(1)}, bf16[640,512]{1,0:T(8,128)(2,1)S(1)}, bf16[512,512]{1,0:T(8,128)(2,...) custom-call(s32[2,8]{1,0:T(2,128)S(1)} %copy-done.3, ...), custom_call_target="tpu_custom_call" | custom-call | flops 12000000000 | bytes 20000000 | tf_op jit(solution)/shard_map/pallas_call | solution.py:64
  23.3 2.1 %collective-permute-start.1 = (bf16[256,512]{1,0:T(8,128)(2,1)S(1)}, bf16[256,512]{1,0:T(8,128)(2,1)S(1)}, u32[]{:S(2)}, u32[]{:S(2)}) collective-permute-start(bf16[256,512]{1,0:T(8,128)(2,1)S(1)} %get-tuple-element.133), channel_id=1, source_target_pairs={{0,16},{16,0},{1,17},{17,1},{2,18},{18,2},{3,19},{19,3},{4,20},{20... | collective-permute-start | bytes 786440 | tf_op jit(solution)/shard_map/ppermute | solution.py:449
  25.5 5.0 %shard_map.293 = (bf16[8,160,512]{2,1,0:T(8,128)(2,1)S(1)}, bf16[8,160,512]{2,1,0:T(8,128)(2,1)S(1)}, bf16[512,1024]{1,0:T(8,128)(2,1)S(1)}, bf16[64,512]{1,0:T(...) custom-call(bf16[512,512]{1,0:T(8,128)(2,1)S(1)} %get-tuple-element., ...), custom_call_target="tpu_custom_call" | custom-call | flops 6000000000 | bytes 10000000 | tf_op jit(solution)/shard_map/pallas_call | solution.py:64
  30.6 3.0 %shard_map.294 = (bf16[8,128,512]{2,1,0:T(8,128)(2,1)S(1)}, bf16[8,128,512]{2,1,0:T(8,128)(2,1)S(1)}, f32[512,512]{1,0:T(8,128)S(1)}, bf16[512,2048]{1,0:T(8,128)(2,1)S(1)}) custom-call(bf16[512,1024]{1,0:T(8,128)(2,1)S(1)} %get-tuple-element.143.refs_0_, bf16[512,1024]{1,0:T(8,128)(2,1)S(1)} %get-tuple-element.140.refs_5_.refs_1_, ...), custom_call_target="tpu_custom_call" | custom-call | flops 10000000000 | bytes 20000000 | tf_op jit(solution)/shard_map/pallas_call | solution.py:64
  33.6 0.6 collective-permute-start.4
  34.1 2.4 %shard_map.295 = (bf16[8,128,512]{2,1,0:T(8,128)(2,1)S(1)}, bf16[8,128,512]{2,1,0:T(8,128)(2,1)S(1)}, f32[512,512]{1,0:T(8,128)S(1)}) custom-call(bf16[512,2048]{1,0:T(8,128)(2,1)S(1)} %get-tuple-element.147.refs_0_, bf16[512,512]{1,0:T(8,128)(2,1)S(1)} %get-tuple-element.148.refs_1_, bf16[512,2048]{1,0:T(8,128)(2,1)S(1)} %get-tuple-element.130.refs_10_.refs_2_, ...), custom_call_target="tpu_custom_call" | custom-call | flops 1000000000 | bytes 20000000 | tf_op jit(solution)/shard_map/pallas_call | solution.py:64
  36.7 1.4 %shard_map.296 = (bf16[8,32,512]{2,1,0:T(8,128)(2,1)S(1)}, bf16[8,32,512]{2,1,0:T(8,128)(2,1)S(1)}, f32[512,512]{1,0:T(8,128)S(1)}, bf16[512,512]{1,0:T(8,128)(2,1)S(1)}, f32[1,512]{1,0:T(1,128)S(1)}) custom-call(f32[512,512]{1,0:T(8,128)S(1)} %get-tuple-element.151.refs_0_, f32[512,512]{1,0:T(8,128)S(1)} %get-tuple-element.152.refs_1_, ...), custom_call_target="tpu_custom_call" | custom-call | flops 100000000 | bytes 1000000 | tf_op jit(solution)/shard_map/pallas_call | solution.py:64
  38.0 0.6 collective-permute-start.6
  38.6 1.2 %collective-permute-done.6 = bf16[8,32,512]{2,1,0:T(8,128)(2,1)S(1)} collective-permute-done((bf16[8,32,512]{2,1,0:T(8,128)(2,1)S(1)}, bf16[8,32,512]{2,1,0:T(8,128)(2,1)S(1)}, u32[]{:S(2)}, u32[]{:S(2)}) %collective-permute-start.6) | collective-permute-done | bytes 262176 | tf_op jit(solution)/shard_map/ppermute | solution.py:450
  39.7 0.8 shard_map.297
  40.6 1.6 %collective-permute-start.9 = (bf16[2,2,160,512]{3,2,1,0:T(8,128)(2,1)S(1)}, bf16[2,2,160,512]{3,2,1,0:T(8,128)(2,1)S(1)}, u32[]{:S(2)}, u32[]{:S(2)}) collective-permute-start(bf16[2,2,160,512]{3,2,1,0:T(8,128)(2,1)S(1)} %get-tuple-element.189), channel_id=1, source_target_pairs={{0,2},{1,3},{2,0},{3,1},{4,6},{5,7},{6,4},{7,5},{8,10},{9,11},{10,... | collective-permute-start | bytes 1966088 | tf_op jit(solution)/shard_map/ppermute | solution.py:450
  42.1 1.3 %collective-permute-start.8 = (bf16[2,2,2,64,512]{4,3,2,1,0:T(8,128)(2,1)S(1)}, bf16[2,2,2,64,512]{4,3,2,1,0:T(8,128)(2,1)S(1)}, u32[]{:S(2)}, u32[]{:S(2)}) collective-permute-start(bf16[2,2,2,64,512]{4,3,2,1,0:T(8,128)(2,1)S(1)} %get-tuple-element.188), channel_id=1, source_target_pairs={{0,16},{16,0},{1,17},{17,1},{2,18},{18,2},{3,19},{19,3},{4,20},{20... | collective-permute-start | bytes 1572872 | tf_op jit(solution)/shard_map/ppermute | solution.py:449
  43.4 1.6 %collective-permute-start.7 = (bf16[2,2,160,512]{3,2,1,0:T(8,128)(2,1)S(1)}, bf16[2,2,160,512]{3,2,1,0:T(8,128)(2,1)S(1)}, u32[]{:S(2)}, u32[]{:S(2)}) collective-permute-start(bf16[2,2,160,512]{3,2,1,0:T(8,128)(2,1)S(1)} %get-tuple-element.186), channel_id=1, source_target_pairs={{0,4},{1,5},{2,6},{3,7},{4,0},{5,1},{6,2},{7,3},{8,12},{9,13},{10,... | collective-permute-start | bytes 1966088 | tf_op jit(solution)/shard_map/ppermute | solution.py:450
  45.0 4.8 %shard_map.298 = (bf16[512,512]{1,0:T(8,128)(2,1)S(1)}, bf16[640,512]{1,0:T(8,128)(2,1)S(1)}, bf16[640,512]{1,0:T(8,128)(2,1)S(1)}) custom-call(bf16[512,512]{1,0:T(8,128)(2,1)S(1)} %get-tuple-element.135.refs_0_, bf16[512,512]{1,0:T(8,128)(2,1)S(1)} %get-tuple-element.156.refs_1_, bf16[640,512]{1,0:T(8,128)(2,1)S(1)} %get-tuple-element.157.refs_2_, ...), custom_call_target="tpu_custom_call" | custom-call | flops 12000000000 | bytes 20000000 | tf_op jit(solution)/shard_map/pallas_call | solution.py:64
  49.8 2.8 %shard_map.299 = (bf16[8,112,512]{2,1,0:T(8,128)(2,1)S(1)}, bf16[8,112,512]{2,1,0:T(8,128)(2,1)S(1)}, f32[256,512]{1,0:T(8,128)S(1)}, f32[32,512]{1,0:T(8,128)S(1)}, bf16[320,512]{1,0:T(8,128)(2,1)S(1)}) custom-call(bf16[640,512]{1,0:T(8,128)(2,1)S(1)} %get-tuple-element.134.refs_9_.refs_0_, bf16[512,512]{1,0:T(8,128)(2,1)S(1)} %get-tuple-element.170.refs_1_, ...), custom_call_target="tpu_custom_call" | custom-call | flops 6000000000 | bytes 20000000 | tf_op jit(solution)/shard_map/pallas_call | solution.py:64
  52.6 5.0 %collective-permute-done.9.refs_1_ = bf16[2,2,160,512]{3,2,1,0:T(8,128)(2,1)S(1)} collective-permute-done((bf16[2,2,160,512]{3,2,1,0:T(8,128)(2,1)S(1)}, bf16[2,2,160,512]{3,2,1,0:T(8,128)(2,1)S(1)}, u32[]{:S(2)}, u32[]{:S(2)}) %collective-permute-start.9) | collective-permute-done | bytes 655392 | tf_op jit(solution)/shard_map/ppermute | solution.py:450
  58.0 1.9 %collective-permute-done.7.refs_1_ = bf16[2,2,160,512]{3,2,1,0:T(8,128)(2,1)S(1)} collective-permute-done((bf16[2,2,160,512]{3,2,1,0:T(8,128)(2,1)S(1)}, bf16[2,2,160,512]{3,2,1,0:T(8,128)(2,1)S(1)}, u32[]{:S(2)}, u32[]{:S(2)}) %collective-permute-start.7) | collective-permute-done | bytes 655392 | tf_op jit(solution)/shard_map/ppermute | solution.py:450
  60.1 0.8 collective-permute-start.11
  60.9 0.5 collective-permute-start.16
  61.4 1.6 %collective-permute-start.14 = (bf16[2,2,64,512]{3,2,1,0:T(8,128)(2,1)S(1)}, bf16[2,2,64,512]{3,2,1,0:T(8,128)(2,1)S(1)}, u32[]{:S(2)}, u32[]{:S(2)}) collective-permute-start(bf16[2,2,64,512]{3,2,1,0:T(8,128)(2,1)S(1)} %get-tuple-element.204), channel_id=1, source_target_pairs={{0,4},{1,5},{2,6},{3,7},{4,0},{5,1},{6,2},{7,3},{8,12},{9,13},{10,... | collective-permute-start | bytes 786440 | tf_op jit(solution)/shard_map/ppermute | solution.py:450
  63.2 1.6 %collective-permute-start.19 = (bf16[2,2,64,512]{3,2,1,0:T(8,128)(2,1)S(1)}, bf16[2,2,64,512]{3,2,1,0:T(8,128)(2,1)S(1)}, u32[]{:S(2)}, u32[]{:S(2)}) collective-permute-start(bf16[2,2,64,512]{3,2,1,0:T(8,128)(2,1)S(1)} %get-tuple-element.211), channel_id=1, source_target_pairs={{0,2},{1,3},{2,0},{3,1},{4,6},{5,7},{6,4},{7,5},{8,10},{9,11},{10,... | collective-permute-start | bytes 786440 | tf_op jit(solution)/shard_map/ppermute | solution.py:450
  64.8 0.5 collective-permute-start.18
  65.4 4.9 %collective-permute-done.11.refs_1_ = bf16[2,2,80,512]{3,2,1,0:T(8,128)(2,1)S(1)} collective-permute-done((bf16[2,2,80,512]{3,2,1,0:T(8,128)(2,1)S(1)}, bf16[2,2,80,512]{3,2,1,0:T(8,128)(2,1)S(1)}, u32[]{:S(2)}, u32[]{:S(2)}) %collective-permute-start.11) | collective-permute-done | bytes 327712 | tf_op jit(solution)/shard_map/ppermute | solution.py:449
  70.7 0.8 collective-permute-done.16.refs_1_
  71.5 1.4 %collective-permute-start.17 = (bf16[2,80,512]{2,1,0:T(8,128)(2,1)S(1)}, bf16[2,80,512]{2,1,0:T(8,128)(2,1)S(1)}, u32[]{:S(2)}, u32[]{:S(2)}) collective-permute-start(bf16[2,80,512]{2,1,0:T(8,128)(2,1)S(1)} %get-tuple-element.209), channel_id=1, source_target_pairs={{0,16},{16,0},{1,17},{17,1},{2,18},{18,2},{3,19},{19,3},{4,20},{20... | collective-permute-start | bytes 491528 | tf_op jit(solution)/shard_map/ppermute | solution.py:449
  72.9 1.6 %collective-permute-start.13 = (bf16[2,80,512]{2,1,0:T(8,128)(2,1)S(1)}, bf16[2,80,512]{2,1,0:T(8,128)(2,1)S(1)}, u32[]{:S(2)}, u32[]{:S(2)}) collective-permute-start(bf16[2,80,512]{2,1,0:T(8,128)(2,1)S(1)} %get-tuple-element.203), channel_id=1, source_target_pairs={{0,4},{1,5},{2,6},{3,7},{4,0},{5,1},{6,2},{7,3},{8,12},{9,13},{10,... | collective-permute-start | bytes 491528 | tf_op jit(solution)/shard_map/ppermute | solution.py:450
  74.5 0.8 collective-permute-start.15
  75.2 1.9 %collective-permute-done.19.refs_1_ = bf16[2,2,64,512]{3,2,1,0:T(8,128)(2,1)S(1)} collective-permute-done((bf16[2,2,64,512]{3,2,1,0:T(8,128)(2,1)S(1)}, bf16[2,2,64,512]{3,2,1,0:T(8,128)(2,1)S(1)}, u32[]{:S(2)}, u32[]{:S(2)}) %collective-permute-start.19) | collective-permute-done | bytes 262176 | tf_op jit(solution)/shard_map/ppermute | solution.py:450
  77.2 2.2 %collective-permute-done.15.refs_3_ = bf16[2,64,512]{2,1,0:T(8,128)(2,1)S(1)} collective-permute-done((bf16[2,64,512]{2,1,0:T(8,128)(2,1)S(1)}, bf16[2,64,512]{2,1,0:T(8,128)(2,1)S(1)}, u32[]{:S(2)}, u32[]{:S(2)}) %collective-permute-start.15) | collective-permute-done | bytes 131104 | tf_op jit(solution)/shard_map/ppermute | solution.py:450
  79.5 2.7 %collective-permute-start.20 = (bf16[224,512]{1,0:T(8,128)(2,1)S(1)}, bf16[224,512]{1,0:T(8,128)(2,1)S(1)}, u32[]{:S(2)}, u32[]{:S(2)}) collective-permute-start(bf16[224,512]{1,0:T(8,128)(2,1)S(1)} %get-tuple-element.215), channel_id=1, source_target_pairs={{0,8},{1,9},{2,10},{3,11},{4,12},{5,13},{6,14},{7,15},{8,0},{9,1},... | collective-permute-start | bytes 688136 | tf_op jit(solution)/shard_map/ppermute | solution.py:450
  82.2 1.3 %collective-permute-start.21 = (bf16[2,64,512]{2,1,0:T(8,128)(2,1)S(1)}, bf16[2,64,512]{2,1,0:T(8,128)(2,1)S(1)}, u32[]{:S(2)}, u32[]{:S(2)}) collective-permute-start(bf16[2,64,512]{2,1,0:T(8,128)(2,1)S(1)} %get-tuple-element.216), channel_id=1, source_target_pairs={{0,4},{1,5},{2,6},{3,7},{4,0},{5,1},{6,2},{7,3},{8,12},{9,13},{10,... | collective-permute-start | bytes 393224 | tf_op jit(solution)/shard_map/ppermute | solution.py:450
  83.5 0.6 collective-permute-start.22
  84.0 1.3 %collective-permute-start.10 = (bf16[320,512]{1,0:T(8,128)(2,1)S(1)}, bf16[320,512]{1,0:T(8,128)(2,1)S(1)}, u32[]{:S(2)}, u32[]{:S(2)}) collective-permute-start(bf16[320,512]{1,0:T(8,128)(2,1)S(1)} %get-tuple-element.193), channel_id=1, source_target_pairs={{0,16},{16,0},{1,17},{17,1},{2,18},{18,2},{3,19},{19,3},{4,20},{20... | collective-permute-start | bytes 983048 | tf_op jit(solution)/shard_map/ppermute | solution.py:449
  85.3 2.8 %collective-permute-done.22.refs_3_ = bf16[2,48,512]{2,1,0:T(8,128)(2,1)S(1)} collective-permute-done((bf16[2,48,512]{2,1,0:T(8,128)(2,1)S(1)}, bf16[2,48,512]{2,1,0:T(8,128)(2,1)S(1)}, u32[]{:S(2)}, u32[]{:S(2)}) %collective-permute-start.22) | collective-permute-done | bytes 98336 | tf_op jit(solution)/shard_map/ppermute | solution.py:450
  88.5 3.1 %collective-permute-start.24 = (bf16[112,512]{1,0:T(8,128)(2,1)S(1)}, bf16[112,512]{1,0:T(8,128)(2,1)S(1)}, u32[]{:S(2)}, u32[]{:S(2)}) collective-permute-start(bf16[112,512]{1,0:T(8,128)(2,1)S(1)} %get-tuple-element.219), channel_id=1, source_target_pairs={{0,8},{1,9},{2,10},{3,11},{4,12},{5,13},{6,14},{7,15},{8,0},{9,1},... | collective-permute-start | bytes 344072 | tf_op jit(solution)/shard_map/ppermute | solution.py:450
  91.6 1.4 %collective-permute-done.20.refs_1_ = bf16[224,512]{1,0:T(8,128)(2,1)S(1)} collective-permute-done((bf16[224,512]{1,0:T(8,128)(2,1)S(1)}, bf16[224,512]{1,0:T(8,128)(2,1)S(1)}, u32[]{:S(2)}, u32[]{:S(2)}) %collective-permute-start.20) | collective-permute-done | bytes 229408 | tf_op jit(solution)/shard_map/ppermute | solution.py:450
  93.0 0.5 collective-permute-start.23
  93.5 1.6 %collective-permute-done.24.refs_1_ = bf16[112,512]{1,0:T(8,128)(2,1)S(1)} collective-permute-done((bf16[112,512]{1,0:T(8,128)(2,1)S(1)}, bf16[112,512]{1,0:T(8,128)(2,1)S(1)}, u32[]{:S(2)}, u32[]{:S(2)}) %collective-permute-start.24) | collective-permute-done | bytes 114720 | tf_op jit(solution)/shard_map/ppermute | solution.py:450
  95.1 1.5 %collective-permute-start.25 = (bf16[112,512]{1,0:T(8,128)(2,1)S(1)}, bf16[112,512]{1,0:T(8,128)(2,1)S(1)}, u32[]{:S(2)}, u32[]{:S(2)}) collective-permute-start(bf16[112,512]{1,0:T(8,128)(2,1)S(1)} %shard_map.314.refs_2_), channel_id=1, source_target_pairs={{0,16},{16,0},{1,17},{17,1},{2,18},{18,2},{3,19},{19,3},{4,20},{20... | collective-permute-start | bytes 344072 | tf_op jit(solution)/shard_map/ppermute | solution.py:449
  96.6 0.8 shard_map.291
  97.4 1.1 %shard_map.303 = (f32[2,256,512]{2,1,0:T(8,128)}, bf16[2,32,512]{2,1,0:T(8,128)(2,1)}, f32[2,32,512]{2,1,0:T(8,128)}) custom-call(f32[256,512]{1,0:T(8,128)S(1)} %get-tuple-element.180.refs_0_, bf16[32,512]{1,0:T(8,128)(2,1)S(1)} %get-tuple-element.181.refs_1_, f32[32,512]{1,0:T(8,128)S(1)} %get-tuple-element.182.refs_2_, ...), custom_call_target="tpu_custom_call" | custom-call | flops 1000000 | bytes 1000000 | tf_op jit(solution)/shard_map/pallas_call | solution.py:64
  98.5 3.0 %collective-permute-done.25.refs_3_ = bf16[112,512]{1,0:T(8,128)(2,1)S(1)} collective-permute-done((bf16[112,512]{1,0:T(8,128)(2,1)S(1)}, bf16[112,512]{1,0:T(8,128)(2,1)S(1)}, u32[]{:S(2)}, u32[]{:S(2)}) %collective-permute-start.25) | collective-permute-done | bytes 114720 | tf_op jit(solution)/shard_map/ppermute | solution.py:449
  101.5 1.0 %shard_map.315 = (f32[32,512]{1,0:T(8,128)}, f32[32,1024]{1,0:T(8,128)}, f32[32,512]{1,0:T(8,128)}, f32[32,2048]{1,0:T(8,128)}, f32[128,512]{1,0:T(8,128)}, /*in...) custom-call(bf16[224,512]{1,0:T(8,128)(2,1)S(1)} %shard_map.313.refs, ...), custom_call_target="tpu_custom_call" | custom-call | flops 1000000 | bytes 1000000 | tf_op jit(solution)/shard_map/pallas_call | solution.py:64
  (40 shorter events, 2.4 us)
Async XLA Ops:
  1.6 10.9 %collective-permute-start = (bf16[288,512]{1,0:T(8,128)(2,1)S(1)}, bf16[288,512]{1,0:T(8,128)(2,1)S(1)}, u32[]{:S(2)}, u32[]{:S(2)}) collective-permute-start(bf16[288,512]{1,0:T(8,128)(2,1)S(1)} %shard_map.289), channel_id=1, source_target_pairs={{0,16},{16,0},{1,17},{17,1},{2,18},{18,2},{3,19},{19,3},{4,20},{20... | collective-permute-start | bytes 884744 | tf_op jit(solution)/shard_map/ppermute | solution.py:449
  5.6 6.9 %copy-start = (f32[512]{0:T(512)S(1)}, f32[512]{0:T(512)}, u32[]{:S(2)}) copy-start(f32[512]{0:T(512)} %param.24) | copy-start | bytes 6148
  5.7 6.9 %copy-start.2 = (f32[512]{0:T(512)S(1)}, f32[512]{0:T(512)}, u32[]{:S(2)}) copy-start(f32[512]{0:T(512)} %param.20) | copy-start | bytes 6148
  5.7 6.8 %copy-start.3 = (s32[2,8]{1,0:T(2,128)S(1)}, s32[2,8]{1,0:T(2,128)}, u32[]{:S(2)}) copy-start(s32[2,8]{1,0:T(2,128)} %refs_0_.3) | copy-start | bytes 196
  5.7 19.8 %collective-permute-start.2 = (bf16[288,512]{1,0:T(8,128)(2,1)S(1)}, bf16[288,512]{1,0:T(8,128)(2,1)S(1)}, u32[]{:S(2)}, u32[]{:S(2)}) collective-permute-start(bf16[288,512]{1,0:T(8,128)(2,1)S(1)} %shard_map.292), channel_id=1, source_target_pairs={{0,16},{16,0},{1,17},{17,1},{2,18},{18,2},{3,19},{19,3},{4,20},{20... | collective-permute-start | bytes 884744 | tf_op jit(solution)/shard_map/ppermute | solution.py:449
  12.5 13.0 %copy-start.1 = (f32[512]{0:T(512)S(1)}, f32[512]{0:T(512)}, u32[]{:S(2)}) copy-start(f32[512]{0:T(512)} %param.31) | copy-start | bytes 6148
  23.3 7.1 %collective-permute-start.1 = (bf16[256,512]{1,0:T(8,128)(2,1)S(1)}, bf16[256,512]{1,0:T(8,128)(2,1)S(1)}, u32[]{:S(2)}, u32[]{:S(2)}) collective-permute-start(bf16[256,512]{1,0:T(8,128)(2,1)S(1)} %get-tuple-element.133), channel_id=1, source_target_pairs={{0,16},{16,0},{1,17},{17,1},{2,18},{18,2},{3,19},{19,3},{4,20},{20... | collective-permute-start | bytes 786440 | tf_op jit(solution)/shard_map/ppermute | solution.py:449
  30.5 3.6 %collective-permute-start.3 = (bf16[8,160,512]{2,1,0:T(8,128)(2,1)S(1)}, bf16[8,160,512]{2,1,0:T(8,128)(2,1)S(1)}, u32[]{:S(2)}, u32[]{:S(2)}) collective-permute-start(bf16[8,160,512]{2,1,0:T(8,128)(2,1)S(1)} %get-tuple-element.150), channel_id=1, source_target_pairs={{0,1},{1,0},{2,3},{3,2},{4,5},{5,4},{6,7},{7,6},{8,9},{9,8},{10,11... | collective-permute-start | bytes 3932168 | tf_op jit(solution)/shard_map/ppermute | solution.py:450
  33.6 3.1 %collective-permute-start.4 = (bf16[8,128,512]{2,1,0:T(8,128)(2,1)S(1)}, bf16[8,128,512]{2,1,0:T(8,128)(2,1)S(1)}, u32[]{:S(2)}, u32[]{:S(2)}) collective-permute-start(bf16[8,128,512]{2,1,0:T(8,128)(2,1)S(1)} %get-tuple-element.155), channel_id=1, source_target_pairs={{0,1},{1,0},{2,3},{3,2},{4,5},{5,4},{6,7},{7,6},{8,9},{9,8},{10,11... | collective-permute-start | bytes 3145736 | tf_op jit(solution)/shard_map/ppermute | solution.py:450
  36.6 3.2 %collective-permute-start.5 = (bf16[8,128,512]{2,1,0:T(8,128)(2,1)S(1)}, bf16[8,128,512]{2,1,0:T(8,128)(2,1)S(1)}, u32[]{:S(2)}, u32[]{:S(2)}) collective-permute-start(bf16[8,128,512]{2,1,0:T(8,128)(2,1)S(1)} %get-tuple-element.165), channel_id=1, source_target_pairs={{0,1},{1,0},{2,3},{3,2},{4,5},{5,4},{6,7},{7,6},{8,9},{9,8},{10,11... | collective-permute-start | bytes 3145736 | tf_op jit(solution)/shard_map/ppermute | solution.py:450
  38.0 1.7 %collective-permute-start.6 = (bf16[8,32,512]{2,1,0:T(8,128)(2,1)S(1)}, bf16[8,32,512]{2,1,0:T(8,128)(2,1)S(1)}, u32[]{:S(2)}, u32[]{:S(2)}) collective-permute-start(bf16[8,32,512]{2,1,0:T(8,128)(2,1)S(1)} %get-tuple-element.168), channel_id=1, source_target_pairs={{0,1},{1,0},{2,3},{3,2},{4,5},{5,4},{6,7},{7,6},{8,9},{9,8},{10,11... | collective-permute-start | bytes 786440 | tf_op jit(solution)/shard_map/ppermute | solution.py:450
  40.6 17.1 %collective-permute-start.9 = (bf16[2,2,160,512]{3,2,1,0:T(8,128)(2,1)S(1)}, bf16[2,2,160,512]{3,2,1,0:T(8,128)(2,1)S(1)}, u32[]{:S(2)}, u32[]{:S(2)}) collective-permute-start(bf16[2,2,160,512]{3,2,1,0:T(8,128)(2,1)S(1)} %get-tuple-element.189), channel_id=1, source_target_pairs={{0,2},{1,3},{2,0},{3,1},{4,6},{5,7},{6,4},{7,5},{8,10},{9,11},{10,... | collective-permute-start | bytes 1966088 | tf_op jit(solution)/shard_map/ppermute | solution.py:450
  42.1 15.7 %collective-permute-start.8 = (bf16[2,2,2,64,512]{4,3,2,1,0:T(8,128)(2,1)S(1)}, bf16[2,2,2,64,512]{4,3,2,1,0:T(8,128)(2,1)S(1)}, u32[]{:S(2)}, u32[]{:S(2)}) collective-permute-start(bf16[2,2,2,64,512]{4,3,2,1,0:T(8,128)(2,1)S(1)} %get-tuple-element.188), channel_id=1, source_target_pairs={{0,16},{16,0},{1,17},{17,1},{2,18},{18,2},{3,19},{19,3},{4,20},{20... | collective-permute-start | bytes 1572872 | tf_op jit(solution)/shard_map/ppermute | solution.py:449
  43.4 16.4 %collective-permute-start.7 = (bf16[2,2,160,512]{3,2,1,0:T(8,128)(2,1)S(1)}, bf16[2,2,160,512]{3,2,1,0:T(8,128)(2,1)S(1)}, u32[]{:S(2)}, u32[]{:S(2)}) collective-permute-start(bf16[2,2,160,512]{3,2,1,0:T(8,128)(2,1)S(1)} %get-tuple-element.186), channel_id=1, source_target_pairs={{0,4},{1,5},{2,6},{3,7},{4,0},{5,1},{6,2},{7,3},{8,12},{9,13},{10,... | collective-permute-start | bytes 1966088 | tf_op jit(solution)/shard_map/ppermute | solution.py:450
  60.0 3.0 %collective-permute-start.12 = (bf16[8,112,512]{2,1,0:T(8,128)(2,1)S(1)}, bf16[8,112,512]{2,1,0:T(8,128)(2,1)S(1)}, u32[]{:S(2)}, u32[]{:S(2)}) collective-permute-start(bf16[8,112,512]{2,1,0:T(8,128)(2,1)S(1)} %get-tuple-element.199.refs_2_), channel_id=1, source_target_pairs={{0,1},{1,0},{2,3},{3,2},{4,5},{5,4},{6,7},{7,6},{8,9},{9,8},{10,11... | collective-permute-start | bytes 2752520 | tf_op jit(solution)/shard_map/ppermute | solution.py:450
  60.1 10.1 %collective-permute-start.11 = (bf16[2,2,80,512]{3,2,1,0:T(8,128)(2,1)S(1)}, bf16[2,2,80,512]{3,2,1,0:T(8,128)(2,1)S(1)}, u32[]{:S(2)}, u32[]{:S(2)}) collective-permute-start(bf16[2,2,80,512]{3,2,1,0:T(8,128)(2,1)S(1)} %get-tuple-element.197), channel_id=1, source_target_pairs={{0,16},{16,0},{1,17},{17,1},{2,18},{18,2},{3,19},{19,3},{4,20},{20... | collective-permute-start | bytes 983048 | tf_op jit(solution)/shard_map/ppermute | solution.py:449
  60.9 10.6 %collective-permute-start.16 = (bf16[2,160,512]{2,1,0:T(8,128)(2,1)S(1)}, bf16[2,160,512]{2,1,0:T(8,128)(2,1)S(1)}, u32[]{:S(2)}, u32[]{:S(2)}) collective-permute-start(bf16[2,160,512]{2,1,0:T(8,128)(2,1)S(1)} %get-tuple-element.207), channel_id=1, source_target_pairs={{0,2},{1,3},{2,0},{3,1},{4,6},{5,7},{6,4},{7,5},{8,10},{9,11},{10,... | collective-permute-start | bytes 983048 | tf_op jit(solution)/shard_map/ppermute | solution.py:450
  61.4 9.2 %collective-permute-start.14 = (bf16[2,2,64,512]{3,2,1,0:T(8,128)(2,1)S(1)}, bf16[2,2,64,512]{3,2,1,0:T(8,128)(2,1)S(1)}, u32[]{:S(2)}, u32[]{:S(2)}) collective-permute-start(bf16[2,2,64,512]{3,2,1,0:T(8,128)(2,1)S(1)} %get-tuple-element.204), channel_id=1, source_target_pairs={{0,4},{1,5},{2,6},{3,7},{4,0},{5,1},{6,2},{7,3},{8,12},{9,13},{10,... | collective-permute-start | bytes 786440 | tf_op jit(solution)/shard_map/ppermute | solution.py:450
  63.2 13.9 %collective-permute-start.19 = (bf16[2,2,64,512]{3,2,1,0:T(8,128)(2,1)S(1)}, bf16[2,2,64,512]{3,2,1,0:T(8,128)(2,1)S(1)}, u32[]{:S(2)}, u32[]{:S(2)}) collective-permute-start(bf16[2,2,64,512]{3,2,1,0:T(8,128)(2,1)S(1)} %get-tuple-element.211), channel_id=1, source_target_pairs={{0,2},{1,3},{2,0},{3,1},{4,6},{5,7},{6,4},{7,5},{8,10},{9,11},{10,... | collective-permute-start | bytes 786440 | tf_op jit(solution)/shard_map/ppermute | solution.py:450
  64.8 12.3 %collective-permute-start.18 = (bf16[2,2,48,512]{3,2,1,0:T(8,128)(2,1)S(1)}, bf16[2,2,48,512]{3,2,1,0:T(8,128)(2,1)S(1)}, u32[]{:S(2)}, u32[]{:S(2)}) collective-permute-start(bf16[2,2,48,512]{3,2,1,0:T(8,128)(2,1)S(1)} %get-tuple-element.210), channel_id=1, source_target_pairs={{0,4},{1,5},{2,6},{3,7},{4,0},{5,1},{6,2},{7,3},{8,12},{9,13},{10,... | collective-permute-start | bytes 589832 | tf_op jit(solution)/shard_map/ppermute | solution.py:450
  71.5 7.9 %collective-permute-start.17 = (bf16[2,80,512]{2,1,0:T(8,128)(2,1)S(1)}, bf16[2,80,512]{2,1,0:T(8,128)(2,1)S(1)}, u32[]{:S(2)}, u32[]{:S(2)}) collective-permute-start(bf16[2,80,512]{2,1,0:T(8,128)(2,1)S(1)} %get-tuple-element.209), channel_id=1, source_target_pairs={{0,16},{16,0},{1,17},{17,1},{2,18},{18,2},{3,19},{19,3},{4,20},{20... | collective-permute-start | bytes 491528 | tf_op jit(solution)/shard_map/ppermute | solution.py:449
  72.9 6.5 %collective-permute-start.13 = (bf16[2,80,512]{2,1,0:T(8,128)(2,1)S(1)}, bf16[2,80,512]{2,1,0:T(8,128)(2,1)S(1)}, u32[]{:S(2)}, u32[]{:S(2)}) collective-permute-start(bf16[2,80,512]{2,1,0:T(8,128)(2,1)S(1)} %get-tuple-element.203), channel_id=1, source_target_pairs={{0,4},{1,5},{2,6},{3,7},{4,0},{5,1},{6,2},{7,3},{8,12},{9,13},{10,... | collective-permute-start | bytes 491528 | tf_op jit(solution)/shard_map/ppermute | solution.py:450
  74.5 5.0 %collective-permute-start.15 = (bf16[2,64,512]{2,1,0:T(8,128)(2,1)S(1)}, bf16[2,64,512]{2,1,0:T(8,128)(2,1)S(1)}, u32[]{:S(2)}, u32[]{:S(2)}) collective-permute-start(bf16[2,64,512]{2,1,0:T(8,128)(2,1)S(1)} %get-tuple-element.206), channel_id=1, source_target_pairs={{0,2},{1,3},{2,0},{3,1},{4,6},{5,7},{6,4},{7,5},{8,10},{9,11},{10,... | collective-permute-start | bytes 393224 | tf_op jit(solution)/shard_map/ppermute | solution.py:450
  79.5 13.4 %collective-permute-start.20 = (bf16[224,512]{1,0:T(8,128)(2,1)S(1)}, bf16[224,512]{1,0:T(8,128)(2,1)S(1)}, u32[]{:S(2)}, u32[]{:S(2)}) collective-permute-start(bf16[224,512]{1,0:T(8,128)(2,1)S(1)} %get-tuple-element.215), channel_id=1, source_target_pairs={{0,8},{1,9},{2,10},{3,11},{4,12},{5,13},{6,14},{7,15},{8,0},{9,1},... | collective-permute-start | bytes 688136 | tf_op jit(solution)/shard_map/ppermute | solution.py:450
  82.2 6.3 %collective-permute-start.21 = (bf16[2,64,512]{2,1,0:T(8,128)(2,1)S(1)}, bf16[2,64,512]{2,1,0:T(8,128)(2,1)S(1)}, u32[]{:S(2)}, u32[]{:S(2)}) collective-permute-start(bf16[2,64,512]{2,1,0:T(8,128)(2,1)S(1)} %get-tuple-element.216), channel_id=1, source_target_pairs={{0,4},{1,5},{2,6},{3,7},{4,0},{5,1},{6,2},{7,3},{8,12},{9,13},{10,... | collective-permute-start | bytes 393224 | tf_op jit(solution)/shard_map/ppermute | solution.py:450
  83.5 4.6 %collective-permute-start.22 = (bf16[2,48,512]{2,1,0:T(8,128)(2,1)S(1)}, bf16[2,48,512]{2,1,0:T(8,128)(2,1)S(1)}, u32[]{:S(2)}, u32[]{:S(2)}) collective-permute-start(bf16[2,48,512]{2,1,0:T(8,128)(2,1)S(1)} %get-tuple-element.217), channel_id=1, source_target_pairs={{0,2},{1,3},{2,0},{3,1},{4,6},{5,7},{6,4},{7,5},{8,10},{9,11},{10,... | collective-permute-start | bytes 294920 | tf_op jit(solution)/shard_map/ppermute | solution.py:450
  84.0 13.4 %collective-permute-start.10 = (bf16[320,512]{1,0:T(8,128)(2,1)S(1)}, bf16[320,512]{1,0:T(8,128)(2,1)S(1)}, u32[]{:S(2)}, u32[]{:S(2)}) collective-permute-start(bf16[320,512]{1,0:T(8,128)(2,1)S(1)} %get-tuple-element.193), channel_id=1, source_target_pairs={{0,16},{16,0},{1,17},{17,1},{2,18},{18,2},{3,19},{19,3},{4,20},{20... | collective-permute-start | bytes 983048 | tf_op jit(solution)/shard_map/ppermute | solution.py:449
  88.5 6.5 %collective-permute-start.24 = (bf16[112,512]{1,0:T(8,128)(2,1)S(1)}, bf16[112,512]{1,0:T(8,128)(2,1)S(1)}, u32[]{:S(2)}, u32[]{:S(2)}) collective-permute-start(bf16[112,512]{1,0:T(8,128)(2,1)S(1)} %get-tuple-element.219), channel_id=1, source_target_pairs={{0,8},{1,9},{2,10},{3,11},{4,12},{5,13},{6,14},{7,15},{8,0},{9,1},... | collective-permute-start | bytes 344072 | tf_op jit(solution)/shard_map/ppermute | solution.py:450
  93.0 8.5 %collective-permute-start.23 = (bf16[224,512]{1,0:T(8,128)(2,1)S(1)}, bf16[224,512]{1,0:T(8,128)(2,1)S(1)}, u32[]{:S(2)}, u32[]{:S(2)}) collective-permute-start(bf16[224,512]{1,0:T(8,128)(2,1)S(1)} %shard_map.313.refs_2_.refs_0_), channel_id=1, source_target_pairs={{0,16},{16,0},{1,17},{17,1},{2,18},{18,2},{3,19},{19,3},{4,20},{20... | collective-permute-start | bytes 688136 | tf_op jit(solution)/shard_map/ppermute | solution.py:449
  95.1 6.5 %collective-permute-start.25 = (bf16[112,512]{1,0:T(8,128)(2,1)S(1)}, bf16[112,512]{1,0:T(8,128)(2,1)S(1)}, u32[]{:S(2)}, u32[]{:S(2)}) collective-permute-start(bf16[112,512]{1,0:T(8,128)(2,1)S(1)} %shard_map.314.refs_2_), channel_id=1, source_target_pairs={{0,16},{16,0},{1,17},{17,1},{2,18},{18,2},{3,19},{19,3},{4,20},{20... | collective-permute-start | bytes 344072 | tf_op jit(solution)/shard_map/ppermute | solution.py:449

commit v5 on v4

--- a/solution.py
+++ b/solution.py
@@ -401,17 +401,17 @@
 def input_back_body(
     place, nall, dq, dk, dv, pair_weight, query_weight, dwquery, write_query, x, mem, attn_gain,
     dresid, dblend, gain2, gain3, newmem,
-    send, keep, own_tok, own_mem, swap, gtok, gmem,
+    qsend, qkeep, ksend, kkeep, vsend, vkeep, gsend, gkeep, own_tok, own_mem, swap, gtok, gmem,
 ):
-    c, ks = place[1], (send, keep)
+    c = place[1]
     rows, width = x.shape
     slots = mem.shape[0]
     half, mhalf = rows // 2, slots // 2
     na = nall[...]
     dqv = dq[...]
-    emit_rows(dot(na[128:], dqv, 0, 0), 32, ks, 0, c)
-    emit_rows(dot(na, dk[...], 0, 0), 32, ks, 32, c)
-    emit_rows(dot(na, dv[...], 0, 0), 32, ks, 64, c)
+    emit_rows(dot(na[128:], dqv, 0, 0), 32, (qsend, qkeep), 0, c)
+    emit_rows(dot(na, dk[...], 0, 0), 32, (ksend, kkeep), 0, c)
+    emit_rows(dot(na, dv[...], 0, 0), 32, (vsend, vkeep), 0, c)
     d_all = dot(dk[...], pair_weight[:, :width], 1, 1)
     d_all = d_all + dot(dv[...], pair_weight[:, width:], 1, 1)
     d_nx = d_all[128:] + dot(dqv, query_weight[...], 1, 1)
@@ -424,8 +424,8 @@
     gains = jnp.concatenate(
         [g_x + g_m, gain2[...], gain3[...], jnp.zeros((13, width), F32)], 0
     ).astype(BF16)
-    for one in ks:
-        one[:, 96:112, :] = jnp.broadcast_to(gains, (GROUPS // 2, 16, width))
+    for one in (gsend, gkeep):
+        one[...] = jnp.broadcast_to(gains, (GROUPS // 2, 16, width))
     gtok[...] = dresid[...] + d_x
     gmem[...] = dblend[...] + d_m
     own_tok[...] = gtok[part(place, half, True), :]
@@ -536,6 +536,49 @@
     return total
 
 
+class Late:
+    def __init__(self, pairs, order):
+        flat = lambda a: a.reshape(-1, a.shape[2])
+        self.arrays = [(flat(keep), flat(recv), [keep.shape[1]]) for keep, recv in pairs]
+        self.order, self.dims = order, "hzx"
+
+    def joined(self, other):
+        self.arrays = self.arrays + other.arrays
+        return self
+
+    def next(self, deps=()):
+        label = self.order[3 - len(self.dims)]
+        at = self.dims.index(label)
+        count = 1 << at
+        plan, target = [], 0
+        for array, (_, _, pieces) in enumerate(self.arrays):
+            source = 0
+            for rows in pieces:
+                size = rows << (len(self.dims) - 1 - at)
+                for b in range(count):
+                    plan.append((array, source + 2 * b * size, target + b * size, size))
+                source += 2 * count * size
+                target += count * size
+
+        def body(place, *refs):
+            bit = place[BIT[label]]
+            for out, b in ((refs[-1], 1 - bit), (refs[-2], bit)):
+                for array, start, to, size in plan:
+                    rows = pl.ds(pl.multiple_of(start + b * size, 16), size)
+                    out[to : to + size, :] = (
+                        refs[2 * array][rows, :].astype(F32)
+                        + refs[2 * array + 1][rows, :].astype(F32)
+                    ).astype(BF16)
+
+        ins = [("v", a) for keep, recv, _ in self.arrays for a in (keep, recv)]
+        ins += [("d", d) for d in deps]
+        width = self.arrays[0][0].shape[1]
+        keep, send = call(body, ins, [((target, width), BF16)] * 2, flops=10**6, nbytes=10**6)
+        pieces = sum([p for _, _, p in self.arrays], [])
+        self.arrays = [(keep, exchanged(send, label), pieces)]
+        self.dims = self.dims.replace(label, "")
+
+
 def in_hbm(a):
     return pltpu.with_memory_space_constraint(a, pltpu.HBM)
 
@@ -631,22 +674,24 @@
 
 
 def final_parts(one, two, ff):
-    t1, o1, split = one
+    ours, theirs, split = one
     t2, o2 = two
-    width = t1.shape[-1]
+    width = t2.shape[-1]
     r = width // GROUPS
     n = ff // 512
+    count = len(ours)
     shapes = [
         (r, width), (r, 2 * width), (r, width), (r, ff), (ff // GROUPS, width),
         (r, width), (r, 2 * width), (r, width), (r, width), (r,), (r,), (r,),
     ]
 
-    def body(place, t1, o1, t2, o2, gq, gp, go, gfi, gfo, gwq, gwp, gwo, gwg, g0, g1, g2, full):
+    def body(place, *refs):
+        t2, o2, gq, gp, go, gfi, gfo, gwq, gwp, gwo, gwg, g0, g1, g2, full = refs[2 * count :]
         y = place[0]
         at = start = 0
         for rows in split:
             half = rows // 2
-            for ref, index in ((t1, y), (o1, 1 - y)):
+            for ref, index in ((refs[0], y), (refs[1], 1 - y)):
                 full[pl.ds(pl.multiple_of(start + index * half, 16), half), :] = ref[
                     at : at + half, :
                 ].astype(F32)
@@ -671,7 +716,7 @@
         go[...] = full[(5 + n) * r + ff // GROUPS :, :]
 
     return call(
-        body, [("v", a) for a in (t1, o1, t2, o2)], [(s, F32) for s in shapes],
+        body, [("v", a) for a in (*ours, *theirs, t2, o2)], [(s, F32) for s in shapes],
         scratch=[((sum(split), width), F32)], flops=10**6, nbytes=10**6, home=False,
     )
 
@@ -785,14 +830,14 @@
         scratch=[((padded, width), F32)] * 2 + [big],
         flops=2 * 6 * 10**9, nbytes=20 * 10**6,
     )
-    send2, keep2, own_tok, own_mem, swap = call(
+    *grads2, own_tok, own_mem, swap = call(
         input_back_body,
         v(
             nall, dq, dk, dv, pair_weight, query_weight, dwquery, write_query, x, mem, ag, dresid,
             dblend, gain2, gain3, newmem,
         ),
         [
-            *keep_send(112), ((half, width), F32), ((mhalf, width), F32),
+            *keep_send(32), *keep_send(32), *keep_send(32), *keep_send(16), ((half, width), F32), ((mhalf, width), F32),
             ((half + 2 * mhalf, width), BF16),
         ],
         scratch=[((rows, width), F32), ((slots, width), F32)],
@@ -801,41 +846,42 @@
     r = width // groups
     (out_both,) = assembled([out_own], out_recv, [BF16])
     if small_mesh:
-        chain = [send2]
-
-        def each(streams, labels):
+        def each(streams, labels, deps=()):
             results = []
             for stream, label in zip(streams, labels):
-                ((keep, send, dims, n),) = stage([stream], [label], deps=chain[-1:])
-                results.append((keep, send, dims, n))
-                chain.append(keep)
+                results += stage([stream], [label], deps=list(deps))
             return moved(results, labels)
 
-        second = each(first, nth(orders, 1))
-        send2, swap, _ = lax.optimization_barrier((send2, swap, chain[-1]))
-        k2, r2 = pair(keep2, send2)
-        late = [Stream(k2, r2, "hzx", 0, 64), Stream(k2, r2, "hzx", 64, 48)]
-        late = each(late, nth(late_orders, 0))
+        second = each(first, nth(orders, 1), [swap])
+        pieces = [(grads2[k + 1], exchanged(grads2[k], "c")) for k in range(0, 8, 2)]
+        by_x, by_z = Late(pieces[:2], "xzh"), Late(pieces[2:], "zxh")
+        by_x.next()
+        by_z.next()
         third = each(second, nth(orders, 2))
-        late = late_second = each(late, nth(late_orders, 1))
-        late = [chain[-1:]]
-        keep, send = stage(third, "hhh", joined=True, deps=[late[0][0]])
-        recv = exchanged(send, "h")
-        late_keep, late_send = stage(late_second, "hh", joined=True, deps=[keep])
-        late_recv = exchanged(late_send, "h")
-        t1 = added(keep, recv, deps=[late_keep])
-        o1 = exchanged(t1, "y")
-        t2 = added(late_keep, late_recv, deps=[t1])
+        behind = [stream.keep for stream in third]
+        by_x.next(behind)
+        by_z.next(behind)
+        keep, send = stage(third, "hhh", joined=True)
+        by_x.joined(by_z).next([keep])
+        t1 = added(keep, exchanged(send, "h"))
+        one, two = [t1], [exchanged(t1, "y")]
+        t2 = added(*by_x.arrays[0][:2])
         o2 = exchanged(t2, "y")
         gq, gp, go, gfi, gfo, gwq, gwp, gwo, gwg, *gains = final_parts(
-            (t1, o1, (160, 128, 160)), (t2, o2), ff
+            (one, two, (160, 128, 160)), (t2, o2), ff
         )
     else:
         w = width // GROUPS
         w0 = reduced_any(keep0, send0, [(w, False)] * 5)
         gfo = reduced_any(keep1, send1, [(ff // GROUPS, False)])
         w1 = reduced_any(keep4, send4, [(w, False)] * (ff // 512))
-        w2 = reduced_any(keep2, send2, [(w, False)] * 3 + [(16, True)])
+        w2 = jnp.concatenate(
+            [
+                reduced_any(grads2[k + 1], grads2[k], [(w, False)] if k < 6 else [(16, True)])
+                for k in range(0, 8, 2)
+            ],
+            0,
+        )
         go = reduced_any(keep3, send3, [(w, False)])
         cut = lambda a, at, n: jnp.concatenate(
             [a[(at + i) * r : (at + i + 1) * r] for i in range(n)], 1

time: 103 us -> 99.4 us (0.965)
  waiting for transfers between devices: 30 us -> 21.8 us
  starting transfers between devices: 30.5 us -> 35.2 us
    ppermute x9, waiting for transfers between devices: 10.7 us -> 5.71 us  [exchanged(): return lax.ppermute(send, 'seq', other_of('seq', 1))]
    ppermute x17 -> x20, starting transfers between devices: 18.5 us -> 22.2 us  [exchanged(): lax.ppermute(send, 'seg', other_of('seg', {'x': 2, 'z': 4, 'h': 8, 'c': 1...]
    ppermute x17 -> x20, waiting for transfers between devices: 19.4 us -> 16.1 us  [exchanged(): lax.ppermute(send, 'seg', other_of('seg', {'x': 2, 'z': 4, 'h': 8, 'c': 1...]
  transfers between devices with their start and end apart: 26 -> 29, of which waited for: 14 -> 10; matrix products, arithmetic and copies ran while one was open for 0% -> 0% of each run, Pallas kernels for 37% -> 39%
where the time goes in v5:
time: 99.4 us; the launch traced here: 99.2 us
  Pallas kernels  41.2 us (41%)
  starting transfers between devices  35.2 us (35%)
  waiting for transfers between devices  21.8 us (22%)
  between operations  1.05 us (1%)
    pallas_call x25, Pallas kernels, call(): pl.pallas_call(kernel, out_shape=[shape(s, d) for s, d in outs], in_specs...  35.3 us
    ppermute x20, starting transfers between devices, exchanged(): lax.ppermute(send, 'seg', other_of('seg', {'x': 2, 'z': 4, 'h': 8, 'c': 1...  22.2 us
    ppermute x20, waiting for transfers between devices, exchanged(): lax.ppermute(send, 'seg', other_of('seg', {'x': 2, 'z': 4, 'h': 8, 'c': 1...  16.1 us
    ppermute x9, starting transfers between devices, exchanged(): return lax.ppermute(send, 'seq', other_of('seq', 1))  13 us
    ppermute x9, waiting for transfers between devices, exchanged(): return lax.ppermute(send, 'seq', other_of('seq', 1))  5.71 us
    pallas_call x1, Pallas kernels, fetched_weights(): pl.pallas_call(kernel, out_shape=[pltpu.VMEM(a.shape, a.dtype) for a in w...  3.97 us
  transfers between devices with their start and end apart: 29, of which 10 were waited for; matrix products, arithmetic and copies ran while one was open for 0% of the time, Pallas kernels for 39%

profile of v5, /device:TPU:0, one launch (start us, length us, event | category | flops | bytes accessed | tf_op | source)
XLA Modules:
  0.0 99.2 jit_solution(14372318218824806421)
XLA Ops:
  0.6 1.0 shard_map.289
  1.6 3.0 %collective-permute-start = (bf16[288,512]{1,0:T(8,128)(2,1)S(1)}, bf16[288,512]{1,0:T(8,128)(2,1)S(1)}, u32[]{:S(2)}, u32[]{:S(2)}) collective-permute-start(bf16[288,512]{1,0:T(8,128)(2,1)S(1)} %shard_map.289), channel_id=1, source_target_pairs={{0,16},{16,0},{1,17},{17,1},{2,18},{18,2},{3,19},{19,3},{4,20},{20... | collective-permute-start | bytes 884744 | tf_op jit(solution)/shard_map/ppermute | solution.py:449
  4.7 1.0 shard_map.292
  5.8 4.0 %shard_map.288 = (bf16[2,256,512]{2,1,0:T(8,128)(2,1)S(1)}, bf16[2,32,512]{2,1,0:T(8,128)(2,1)S(1)}, bf16[2,256,512]{2,1,0:T(8,128)(2,1)S(1)}, bf16[2,32,512]{2,...) custom-call(bf16[2,256,512]{2,1,0:T(8,128)(2,1)} %a.2, ...), custom_call_target="tpu_custom_call" | custom-call | flops 1000000000 | bytes 10000000 | tf_op jit(solution)/shard_map/pallas_call | solution.py:642
  9.7 2.8 %collective-permute-done.refs_3_ = bf16[288,512]{1,0:T(8,128)(2,1)S(1)} collective-permute-done((bf16[288,512]{1,0:T(8,128)(2,1)S(1)}, bf16[288,512]{1,0:T(8,128)(2,1)S(1)}, u32[]{:S(2)}, u32[]{:S(2)}) %collective-permute-start) | collective-permute-done | bytes 294944 | tf_op jit(solution)/shard_map/ppermute | solution.py:449
  12.5 10.8 %shard_map.290 = (bf16[512,512]{1,0:T(8,128)(2,1)S(1)}, bf16[64,512]{1,0:T(8,128)(2,1)S(1)}, bf16[640,512]{1,0:T(8,128)(2,1)S(1)}, bf16[512,512]{1,0:T(8,128)(2,...) custom-call(s32[2,8]{1,0:T(2,128)S(1)} %copy-done.3, ...), custom_call_target="tpu_custom_call" | custom-call | flops 12000000000 | bytes 20000000 | tf_op jit(solution)/shard_map/pallas_call | solution.py:64
  23.3 2.1 %collective-permute-start.1 = (bf16[256,512]{1,0:T(8,128)(2,1)S(1)}, bf16[256,512]{1,0:T(8,128)(2,1)S(1)}, u32[]{:S(2)}, u32[]{:S(2)}) collective-permute-start(bf16[256,512]{1,0:T(8,128)(2,1)S(1)} %get-tuple-element.137), channel_id=1, source_target_pairs={{0,16},{16,0},{1,17},{17,1},{2,18},{18,2},{3,19},{19,3},{4,20},{20... | collective-permute-start | bytes 786440 | tf_op jit(solution)/shard_map/ppermute | solution.py:449
  25.5 5.0 %shard_map.293 = (bf16[8,160,512]{2,1,0:T(8,128)(2,1)S(1)}, bf16[8,160,512]{2,1,0:T(8,128)(2,1)S(1)}, bf16[512,1024]{1,0:T(8,128)(2,1)S(1)}, bf16[64,512]{1,0:T(...) custom-call(bf16[512,512]{1,0:T(8,128)(2,1)S(1)} %get-tuple-element., ...), custom_call_target="tpu_custom_call" | custom-call | flops 6000000000 | bytes 10000000 | tf_op jit(solution)/shard_map/pallas_call | solution.py:64
  30.6 3.0 %shard_map.294 = (bf16[8,128,512]{2,1,0:T(8,128)(2,1)S(1)}, bf16[8,128,512]{2,1,0:T(8,128)(2,1)S(1)}, f32[512,512]{1,0:T(8,128)S(1)}, bf16[512,2048]{1,0:T(8,128)(2,1)S(1)}) custom-call(bf16[512,1024]{1,0:T(8,128)(2,1)S(1)} %get-tuple-element.147.refs_0_, bf16[512,1024]{1,0:T(8,128)(2,1)S(1)} %get-tuple-element.144.refs_5_.refs_1_, ...), custom_call_target="tpu_custom_call" | custom-call | flops 10000000000 | bytes 20000000 | tf_op jit(solution)/shard_map/pallas_call | solution.py:64
  33.6 0.6 collective-permute-start.4
  34.1 2.4 %shard_map.295 = (bf16[8,128,512]{2,1,0:T(8,128)(2,1)S(1)}, bf16[8,128,512]{2,1,0:T(8,128)(2,1)S(1)}, f32[512,512]{1,0:T(8,128)S(1)}) custom-call(bf16[512,2048]{1,0:T(8,128)(2,1)S(1)} %get-tuple-element.151.refs_0_, bf16[512,512]{1,0:T(8,128)(2,1)S(1)} %get-tuple-element.152.refs_1_, bf16[512,2048]{1,0:T(8,128)(2,1)S(1)} %get-tuple-element.134.refs_10_.refs_2_, ...), custom_call_target="tpu_custom_call" | custom-call | flops 1000000000 | bytes 20000000 | tf_op jit(solution)/shard_map/pallas_call | solution.py:64
  36.7 1.4 %shard_map.296 = (bf16[8,32,512]{2,1,0:T(8,128)(2,1)S(1)}, bf16[8,32,512]{2,1,0:T(8,128)(2,1)S(1)}, f32[512,512]{1,0:T(8,128)S(1)}, bf16[512,512]{1,0:T(8,128)(2,1)S(1)}, f32[1,512]{1,0:T(1,128)S(1)}) custom-call(f32[512,512]{1,0:T(8,128)S(1)} %get-tuple-element.155.refs_0_, f32[512,512]{1,0:T(8,128)S(1)} %get-tuple-element.156.refs_1_, ...), custom_call_target="tpu_custom_call" | custom-call | flops 100000000 | bytes 1000000 | tf_op jit(solution)/shard_map/pallas_call | solution.py:64
  38.0 0.6 collective-permute-start.6
  38.6 1.2 %collective-permute-done.6 = bf16[8,32,512]{2,1,0:T(8,128)(2,1)S(1)} collective-permute-done((bf16[8,32,512]{2,1,0:T(8,128)(2,1)S(1)}, bf16[8,32,512]{2,1,0:T(8,128)(2,1)S(1)}, u32[]{:S(2)}, u32[]{:S(2)}) %collective-permute-start.6) | collective-permute-done | bytes 262176 | tf_op jit(solution)/shard_map/ppermute | solution.py:450
  39.7 0.8 shard_map.297
  40.6 1.6 %collective-permute-start.14 = (bf16[2,2,160,512]{3,2,1,0:T(8,128)(2,1)S(1)}, bf16[2,2,160,512]{3,2,1,0:T(8,128)(2,1)S(1)}, u32[]{:S(2)}, u32[]{:S(2)}) collective-permute-start(bf16[2,2,160,512]{3,2,1,0:T(8,128)(2,1)S(1)} %get-tuple-element.203), channel_id=1, source_target_pairs={{0,4},{1,5},{2,6},{3,7},{4,0},{5,1},{6,2},{7,3},{8,12},{9,13},{10,... | collective-permute-start | bytes 1966088 | tf_op jit(solution)/shard_map/ppermute | solution.py:450
  42.2 1.3 %collective-permute-start.11 = (bf16[2,2,2,64,512]{4,3,2,1,0:T(8,128)(2,1)S(1)}, bf16[2,2,2,64,512]{4,3,2,1,0:T(8,128)(2,1)S(1)}, u32[]{:S(2)}, u32[]{:S(2)}) collective-permute-start(bf16[2,2,2,64,512]{4,3,2,1,0:T(8,128)(2,1)S(1)} %get-tuple-element.197), channel_id=1, source_target_pairs={{0,16},{16,0},{1,17},{17,1},{2,18},{18,2},{3,19},{19,3},{4,20},{20... | collective-permute-start | bytes 1572872 | tf_op jit(solution)/shard_map/ppermute | solution.py:449
  43.5 1.5 %collective-permute-start.8 = (bf16[2,2,160,512]{3,2,1,0:T(8,128)(2,1)S(1)}, bf16[2,2,160,512]{3,2,1,0:T(8,128)(2,1)S(1)}, u32[]{:S(2)}, u32[]{:S(2)}) collective-permute-start(bf16[2,2,160,512]{3,2,1,0:T(8,128)(2,1)S(1)} %get-tuple-element.191), channel_id=1, source_target_pairs={{0,2},{1,3},{2,0},{3,1},{4,6},{5,7},{6,4},{7,5},{8,10},{9,11},{10,... | collective-permute-start | bytes 1966088 | tf_op jit(solution)/shard_map/ppermute | solution.py:450
  45.0 4.8 %shard_map.298 = (bf16[512,512]{1,0:T(8,128)(2,1)S(1)}, bf16[640,512]{1,0:T(8,128)(2,1)S(1)}, bf16[640,512]{1,0:T(8,128)(2,1)S(1)}) custom-call(bf16[512,512]{1,0:T(8,128)(2,1)S(1)} %get-tuple-element.139.refs_0_, bf16[512,512]{1,0:T(8,128)(2,1)S(1)} %get-tuple-element.160.refs_1_, bf16[640,512]{1,0:T(8,128)(2,1)S(1)} %get-tuple-element.161.refs_2_, ...), custom_call_target="tpu_custom_call" | custom-call | flops 12000000000 | bytes 20000000 | tf_op jit(solution)/shard_map/pallas_call | solution.py:64
  49.8 2.9 %shard_map.299 = (bf16[8,32,512]{2,1,0:T(8,128)(2,1)S(1)}, bf16[8,32,512]{2,1,0:T(8,128)(2,1)S(1)}, bf16[8,32,512]{2,1,0:T(8,128)(2,1)S(1)}, bf16[8,32,512]{2,1,...) custom-call(bf16[640,512]{1,0:T(8,128)(2,1)S(1)} %get-tuple-element., ...), custom_call_target="tpu_custom_call" | custom-call | flops 6000000000 | bytes 20000000 | tf_op jit(solution)/shard_map/pallas_call | solution.py:64
  52.7 0.5 collective-permute-start.20
  53.2 4.4 %collective-permute-done.14.refs_1_ = bf16[2,2,160,512]{3,2,1,0:T(8,128)(2,1)S(1)} collective-permute-done((bf16[2,2,160,512]{3,2,1,0:T(8,128)(2,1)S(1)}, bf16[2,2,160,512]{3,2,1,0:T(8,128)(2,1)S(1)}, u32[]{:S(2)}, u32[]{:S(2)}) %collective-permute-start.14) | collective-permute-done | bytes 655392 | tf_op jit(solution)/shard_map/ppermute | solution.py:450
  57.8 1.6 %collective-permute-start.15 = (bf16[2,160,512]{2,1,0:T(8,128)(2,1)S(1)}, bf16[2,160,512]{2,1,0:T(8,128)(2,1)S(1)}, u32[]{:S(2)}, u32[]{:S(2)}) collective-permute-start(bf16[2,160,512]{2,1,0:T(8,128)(2,1)S(1)} %get-tuple-element.205), channel_id=1, source_target_pairs={{0,2},{1,3},{2,0},{3,1},{4,6},{5,7},{6,4},{7,5},{8,10},{9,11},{10,... | collective-permute-start | bytes 983048 | tf_op jit(solution)/shard_map/ppermute | solution.py:450
  59.4 0.6 collective-permute-done.8.refs_1_
  59.9 0.2 shard_map.301
  60.1 0.8 collective-permute-start.9
  61.0 1.6 %collective-permute-start.12 = (bf16[2,2,64,512]{3,2,1,0:T(8,128)(2,1)S(1)}, bf16[2,2,64,512]{3,2,1,0:T(8,128)(2,1)S(1)}, u32[]{:S(2)}, u32[]{:S(2)}) collective-permute-start(bf16[2,2,64,512]{3,2,1,0:T(8,128)(2,1)S(1)} %get-tuple-element.199), channel_id=1, source_target_pairs={{0,4},{1,5},{2,6},{3,7},{4,0},{5,1},{6,2},{7,3},{8,12},{9,13},{10,... | collective-permute-start | bytes 786440 | tf_op jit(solution)/shard_map/ppermute | solution.py:450
  62.6 0.5 collective-permute-start.24
  63.3 3.8 %collective-permute-done.15.refs_1_ = bf16[2,160,512]{2,1,0:T(8,128)(2,1)S(1)} collective-permute-done((bf16[2,160,512]{2,1,0:T(8,128)(2,1)S(1)}, bf16[2,160,512]{2,1,0:T(8,128)(2,1)S(1)}, u32[]{:S(2)}, u32[]{:S(2)}) %collective-permute-start.15) | collective-permute-done | bytes 327712 | tf_op jit(solution)/shard_map/ppermute | solution.py:450
  67.0 1.5 %collective-permute-start.21 = (bf16[256,512]{1,0:T(8,128)(2,1)S(1)}, bf16[256,512]{1,0:T(8,128)(2,1)S(1)}, u32[]{:S(2)}, u32[]{:S(2)}) collective-permute-start(bf16[256,512]{1,0:T(8,128)(2,1)S(1)} %get-tuple-element.215), channel_id=1, source_target_pairs={{0,2},{1,3},{2,0},{3,1},{4,6},{5,7},{6,4},{7,5},{8,10},{9,11},{10,... | collective-permute-start | bytes 786440 | tf_op jit(solution)/shard_map/ppermute | solution.py:450
  68.7 1.3 %collective-permute-start.16 = (bf16[2,80,512]{2,1,0:T(8,128)(2,1)S(1)}, bf16[2,80,512]{2,1,0:T(8,128)(2,1)S(1)}, u32[]{:S(2)}, u32[]{:S(2)}) collective-permute-start(bf16[2,80,512]{2,1,0:T(8,128)(2,1)S(1)} %get-tuple-element.207), channel_id=1, source_target_pairs={{0,16},{16,0},{1,17},{17,1},{2,18},{18,2},{3,19},{19,3},{4,20},{20... | collective-permute-start | bytes 491528 | tf_op jit(solution)/shard_map/ppermute | solution.py:449
  70.1 1.6 %collective-permute-start.10 = (bf16[2,80,512]{2,1,0:T(8,128)(2,1)S(1)}, bf16[2,80,512]{2,1,0:T(8,128)(2,1)S(1)}, u32[]{:S(2)}, u32[]{:S(2)}) collective-permute-start(bf16[2,80,512]{2,1,0:T(8,128)(2,1)S(1)} %get-tuple-element.195), channel_id=1, source_target_pairs={{0,4},{1,5},{2,6},{3,7},{4,0},{5,1},{6,2},{7,3},{8,12},{9,13},{10,... | collective-permute-start | bytes 491528 | tf_op jit(solution)/shard_map/ppermute | solution.py:450
  71.8 0.6 collective-permute-start.13
  72.5 0.9 collective-permute-start.25
  73.4 3.4 %collective-permute-done.13.refs_3_ = bf16[2,64,512]{2,1,0:T(8,128)(2,1)S(1)} collective-permute-done((bf16[2,64,512]{2,1,0:T(8,128)(2,1)S(1)}, bf16[2,64,512]{2,1,0:T(8,128)(2,1)S(1)}, u32[]{:S(2)}, u32[]{:S(2)}) %collective-permute-start.13) | collective-permute-done | bytes 131104 | tf_op jit(solution)/shard_map/ppermute | solution.py:450
  76.9 2.7 %collective-permute-start.17 = (bf16[224,512]{1,0:T(8,128)(2,1)S(1)}, bf16[224,512]{1,0:T(8,128)(2,1)S(1)}, u32[]{:S(2)}, u32[]{:S(2)}) collective-permute-start(bf16[224,512]{1,0:T(8,128)(2,1)S(1)} %get-tuple-element.209), channel_id=1, source_target_pairs={{0,8},{1,9},{2,10},{3,11},{4,12},{5,13},{6,14},{7,15},{8,0},{9,1},... | collective-permute-start | bytes 688136 | tf_op jit(solution)/shard_map/ppermute | solution.py:450
  79.7 1.5 %collective-permute-start.22 = (bf16[128,512]{1,0:T(8,128)(2,1)S(1)}, bf16[128,512]{1,0:T(8,128)(2,1)S(1)}, u32[]{:S(2)}, u32[]{:S(2)}) collective-permute-start(bf16[128,512]{1,0:T(8,128)(2,1)S(1)} %get-tuple-element.217), channel_id=1, source_target_pairs={{0,4},{1,5},{2,6},{3,7},{4,0},{5,1},{6,2},{7,3},{8,12},{9,13},{10,... | collective-permute-start | bytes 393224 | tf_op jit(solution)/shard_map/ppermute | solution.py:450
  81.3 1.5 %collective-permute-start.26 = (bf16[96,512]{1,0:T(8,128)(2,1)S(1)}, bf16[96,512]{1,0:T(8,128)(2,1)S(1)}, u32[]{:S(2)}, u32[]{:S(2)}) collective-permute-start(bf16[96,512]{1,0:T(8,128)(2,1)S(1)} %get-tuple-element.225), channel_id=1, source_target_pairs={{0,2},{1,3},{2,0},{3,1},{4,6},{5,7},{6,4},{7,5},{8,10},{9,11},{10,... | collective-permute-start | bytes 294920 | tf_op jit(solution)/shard_map/ppermute | solution.py:450
  82.8 1.3 %collective-permute-start.7 = (bf16[320,512]{1,0:T(8,128)(2,1)S(1)}, bf16[320,512]{1,0:T(8,128)(2,1)S(1)}, u32[]{:S(2)}, u32[]{:S(2)}) collective-permute-start(bf16[320,512]{1,0:T(8,128)(2,1)S(1)} %get-tuple-element.187.refs_2_), channel_id=1, source_target_pairs={{0,16},{16,0},{1,17},{17,1},{2,18},{18,2},{3,19},{19,3},{4,20},{20... | collective-permute-start | bytes 983048 | tf_op jit(solution)/shard_map/ppermute | solution.py:449
  84.1 1.9 %collective-permute-done.26.refs_3_ = bf16[96,512]{1,0:T(8,128)(2,1)S(1)} collective-permute-done((bf16[96,512]{1,0:T(8,128)(2,1)S(1)}, bf16[96,512]{1,0:T(8,128)(2,1)S(1)}, u32[]{:S(2)}, u32[]{:S(2)}) %collective-permute-start.26) | collective-permute-done | bytes 98336 | tf_op jit(solution)/shard_map/ppermute | solution.py:450
  86.0 3.1 %collective-permute-start.27 = (bf16[112,512]{1,0:T(8,128)(2,1)S(1)}, bf16[112,512]{1,0:T(8,128)(2,1)S(1)}, u32[]{:S(2)}, u32[]{:S(2)}) collective-permute-start(bf16[112,512]{1,0:T(8,128)(2,1)S(1)} %get-tuple-element.227), channel_id=1, source_target_pairs={{0,8},{1,9},{2,10},{3,11},{4,12},{5,13},{6,14},{7,15},{8,0},{9,1},... | collective-permute-start | bytes 344072 | tf_op jit(solution)/shard_map/ppermute | solution.py:450
  89.2 2.3 %collective-permute-start.18 = (bf16[224,512]{1,0:T(8,128)(2,1)S(1)}, bf16[224,512]{1,0:T(8,128)(2,1)S(1)}, u32[]{:S(2)}, u32[]{:S(2)}) collective-permute-start(bf16[224,512]{1,0:T(8,128)(2,1)S(1)} %shard_map.308.refs_0_), channel_id=1, source_target_pairs={{0,16},{16,0},{1,17},{17,1},{2,18},{18,2},{3,19},{19,3},{4,20},{20... | collective-permute-start | bytes 688136 | tf_op jit(solution)/shard_map/ppermute | solution.py:449
  91.5 0.9 collective-permute-done.27.refs_1_
  92.5 0.7 collective-permute-start.28
  93.2 0.8 shard_map.291
  94.0 1.1 %shard_map.300 = (f32[2,256,512]{2,1,0:T(8,128)}, bf16[2,32,512]{2,1,0:T(8,128)(2,1)}, f32[2,32,512]{2,1,0:T(8,128)}) custom-call(f32[256,512]{1,0:T(8,128)S(1)} %get-tuple-element.184.refs_0_, bf16[32,512]{1,0:T(8,128)(2,1)S(1)} %get-tuple-element.185.refs_1_, f32[32,512]{1,0:T(8,128)S(1)} %get-tuple-element.186.refs_2_, ...), custom_call_target="tpu_custom_call" | custom-call | flops 1000000 | bytes 1000000 | tf_op jit(solution)/shard_map/pallas_call | solution.py:64
  95.1 2.8 %collective-permute-done.28.refs_3_ = bf16[112,512]{1,0:T(8,128)(2,1)S(1)} collective-permute-done((bf16[112,512]{1,0:T(8,128)(2,1)S(1)}, bf16[112,512]{1,0:T(8,128)(2,1)S(1)}, u32[]{:S(2)}, u32[]{:S(2)}) %collective-permute-start.28) | collective-permute-done | bytes 114720 | tf_op jit(solution)/shard_map/ppermute | solution.py:449
  98.0 1.0 %shard_map.315 = (f32[32,512]{1,0:T(8,128)}, f32[32,1024]{1,0:T(8,128)}, f32[32,512]{1,0:T(8,128)}, f32[32,2048]{1,0:T(8,128)}, f32[128,512]{1,0:T(8,128)}, /*in...) custom-call(bf16[224,512]{1,0:T(8,128)(2,1)S(1)} %shard_map.308.refs, ...), custom_call_target="tpu_custom_call" | custom-call | flops 1000000 | bytes 1000000 | tf_op jit(solution)/shard_map/pallas_call | solution.py:64
  (46 shorter events, 1.6 us)
Async XLA Ops:
  1.6 10.9 %collective-permute-start = (bf16[288,512]{1,0:T(8,128)(2,1)S(1)}, bf16[288,512]{1,0:T(8,128)(2,1)S(1)}, u32[]{:S(2)}, u32[]{:S(2)}) collective-permute-start(bf16[288,512]{1,0:T(8,128)(2,1)S(1)} %shard_map.289), channel_id=1, source_target_pairs={{0,16},{16,0},{1,17},{17,1},{2,18},{18,2},{3,19},{19,3},{4,20},{20... | collective-permute-start | bytes 884744 | tf_op jit(solution)/shard_map/ppermute | solution.py:449
  5.6 6.9 %copy-start = (f32[512]{0:T(512)S(1)}, f32[512]{0:T(512)}, u32[]{:S(2)}) copy-start(f32[512]{0:T(512)} %param.24) | copy-start | bytes 6148
  5.7 6.9 %copy-start.2 = (f32[512]{0:T(512)S(1)}, f32[512]{0:T(512)}, u32[]{:S(2)}) copy-start(f32[512]{0:T(512)} %param.20) | copy-start | bytes 6148
  5.7 6.8 %copy-start.3 = (s32[2,8]{1,0:T(2,128)S(1)}, s32[2,8]{1,0:T(2,128)}, u32[]{:S(2)}) copy-start(s32[2,8]{1,0:T(2,128)} %refs_0_.3) | copy-start | bytes 196
  5.7 19.8 %collective-permute-start.2 = (bf16[288,512]{1,0:T(8,128)(2,1)S(1)}, bf16[288,512]{1,0:T(8,128)(2,1)S(1)}, u32[]{:S(2)}, u32[]{:S(2)}) collective-permute-start(bf16[288,512]{1,0:T(8,128)(2,1)S(1)} %shard_map.292), channel_id=1, source_target_pairs={{0,16},{16,0},{1,17},{17,1},{2,18},{18,2},{3,19},{19,3},{4,20},{20... | collective-permute-start | bytes 884744 | tf_op jit(solution)/shard_map/ppermute | solution.py:449
  12.5 13.0 %copy-start.1 = (f32[512]{0:T(512)S(1)}, f32[512]{0:T(512)}, u32[]{:S(2)}) copy-start(f32[512]{0:T(512)} %param.31) | copy-start | bytes 6148
  23.3 7.1 %collective-permute-start.1 = (bf16[256,512]{1,0:T(8,128)(2,1)S(1)}, bf16[256,512]{1,0:T(8,128)(2,1)S(1)}, u32[]{:S(2)}, u32[]{:S(2)}) collective-permute-start(bf16[256,512]{1,0:T(8,128)(2,1)S(1)} %get-tuple-element.137), channel_id=1, source_target_pairs={{0,16},{16,0},{1,17},{17,1},{2,18},{18,2},{3,19},{19,3},{4,20},{20... | collective-permute-start | bytes 786440 | tf_op jit(solution)/shard_map/ppermute | solution.py:449
  30.5 3.6 %collective-permute-start.3 = (bf16[8,160,512]{2,1,0:T(8,128)(2,1)S(1)}, bf16[8,160,512]{2,1,0:T(8,128)(2,1)S(1)}, u32[]{:S(2)}, u32[]{:S(2)}) collective-permute-start(bf16[8,160,512]{2,1,0:T(8,128)(2,1)S(1)} %get-tuple-element.154), channel_id=1, source_target_pairs={{0,1},{1,0},{2,3},{3,2},{4,5},{5,4},{6,7},{7,6},{8,9},{9,8},{10,11... | collective-permute-start | bytes 3932168 | tf_op jit(solution)/shard_map/ppermute | solution.py:450
  33.6 3.1 %collective-permute-start.4 = (bf16[8,128,512]{2,1,0:T(8,128)(2,1)S(1)}, bf16[8,128,512]{2,1,0:T(8,128)(2,1)S(1)}, u32[]{:S(2)}, u32[]{:S(2)}) collective-permute-start(bf16[8,128,512]{2,1,0:T(8,128)(2,1)S(1)} %get-tuple-element.159), channel_id=1, source_target_pairs={{0,1},{1,0},{2,3},{3,2},{4,5},{5,4},{6,7},{7,6},{8,9},{9,8},{10,11... | collective-permute-start | bytes 3145736 | tf_op jit(solution)/shard_map/ppermute | solution.py:450
  36.6 3.2 %collective-permute-start.5 = (bf16[8,128,512]{2,1,0:T(8,128)(2,1)S(1)}, bf16[8,128,512]{2,1,0:T(8,128)(2,1)S(1)}, u32[]{:S(2)}, u32[]{:S(2)}) collective-permute-start(bf16[8,128,512]{2,1,0:T(8,128)(2,1)S(1)} %get-tuple-element.169), channel_id=1, source_target_pairs={{0,1},{1,0},{2,3},{3,2},{4,5},{5,4},{6,7},{7,6},{8,9},{9,8},{10,11... | collective-permute-start | bytes 3145736 | tf_op jit(solution)/shard_map/ppermute | solution.py:450
  38.0 1.7 %collective-permute-start.6 = (bf16[8,32,512]{2,1,0:T(8,128)(2,1)S(1)}, bf16[8,32,512]{2,1,0:T(8,128)(2,1)S(1)}, u32[]{:S(2)}, u32[]{:S(2)}) collective-permute-start(bf16[8,32,512]{2,1,0:T(8,128)(2,1)S(1)} %get-tuple-element.172), channel_id=1, source_target_pairs={{0,1},{1,0},{2,3},{3,2},{4,5},{5,4},{6,7},{7,6},{8,9},{9,8},{10,11... | collective-permute-start | bytes 786440 | tf_op jit(solution)/shard_map/ppermute | solution.py:450
  40.6 17.1 %collective-permute-start.14 = (bf16[2,2,160,512]{3,2,1,0:T(8,128)(2,1)S(1)}, bf16[2,2,160,512]{3,2,1,0:T(8,128)(2,1)S(1)}, u32[]{:S(2)}, u32[]{:S(2)}) collective-permute-start(bf16[2,2,160,512]{3,2,1,0:T(8,128)(2,1)S(1)} %get-tuple-element.203), channel_id=1, source_target_pairs={{0,4},{1,5},{2,6},{3,7},{4,0},{5,1},{6,2},{7,3},{8,12},{9,13},{10,... | collective-permute-start | bytes 1966088 | tf_op jit(solution)/shard_map/ppermute | solution.py:450
  42.2 18.7 %collective-permute-start.11 = (bf16[2,2,2,64,512]{4,3,2,1,0:T(8,128)(2,1)S(1)}, bf16[2,2,2,64,512]{4,3,2,1,0:T(8,128)(2,1)S(1)}, u32[]{:S(2)}, u32[]{:S(2)}) collective-permute-start(bf16[2,2,2,64,512]{4,3,2,1,0:T(8,128)(2,1)S(1)} %get-tuple-element.197), channel_id=1, source_target_pairs={{0,16},{16,0},{1,17},{17,1},{2,18},{18,2},{3,19},{19,3},{4,20},{20... | collective-permute-start | bytes 1572872 | tf_op jit(solution)/shard_map/ppermute | solution.py:449
  43.5 16.4 %collective-permute-start.8 = (bf16[2,2,160,512]{3,2,1,0:T(8,128)(2,1)S(1)}, bf16[2,2,160,512]{3,2,1,0:T(8,128)(2,1)S(1)}, u32[]{:S(2)}, u32[]{:S(2)}) collective-permute-start(bf16[2,2,160,512]{3,2,1,0:T(8,128)(2,1)S(1)} %get-tuple-element.191), channel_id=1, source_target_pairs={{0,2},{1,3},{2,0},{3,1},{4,6},{5,7},{6,4},{7,5},{8,10},{9,11},{10,... | collective-permute-start | bytes 1966088 | tf_op jit(solution)/shard_map/ppermute | solution.py:450
  52.6 10.0 %collective-permute-start.19 = (bf16[8,32,512]{2,1,0:T(8,128)(2,1)S(1)}, bf16[8,32,512]{2,1,0:T(8,128)(2,1)S(1)}, u32[]{:S(2)}, u32[]{:S(2)}) collective-permute-start(bf16[8,32,512]{2,1,0:T(8,128)(2,1)S(1)} %get-tuple-element.211), channel_id=1, source_target_pairs={{0,1},{1,0},{2,3},{3,2},{4,5},{5,4},{6,7},{7,6},{8,9},{9,8},{10,11... | collective-permute-start | bytes 786440 | tf_op jit(solution)/shard_map/ppermute | solution.py:450
  52.7 9.9 %collective-permute-start.20 = (bf16[8,32,512]{2,1,0:T(8,128)(2,1)S(1)}, bf16[8,32,512]{2,1,0:T(8,128)(2,1)S(1)}, u32[]{:S(2)}, u32[]{:S(2)}) collective-permute-start(bf16[8,32,512]{2,1,0:T(8,128)(2,1)S(1)} %get-tuple-element.213), channel_id=1, source_target_pairs={{0,1},{1,0},{2,3},{3,2},{4,5},{5,4},{6,7},{7,6},{8,9},{9,8},{10,11... | collective-permute-start | bytes 786440 | tf_op jit(solution)/shard_map/ppermute | solution.py:450
  57.8 9.2 %collective-permute-start.15 = (bf16[2,160,512]{2,1,0:T(8,128)(2,1)S(1)}, bf16[2,160,512]{2,1,0:T(8,128)(2,1)S(1)}, u32[]{:S(2)}, u32[]{:S(2)}) collective-permute-start(bf16[2,160,512]{2,1,0:T(8,128)(2,1)S(1)} %get-tuple-element.205), channel_id=1, source_target_pairs={{0,2},{1,3},{2,0},{3,1},{4,6},{5,7},{6,4},{7,5},{8,10},{9,11},{10,... | collective-permute-start | bytes 983048 | tf_op jit(solution)/shard_map/ppermute | solution.py:450
  60.1 8.6 %collective-permute-start.9 = (bf16[2,2,80,512]{3,2,1,0:T(8,128)(2,1)S(1)}, bf16[2,2,80,512]{3,2,1,0:T(8,128)(2,1)S(1)}, u32[]{:S(2)}, u32[]{:S(2)}) collective-permute-start(bf16[2,2,80,512]{3,2,1,0:T(8,128)(2,1)S(1)} %get-tuple-element.193), channel_id=1, source_target_pairs={{0,16},{16,0},{1,17},{17,1},{2,18},{18,2},{3,19},{19,3},{4,20},{20... | collective-permute-start | bytes 983048 | tf_op jit(solution)/shard_map/ppermute | solution.py:449
  61.0 9.0 %collective-permute-start.12 = (bf16[2,2,64,512]{3,2,1,0:T(8,128)(2,1)S(1)}, bf16[2,2,64,512]{3,2,1,0:T(8,128)(2,1)S(1)}, u32[]{:S(2)}, u32[]{:S(2)}) collective-permute-start(bf16[2,2,64,512]{3,2,1,0:T(8,128)(2,1)S(1)} %get-tuple-element.199), channel_id=1, source_target_pairs={{0,4},{1,5},{2,6},{3,7},{4,0},{5,1},{6,2},{7,3},{8,12},{9,13},{10,... | collective-permute-start | bytes 786440 | tf_op jit(solution)/shard_map/ppermute | solution.py:450
  62.6 9.7 %collective-permute-start.23 = (bf16[8,32,512]{2,1,0:T(8,128)(2,1)S(1)}, bf16[8,32,512]{2,1,0:T(8,128)(2,1)S(1)}, u32[]{:S(2)}, u32[]{:S(2)}) collective-permute-start(bf16[8,32,512]{2,1,0:T(8,128)(2,1)S(1)} %get-tuple-element.219), channel_id=1, source_target_pairs={{0,1},{1,0},{2,3},{3,2},{4,5},{5,4},{6,7},{7,6},{8,9},{9,8},{10,11... | collective-permute-start | bytes 786440 | tf_op jit(solution)/shard_map/ppermute | solution.py:450
  62.6 9.1 %collective-permute-start.24 = (bf16[8,16,512]{2,1,0:T(8,128)(2,1)S(1)}, bf16[8,16,512]{2,1,0:T(8,128)(2,1)S(1)}, u32[]{:S(2)}, u32[]{:S(2)}) collective-permute-start(bf16[8,16,512]{2,1,0:T(8,128)(2,1)S(1)} %get-tuple-element.221), channel_id=1, source_target_pairs={{0,1},{1,0},{2,3},{3,2},{4,5},{5,4},{6,7},{7,6},{8,9},{9,8},{10,11... | collective-permute-start | bytes 393224 | tf_op jit(solution)/shard_map/ppermute | solution.py:450
  67.0 12.5 %collective-permute-start.21 = (bf16[256,512]{1,0:T(8,128)(2,1)S(1)}, bf16[256,512]{1,0:T(8,128)(2,1)S(1)}, u32[]{:S(2)}, u32[]{:S(2)}) collective-permute-start(bf16[256,512]{1,0:T(8,128)(2,1)S(1)} %get-tuple-element.215), channel_id=1, source_target_pairs={{0,2},{1,3},{2,0},{3,1},{4,6},{5,7},{6,4},{7,5},{8,10},{9,11},{10,... | collective-permute-start | bytes 786440 | tf_op jit(solution)/shard_map/ppermute | solution.py:450
  68.7 8.1 %collective-permute-start.16 = (bf16[2,80,512]{2,1,0:T(8,128)(2,1)S(1)}, bf16[2,80,512]{2,1,0:T(8,128)(2,1)S(1)}, u32[]{:S(2)}, u32[]{:S(2)}) collective-permute-start(bf16[2,80,512]{2,1,0:T(8,128)(2,1)S(1)} %get-tuple-element.207), channel_id=1, source_target_pairs={{0,16},{16,0},{1,17},{17,1},{2,18},{18,2},{3,19},{19,3},{4,20},{20... | collective-permute-start | bytes 491528 | tf_op jit(solution)/shard_map/ppermute | solution.py:449
  70.1 6.7 %collective-permute-start.10 = (bf16[2,80,512]{2,1,0:T(8,128)(2,1)S(1)}, bf16[2,80,512]{2,1,0:T(8,128)(2,1)S(1)}, u32[]{:S(2)}, u32[]{:S(2)}) collective-permute-start(bf16[2,80,512]{2,1,0:T(8,128)(2,1)S(1)} %get-tuple-element.195), channel_id=1, source_target_pairs={{0,4},{1,5},{2,6},{3,7},{4,0},{5,1},{6,2},{7,3},{8,12},{9,13},{10,... | collective-permute-start | bytes 491528 | tf_op jit(solution)/shard_map/ppermute | solution.py:450
  71.8 5.0 %collective-permute-start.13 = (bf16[2,64,512]{2,1,0:T(8,128)(2,1)S(1)}, bf16[2,64,512]{2,1,0:T(8,128)(2,1)S(1)}, u32[]{:S(2)}, u32[]{:S(2)}) collective-permute-start(bf16[2,64,512]{2,1,0:T(8,128)(2,1)S(1)} %get-tuple-element.201), channel_id=1, source_target_pairs={{0,2},{1,3},{2,0},{3,1},{4,6},{5,7},{6,4},{7,5},{8,10},{9,11},{10,... | collective-permute-start | bytes 393224 | tf_op jit(solution)/shard_map/ppermute | solution.py:450
  72.5 8.7 %collective-permute-start.25 = (bf16[192,512]{1,0:T(8,128)(2,1)S(1)}, bf16[192,512]{1,0:T(8,128)(2,1)S(1)}, u32[]{:S(2)}, u32[]{:S(2)}) collective-permute-start(bf16[192,512]{1,0:T(8,128)(2,1)S(1)} %get-tuple-element.223), channel_id=1, source_target_pairs={{0,4},{1,5},{2,6},{3,7},{4,0},{5,1},{6,2},{7,3},{8,12},{9,13},{10,... | collective-permute-start | bytes 589832 | tf_op jit(solution)/shard_map/ppermute | solution.py:450
  76.9 12.2 %collective-permute-start.17 = (bf16[224,512]{1,0:T(8,128)(2,1)S(1)}, bf16[224,512]{1,0:T(8,128)(2,1)S(1)}, u32[]{:S(2)}, u32[]{:S(2)}) collective-permute-start(bf16[224,512]{1,0:T(8,128)(2,1)S(1)} %get-tuple-element.209), channel_id=1, source_target_pairs={{0,8},{1,9},{2,10},{3,11},{4,12},{5,13},{6,14},{7,15},{8,0},{9,1},... | collective-permute-start | bytes 688136 | tf_op jit(solution)/shard_map/ppermute | solution.py:450
  79.7 6.3 %collective-permute-start.22 = (bf16[128,512]{1,0:T(8,128)(2,1)S(1)}, bf16[128,512]{1,0:T(8,128)(2,1)S(1)}, u32[]{:S(2)}, u32[]{:S(2)}) collective-permute-start(bf16[128,512]{1,0:T(8,128)(2,1)S(1)} %get-tuple-element.217), channel_id=1, source_target_pairs={{0,4},{1,5},{2,6},{3,7},{4,0},{5,1},{6,2},{7,3},{8,12},{9,13},{10,... | collective-permute-start | bytes 393224 | tf_op jit(solution)/shard_map/ppermute | solution.py:450
  81.3 4.7 %collective-permute-start.26 = (bf16[96,512]{1,0:T(8,128)(2,1)S(1)}, bf16[96,512]{1,0:T(8,128)(2,1)S(1)}, u32[]{:S(2)}, u32[]{:S(2)}) collective-permute-start(bf16[96,512]{1,0:T(8,128)(2,1)S(1)} %get-tuple-element.225), channel_id=1, source_target_pairs={{0,2},{1,3},{2,0},{3,1},{4,6},{5,7},{6,4},{7,5},{8,10},{9,11},{10,... | collective-permute-start | bytes 294920 | tf_op jit(solution)/shard_map/ppermute | solution.py:450
  82.8 11.2 %collective-permute-start.7 = (bf16[320,512]{1,0:T(8,128)(2,1)S(1)}, bf16[320,512]{1,0:T(8,128)(2,1)S(1)}, u32[]{:S(2)}, u32[]{:S(2)}) collective-permute-start(bf16[320,512]{1,0:T(8,128)(2,1)S(1)} %get-tuple-element.187.refs_2_), channel_id=1, source_target_pairs={{0,16},{16,0},{1,17},{17,1},{2,18},{18,2},{3,19},{19,3},{4,20},{20... | collective-permute-start | bytes 983048 | tf_op jit(solution)/shard_map/ppermute | solution.py:449
  86.0 6.4 %collective-permute-start.27 = (bf16[112,512]{1,0:T(8,128)(2,1)S(1)}, bf16[112,512]{1,0:T(8,128)(2,1)S(1)}, u32[]{:S(2)}, u32[]{:S(2)}) collective-permute-start(bf16[112,512]{1,0:T(8,128)(2,1)S(1)} %get-tuple-element.227), channel_id=1, source_target_pairs={{0,8},{1,9},{2,10},{3,11},{4,12},{5,13},{6,14},{7,15},{8,0},{9,1},... | collective-permute-start | bytes 344072 | tf_op jit(solution)/shard_map/ppermute | solution.py:450
  89.2 8.8 %collective-permute-start.18 = (bf16[224,512]{1,0:T(8,128)(2,1)S(1)}, bf16[224,512]{1,0:T(8,128)(2,1)S(1)}, u32[]{:S(2)}, u32[]{:S(2)}) collective-permute-start(bf16[224,512]{1,0:T(8,128)(2,1)S(1)} %shard_map.308.refs_0_), channel_id=1, source_target_pairs={{0,16},{16,0},{1,17},{17,1},{2,18},{18,2},{3,19},{19,3},{4,20},{20... | collective-permute-start | bytes 688136 | tf_op jit(solution)/shard_map/ppermute | solution.py:449
  92.5 5.5 %collective-permute-start.28 = (bf16[112,512]{1,0:T(8,128)(2,1)S(1)}, bf16[112,512]{1,0:T(8,128)(2,1)S(1)}, u32[]{:S(2)}, u32[]{:S(2)}) collective-permute-start(bf16[112,512]{1,0:T(8,128)(2,1)S(1)} %shard_map.314.refs_2_), channel_id=1, source_target_pairs={{0,16},{16,0},{1,17},{17,1},{2,18},{18,2},{3,19},{19,3},{4,20},{20... | collective-permute-start | bytes 344072 | tf_op jit(solution)/shard_map/ppermute | solution.py:449

commit v6 on v5

--- a/solution.py
+++ b/solution.py
@@ -149,30 +149,39 @@
 
 
 def forward_body(
-    place, lengths, tokens, memory, recv, attn_gain, query_weight, pair_weight, write_query, out_weight,
+    place, lengths, x_own, n_own, q_own, k_own, v_own, memory, recv, attn_gain, query_weight, pair_weight, write_query, out_weight,
     ffn_gain, ffn_in, ffn_out,
     x, mem, nall, qs, kall, vall, p0, p1, p2, p3, mixed, resid, n2, act, dg,
-    out_send, out_own, out, wqs, kt, vt,
+    out_own, out, wqs, vt,
 ):
     y = place[0]
     width = pair_weight.shape[0]
     rows = x.shape[0]
     slots = mem.shape[0]
     half = rows // 2
-    x[...] = whole_rows(place, tokens, recv, 0, half)
+    own, other = part(place, half, True), part(place, half, False)
+    x[own, :] = x_own[...]
+    x_other = recv[0:half, :]
+    x[other, :] = x_other
     mem[...] = whole_rows(place, memory, recv, half, slots // 2)
     gain = attn_gain[...]
-    xhat, _ = norm_parts(x[...].astype(F32))
+    xhat, _ = norm_parts(x_other.astype(F32))
     nx = (xhat * gain).astype(BF16)
     mhat, _ = norm_parts(mem[...].astype(F32))
     nm = (mhat * gain).astype(BF16)
-    nall[0:slots, :] = nm
-    nall[slots:128, :] = jnp.zeros((128 - slots, width), BF16)
-    nall[128:, :] = nx
-    qs[...] = (dot(nx, query_weight[...]) * 0.125).astype(BF16)
-    na = nall[...]
-    kall[...] = dot(na, pair_weight[:, :width]).astype(BF16)
-    vall[...] = dot(na, pair_weight[:, width:]).astype(BF16)
+    some = jnp.concatenate([nm, jnp.zeros((128 - slots, width), BF16), nx], 0)
+    own_at = pl.ds(pl.multiple_of(128 + place[0] * half, 128), half)
+    other_at = pl.ds(pl.multiple_of(128 + (1 - place[0]) * half, 128), half)
+    qs[own, :] = q_own[...]
+    qs[other, :] = (dot(nx, query_weight[...]) * 0.125).astype(BF16)
+    for ref, mine, value in (
+        (nall, n_own, some),
+        (kall, k_own, dot(some, pair_weight[:, :width]).astype(BF16)),
+        (vall, v_own, dot(some, pair_weight[:, width:]).astype(BF16)),
+    ):
+        ref[0:128, :] = value[:128]
+        ref[own_at, :] = mine[...]
+        ref[other_at, :] = value[128:]
     wqs[...] = (dot(nm, write_query[...]) * 0.125).astype(BF16)
     bounds = []
     total = 0
@@ -184,7 +193,6 @@
     mem_bias = jnp.where(
         lax.broadcasted_iota(jnp.int32, (128, 128), 0) < slots, 0.0, MASKED
     ).astype(F32)
-    kt[...] = kall[...].T
     vt[...] = vall[...].T
     biases = []
     for i in range(4):
@@ -259,7 +267,6 @@
         held = (n // chunks, n % chunks, now)
     bottom(1)
     out_own[...] = out[part(place, half, True), :]
-    out_send[...] = out[part(place, half, False), :]
 
 
 def write_body(
@@ -343,8 +350,8 @@
 
 
 def resid_back_body(
-    place, total, dout, resid, ffn_gain, out_weight, mixed,
-    send, keep, dresid, dmixed, gain_out,
+    place, total, dout, resid, ffn_gain, mixed,
+    send, keep, dresid, gain_out,
 ):
     rhat, rr = norm_parts(resid[...])
     d_norm, d_gain = norm_back(total[...], rhat, rr, ffn_gain[...])
@@ -353,13 +360,14 @@
     dresid[...] = d
     d_attn = d.astype(BF16)
     emit_rows(dot(mixed[...], d_attn), 32, (send, keep), 0, place[1])
-    dmixed[...] = dot(d_attn, out_weight[...], 1, 1).astype(BF16)
 
 
 def attn_back_body(
-    place, qs, dm, vall, p3, kt, p2, p1, p0,
-    dq_out, dk_out, dv_out, dk_ref, dv_ref, dqt_ref,
+    place, qs, dresid, out_weight, vall, p3, kall, p2, p1, p0,
+    dq_out, dk_out, dv_out, dk_ref, dv_ref, dqt_ref, dm, kt,
 ):
+    dm[...] = dot(dresid[...].astype(BF16), out_weight[...], 1, 1).astype(BF16)
+    kt[...] = kall[...].T
     probs = (p0, p1, p2, p3)
 
     def first(i, p):
@@ -400,7 +408,7 @@
 
 def input_back_body(
     place, nall, dq, dk, dv, pair_weight, query_weight, dwquery, write_query, x, mem, attn_gain,
-    dresid, dblend, gain2, gain3, newmem,
+    dresid, dblend, gain2, gain3, newmem, out,
     qsend, qkeep, ksend, kkeep, vsend, vkeep, gsend, gkeep, own_tok, own_mem, swap, gtok, gmem,
 ):
     c = place[1]
@@ -434,7 +442,8 @@
     mother = part(place, mhalf, False)
     swap[0:half, :] = gtok[other, :].astype(BF16)
     swap[half : half + mhalf, :] = newmem[mother, :]
-    swap[half + mhalf :, :] = gmem[mother, :].astype(BF16)
+    swap[half + mhalf : half + 2 * mhalf, :] = gmem[mother, :].astype(BF16)
+    swap[half + 2 * mhalf :, :] = out[other, :]
 
 
 BIT = {"y": 0, "x": 2, "z": 3, "h": 4}
@@ -628,26 +637,45 @@
     )
 
 
-def fetched_weights(weights):
-    def kernel(*refs):
-        n = len(weights)
-        copies = [
-            pltpu.make_async_copy(refs[k], refs[n + k], refs[-1].at[k]) for k in range(n)
-        ]
-        for copy in copies:
-            copy.start()
-        for copy in copies:
-            copy.wait()
-
-    return pl.pallas_call(
+def fetched_weights(weights, tokens, gain):
+    half, width = tokens.shape[1:]
+    n = len(weights)
+
+    def kernel(tokens, gain, *refs):
+        y = lax.axis_index("seq")
+        own, sem = refs[-2], refs[-1]
+        copies = [pltpu.make_async_copy(tokens.at[y], own, sem.at[n])]
+        order = [n - 2, n - 1] + list(range(n - 2))
+        waits = {k: pltpu.make_async_copy(refs[k], refs[n + k], sem.at[k]) for k in order}
+        copies[0].start()
+        for k in order:
+            waits[k].start()
+        x_ref, n_ref, q_ref, k_ref, v_ref = refs[2 * n : 2 * n + 5]
+        copies[0].wait()
+        x_ref[...] = own[...]
+        xhat, _ = norm_parts(own[...].astype(F32))
+        nx = (xhat * gain[...]).astype(BF16)
+        n_ref[...] = nx
+        waits[n - 2].wait()
+        q_ref[...] = (dot(nx, refs[2 * n - 2][...]) * 0.125).astype(BF16)
+        waits[n - 1].wait()
+        k_ref[...] = dot(nx, refs[2 * n - 1][:, :width]).astype(BF16)
+        v_ref[...] = dot(nx, refs[2 * n - 1][:, width:]).astype(BF16)
+        for k in order[2:]:
+            waits[k].wait()
+
+    one = pltpu.VMEM((half, width), BF16)
+    results = pl.pallas_call(
         kernel,
-        out_shape=[pltpu.VMEM(a.shape, a.dtype) for a in weights],
-        in_specs=[pl.BlockSpec(memory_space=pltpu.HBM)] * len(weights),
-        out_specs=[pl.BlockSpec(memory_space=pltpu.VMEM)] * len(weights),
-        scratch_shapes=[pltpu.SemaphoreType.DMA((len(weights),))],
-        compiler_params=pltpu.CompilerParams(vmem_limit_bytes=4 * 1024 * 1024),
+        out_shape=[pltpu.VMEM(a.shape, a.dtype) for a in weights] + [one] * 5,
+        in_specs=[pl.BlockSpec(memory_space=pltpu.HBM), pl.BlockSpec(memory_space=pltpu.VMEM)]
+        + [pl.BlockSpec(memory_space=pltpu.HBM)] * n,
+        out_specs=[pl.BlockSpec(memory_space=pltpu.VMEM)] * (n + 5),
+        scratch_shapes=[pltpu.VMEM((half, width), BF16), pltpu.SemaphoreType.DMA((n + 1,))],
+        compiler_params=pltpu.CompilerParams(vmem_limit_bytes=8 * 1024 * 1024),
         cost_estimate=pl.CostEstimate(flops=10**9, bytes_accessed=10**7, transcendentals=0),
-    )(*[in_hbm(a) for a in weights])
+    )(in_hbm(tokens), gain, *[in_hbm(a) for a in weights])
+    return results[:n], results[n:]
 
 
 def reduced_any(keep, send, pieces):
@@ -734,13 +762,14 @@
     recv_a = exchanged(packed(tokens, memory), "y")
     recv_b = exchanged(packed(out_cotangent, memory_cotangent), "y")
     (
-        tokens, memory, out_cotangent, memory_cotangent, query_weight, pair_weight, out_weight,
-        ffn_in, ffn_out, write_query, write_pair, write_out, write_gate,
-    ) = fetched_weights(
+        memory, out_cotangent, memory_cotangent, out_weight, ffn_in, ffn_out, write_query,
+        write_pair, write_out, write_gate, query_weight, pair_weight,
+    ), own_rows = fetched_weights(
         (
-            tokens, memory, out_cotangent, memory_cotangent, query_weight, pair_weight, out_weight,
-            ffn_in, ffn_out, write_query, write_pair, write_out, write_gate,
-        )
+            memory, out_cotangent, memory_cotangent, out_weight, ffn_in, ffn_out, write_query,
+            write_pair, write_out, write_gate, query_weight, pair_weight,
+        ),
+        tokens, attn_gain[None],
     )
     ag, fg, wg = attn_gain[None], ffn_gain[None], write_gain[None]
     v = lambda *arrs: [("v", a) for a in arrs]
@@ -756,18 +785,17 @@
     gain_row = ((1, width), F32)
     (
         x, mem, nall, qs, kall, vall, p0, p1, p2, p3, mixed, resid, n2, act, dg,
-        out_send, out_own, out, wqs, kt,
+        out_own, out, wqs,
     ) = call(
         forward_body,
-        [("s", lengths)] + v(tokens, memory, recv_a, ag, query_weight, pair_weight)
+        [("s", lengths)] + v(*own_rows, memory, recv_a, ag, query_weight, pair_weight)
         + v(write_query, out_weight, fg, ffn_in, ffn_out),
         [big, small, wide, big, wide, wide]
         + [((H // 2, 128 * (i + 2), 256), BF16) for i in range(4)]
-        + [big, full_f, big, deep, deep, half_b, half_b, big, small, ((width, padded), BF16)],
+        + [big, full_f, big, deep, deep, half_b, big, small],
         scratch=[((width, padded), BF16)],
         flops=2 * 6 * 10**9, nbytes=20 * 10**6, limit=16,
     )
-    out_recv = exchanged(out_send, "y")
     send0, keep0, dwpair, dwquery, dblend, own_new, newmem, gain3 = call(
         write_body,
         v(out, wqs, mem, memory_cotangent, recv_b, write_pair, write_out, write_gate, wg, nall),
@@ -783,12 +811,11 @@
     deps0 = deps1 = []
     send1, keep1, dout, dinner = call(
         ffn_back_body,
-        v(dwpair, write_pair, out_cotangent, recv_b, ffn_out, dg, act) + deps(out_recv),
+        v(dwpair, write_pair, out_cotangent, recv_b, ffn_out, dg, act),
         [*keep_send(128), full_f, deep],
         flops=2 * 5 * 10**9, nbytes=20 * 10**6,
     )
     if small_mesh:
-        send0, _ = lax.optimization_barrier((send0, out_recv))
         k0, r0 = pair(keep0, send0)
         deps0 = deps(r0)
     send4, keep4, total = call(
@@ -798,9 +825,9 @@
     if small_mesh:
         k1, r1 = pair(keep1, send1)
         deps0 = deps(r1)
-    send3, keep3, dresid, dmixed, gain2 = call(
-        resid_back_body, v(total, dout, resid, fg, out_weight, mixed) + deps0,
-        [*keep_send(32), full_f, big, gain_row],
+    send3, keep3, dresid, gain2 = call(
+        resid_back_body, v(total, dout, resid, fg, mixed) + deps0,
+        [*keep_send(32), full_f, gain_row],
         flops=10**8, nbytes=10**6,
     )
     orders = ("xyz", "yzx", "zxy")
@@ -825,26 +852,25 @@
         first = moved(parts, nth(orders, 0))
     dq, dk, dv = call(
         attn_back_body,
-        v(qs, dmixed, vall, p3, kt, p2, p1, p0) + deps1,
+        v(qs, dresid, out_weight, vall, p3, kall, p2, p1, p0) + deps1,
         [big, wide, wide],
-        scratch=[((padded, width), F32)] * 2 + [big],
+        scratch=[((padded, width), F32)] * 2 + [big, big, ((width, padded), BF16)],
         flops=2 * 6 * 10**9, nbytes=20 * 10**6,
     )
     *grads2, own_tok, own_mem, swap = call(
         input_back_body,
         v(
             nall, dq, dk, dv, pair_weight, query_weight, dwquery, write_query, x, mem, ag, dresid,
-            dblend, gain2, gain3, newmem,
+            dblend, gain2, gain3, newmem, out,
         ),
         [
             *keep_send(32), *keep_send(32), *keep_send(32), *keep_send(16), ((half, width), F32), ((mhalf, width), F32),
-            ((half + 2 * mhalf, width), BF16),
+            ((2 * half + 2 * mhalf, width), BF16),
         ],
         scratch=[((rows, width), F32), ((slots, width), F32)],
         flops=2 * 3 * 10**9, nbytes=20 * 10**6,
     )
     r = width // groups
-    (out_both,) = assembled([out_own], out_recv, [BF16])
     if small_mesh:
         def each(streams, labels, deps=()):
             results = []
@@ -862,6 +888,7 @@
         by_x.next(behind)
         by_z.next(behind)
         keep, send = stage(third, "hhh", joined=True)
+        swapped = exchanged(swap, "y")
         by_x.joined(by_z).next([keep])
         t1 = added(keep, exchanged(send, "h"))
         one, two = [t1], [exchanged(t1, "y")]
@@ -891,8 +918,11 @@
         gwq, gwp, gwo, gwg = cut(w0, 0, 1), cut(w0, 1, 2), cut(w0, 3, 1), cut(w0, 4, 1)
         at = lax.axis_index("seg") * r
         gains = [lax.dynamic_slice_in_dim(w2[3 * r + i], at, r, 0) for i in range(3)]
-    swapped = exchanged(swap, "y")
-    tok_both, new_both, mem_both = assembled([own_tok, own_new, own_mem], swapped, [F32, BF16, F32])
+    if not small_mesh:
+        swapped = exchanged(swap, "y")
+    tok_both, new_both, mem_both, out_both = assembled(
+        [own_tok, own_new, own_mem, out_own], swapped, [F32, BF16, F32, BF16]
+    )
     return (
         out_both, new_both, tok_both, mem_both,
         gains[0], gq, gp, go, gains[1], gfi, gfo, gwq, gwp, gwo, gwg, gains[2],

time: 99.4 us -> 98.2 us (0.988)
  starting transfers between devices: 35.2 us -> 30.1 us
  waiting for transfers between devices: 21.8 us -> 25.8 us
    ppermute x20, starting transfers between devices: 22.2 us -> 18.9 us  [exchanged(): lax.ppermute(send, 'seg', other_of('seg', {'x': 2, 'z': 4, 'h': 8, 'c': 1...]
    ppermute x9 -> x8, waiting for transfers between devices: 5.71 us -> 8.82 us  [exchanged(): return lax.ppermute(send, 'seq', other_of('seq', 1))]
    ppermute x9 -> x8, starting transfers between devices: 13 us -> 11.2 us  [exchanged(): return lax.ppermute(send, 'seq', other_of('seq', 1))]
    pallas_call x25 -> x24, Pallas kernels: 35.3 us -> 34.5 us  [call(): pl.pallas_call(kernel, out_shape=[shape(s, d) for s, d in outs], in_specs...]
  transfers between devices with their start and end apart: 29 -> 28, of which waited for: 10 -> 14; matrix products, arithmetic and copies ran while one was open for 0% -> 0% of each run, Pallas kernels for 39% -> 33%
where the time goes in v6:
time: 98.2 us; the launch traced here: 98 us
  Pallas kernels  40.4 us (41%)
  starting transfers between devices  30.1 us (31%)
  waiting for transfers between devices  25.8 us (26%)
  between operations  1.04 us (1%)
    pallas_call x24, Pallas kernels, call(): pl.pallas_call(kernel, out_shape=[shape(s, d) for s, d in outs], in_specs...  34.5 us
    ppermute x20, starting transfers between devices, exchanged(): lax.ppermute(send, 'seg', other_of('seg', {'x': 2, 'z': 4, 'h': 8, 'c': 1...  18.9 us
    ppermute x20, waiting for transfers between devices, exchanged(): lax.ppermute(send, 'seg', other_of('seg', {'x': 2, 'z': 4, 'h': 8, 'c': 1...  17 us
    ppermute x8, starting transfers between devices, exchanged(): return lax.ppermute(send, 'seq', other_of('seq', 1))  11.2 us
    ppermute x8, waiting for transfers between devices, exchanged(): return lax.ppermute(send, 'seq', other_of('seq', 1))  8.82 us
    pallas_call x1, Pallas kernels, fetched_weights(): pl.pallas_call(kernel, out_shape=[pltpu.VMEM(a.shape, a.dtype) for a in w...  3.92 us
  transfers between devices with their start and end apart: 28, of which 14 were waited for; matrix products, arithmetic and copies ran while one was open for 0% of the time, Pallas kernels for 33%

profile of v6, /device:TPU:0, one launch (start us, length us, event | category | flops | bytes accessed | tf_op | source)
XLA Modules:
  0.0 98.0 jit_solution(15232015834024641554)
XLA Ops:
  0.6 1.0 %shard_map.289 = bf16[288,512]{1,0:T(8,128)(2,1)S(1)} custom-call(bf16[2,256,512]{2,1,0:T(8,128)(2,1)} %a.2, bf16[2,32,512]{2,1,0:T(8,128)(2,1)} %b.2), custom_call_target="tpu_custom_call" | custom-call | tf_op jit(solution)/shard_map/pallas_call | solution.py:610
  1.6 3.0 %collective-permute-start = (bf16[288,512]{1,0:T(8,128)(2,1)S(1)}, bf16[288,512]{1,0:T(8,128)(2,1)S(1)}, u32[]{:S(2)}, u32[]{:S(2)}) collective-permute-start(bf16[288,512]{1,0:T(8,128)(2,1)S(1)} %shard_map.289), channel_id=1, source_target_pairs={{0,16},{16,0},{1,17},{17,1},{2,18},{18,2},{3,19},{19,3},{4,20},{20... | collective-permute-start | bytes 884744 | tf_op jit(solution)/shard_map/ppermute | solution.py:458
  4.7 1.0 shard_map.291
  5.7 0.7 copy-done.1
  6.4 3.9 %shard_map.288 = (bf16[2,32,512]{2,1,0:T(8,128)(2,1)S(1)}, bf16[2,256,512]{2,1,0:T(8,128)(2,1)S(1)}, bf16[2,32,512]{2,1,0:T(8,128)(2,1)S(1)}, bf16[512,512]{1,0:...) custom-call(bf16[2,256,512]{2,1,0:T(8,128)(2,1)} %a.2, ...), custom_call_target="tpu_custom_call" | custom-call | flops 1000000000 | bytes 10000000 | tf_op jit(solution)/shard_map/pallas_call | solution.py:668
  10.3 2.2 %collective-permute-done.refs_7_ = bf16[288,512]{1,0:T(8,128)(2,1)S(1)} collective-permute-done((bf16[288,512]{1,0:T(8,128)(2,1)S(1)}, bf16[288,512]{1,0:T(8,128)(2,1)S(1)}, u32[]{:S(2)}, u32[]{:S(2)}) %collective-permute-start) | collective-permute-done | bytes 294944 | tf_op jit(solution)/shard_map/ppermute | solution.py:458
  12.5 10.5 %shard_map.290 = (bf16[512,512]{1,0:T(8,128)(2,1)S(1)}, bf16[64,512]{1,0:T(8,128)(2,1)S(1)}, bf16[640,512]{1,0:T(8,128)(2,1)S(1)}, bf16[512,512]{1,0:T(8,128)(2,...) custom-call(s32[2,8]{1,0:T(2,128)S(1)} %copy-done.4, ...), custom_call_target="tpu_custom_call" | custom-call | flops 12000000000 | bytes 20000000 | tf_op jit(solution)/shard_map/pallas_call | solution.py:64
  23.1 5.0 %shard_map.292 = (bf16[8,160,512]{2,1,0:T(8,128)(2,1)S(1)}, bf16[8,160,512]{2,1,0:T(8,128)(2,1)S(1)}, bf16[512,1024]{1,0:T(8,128)(2,1)S(1)}, bf16[64,512]{1,0:T(...) custom-call(bf16[512,512]{1,0:T(8,128)(2,1)S(1)} %get-tuple-element., ...), custom_call_target="tpu_custom_call" | custom-call | flops 6000000000 | bytes 10000000 | tf_op jit(solution)/shard_map/pallas_call | solution.py:64
  28.2 3.0 %shard_map.293 = (bf16[8,128,512]{2,1,0:T(8,128)(2,1)S(1)}, bf16[8,128,512]{2,1,0:T(8,128)(2,1)S(1)}, f32[512,512]{1,0:T(8,128)S(1)}, bf16[512,2048]{1,0:T(8,128)(2,1)S(1)}) custom-call(bf16[512,1024]{1,0:T(8,128)(2,1)S(1)} %get-tuple-element.151.refs_0_, bf16[512,1024]{1,0:T(8,128)(2,1)S(1)} %get-tuple-element.148.refs_5_.refs_1_, ...), custom_call_target="tpu_custom_call" | custom-call | flops 10000000000 | bytes 20000000 | tf_op jit(solution)/shard_map/pallas_call | solution.py:64
  31.2 0.6 collective-permute-start.3
  31.8 2.4 %shard_map.294 = (bf16[8,128,512]{2,1,0:T(8,128)(2,1)S(1)}, bf16[8,128,512]{2,1,0:T(8,128)(2,1)S(1)}, f32[512,512]{1,0:T(8,128)S(1)}) custom-call(bf16[512,2048]{1,0:T(8,128)(2,1)S(1)} %get-tuple-element.155.refs_0_, bf16[512,512]{1,0:T(8,128)(2,1)S(1)} %get-tuple-element.156.refs_1_, bf16[512,2048]{1,0:T(8,128)(2,1)S(1)} %get-tuple-element.140.refs_14_.refs_2_, ...), custom_call_target="tpu_custom_call" | custom-call | flops 1000000000 | bytes 20000000 | tf_op jit(solution)/shard_map/pallas_call | solution.py:64
  34.3 1.1 %shard_map.295 = (bf16[8,32,512]{2,1,0:T(8,128)(2,1)S(1)}, bf16[8,32,512]{2,1,0:T(8,128)(2,1)S(1)}, f32[512,512]{1,0:T(8,128)S(1)}, f32[1,512]{1,0:T(1,128)S(1)}) custom-call(f32[512,512]{1,0:T(8,128)S(1)} %get-tuple-element.158.refs_0_, f32[512,512]{1,0:T(8,128)S(1)} %get-tuple-element.159.refs_1_, f32[512,512]{1,0:T(8,128)S(1)} %get-tuple-element.160.refs_2_, ...), custom_call_target="tpu_custom_call" | custom-call | flops 100000000 | bytes 1000000 | tf_op jit(solution)/shard_map/pallas_call | solution.py:64
  35.4 0.6 collective-permute-start.5
  35.9 1.4 %collective-permute-done.5 = bf16[8,32,512]{2,1,0:T(8,128)(2,1)S(1)} collective-permute-done((bf16[8,32,512]{2,1,0:T(8,128)(2,1)S(1)}, bf16[8,32,512]{2,1,0:T(8,128)(2,1)S(1)}, u32[]{:S(2)}, u32[]{:S(2)}) %collective-permute-start.5) | collective-permute-done | bytes 262176 | tf_op jit(solution)/shard_map/ppermute | solution.py:459
  37.3 0.8 shard_map.296
  38.1 2.1 %collective-permute-start.10 = (bf16[2,2,2,64,512]{4,3,2,1,0:T(8,128)(2,1)S(1)}, bf16[2,2,2,64,512]{4,3,2,1,0:T(8,128)(2,1)S(1)}, u32[]{:S(2)}, u32[]{:S(2)}) collective-permute-start(bf16[2,2,2,64,512]{4,3,2,1,0:T(8,128)(2,1)S(1)} %get-tuple-element.201), channel_id=1, source_target_pairs={{0,16},{16,0},{1,17},{17,1},{2,18},{18,2},{3,19},{19,3},{4,20},{20... | collective-permute-start | bytes 1572872 | tf_op jit(solution)/shard_map/ppermute | solution.py:458
  40.3 1.5 %collective-permute-start.7 = (bf16[2,2,160,512]{3,2,1,0:T(8,128)(2,1)S(1)}, bf16[2,2,160,512]{3,2,1,0:T(8,128)(2,1)S(1)}, u32[]{:S(2)}, u32[]{:S(2)}) collective-permute-start(bf16[2,2,160,512]{3,2,1,0:T(8,128)(2,1)S(1)} %get-tuple-element.195), channel_id=1, source_target_pairs={{0,2},{1,3},{2,0},{3,1},{4,6},{5,7},{6,4},{7,5},{8,10},{9,11},{10,... | collective-permute-start | bytes 1966088 | tf_op jit(solution)/shard_map/ppermute | solution.py:459
  41.8 1.6 %collective-permute-start.13 = (bf16[2,2,160,512]{3,2,1,0:T(8,128)(2,1)S(1)}, bf16[2,2,160,512]{3,2,1,0:T(8,128)(2,1)S(1)}, u32[]{:S(2)}, u32[]{:S(2)}) collective-permute-start(bf16[2,2,160,512]{3,2,1,0:T(8,128)(2,1)S(1)} %get-tuple-element.207), channel_id=1, source_target_pairs={{0,4},{1,5},{2,6},{3,7},{4,0},{5,1},{6,2},{7,3},{8,12},{9,13},{10,... | collective-permute-start | bytes 1966088 | tf_op jit(solution)/shard_map/ppermute | solution.py:459
  43.3 5.1 %shard_map.297 = (bf16[512,512]{1,0:T(8,128)(2,1)S(1)}, bf16[640,512]{1,0:T(8,128)(2,1)S(1)}, bf16[640,512]{1,0:T(8,128)(2,1)S(1)}) custom-call(bf16[512,512]{1,0:T(8,128)(2,1)S(1)} %get-tuple-element.143.refs_0_, f32[512,512]{1,0:T(8,128)S(1)} %get-tuple-element.163.refs_1_.refs_11_, bf16[512,512]{1,0:T(8,128)(2,1)S(1)} %get-tuple-element.139.refs_12_.refs_2_, ...), custom_call_target="tpu_custom_call" | custom-call | flops 12000000000 | bytes 20000000 | tf_op jit(solution)/shard_map/pallas_call | solution.py:64
  48.4 2.9 %shard_map.298 = (bf16[8,32,512]{2,1,0:T(8,128)(2,1)S(1)}, bf16[8,32,512]{2,1,0:T(8,128)(2,1)S(1)}, bf16[8,32,512]{2,1,0:T(8,128)(2,1)S(1)}, bf16[8,32,512]{2,1,...) custom-call(bf16[640,512]{1,0:T(8,128)(2,1)S(1)} %get-tuple-element., ...), custom_call_target="tpu_custom_call" | custom-call | flops 6000000000 | bytes 20000000 | tf_op jit(solution)/shard_map/pallas_call | solution.py:64
  51.4 1.1 %collective-permute-done.10.refs_1_ = bf16[2,2,2,64,512]{4,3,2,1,0:T(8,128)(2,1)S(1)} collective-permute-done((bf16[2,2,2,64,512]{4,3,2,1,0:T(8,128)(2,1)S(1)}, bf16[2,2,2,64,512]{4,3,2,1,0:T(8,128)(2,1)S(1)}, u32[]{:S(2)}, u32[]{:S(2)}) %collective-permute-start.10) | collective-permute-done | bytes 524320 | tf_op jit(solution)/shard_map/ppermute | solution.py:458
  52.6 1.8 %collective-permute-start.11 = (bf16[2,2,64,512]{3,2,1,0:T(8,128)(2,1)S(1)}, bf16[2,2,64,512]{3,2,1,0:T(8,128)(2,1)S(1)}, u32[]{:S(2)}, u32[]{:S(2)}) collective-permute-start(bf16[2,2,64,512]{3,2,1,0:T(8,128)(2,1)S(1)} %get-tuple-element.203), channel_id=1, source_target_pairs={{0,4},{1,5},{2,6},{3,7},{4,0},{5,1},{6,2},{7,3},{8,12},{9,13},{10,... | collective-permute-start | bytes 786440 | tf_op jit(solution)/shard_map/ppermute | solution.py:459
  54.5 2.3 %collective-permute-done.7.refs_1_ = bf16[2,2,160,512]{3,2,1,0:T(8,128)(2,1)S(1)} collective-permute-done((bf16[2,2,160,512]{3,2,1,0:T(8,128)(2,1)S(1)}, bf16[2,2,160,512]{3,2,1,0:T(8,128)(2,1)S(1)}, u32[]{:S(2)}, u32[]{:S(2)}) %collective-permute-start.7) | collective-permute-done | bytes 655392 | tf_op jit(solution)/shard_map/ppermute | solution.py:459
  56.9 0.4 collective-permute-start.8
  57.4 2.1 %collective-permute-done.13.refs_1_ = bf16[2,2,160,512]{3,2,1,0:T(8,128)(2,1)S(1)} collective-permute-done((bf16[2,2,160,512]{3,2,1,0:T(8,128)(2,1)S(1)}, bf16[2,2,160,512]{3,2,1,0:T(8,128)(2,1)S(1)}, u32[]{:S(2)}, u32[]{:S(2)}) %collective-permute-start.13) | collective-permute-done | bytes 655392 | tf_op jit(solution)/shard_map/ppermute | solution.py:459
  59.6 0.6 collective-permute-start.14
  60.2 0.5 collective-permute-start.22
  60.7 2.9 %collective-permute-done.11.refs_1_ = bf16[2,2,64,512]{3,2,1,0:T(8,128)(2,1)S(1)} collective-permute-done((bf16[2,2,64,512]{3,2,1,0:T(8,128)(2,1)S(1)}, bf16[2,2,64,512]{3,2,1,0:T(8,128)(2,1)S(1)}, u32[]{:S(2)}, u32[]{:S(2)}) %collective-permute-start.11) | collective-permute-done | bytes 262176 | tf_op jit(solution)/shard_map/ppermute | solution.py:459
  63.7 0.6 collective-permute-start.12
  64.4 1.2 %collective-permute-done.8.refs_1_ = bf16[2,2,80,512]{3,2,1,0:T(8,128)(2,1)S(1)} collective-permute-done((bf16[2,2,80,512]{3,2,1,0:T(8,128)(2,1)S(1)}, bf16[2,2,80,512]{3,2,1,0:T(8,128)(2,1)S(1)}, u32[]{:S(2)}, u32[]{:S(2)}) %collective-permute-start.8) | collective-permute-done | bytes 327712 | tf_op jit(solution)/shard_map/ppermute | solution.py:458
  65.6 1.5 %collective-permute-start.20 = (bf16[256,512]{1,0:T(8,128)(2,1)S(1)}, bf16[256,512]{1,0:T(8,128)(2,1)S(1)}, u32[]{:S(2)}, u32[]{:S(2)}) collective-permute-start(bf16[256,512]{1,0:T(8,128)(2,1)S(1)} %get-tuple-element.219), channel_id=1, source_target_pairs={{0,2},{1,3},{2,0},{3,1},{4,6},{5,7},{6,4},{7,5},{8,10},{9,11},{10,... | collective-permute-start | bytes 786440 | tf_op jit(solution)/shard_map/ppermute | solution.py:459
  67.2 1.6 %collective-permute-start.9 = (bf16[2,80,512]{2,1,0:T(8,128)(2,1)S(1)}, bf16[2,80,512]{2,1,0:T(8,128)(2,1)S(1)}, u32[]{:S(2)}, u32[]{:S(2)}) collective-permute-start(bf16[2,80,512]{2,1,0:T(8,128)(2,1)S(1)} %get-tuple-element.199), channel_id=1, source_target_pairs={{0,4},{1,5},{2,6},{3,7},{4,0},{5,1},{6,2},{7,3},{8,12},{9,13},{10,... | collective-permute-start | bytes 491528 | tf_op jit(solution)/shard_map/ppermute | solution.py:459
  68.9 0.6 collective-permute-start.15
  69.5 1.5 %collective-permute-start.6 = (bf16[576,512]{1,0:T(8,128)(2,1)S(1)}, bf16[576,512]{1,0:T(8,128)(2,1)S(1)}, u32[]{:S(2)}, u32[]{:S(2)}) collective-permute-start(bf16[576,512]{1,0:T(8,128)(2,1)S(1)} %get-tuple-element.190.refs_2_), channel_id=1, source_target_pairs={{0,16},{16,0},{1,17},{17,1},{2,18},{18,2},{3,19},{19,3},{4,20},{20... | collective-permute-start | bytes 1769480 | tf_op jit(solution)/shard_map/ppermute | solution.py:458
  71.1 0.5 collective-permute-start.24
  71.6 1.5 %collective-permute-done.9.refs_1_ = bf16[2,80,512]{2,1,0:T(8,128)(2,1)S(1)} collective-permute-done((bf16[2,80,512]{2,1,0:T(8,128)(2,1)S(1)}, bf16[2,80,512]{2,1,0:T(8,128)(2,1)S(1)}, u32[]{:S(2)}, u32[]{:S(2)}) %collective-permute-start.9) | collective-permute-done | bytes 163872 | tf_op jit(solution)/shard_map/ppermute | solution.py:459
  73.1 3.0 %collective-permute-done.15.refs_5_ = bf16[2,80,512]{2,1,0:T(8,128)(2,1)S(1)} collective-permute-done((bf16[2,80,512]{2,1,0:T(8,128)(2,1)S(1)}, bf16[2,80,512]{2,1,0:T(8,128)(2,1)S(1)}, u32[]{:S(2)}, u32[]{:S(2)}) %collective-permute-start.15) | collective-permute-done | bytes 163872 | tf_op jit(solution)/shard_map/ppermute | solution.py:458
  76.2 2.7 %collective-permute-start.16 = (bf16[224,512]{1,0:T(8,128)(2,1)S(1)}, bf16[224,512]{1,0:T(8,128)(2,1)S(1)}, u32[]{:S(2)}, u32[]{:S(2)}) collective-permute-start(bf16[224,512]{1,0:T(8,128)(2,1)S(1)} %get-tuple-element.213), channel_id=1, source_target_pairs={{0,8},{1,9},{2,10},{3,11},{4,12},{5,13},{6,14},{7,15},{8,0},{9,1},... | collective-permute-start | bytes 688136 | tf_op jit(solution)/shard_map/ppermute | solution.py:459
  78.9 0.5 collective-permute-start.21
  79.8 1.2 %collective-permute-start.25 = (bf16[96,512]{1,0:T(8,128)(2,1)S(1)}, bf16[96,512]{1,0:T(8,128)(2,1)S(1)}, u32[]{:S(2)}, u32[]{:S(2)}) collective-permute-start(bf16[96,512]{1,0:T(8,128)(2,1)S(1)} %get-tuple-element.229), channel_id=1, source_target_pairs={{0,2},{1,3},{2,0},{3,1},{4,6},{5,7},{6,4},{7,5},{8,10},{9,11},{10,... | collective-permute-start | bytes 294920 | tf_op jit(solution)/shard_map/ppermute | solution.py:459
  81.0 3.5 %collective-permute-done.25.refs_3_ = bf16[96,512]{1,0:T(8,128)(2,1)S(1)} collective-permute-done((bf16[96,512]{1,0:T(8,128)(2,1)S(1)}, bf16[96,512]{1,0:T(8,128)(2,1)S(1)}, u32[]{:S(2)}, u32[]{:S(2)}) %collective-permute-start.25) | collective-permute-done | bytes 98336 | tf_op jit(solution)/shard_map/ppermute | solution.py:459
  84.5 0.4 collective-permute-done.21.refs_1_
  84.9 2.9 %collective-permute-start.26 = (bf16[112,512]{1,0:T(8,128)(2,1)S(1)}, bf16[112,512]{1,0:T(8,128)(2,1)S(1)}, u32[]{:S(2)}, u32[]{:S(2)}) collective-permute-start(bf16[112,512]{1,0:T(8,128)(2,1)S(1)} %get-tuple-element.231), channel_id=1, source_target_pairs={{0,8},{1,9},{2,10},{3,11},{4,12},{5,13},{6,14},{7,15},{8,0},{9,1},... | collective-permute-start | bytes 344072 | tf_op jit(solution)/shard_map/ppermute | solution.py:459
  87.9 2.7 %collective-permute-done.26.refs_1_ = bf16[112,512]{1,0:T(8,128)(2,1)S(1)} collective-permute-done((bf16[112,512]{1,0:T(8,128)(2,1)S(1)}, bf16[112,512]{1,0:T(8,128)(2,1)S(1)}, u32[]{:S(2)}, u32[]{:S(2)}) %collective-permute-start.26) | collective-permute-done | bytes 114720 | tf_op jit(solution)/shard_map/ppermute | solution.py:459
  90.7 3.4 %collective-permute-start.27 = (bf16[112,512]{1,0:T(8,128)(2,1)S(1)}, bf16[112,512]{1,0:T(8,128)(2,1)S(1)}, u32[]{:S(2)}, u32[]{:S(2)}) collective-permute-start(bf16[112,512]{1,0:T(8,128)(2,1)S(1)} %shard_map.313.refs_2_), channel_id=1, source_target_pairs={{0,16},{16,0},{1,17},{17,1},{2,18},{18,2},{3,19},{19,3},{4,20},{20... | collective-permute-start | bytes 344072 | tf_op jit(solution)/shard_map/ppermute | solution.py:458
  94.0 1.3 %shard_map.299 = (f32[2,256,512]{2,1,0:T(8,128)}, bf16[2,32,512]{2,1,0:T(8,128)(2,1)}, f32[2,32,512]{2,1,0:T(8,128)}, bf16[2,256,512]{2,1,0:T(8,128)(2,1)}) custom-call(f32[256,512]{1,0:T(8,128)S(1)} %get-tuple-element.186.refs_0_, bf16[32,512]{1,0:T(8,128)(2,1)S(1)} %get-tuple-element.187.refs_1_, f32[32,512]{1,0:T(8,128)S(1)} %get-tuple-element.188.refs_2_, ...), custom_call_target="tpu_custom_call" | custom-call | flops 1000000 | bytes 1000000 | tf_op jit(solution)/shard_map/pallas_call | solution.py:64
  95.4 1.4 %collective-permute-done.27.refs_3_ = bf16[112,512]{1,0:T(8,128)(2,1)S(1)} collective-permute-done((bf16[112,512]{1,0:T(8,128)(2,1)S(1)}, bf16[112,512]{1,0:T(8,128)(2,1)S(1)}, u32[]{:S(2)}, u32[]{:S(2)}) %collective-permute-start.27) | collective-permute-done | bytes 114720 | tf_op jit(solution)/shard_map/ppermute | solution.py:458
  96.8 1.0 %shard_map.314 = (f32[32,512]{1,0:T(8,128)}, f32[32,1024]{1,0:T(8,128)}, f32[32,512]{1,0:T(8,128)}, f32[32,2048]{1,0:T(8,128)}, f32[128,512]{1,0:T(8,128)}, /*in...) custom-call(bf16[224,512]{1,0:T(8,128)(2,1)S(1)} %shard_map.307.refs, ...), custom_call_target="tpu_custom_call" | custom-call | flops 1000000 | bytes 1000000 | tf_op jit(solution)/shard_map/pallas_call | solution.py:64
  (45 shorter events, 2.0 us)
Async XLA Ops:
  1.6 10.9 %collective-permute-start = (bf16[288,512]{1,0:T(8,128)(2,1)S(1)}, bf16[288,512]{1,0:T(8,128)(2,1)S(1)}, u32[]{:S(2)}, u32[]{:S(2)}) collective-permute-start(bf16[288,512]{1,0:T(8,128)(2,1)S(1)} %shard_map.289), channel_id=1, source_target_pairs={{0,16},{16,0},{1,17},{17,1},{2,18},{18,2},{3,19},{19,3},{4,20},{20... | collective-permute-start | bytes 884744 | tf_op jit(solution)/shard_map/ppermute | solution.py:458
  5.6 17.4 %collective-permute-start.1 = (bf16[288,512]{1,0:T(8,128)(2,1)S(1)}, bf16[288,512]{1,0:T(8,128)(2,1)S(1)}, u32[]{:S(2)}, u32[]{:S(2)}) collective-permute-start(bf16[288,512]{1,0:T(8,128)(2,1)S(1)} %shard_map.291), channel_id=1, source_target_pairs={{0,16},{16,0},{1,17},{17,1},{2,18},{18,2},{3,19},{19,3},{4,20},{20... | collective-permute-start | bytes 884744 | tf_op jit(solution)/shard_map/ppermute | solution.py:458
  5.7 0.7 copy-start.1
  6.4 6.1 %copy-start = (f32[512]{0:T(512)S(1)}, f32[512]{0:T(512)}, u32[]{:S(2)}) copy-start(f32[512]{0:T(512)} %param.24) | copy-start | bytes 6148
  6.4 6.1 %copy-start.2 = (f32[512]{0:T(512)S(1)}, f32[512]{0:T(512)}, u32[]{:S(2)}) copy-start(f32[512]{0:T(512)} %param.20) | copy-start | bytes 6148
  6.4 6.1 %copy-start.4 = (s32[2,8]{1,0:T(2,128)S(1)}, s32[2,8]{1,0:T(2,128)}, u32[]{:S(2)}) copy-start(s32[2,8]{1,0:T(2,128)} %refs_0_.3) | copy-start | bytes 196
  12.5 10.6 %copy-start.3 = (f32[512]{0:T(512)S(1)}, f32[512]{0:T(512)}, u32[]{:S(2)}) copy-start(f32[512]{0:T(512)} %param.31) | copy-start | bytes 6148
  28.1 3.7 %collective-permute-start.2 = (bf16[8,160,512]{2,1,0:T(8,128)(2,1)S(1)}, bf16[8,160,512]{2,1,0:T(8,128)(2,1)S(1)}, u32[]{:S(2)}, u32[]{:S(2)}) collective-permute-start(bf16[8,160,512]{2,1,0:T(8,128)(2,1)S(1)} %get-tuple-element.157), channel_id=1, source_target_pairs={{0,1},{1,0},{2,3},{3,2},{4,5},{5,4},{6,7},{7,6},{8,9},{9,8},{10,11... | collective-permute-start | bytes 3932168 | tf_op jit(solution)/shard_map/ppermute | solution.py:459
  31.2 3.1 %collective-permute-start.3 = (bf16[8,128,512]{2,1,0:T(8,128)(2,1)S(1)}, bf16[8,128,512]{2,1,0:T(8,128)(2,1)S(1)}, u32[]{:S(2)}, u32[]{:S(2)}) collective-permute-start(bf16[8,128,512]{2,1,0:T(8,128)(2,1)S(1)} %get-tuple-element.162), channel_id=1, source_target_pairs={{0,1},{1,0},{2,3},{3,2},{4,5},{5,4},{6,7},{7,6},{8,9},{9,8},{10,11... | collective-permute-start | bytes 3145736 | tf_op jit(solution)/shard_map/ppermute | solution.py:459
  34.2 3.1 %collective-permute-start.4 = (bf16[8,128,512]{2,1,0:T(8,128)(2,1)S(1)}, bf16[8,128,512]{2,1,0:T(8,128)(2,1)S(1)}, u32[]{:S(2)}, u32[]{:S(2)}) collective-permute-start(bf16[8,128,512]{2,1,0:T(8,128)(2,1)S(1)} %get-tuple-element.172), channel_id=1, source_target_pairs={{0,1},{1,0},{2,3},{3,2},{4,5},{5,4},{6,7},{7,6},{8,9},{9,8},{10,11... | collective-permute-start | bytes 3145736 | tf_op jit(solution)/shard_map/ppermute | solution.py:459
  35.4 1.9 %collective-permute-start.5 = (bf16[8,32,512]{2,1,0:T(8,128)(2,1)S(1)}, bf16[8,32,512]{2,1,0:T(8,128)(2,1)S(1)}, u32[]{:S(2)}, u32[]{:S(2)}) collective-permute-start(bf16[8,32,512]{2,1,0:T(8,128)(2,1)S(1)} %get-tuple-element.175), channel_id=1, source_target_pairs={{0,1},{1,0},{2,3},{3,2},{4,5},{5,4},{6,7},{7,6},{8,9},{9,8},{10,11... | collective-permute-start | bytes 786440 | tf_op jit(solution)/shard_map/ppermute | solution.py:459
  38.1 14.4 %collective-permute-start.10 = (bf16[2,2,2,64,512]{4,3,2,1,0:T(8,128)(2,1)S(1)}, bf16[2,2,2,64,512]{4,3,2,1,0:T(8,128)(2,1)S(1)}, u32[]{:S(2)}, u32[]{:S(2)}) collective-permute-start(bf16[2,2,2,64,512]{4,3,2,1,0:T(8,128)(2,1)S(1)} %get-tuple-element.201), channel_id=1, source_target_pairs={{0,16},{16,0},{1,17},{17,1},{2,18},{18,2},{3,19},{19,3},{4,20},{20... | collective-permute-start | bytes 1572872 | tf_op jit(solution)/shard_map/ppermute | solution.py:458
  40.3 16.5 %collective-permute-start.7 = (bf16[2,2,160,512]{3,2,1,0:T(8,128)(2,1)S(1)}, bf16[2,2,160,512]{3,2,1,0:T(8,128)(2,1)S(1)}, u32[]{:S(2)}, u32[]{:S(2)}) collective-permute-start(bf16[2,2,160,512]{3,2,1,0:T(8,128)(2,1)S(1)} %get-tuple-element.195), channel_id=1, source_target_pairs={{0,2},{1,3},{2,0},{3,1},{4,6},{5,7},{6,4},{7,5},{8,10},{9,11},{10,... | collective-permute-start | bytes 1966088 | tf_op jit(solution)/shard_map/ppermute | solution.py:459
  41.8 17.7 %collective-permute-start.13 = (bf16[2,2,160,512]{3,2,1,0:T(8,128)(2,1)S(1)}, bf16[2,2,160,512]{3,2,1,0:T(8,128)(2,1)S(1)}, u32[]{:S(2)}, u32[]{:S(2)}) collective-permute-start(bf16[2,2,160,512]{3,2,1,0:T(8,128)(2,1)S(1)} %get-tuple-element.207), channel_id=1, source_target_pairs={{0,4},{1,5},{2,6},{3,7},{4,0},{5,1},{6,2},{7,3},{8,12},{9,13},{10,... | collective-permute-start | bytes 1966088 | tf_op jit(solution)/shard_map/ppermute | solution.py:459
  51.4 8.8 %collective-permute-start.18 = (bf16[8,32,512]{2,1,0:T(8,128)(2,1)S(1)}, bf16[8,32,512]{2,1,0:T(8,128)(2,1)S(1)}, u32[]{:S(2)}, u32[]{:S(2)}) collective-permute-start(bf16[8,32,512]{2,1,0:T(8,128)(2,1)S(1)} %get-tuple-element.215), channel_id=1, source_target_pairs={{0,1},{1,0},{2,3},{3,2},{4,5},{5,4},{6,7},{7,6},{8,9},{9,8},{10,11... | collective-permute-start | bytes 786440 | tf_op jit(solution)/shard_map/ppermute | solution.py:459
  52.6 11.0 %collective-permute-start.11 = (bf16[2,2,64,512]{3,2,1,0:T(8,128)(2,1)S(1)}, bf16[2,2,64,512]{3,2,1,0:T(8,128)(2,1)S(1)}, u32[]{:S(2)}, u32[]{:S(2)}) collective-permute-start(bf16[2,2,64,512]{3,2,1,0:T(8,128)(2,1)S(1)} %get-tuple-element.203), channel_id=1, source_target_pairs={{0,4},{1,5},{2,6},{3,7},{4,0},{5,1},{6,2},{7,3},{8,12},{9,13},{10,... | collective-permute-start | bytes 786440 | tf_op jit(solution)/shard_map/ppermute | solution.py:459
  56.9 8.7 %collective-permute-start.8 = (bf16[2,2,80,512]{3,2,1,0:T(8,128)(2,1)S(1)}, bf16[2,2,80,512]{3,2,1,0:T(8,128)(2,1)S(1)}, u32[]{:S(2)}, u32[]{:S(2)}) collective-permute-start(bf16[2,2,80,512]{3,2,1,0:T(8,128)(2,1)S(1)} %get-tuple-element.197), channel_id=1, source_target_pairs={{0,16},{16,0},{1,17},{17,1},{2,18},{18,2},{3,19},{19,3},{4,20},{20... | collective-permute-start | bytes 983048 | tf_op jit(solution)/shard_map/ppermute | solution.py:458
  59.6 7.6 %collective-permute-start.14 = (bf16[2,160,512]{2,1,0:T(8,128)(2,1)S(1)}, bf16[2,160,512]{2,1,0:T(8,128)(2,1)S(1)}, u32[]{:S(2)}, u32[]{:S(2)}) collective-permute-start(bf16[2,160,512]{2,1,0:T(8,128)(2,1)S(1)} %get-tuple-element.209), channel_id=1, source_target_pairs={{0,2},{1,3},{2,0},{3,1},{4,6},{5,7},{6,4},{7,5},{8,10},{9,11},{10,... | collective-permute-start | bytes 983048 | tf_op jit(solution)/shard_map/ppermute | solution.py:459
  60.2 3.5 %collective-permute-start.19 = (bf16[8,32,512]{2,1,0:T(8,128)(2,1)S(1)}, bf16[8,32,512]{2,1,0:T(8,128)(2,1)S(1)}, u32[]{:S(2)}, u32[]{:S(2)}) collective-permute-start(bf16[8,32,512]{2,1,0:T(8,128)(2,1)S(1)} %get-tuple-element.217), channel_id=1, source_target_pairs={{0,1},{1,0},{2,3},{3,2},{4,5},{5,4},{6,7},{7,6},{8,9},{9,8},{10,11... | collective-permute-start | bytes 786440 | tf_op jit(solution)/shard_map/ppermute | solution.py:459
  60.2 9.3 %collective-permute-start.22 = (bf16[8,32,512]{2,1,0:T(8,128)(2,1)S(1)}, bf16[8,32,512]{2,1,0:T(8,128)(2,1)S(1)}, u32[]{:S(2)}, u32[]{:S(2)}) collective-permute-start(bf16[8,32,512]{2,1,0:T(8,128)(2,1)S(1)} %get-tuple-element.223), channel_id=1, source_target_pairs={{0,1},{1,0},{2,3},{3,2},{4,5},{5,4},{6,7},{7,6},{8,9},{9,8},{10,11... | collective-permute-start | bytes 786440 | tf_op jit(solution)/shard_map/ppermute | solution.py:459
  63.6 5.3 %collective-permute-start.23 = (bf16[8,16,512]{2,1,0:T(8,128)(2,1)S(1)}, bf16[8,16,512]{2,1,0:T(8,128)(2,1)S(1)}, u32[]{:S(2)}, u32[]{:S(2)}) collective-permute-start(bf16[8,16,512]{2,1,0:T(8,128)(2,1)S(1)} %get-tuple-element.225), channel_id=1, source_target_pairs={{0,1},{1,0},{2,3},{3,2},{4,5},{5,4},{6,7},{7,6},{8,9},{9,8},{10,11... | collective-permute-start | bytes 393224 | tf_op jit(solution)/shard_map/ppermute | solution.py:459
  63.7 7.4 %collective-permute-start.12 = (bf16[2,64,512]{2,1,0:T(8,128)(2,1)S(1)}, bf16[2,64,512]{2,1,0:T(8,128)(2,1)S(1)}, u32[]{:S(2)}, u32[]{:S(2)}) collective-permute-start(bf16[2,64,512]{2,1,0:T(8,128)(2,1)S(1)} %get-tuple-element.205), channel_id=1, source_target_pairs={{0,2},{1,3},{2,0},{3,1},{4,6},{5,7},{6,4},{7,5},{8,10},{9,11},{10,... | collective-permute-start | bytes 393224 | tf_op jit(solution)/shard_map/ppermute | solution.py:459
  65.6 13.3 %collective-permute-start.20 = (bf16[256,512]{1,0:T(8,128)(2,1)S(1)}, bf16[256,512]{1,0:T(8,128)(2,1)S(1)}, u32[]{:S(2)}, u32[]{:S(2)}) collective-permute-start(bf16[256,512]{1,0:T(8,128)(2,1)S(1)} %get-tuple-element.219), channel_id=1, source_target_pairs={{0,2},{1,3},{2,0},{3,1},{4,6},{5,7},{6,4},{7,5},{8,10},{9,11},{10,... | collective-permute-start | bytes 786440 | tf_op jit(solution)/shard_map/ppermute | solution.py:459
  67.2 5.9 %collective-permute-start.9 = (bf16[2,80,512]{2,1,0:T(8,128)(2,1)S(1)}, bf16[2,80,512]{2,1,0:T(8,128)(2,1)S(1)}, u32[]{:S(2)}, u32[]{:S(2)}) collective-permute-start(bf16[2,80,512]{2,1,0:T(8,128)(2,1)S(1)} %get-tuple-element.199), channel_id=1, source_target_pairs={{0,4},{1,5},{2,6},{3,7},{4,0},{5,1},{6,2},{7,3},{8,12},{9,13},{10,... | collective-permute-start | bytes 491528 | tf_op jit(solution)/shard_map/ppermute | solution.py:459
  68.9 7.2 %collective-permute-start.15 = (bf16[2,80,512]{2,1,0:T(8,128)(2,1)S(1)}, bf16[2,80,512]{2,1,0:T(8,128)(2,1)S(1)}, u32[]{:S(2)}, u32[]{:S(2)}) collective-permute-start(bf16[2,80,512]{2,1,0:T(8,128)(2,1)S(1)} %get-tuple-element.211), channel_id=1, source_target_pairs={{0,16},{16,0},{1,17},{17,1},{2,18},{18,2},{3,19},{19,3},{4,20},{20... | collective-permute-start | bytes 491528 | tf_op jit(solution)/shard_map/ppermute | solution.py:458
  69.5 24.6 %collective-permute-start.6 = (bf16[576,512]{1,0:T(8,128)(2,1)S(1)}, bf16[576,512]{1,0:T(8,128)(2,1)S(1)}, u32[]{:S(2)}, u32[]{:S(2)}) collective-permute-start(bf16[576,512]{1,0:T(8,128)(2,1)S(1)} %get-tuple-element.190.refs_2_), channel_id=1, source_target_pairs={{0,16},{16,0},{1,17},{17,1},{2,18},{18,2},{3,19},{19,3},{4,20},{20... | collective-permute-start | bytes 1769480 | tf_op jit(solution)/shard_map/ppermute | solution.py:458
  71.1 8.6 %collective-permute-start.24 = (bf16[192,512]{1,0:T(8,128)(2,1)S(1)}, bf16[192,512]{1,0:T(8,128)(2,1)S(1)}, u32[]{:S(2)}, u32[]{:S(2)}) collective-permute-start(bf16[192,512]{1,0:T(8,128)(2,1)S(1)} %get-tuple-element.227), channel_id=1, source_target_pairs={{0,4},{1,5},{2,6},{3,7},{4,0},{5,1},{6,2},{7,3},{8,12},{9,13},{10,... | collective-permute-start | bytes 589832 | tf_op jit(solution)/shard_map/ppermute | solution.py:459
  76.2 11.6 %collective-permute-start.16 = (bf16[224,512]{1,0:T(8,128)(2,1)S(1)}, bf16[224,512]{1,0:T(8,128)(2,1)S(1)}, u32[]{:S(2)}, u32[]{:S(2)}) collective-permute-start(bf16[224,512]{1,0:T(8,128)(2,1)S(1)} %get-tuple-element.213), channel_id=1, source_target_pairs={{0,8},{1,9},{2,10},{3,11},{4,12},{5,13},{6,14},{7,15},{8,0},{9,1},... | collective-permute-start | bytes 688136 | tf_op jit(solution)/shard_map/ppermute | solution.py:459
  78.9 5.9 %collective-permute-start.21 = (bf16[128,512]{1,0:T(8,128)(2,1)S(1)}, bf16[128,512]{1,0:T(8,128)(2,1)S(1)}, u32[]{:S(2)}, u32[]{:S(2)}) collective-permute-start(bf16[128,512]{1,0:T(8,128)(2,1)S(1)} %get-tuple-element.221), channel_id=1, source_target_pairs={{0,4},{1,5},{2,6},{3,7},{4,0},{5,1},{6,2},{7,3},{8,12},{9,13},{10,... | collective-permute-start | bytes 393224 | tf_op jit(solution)/shard_map/ppermute | solution.py:459
  79.8 4.7 %collective-permute-start.25 = (bf16[96,512]{1,0:T(8,128)(2,1)S(1)}, bf16[96,512]{1,0:T(8,128)(2,1)S(1)}, u32[]{:S(2)}, u32[]{:S(2)}) collective-permute-start(bf16[96,512]{1,0:T(8,128)(2,1)S(1)} %get-tuple-element.229), channel_id=1, source_target_pairs={{0,2},{1,3},{2,0},{3,1},{4,6},{5,7},{6,4},{7,5},{8,10},{9,11},{10,... | collective-permute-start | bytes 294920 | tf_op jit(solution)/shard_map/ppermute | solution.py:459
  84.9 5.8 %collective-permute-start.26 = (bf16[112,512]{1,0:T(8,128)(2,1)S(1)}, bf16[112,512]{1,0:T(8,128)(2,1)S(1)}, u32[]{:S(2)}, u32[]{:S(2)}) collective-permute-start(bf16[112,512]{1,0:T(8,128)(2,1)S(1)} %get-tuple-element.231), channel_id=1, source_target_pairs={{0,8},{1,9},{2,10},{3,11},{4,12},{5,13},{6,14},{7,15},{8,0},{9,1},... | collective-permute-start | bytes 344072 | tf_op jit(solution)/shard_map/ppermute | solution.py:459
  87.8 9.0 %collective-permute-start.17 = (bf16[224,512]{1,0:T(8,128)(2,1)S(1)}, bf16[224,512]{1,0:T(8,128)(2,1)S(1)}, u32[]{:S(2)}, u32[]{:S(2)}) collective-permute-start(bf16[224,512]{1,0:T(8,128)(2,1)S(1)} %shard_map.307.refs_0_), channel_id=1, source_target_pairs={{0,16},{16,0},{1,17},{17,1},{2,18},{18,2},{3,19},{19,3},{4,20},{20... | collective-permute-start | bytes 688136 | tf_op jit(solution)/shard_map/ppermute | solution.py:458
  90.7 6.1 %collective-permute-start.27 = (bf16[112,512]{1,0:T(8,128)(2,1)S(1)}, bf16[112,512]{1,0:T(8,128)(2,1)S(1)}, u32[]{:S(2)}, u32[]{:S(2)}) collective-permute-start(bf16[112,512]{1,0:T(8,128)(2,1)S(1)} %shard_map.313.refs_2_), channel_id=1, source_target_pairs={{0,16},{16,0},{1,17},{17,1},{2,18},{18,2},{3,19},{19,3},{4,20},{20... | collective-permute-start | bytes 344072 | tf_op jit(solution)/shard_map/ppermute | solution.py:458

commit v7 on v6

--- a/solution.py
+++ b/solution.py
@@ -760,7 +760,6 @@
     padded = rows + 128
     groups = lax.axis_size("seg")
     recv_a = exchanged(packed(tokens, memory), "y")
-    recv_b = exchanged(packed(out_cotangent, memory_cotangent), "y")
     (
         memory, out_cotangent, memory_cotangent, out_weight, ffn_in, ffn_out, write_query,
         write_pair, write_out, write_gate, query_weight, pair_weight,
@@ -773,7 +772,16 @@
     )
     ag, fg, wg = attn_gain[None], ffn_gain[None], write_gain[None]
     v = lambda *arrs: [("v", a) for a in arrs]
-    h = lambda *arrs: [("h", a) for a in arrs]
+
+    def half_pack(place, a, b, pack):
+        pack[0:half, :] = a[1 - place[0]]
+        pack[half:, :] = b[1 - place[0]]
+
+    (pack,) = call(
+        half_pack, v(out_cotangent, memory_cotangent), [((half + mhalf, width), BF16)],
+        flops=10**6, nbytes=10**6,
+    )
+    recv_b = exchanged(pack, "y")
     deps = lambda *arrs: [("d", a) for a in arrs]
     big = ((rows, width), BF16)
     wide = ((padded, width), BF16)

time: 98.2 us -> 98.3 us (level)
  starting transfers between devices: 30.1 us -> 31.4 us
  Pallas kernels: 40.4 us -> 39.4 us
    ppermute x8, starting transfers between devices: 11.2 us -> 12.4 us  [exchanged(): return lax.ppermute(send, 'seq', other_of('seq', 1))]
    pallas_call x24 -> x25, Pallas kernels: 34.5 us -> 34.5 us  [call(): pl.pallas_call(kernel, out_shape=[shape(s, d) for s, d in outs], in_specs...]
  transfers between devices with their start and end apart: 28 -> 28, of which waited for: 14 -> 14; matrix products, arithmetic and copies ran while one was open for 0% -> 0% of each run, Pallas kernels for 33% -> 32%
where the time goes in v7:
time: 98.3 us; the launch traced here: 98.1 us
  Pallas kernels  39.4 us (40%)
  starting transfers between devices  31.4 us (32%)
  waiting for transfers between devices  25.5 us (26%)
  between operations  1.04 us (1%)
    pallas_call x25, Pallas kernels, call(): pl.pallas_call(kernel, out_shape=[shape(s, d) for s, d in outs], in_specs...  34.5 us
    ppermute x20, starting transfers between devices, exchanged(): lax.ppermute(send, 'seg', other_of('seg', {'x': 2, 'z': 4, 'h': 8, 'c': 1...  19 us
    ppermute x20, waiting for transfers between devices, exchanged(): lax.ppermute(send, 'seg', other_of('seg', {'x': 2, 'z': 4, 'h': 8, 'c': 1...  16.2 us
    ppermute x8, starting transfers between devices, exchanged(): return lax.ppermute(send, 'seq', other_of('seq', 1))  12.4 us
    ppermute x8, waiting for transfers between devices, exchanged(): return lax.ppermute(send, 'seq', other_of('seq', 1))  9.34 us
    pallas_call x1, Pallas kernels, fetched_weights(): pl.pallas_call(kernel, out_shape=[pltpu.VMEM(a.shape, a.dtype) for a in w...  3.92 us
  transfers between devices with their start and end apart: 28, of which 14 were waited for; matrix products, arithmetic and copies ran while one was open for 0% of the time, Pallas kernels for 32%

profile of v7, /device:TPU:0, one launch (start us, length us, event | category | flops | bytes accessed | tf_op | source)
XLA Modules:
  0.0 98.1 jit_solution(13901151201867910813)
XLA Ops:
  0.6 1.0 shard_map.289
  1.6 3.0 %collective-permute-start = (bf16[288,512]{1,0:T(8,128)(2,1)S(1)}, bf16[288,512]{1,0:T(8,128)(2,1)S(1)}, u32[]{:S(2)}, u32[]{:S(2)}) collective-permute-start(bf16[288,512]{1,0:T(8,128)(2,1)S(1)} %shard_map.289), channel_id=1, source_target_pairs={{0,16},{16,0},{1,17},{17,1},{2,18},{18,2},{3,19},{19,3},{4,20},{20... | collective-permute-start | bytes 884744 | tf_op jit(solution)/shard_map/ppermute | solution.py:458
  4.7 0.7 copy-done.1
  5.4 3.9 %shard_map.288 = (bf16[2,32,512]{2,1,0:T(8,128)(2,1)S(1)}, bf16[2,256,512]{2,1,0:T(8,128)(2,1)S(1)}, bf16[2,32,512]{2,1,0:T(8,128)(2,1)S(1)}, bf16[512,512]{1,0:...) custom-call(bf16[2,256,512]{2,1,0:T(8,128)(2,1)} %a.1, ...), custom_call_target="tpu_custom_call" | custom-call | flops 1000000000 | bytes 10000000 | tf_op jit(solution)/shard_map/pallas_call | solution.py:668
  9.4 2.7 %collective-permute-done.refs_7_ = bf16[288,512]{1,0:T(8,128)(2,1)S(1)} collective-permute-done((bf16[288,512]{1,0:T(8,128)(2,1)S(1)}, bf16[288,512]{1,0:T(8,128)(2,1)S(1)}, u32[]{:S(2)}, u32[]{:S(2)}) %collective-permute-start) | collective-permute-done | bytes 294944 | tf_op jit(solution)/shard_map/ppermute | solution.py:458
  12.1 10.5 %shard_map.290 = (bf16[512,512]{1,0:T(8,128)(2,1)S(1)}, bf16[64,512]{1,0:T(8,128)(2,1)S(1)}, bf16[640,512]{1,0:T(8,128)(2,1)S(1)}, bf16[512,512]{1,0:T(8,128)(2,...) custom-call(s32[2,8]{1,0:T(2,128)S(1)} %copy-done.4, ...), custom_call_target="tpu_custom_call" | custom-call | flops 12000000000 | bytes 20000000 | tf_op jit(solution)/shard_map/pallas_call | solution.py:64
  22.7 5.0 %shard_map.292 = (bf16[8,160,512]{2,1,0:T(8,128)(2,1)S(1)}, bf16[8,160,512]{2,1,0:T(8,128)(2,1)S(1)}, bf16[512,1024]{1,0:T(8,128)(2,1)S(1)}, bf16[64,512]{1,0:T(...) custom-call(bf16[512,512]{1,0:T(8,128)(2,1)S(1)} %get-tuple-element., ...), custom_call_target="tpu_custom_call" | custom-call | flops 6000000000 | bytes 10000000 | tf_op jit(solution)/shard_map/pallas_call | solution.py:64
  27.8 3.0 %shard_map.293 = (bf16[8,128,512]{2,1,0:T(8,128)(2,1)S(1)}, bf16[8,128,512]{2,1,0:T(8,128)(2,1)S(1)}, f32[512,512]{1,0:T(8,128)S(1)}, bf16[512,2048]{1,0:T(8,128)(2,1)S(1)}) custom-call(bf16[512,1024]{1,0:T(8,128)(2,1)S(1)} %get-tuple-element.152.refs_0_, bf16[512,1024]{1,0:T(8,128)(2,1)S(1)} %get-tuple-element.149.refs_5_.refs_1_, ...), custom_call_target="tpu_custom_call" | custom-call | flops 10000000000 | bytes 20000000 | tf_op jit(solution)/shard_map/pallas_call | solution.py:64
  30.8 0.6 collective-permute-start.3
  31.3 2.4 %shard_map.294 = (bf16[8,128,512]{2,1,0:T(8,128)(2,1)S(1)}, bf16[8,128,512]{2,1,0:T(8,128)(2,1)S(1)}, f32[512,512]{1,0:T(8,128)S(1)}) custom-call(bf16[512,2048]{1,0:T(8,128)(2,1)S(1)} %get-tuple-element.155.refs_0_, bf16[512,512]{1,0:T(8,128)(2,1)S(1)} %get-tuple-element.156.refs_1_, bf16[512,2048]{1,0:T(8,128)(2,1)S(1)} %get-tuple-element.140.refs_14_.refs_2_, ...), custom_call_target="tpu_custom_call" | custom-call | flops 1000000000 | bytes 20000000 | tf_op jit(solution)/shard_map/pallas_call | solution.py:64
  33.9 1.1 %shard_map.295 = (bf16[8,32,512]{2,1,0:T(8,128)(2,1)S(1)}, bf16[8,32,512]{2,1,0:T(8,128)(2,1)S(1)}, f32[512,512]{1,0:T(8,128)S(1)}, f32[1,512]{1,0:T(1,128)S(1)}) custom-call(f32[512,512]{1,0:T(8,128)S(1)} %get-tuple-element.158.refs_0_, f32[512,512]{1,0:T(8,128)S(1)} %get-tuple-element.159.refs_1_, f32[512,512]{1,0:T(8,128)S(1)} %get-tuple-element.160.refs_2_, ...), custom_call_target="tpu_custom_call" | custom-call | flops 100000000 | bytes 1000000 | tf_op jit(solution)/shard_map/pallas_call | solution.py:64
  34.9 0.6 collective-permute-start.5
  35.5 1.4 %collective-permute-done.5 = bf16[8,32,512]{2,1,0:T(8,128)(2,1)S(1)} collective-permute-done((bf16[8,32,512]{2,1,0:T(8,128)(2,1)S(1)}, bf16[8,32,512]{2,1,0:T(8,128)(2,1)S(1)}, u32[]{:S(2)}, u32[]{:S(2)}) %collective-permute-start.5) | collective-permute-done | bytes 262176 | tf_op jit(solution)/shard_map/ppermute | solution.py:459
  36.9 0.8 shard_map.296
  37.7 2.6 %collective-permute-start.10 = (bf16[2,2,2,64,512]{4,3,2,1,0:T(8,128)(2,1)S(1)}, bf16[2,2,2,64,512]{4,3,2,1,0:T(8,128)(2,1)S(1)}, u32[]{:S(2)}, u32[]{:S(2)}) collective-permute-start(bf16[2,2,2,64,512]{4,3,2,1,0:T(8,128)(2,1)S(1)} %get-tuple-element.201), channel_id=1, source_target_pairs={{0,16},{16,0},{1,17},{17,1},{2,18},{18,2},{3,19},{19,3},{4,20},{20... | collective-permute-start | bytes 1572872 | tf_op jit(solution)/shard_map/ppermute | solution.py:458
  40.3 1.5 %collective-permute-start.7 = (bf16[2,2,160,512]{3,2,1,0:T(8,128)(2,1)S(1)}, bf16[2,2,160,512]{3,2,1,0:T(8,128)(2,1)S(1)}, u32[]{:S(2)}, u32[]{:S(2)}) collective-permute-start(bf16[2,2,160,512]{3,2,1,0:T(8,128)(2,1)S(1)} %get-tuple-element.195), channel_id=1, source_target_pairs={{0,2},{1,3},{2,0},{3,1},{4,6},{5,7},{6,4},{7,5},{8,10},{9,11},{10,... | collective-permute-start | bytes 1966088 | tf_op jit(solution)/shard_map/ppermute | solution.py:459
  41.8 1.6 %collective-permute-start.13 = (bf16[2,2,160,512]{3,2,1,0:T(8,128)(2,1)S(1)}, bf16[2,2,160,512]{3,2,1,0:T(8,128)(2,1)S(1)}, u32[]{:S(2)}, u32[]{:S(2)}) collective-permute-start(bf16[2,2,160,512]{3,2,1,0:T(8,128)(2,1)S(1)} %get-tuple-element.207), channel_id=1, source_target_pairs={{0,4},{1,5},{2,6},{3,7},{4,0},{5,1},{6,2},{7,3},{8,12},{9,13},{10,... | collective-permute-start | bytes 1966088 | tf_op jit(solution)/shard_map/ppermute | solution.py:459
  43.4 5.1 %shard_map.297 = (bf16[512,512]{1,0:T(8,128)(2,1)S(1)}, bf16[640,512]{1,0:T(8,128)(2,1)S(1)}, bf16[640,512]{1,0:T(8,128)(2,1)S(1)}) custom-call(bf16[512,512]{1,0:T(8,128)(2,1)S(1)} %get-tuple-element.143.refs_0_, f32[512,512]{1,0:T(8,128)S(1)} %get-tuple-element.163.refs_1_.refs_11_, bf16[512,512]{1,0:T(8,128)(2,1)S(1)} %get-tuple-element.139.refs_12_.refs_2_, ...), custom_call_target="tpu_custom_call" | custom-call | flops 12000000000 | bytes 20000000 | tf_op jit(solution)/shard_map/pallas_call | solution.py:64
  48.4 2.9 %shard_map.298 = (bf16[8,32,512]{2,1,0:T(8,128)(2,1)S(1)}, bf16[8,32,512]{2,1,0:T(8,128)(2,1)S(1)}, bf16[8,32,512]{2,1,0:T(8,128)(2,1)S(1)}, bf16[8,32,512]{2,1,...) custom-call(bf16[640,512]{1,0:T(8,128)(2,1)S(1)} %get-tuple-element., ...), custom_call_target="tpu_custom_call" | custom-call | flops 6000000000 | bytes 20000000 | tf_op jit(solution)/shard_map/pallas_call | solution.py:64
  51.5 1.0 %collective-permute-done.10.refs_1_ = bf16[2,2,2,64,512]{4,3,2,1,0:T(8,128)(2,1)S(1)} collective-permute-done((bf16[2,2,2,64,512]{4,3,2,1,0:T(8,128)(2,1)S(1)}, bf16[2,2,2,64,512]{4,3,2,1,0:T(8,128)(2,1)S(1)}, u32[]{:S(2)}, u32[]{:S(2)}) %collective-permute-start.10) | collective-permute-done | bytes 524320 | tf_op jit(solution)/shard_map/ppermute | solution.py:458
  52.6 1.6 %collective-permute-start.11 = (bf16[2,2,64,512]{3,2,1,0:T(8,128)(2,1)S(1)}, bf16[2,2,64,512]{3,2,1,0:T(8,128)(2,1)S(1)}, u32[]{:S(2)}, u32[]{:S(2)}) collective-permute-start(bf16[2,2,64,512]{3,2,1,0:T(8,128)(2,1)S(1)} %get-tuple-element.203), channel_id=1, source_target_pairs={{0,4},{1,5},{2,6},{3,7},{4,0},{5,1},{6,2},{7,3},{8,12},{9,13},{10,... | collective-permute-start | bytes 786440 | tf_op jit(solution)/shard_map/ppermute | solution.py:459
  54.3 2.5 %collective-permute-done.7.refs_1_ = bf16[2,2,160,512]{3,2,1,0:T(8,128)(2,1)S(1)} collective-permute-done((bf16[2,2,160,512]{3,2,1,0:T(8,128)(2,1)S(1)}, bf16[2,2,160,512]{3,2,1,0:T(8,128)(2,1)S(1)}, u32[]{:S(2)}, u32[]{:S(2)}) %collective-permute-start.7) | collective-permute-done | bytes 655392 | tf_op jit(solution)/shard_map/ppermute | solution.py:459
  56.9 0.4 collective-permute-start.8
  57.4 2.1 %collective-permute-done.13.refs_1_ = bf16[2,2,160,512]{3,2,1,0:T(8,128)(2,1)S(1)} collective-permute-done((bf16[2,2,160,512]{3,2,1,0:T(8,128)(2,1)S(1)}, bf16[2,2,160,512]{3,2,1,0:T(8,128)(2,1)S(1)}, u32[]{:S(2)}, u32[]{:S(2)}) %collective-permute-start.13) | collective-permute-done | bytes 655392 | tf_op jit(solution)/shard_map/ppermute | solution.py:459
  59.6 0.6 collective-permute-start.14
  60.2 0.5 collective-permute-start.22
  60.7 2.9 %collective-permute-done.11.refs_1_ = bf16[2,2,64,512]{3,2,1,0:T(8,128)(2,1)S(1)} collective-permute-done((bf16[2,2,64,512]{3,2,1,0:T(8,128)(2,1)S(1)}, bf16[2,2,64,512]{3,2,1,0:T(8,128)(2,1)S(1)}, u32[]{:S(2)}, u32[]{:S(2)}) %collective-permute-start.11) | collective-permute-done | bytes 262176 | tf_op jit(solution)/shard_map/ppermute | solution.py:459
  63.7 0.6 collective-permute-start.12
  64.4 1.2 %collective-permute-done.8.refs_1_ = bf16[2,2,80,512]{3,2,1,0:T(8,128)(2,1)S(1)} collective-permute-done((bf16[2,2,80,512]{3,2,1,0:T(8,128)(2,1)S(1)}, bf16[2,2,80,512]{3,2,1,0:T(8,128)(2,1)S(1)}, u32[]{:S(2)}, u32[]{:S(2)}) %collective-permute-start.8) | collective-permute-done | bytes 327712 | tf_op jit(solution)/shard_map/ppermute | solution.py:458
  65.6 1.5 %collective-permute-start.20 = (bf16[256,512]{1,0:T(8,128)(2,1)S(1)}, bf16[256,512]{1,0:T(8,128)(2,1)S(1)}, u32[]{:S(2)}, u32[]{:S(2)}) collective-permute-start(bf16[256,512]{1,0:T(8,128)(2,1)S(1)} %get-tuple-element.219), channel_id=1, source_target_pairs={{0,2},{1,3},{2,0},{3,1},{4,6},{5,7},{6,4},{7,5},{8,10},{9,11},{10,... | collective-permute-start | bytes 786440 | tf_op jit(solution)/shard_map/ppermute | solution.py:459
  67.2 1.7 %collective-permute-start.9 = (bf16[2,80,512]{2,1,0:T(8,128)(2,1)S(1)}, bf16[2,80,512]{2,1,0:T(8,128)(2,1)S(1)}, u32[]{:S(2)}, u32[]{:S(2)}) collective-permute-start(bf16[2,80,512]{2,1,0:T(8,128)(2,1)S(1)} %get-tuple-element.199), channel_id=1, source_target_pairs={{0,4},{1,5},{2,6},{3,7},{4,0},{5,1},{6,2},{7,3},{8,12},{9,13},{10,... | collective-permute-start | bytes 491528 | tf_op jit(solution)/shard_map/ppermute | solution.py:459
  68.9 0.7 collective-permute-start.15
  69.7 1.3 %collective-permute-start.6 = (bf16[576,512]{1,0:T(8,128)(2,1)S(1)}, bf16[576,512]{1,0:T(8,128)(2,1)S(1)}, u32[]{:S(2)}, u32[]{:S(2)}) collective-permute-start(bf16[576,512]{1,0:T(8,128)(2,1)S(1)} %get-tuple-element.190.refs_2_), channel_id=1, source_target_pairs={{0,16},{16,0},{1,17},{17,1},{2,18},{18,2},{3,19},{19,3},{4,20},{20... | collective-permute-start | bytes 1769480 | tf_op jit(solution)/shard_map/ppermute | solution.py:458
  71.1 0.5 collective-permute-start.24
  71.6 1.5 %collective-permute-done.9.refs_1_ = bf16[2,80,512]{2,1,0:T(8,128)(2,1)S(1)} collective-permute-done((bf16[2,80,512]{2,1,0:T(8,128)(2,1)S(1)}, bf16[2,80,512]{2,1,0:T(8,128)(2,1)S(1)}, u32[]{:S(2)}, u32[]{:S(2)}) %collective-permute-start.9) | collective-permute-done | bytes 163872 | tf_op jit(solution)/shard_map/ppermute | solution.py:459
  73.1 3.0 %collective-permute-done.15.refs_5_ = bf16[2,80,512]{2,1,0:T(8,128)(2,1)S(1)} collective-permute-done((bf16[2,80,512]{2,1,0:T(8,128)(2,1)S(1)}, bf16[2,80,512]{2,1,0:T(8,128)(2,1)S(1)}, u32[]{:S(2)}, u32[]{:S(2)}) %collective-permute-start.15) | collective-permute-done | bytes 163872 | tf_op jit(solution)/shard_map/ppermute | solution.py:458
  76.2 2.6 %collective-permute-start.16 = (bf16[224,512]{1,0:T(8,128)(2,1)S(1)}, bf16[224,512]{1,0:T(8,128)(2,1)S(1)}, u32[]{:S(2)}, u32[]{:S(2)}) collective-permute-start(bf16[224,512]{1,0:T(8,128)(2,1)S(1)} %get-tuple-element.213), channel_id=1, source_target_pairs={{0,8},{1,9},{2,10},{3,11},{4,12},{5,13},{6,14},{7,15},{8,0},{9,1},... | collective-permute-start | bytes 688136 | tf_op jit(solution)/shard_map/ppermute | solution.py:459
  78.9 0.5 collective-permute-start.21
  79.8 1.5 %collective-permute-start.25 = (bf16[96,512]{1,0:T(8,128)(2,1)S(1)}, bf16[96,512]{1,0:T(8,128)(2,1)S(1)}, u32[]{:S(2)}, u32[]{:S(2)}) collective-permute-start(bf16[96,512]{1,0:T(8,128)(2,1)S(1)} %get-tuple-element.229), channel_id=1, source_target_pairs={{0,2},{1,3},{2,0},{3,1},{4,6},{5,7},{6,4},{7,5},{8,10},{9,11},{10,... | collective-permute-start | bytes 294920 | tf_op jit(solution)/shard_map/ppermute | solution.py:459
  81.3 3.2 %collective-permute-done.25.refs_3_ = bf16[96,512]{1,0:T(8,128)(2,1)S(1)} collective-permute-done((bf16[96,512]{1,0:T(8,128)(2,1)S(1)}, bf16[96,512]{1,0:T(8,128)(2,1)S(1)}, u32[]{:S(2)}, u32[]{:S(2)}) %collective-permute-start.25) | collective-permute-done | bytes 98336 | tf_op jit(solution)/shard_map/ppermute | solution.py:459
  84.5 0.4 collective-permute-done.21.refs_1_
  84.9 2.9 %collective-permute-start.26 = (bf16[112,512]{1,0:T(8,128)(2,1)S(1)}, bf16[112,512]{1,0:T(8,128)(2,1)S(1)}, u32[]{:S(2)}, u32[]{:S(2)}) collective-permute-start(bf16[112,512]{1,0:T(8,128)(2,1)S(1)} %get-tuple-element.231), channel_id=1, source_target_pairs={{0,8},{1,9},{2,10},{3,11},{4,12},{5,13},{6,14},{7,15},{8,0},{9,1},... | collective-permute-start | bytes 344072 | tf_op jit(solution)/shard_map/ppermute | solution.py:459
  87.8 0.8 collective-permute-start.17
  88.7 2.0 %collective-permute-done.26.refs_1_ = bf16[112,512]{1,0:T(8,128)(2,1)S(1)} collective-permute-done((bf16[112,512]{1,0:T(8,128)(2,1)S(1)}, bf16[112,512]{1,0:T(8,128)(2,1)S(1)}, u32[]{:S(2)}, u32[]{:S(2)}) %collective-permute-start.26) | collective-permute-done | bytes 114720 | tf_op jit(solution)/shard_map/ppermute | solution.py:459
  90.7 3.4 %collective-permute-start.27 = (bf16[112,512]{1,0:T(8,128)(2,1)S(1)}, bf16[112,512]{1,0:T(8,128)(2,1)S(1)}, u32[]{:S(2)}, u32[]{:S(2)}) collective-permute-start(bf16[112,512]{1,0:T(8,128)(2,1)S(1)} %shard_map.313.refs_2_), channel_id=1, source_target_pairs={{0,16},{16,0},{1,17},{17,1},{2,18},{18,2},{3,19},{19,3},{4,20},{20... | collective-permute-start | bytes 344072 | tf_op jit(solution)/shard_map/ppermute | solution.py:458
  94.1 1.3 %shard_map.299 = (f32[2,256,512]{2,1,0:T(8,128)}, bf16[2,32,512]{2,1,0:T(8,128)(2,1)}, f32[2,32,512]{2,1,0:T(8,128)}, bf16[2,256,512]{2,1,0:T(8,128)(2,1)}) custom-call(f32[256,512]{1,0:T(8,128)S(1)} %get-tuple-element.186.refs_0_, bf16[32,512]{1,0:T(8,128)(2,1)S(1)} %get-tuple-element.187.refs_1_, f32[32,512]{1,0:T(8,128)S(1)} %get-tuple-element.188.refs_2_, ...), custom_call_target="tpu_custom_call" | custom-call | flops 1000000 | bytes 1000000 | tf_op jit(solution)/shard_map/pallas_call | solution.py:64
  95.4 1.4 %collective-permute-done.27.refs_3_ = bf16[112,512]{1,0:T(8,128)(2,1)S(1)} collective-permute-done((bf16[112,512]{1,0:T(8,128)(2,1)S(1)}, bf16[112,512]{1,0:T(8,128)(2,1)S(1)}, u32[]{:S(2)}, u32[]{:S(2)}) %collective-permute-start.27) | collective-permute-done | bytes 114720 | tf_op jit(solution)/shard_map/ppermute | solution.py:458
  96.9 1.0 %shard_map.314 = (f32[32,512]{1,0:T(8,128)}, f32[32,1024]{1,0:T(8,128)}, f32[32,512]{1,0:T(8,128)}, f32[32,2048]{1,0:T(8,128)}, f32[128,512]{1,0:T(8,128)}, /*in...) custom-call(bf16[224,512]{1,0:T(8,128)(2,1)S(1)} %shard_map.307.refs, ...), custom_call_target="tpu_custom_call" | custom-call | flops 1000000 | bytes 1000000 | tf_op jit(solution)/shard_map/pallas_call | solution.py:64
  (45 shorter events, 1.9 us)
Async XLA Ops:
  1.6 10.4 %collective-permute-start = (bf16[288,512]{1,0:T(8,128)(2,1)S(1)}, bf16[288,512]{1,0:T(8,128)(2,1)S(1)}, u32[]{:S(2)}, u32[]{:S(2)}) collective-permute-start(bf16[288,512]{1,0:T(8,128)(2,1)S(1)} %shard_map.289), channel_id=1, source_target_pairs={{0,16},{16,0},{1,17},{17,1},{2,18},{18,2},{3,19},{19,3},{4,20},{20... | collective-permute-start | bytes 884744 | tf_op jit(solution)/shard_map/ppermute | solution.py:458
  4.7 0.7 copy-start.1
  5.3 6.7 %copy-start = (f32[512]{0:T(512)S(1)}, f32[512]{0:T(512)}, u32[]{:S(2)}) copy-start(f32[512]{0:T(512)} %param.24) | copy-start | bytes 6148
  5.3 6.7 %copy-start.2 = (f32[512]{0:T(512)S(1)}, f32[512]{0:T(512)}, u32[]{:S(2)}) copy-start(f32[512]{0:T(512)} %param.20) | copy-start | bytes 6148
  5.4 6.7 %copy-start.4 = (s32[2,8]{1,0:T(2,128)S(1)}, s32[2,8]{1,0:T(2,128)}, u32[]{:S(2)}) copy-start(s32[2,8]{1,0:T(2,128)} %refs_0_.3) | copy-start | bytes 196
  9.3 13.3 %collective-permute-start.1 = (bf16[288,512]{1,0:T(8,128)(2,1)S(1)}, bf16[288,512]{1,0:T(8,128)(2,1)S(1)}, u32[]{:S(2)}, u32[]{:S(2)}) collective-permute-start(bf16[288,512]{1,0:T(8,128)(2,1)S(1)} %shard_map.291), channel_id=1, source_target_pairs={{0,16},{16,0},{1,17},{17,1},{2,18},{18,2},{3,19},{19,3},{4,20},{20... | collective-permute-start | bytes 884744 | tf_op jit(solution)/shard_map/ppermute | solution.py:458
  12.1 10.6 %copy-start.3 = (f32[512]{0:T(512)S(1)}, f32[512]{0:T(512)}, u32[]{:S(2)}) copy-start(f32[512]{0:T(512)} %param.31) | copy-start | bytes 6148
  27.7 3.7 %collective-permute-start.2 = (bf16[8,160,512]{2,1,0:T(8,128)(2,1)S(1)}, bf16[8,160,512]{2,1,0:T(8,128)(2,1)S(1)}, u32[]{:S(2)}, u32[]{:S(2)}) collective-permute-start(bf16[8,160,512]{2,1,0:T(8,128)(2,1)S(1)} %get-tuple-element.157), channel_id=1, source_target_pairs={{0,1},{1,0},{2,3},{3,2},{4,5},{5,4},{6,7},{7,6},{8,9},{9,8},{10,11... | collective-permute-start | bytes 3932168 | tf_op jit(solution)/shard_map/ppermute | solution.py:459
  30.8 3.1 %collective-permute-start.3 = (bf16[8,128,512]{2,1,0:T(8,128)(2,1)S(1)}, bf16[8,128,512]{2,1,0:T(8,128)(2,1)S(1)}, u32[]{:S(2)}, u32[]{:S(2)}) collective-permute-start(bf16[8,128,512]{2,1,0:T(8,128)(2,1)S(1)} %get-tuple-element.162), channel_id=1, source_target_pairs={{0,1},{1,0},{2,3},{3,2},{4,5},{5,4},{6,7},{7,6},{8,9},{9,8},{10,11... | collective-permute-start | bytes 3145736 | tf_op jit(solution)/shard_map/ppermute | solution.py:459
  33.8 3.1 %collective-permute-start.4 = (bf16[8,128,512]{2,1,0:T(8,128)(2,1)S(1)}, bf16[8,128,512]{2,1,0:T(8,128)(2,1)S(1)}, u32[]{:S(2)}, u32[]{:S(2)}) collective-permute-start(bf16[8,128,512]{2,1,0:T(8,128)(2,1)S(1)} %get-tuple-element.172), channel_id=1, source_target_pairs={{0,1},{1,0},{2,3},{3,2},{4,5},{5,4},{6,7},{7,6},{8,9},{9,8},{10,11... | collective-permute-start | bytes 3145736 | tf_op jit(solution)/shard_map/ppermute | solution.py:459
  34.9 2.0 %collective-permute-start.5 = (bf16[8,32,512]{2,1,0:T(8,128)(2,1)S(1)}, bf16[8,32,512]{2,1,0:T(8,128)(2,1)S(1)}, u32[]{:S(2)}, u32[]{:S(2)}) collective-permute-start(bf16[8,32,512]{2,1,0:T(8,128)(2,1)S(1)} %get-tuple-element.175), channel_id=1, source_target_pairs={{0,1},{1,0},{2,3},{3,2},{4,5},{5,4},{6,7},{7,6},{8,9},{9,8},{10,11... | collective-permute-start | bytes 786440 | tf_op jit(solution)/shard_map/ppermute | solution.py:459
  37.7 14.8 %collective-permute-start.10 = (bf16[2,2,2,64,512]{4,3,2,1,0:T(8,128)(2,1)S(1)}, bf16[2,2,2,64,512]{4,3,2,1,0:T(8,128)(2,1)S(1)}, u32[]{:S(2)}, u32[]{:S(2)}) collective-permute-start(bf16[2,2,2,64,512]{4,3,2,1,0:T(8,128)(2,1)S(1)} %get-tuple-element.201), channel_id=1, source_target_pairs={{0,16},{16,0},{1,17},{17,1},{2,18},{18,2},{3,19},{19,3},{4,20},{20... | collective-permute-start | bytes 1572872 | tf_op jit(solution)/shard_map/ppermute | solution.py:458
  40.3 16.5 %collective-permute-start.7 = (bf16[2,2,160,512]{3,2,1,0:T(8,128)(2,1)S(1)}, bf16[2,2,160,512]{3,2,1,0:T(8,128)(2,1)S(1)}, u32[]{:S(2)}, u32[]{:S(2)}) collective-permute-start(bf16[2,2,160,512]{3,2,1,0:T(8,128)(2,1)S(1)} %get-tuple-element.195), channel_id=1, source_target_pairs={{0,2},{1,3},{2,0},{3,1},{4,6},{5,7},{6,4},{7,5},{8,10},{9,11},{10,... | collective-permute-start | bytes 1966088 | tf_op jit(solution)/shard_map/ppermute | solution.py:459
  41.8 17.7 %collective-permute-start.13 = (bf16[2,2,160,512]{3,2,1,0:T(8,128)(2,1)S(1)}, bf16[2,2,160,512]{3,2,1,0:T(8,128)(2,1)S(1)}, u32[]{:S(2)}, u32[]{:S(2)}) collective-permute-start(bf16[2,2,160,512]{3,2,1,0:T(8,128)(2,1)S(1)} %get-tuple-element.207), channel_id=1, source_target_pairs={{0,4},{1,5},{2,6},{3,7},{4,0},{5,1},{6,2},{7,3},{8,12},{9,13},{10,... | collective-permute-start | bytes 1966088 | tf_op jit(solution)/shard_map/ppermute | solution.py:459
  51.4 8.8 %collective-permute-start.18 = (bf16[8,32,512]{2,1,0:T(8,128)(2,1)S(1)}, bf16[8,32,512]{2,1,0:T(8,128)(2,1)S(1)}, u32[]{:S(2)}, u32[]{:S(2)}) collective-permute-start(bf16[8,32,512]{2,1,0:T(8,128)(2,1)S(1)} %get-tuple-element.215), channel_id=1, source_target_pairs={{0,1},{1,0},{2,3},{3,2},{4,5},{5,4},{6,7},{7,6},{8,9},{9,8},{10,11... | collective-permute-start | bytes 786440 | tf_op jit(solution)/shard_map/ppermute | solution.py:459
  52.6 11.0 %collective-permute-start.11 = (bf16[2,2,64,512]{3,2,1,0:T(8,128)(2,1)S(1)}, bf16[2,2,64,512]{3,2,1,0:T(8,128)(2,1)S(1)}, u32[]{:S(2)}, u32[]{:S(2)}) collective-permute-start(bf16[2,2,64,512]{3,2,1,0:T(8,128)(2,1)S(1)} %get-tuple-element.203), channel_id=1, source_target_pairs={{0,4},{1,5},{2,6},{3,7},{4,0},{5,1},{6,2},{7,3},{8,12},{9,13},{10,... | collective-permute-start | bytes 786440 | tf_op jit(solution)/shard_map/ppermute | solution.py:459
  56.9 8.7 %collective-permute-start.8 = (bf16[2,2,80,512]{3,2,1,0:T(8,128)(2,1)S(1)}, bf16[2,2,80,512]{3,2,1,0:T(8,128)(2,1)S(1)}, u32[]{:S(2)}, u32[]{:S(2)}) collective-permute-start(bf16[2,2,80,512]{3,2,1,0:T(8,128)(2,1)S(1)} %get-tuple-element.197), channel_id=1, source_target_pairs={{0,16},{16,0},{1,17},{17,1},{2,18},{18,2},{3,19},{19,3},{4,20},{20... | collective-permute-start | bytes 983048 | tf_op jit(solution)/shard_map/ppermute | solution.py:458
  59.6 7.6 %collective-permute-start.14 = (bf16[2,160,512]{2,1,0:T(8,128)(2,1)S(1)}, bf16[2,160,512]{2,1,0:T(8,128)(2,1)S(1)}, u32[]{:S(2)}, u32[]{:S(2)}) collective-permute-start(bf16[2,160,512]{2,1,0:T(8,128)(2,1)S(1)} %get-tuple-element.209), channel_id=1, source_target_pairs={{0,2},{1,3},{2,0},{3,1},{4,6},{5,7},{6,4},{7,5},{8,10},{9,11},{10,... | collective-permute-start | bytes 983048 | tf_op jit(solution)/shard_map/ppermute | solution.py:459
  60.2 3.5 %collective-permute-start.19 = (bf16[8,32,512]{2,1,0:T(8,128)(2,1)S(1)}, bf16[8,32,512]{2,1,0:T(8,128)(2,1)S(1)}, u32[]{:S(2)}, u32[]{:S(2)}) collective-permute-start(bf16[8,32,512]{2,1,0:T(8,128)(2,1)S(1)} %get-tuple-element.217), channel_id=1, source_target_pairs={{0,1},{1,0},{2,3},{3,2},{4,5},{5,4},{6,7},{7,6},{8,9},{9,8},{10,11... | collective-permute-start | bytes 786440 | tf_op jit(solution)/shard_map/ppermute | solution.py:459
  60.2 9.5 %collective-permute-start.22 = (bf16[8,32,512]{2,1,0:T(8,128)(2,1)S(1)}, bf16[8,32,512]{2,1,0:T(8,128)(2,1)S(1)}, u32[]{:S(2)}, u32[]{:S(2)}) collective-permute-start(bf16[8,32,512]{2,1,0:T(8,128)(2,1)S(1)} %get-tuple-element.223), channel_id=1, source_target_pairs={{0,1},{1,0},{2,3},{3,2},{4,5},{5,4},{6,7},{7,6},{8,9},{9,8},{10,11... | collective-permute-start | bytes 786440 | tf_op jit(solution)/shard_map/ppermute | solution.py:459
  63.6 5.3 %collective-permute-start.23 = (bf16[8,16,512]{2,1,0:T(8,128)(2,1)S(1)}, bf16[8,16,512]{2,1,0:T(8,128)(2,1)S(1)}, u32[]{:S(2)}, u32[]{:S(2)}) collective-permute-start(bf16[8,16,512]{2,1,0:T(8,128)(2,1)S(1)} %get-tuple-element.225), channel_id=1, source_target_pairs={{0,1},{1,0},{2,3},{3,2},{4,5},{5,4},{6,7},{7,6},{8,9},{9,8},{10,11... | collective-permute-start | bytes 393224 | tf_op jit(solution)/shard_map/ppermute | solution.py:459
  63.7 7.4 %collective-permute-start.12 = (bf16[2,64,512]{2,1,0:T(8,128)(2,1)S(1)}, bf16[2,64,512]{2,1,0:T(8,128)(2,1)S(1)}, u32[]{:S(2)}, u32[]{:S(2)}) collective-permute-start(bf16[2,64,512]{2,1,0:T(8,128)(2,1)S(1)} %get-tuple-element.205), channel_id=1, source_target_pairs={{0,2},{1,3},{2,0},{3,1},{4,6},{5,7},{6,4},{7,5},{8,10},{9,11},{10,... | collective-permute-start | bytes 393224 | tf_op jit(solution)/shard_map/ppermute | solution.py:459
  65.6 13.3 %collective-permute-start.20 = (bf16[256,512]{1,0:T(8,128)(2,1)S(1)}, bf16[256,512]{1,0:T(8,128)(2,1)S(1)}, u32[]{:S(2)}, u32[]{:S(2)}) collective-permute-start(bf16[256,512]{1,0:T(8,128)(2,1)S(1)} %get-tuple-element.219), channel_id=1, source_target_pairs={{0,2},{1,3},{2,0},{3,1},{4,6},{5,7},{6,4},{7,5},{8,10},{9,11},{10,... | collective-permute-start | bytes 786440 | tf_op jit(solution)/shard_map/ppermute | solution.py:459
  67.2 5.9 %collective-permute-start.9 = (bf16[2,80,512]{2,1,0:T(8,128)(2,1)S(1)}, bf16[2,80,512]{2,1,0:T(8,128)(2,1)S(1)}, u32[]{:S(2)}, u32[]{:S(2)}) collective-permute-start(bf16[2,80,512]{2,1,0:T(8,128)(2,1)S(1)} %get-tuple-element.199), channel_id=1, source_target_pairs={{0,4},{1,5},{2,6},{3,7},{4,0},{5,1},{6,2},{7,3},{8,12},{9,13},{10,... | collective-permute-start | bytes 491528 | tf_op jit(solution)/shard_map/ppermute | solution.py:459
  68.9 7.2 %collective-permute-start.15 = (bf16[2,80,512]{2,1,0:T(8,128)(2,1)S(1)}, bf16[2,80,512]{2,1,0:T(8,128)(2,1)S(1)}, u32[]{:S(2)}, u32[]{:S(2)}) collective-permute-start(bf16[2,80,512]{2,1,0:T(8,128)(2,1)S(1)} %get-tuple-element.211), channel_id=1, source_target_pairs={{0,16},{16,0},{1,17},{17,1},{2,18},{18,2},{3,19},{19,3},{4,20},{20... | collective-permute-start | bytes 491528 | tf_op jit(solution)/shard_map/ppermute | solution.py:458
  69.7 24.4 %collective-permute-start.6 = (bf16[576,512]{1,0:T(8,128)(2,1)S(1)}, bf16[576,512]{1,0:T(8,128)(2,1)S(1)}, u32[]{:S(2)}, u32[]{:S(2)}) collective-permute-start(bf16[576,512]{1,0:T(8,128)(2,1)S(1)} %get-tuple-element.190.refs_2_), channel_id=1, source_target_pairs={{0,16},{16,0},{1,17},{17,1},{2,18},{18,2},{3,19},{19,3},{4,20},{20... | collective-permute-start | bytes 1769480 | tf_op jit(solution)/shard_map/ppermute | solution.py:458
  71.1 8.6 %collective-permute-start.24 = (bf16[192,512]{1,0:T(8,128)(2,1)S(1)}, bf16[192,512]{1,0:T(8,128)(2,1)S(1)}, u32[]{:S(2)}, u32[]{:S(2)}) collective-permute-start(bf16[192,512]{1,0:T(8,128)(2,1)S(1)} %get-tuple-element.227), channel_id=1, source_target_pairs={{0,4},{1,5},{2,6},{3,7},{4,0},{5,1},{6,2},{7,3},{8,12},{9,13},{10,... | collective-permute-start | bytes 589832 | tf_op jit(solution)/shard_map/ppermute | solution.py:459
  76.2 11.6 %collective-permute-start.16 = (bf16[224,512]{1,0:T(8,128)(2,1)S(1)}, bf16[224,512]{1,0:T(8,128)(2,1)S(1)}, u32[]{:S(2)}, u32[]{:S(2)}) collective-permute-start(bf16[224,512]{1,0:T(8,128)(2,1)S(1)} %get-tuple-element.213), channel_id=1, source_target_pairs={{0,8},{1,9},{2,10},{3,11},{4,12},{5,13},{6,14},{7,15},{8,0},{9,1},... | collective-permute-start | bytes 688136 | tf_op jit(solution)/shard_map/ppermute | solution.py:459
  78.9 5.9 %collective-permute-start.21 = (bf16[128,512]{1,0:T(8,128)(2,1)S(1)}, bf16[128,512]{1,0:T(8,128)(2,1)S(1)}, u32[]{:S(2)}, u32[]{:S(2)}) collective-permute-start(bf16[128,512]{1,0:T(8,128)(2,1)S(1)} %get-tuple-element.221), channel_id=1, source_target_pairs={{0,4},{1,5},{2,6},{3,7},{4,0},{5,1},{6,2},{7,3},{8,12},{9,13},{10,... | collective-permute-start | bytes 393224 | tf_op jit(solution)/shard_map/ppermute | solution.py:459
  79.8 4.7 %collective-permute-start.25 = (bf16[96,512]{1,0:T(8,128)(2,1)S(1)}, bf16[96,512]{1,0:T(8,128)(2,1)S(1)}, u32[]{:S(2)}, u32[]{:S(2)}) collective-permute-start(bf16[96,512]{1,0:T(8,128)(2,1)S(1)} %get-tuple-element.229), channel_id=1, source_target_pairs={{0,2},{1,3},{2,0},{3,1},{4,6},{5,7},{6,4},{7,5},{8,10},{9,11},{10,... | collective-permute-start | bytes 294920 | tf_op jit(solution)/shard_map/ppermute | solution.py:459
  84.9 5.8 %collective-permute-start.26 = (bf16[112,512]{1,0:T(8,128)(2,1)S(1)}, bf16[112,512]{1,0:T(8,128)(2,1)S(1)}, u32[]{:S(2)}, u32[]{:S(2)}) collective-permute-start(bf16[112,512]{1,0:T(8,128)(2,1)S(1)} %get-tuple-element.231), channel_id=1, source_target_pairs={{0,8},{1,9},{2,10},{3,11},{4,12},{5,13},{6,14},{7,15},{8,0},{9,1},... | collective-permute-start | bytes 344072 | tf_op jit(solution)/shard_map/ppermute | solution.py:459
  87.8 9.0 %collective-permute-start.17 = (bf16[224,512]{1,0:T(8,128)(2,1)S(1)}, bf16[224,512]{1,0:T(8,128)(2,1)S(1)}, u32[]{:S(2)}, u32[]{:S(2)}) collective-permute-start(bf16[224,512]{1,0:T(8,128)(2,1)S(1)} %shard_map.307.refs_0_), channel_id=1, source_target_pairs={{0,16},{16,0},{1,17},{17,1},{2,18},{18,2},{3,19},{19,3},{4,20},{20... | collective-permute-start | bytes 688136 | tf_op jit(solution)/shard_map/ppermute | solution.py:458
  90.7 6.2 %collective-permute-start.27 = (bf16[112,512]{1,0:T(8,128)(2,1)S(1)}, bf16[112,512]{1,0:T(8,128)(2,1)S(1)}, u32[]{:S(2)}, u32[]{:S(2)}) collective-permute-start(bf16[112,512]{1,0:T(8,128)(2,1)S(1)} %shard_map.313.refs_2_), channel_id=1, source_target_pairs={{0,16},{16,0},{1,17},{17,1},{2,18},{18,2},{3,19},{19,3},{4,20},{20... | collective-permute-start | bytes 344072 | tf_op jit(solution)/shard_map/ppermute | solution.py:458
